TPU v7x, 256 devices: a whole 4x4x8 slice. The times are simulated.
256 devices in a mesh: dp: 32 (over z, y), seq: 8 (over x, core).
Axes of the slice: x: 4, y: 4, z: 8, core: 2. Of those that a mesh axis runs over, the one named last changes fastest.
Arguments:
- qkv_time: bfloat16 [3, 32, 8, 128, 1536], P(None, 'dp', 'seq'), may hold values from -6 to 6
- shard_sizes: int32 [32, 8], P('dp'), may hold values from 1 to 32, 128 in all within a row
- bias_time: float32 [12, 15], replicated, may hold values from -4 to 4
- w_out: bfloat16 [1536, 1536], P(('dp', 'seq')), may hold values from -0.15625 to 0.15625
- cot_out: bfloat16 [32, 8, 8, 32, 1536], P('dp', 'seq'), may hold values from -17 to 17
Outputs:
- grad_qkv_time: bfloat16 [3, 32, 8, 128, 1536], P(None, 'dp', 'seq')
- grad_bias_time: float32 [12, 15], replicated
- grad_w_out: float32 [1536, 1536], P(('dp', 'seq'))
Inputs may be any that keep to these rules, and one draw needn't show every extreme that they name: `shard_sizes`: each clip's 8 sizes sum to 128 and the largest is exactly 32; seq device j holds the positions that follow the first j shards.
All inputs are finite; a program needn't handle non-finite values.
Results may differ from a plain program's by a relative error of at most 0.0058.
Values may be sent and summed in bfloat16 or wider, within the bound.
No kernel may reach another device: no remote copies, remote signals or barrier semaphores. Data moves between devices by JAX's collectives and lax.ppermute only.
A program may use at most 128 MiB of HBM per device.

v0:
```python
import math

import jax
import jax.numpy as jnp
from jax import lax
from jax.sharding import PartitionSpec as P


def offset_table(count):
    index_row = jnp.arange(count, dtype=jnp.int32)
    shifted = index_row[None, :] - index_row[:, None] + count - 1
    labels = jnp.arange(2 * count - 1, dtype=jnp.int32)
    return (shifted[None, :, :] == labels[:, None, None]).astype(jnp.float32)


def normalize(scores):
    row_top = jnp.max(scores, axis=-1, keepdims=True)
    weights = jnp.exp(scores - row_top)
    return weights / jnp.sum(weights, axis=-1, keepdims=True)


def time_forward(queries, keys_in, values, pair_bias):
    frame_n, length, width = queries.shape
    heads_n = pair_bias.shape[0]
    head_len = width // heads_n
    factor = 1.0 / math.sqrt(head_len)
    q_heads = queries.reshape(frame_n, length, heads_n, head_len)
    k_heads = keys_in.reshape(frame_n, length, heads_n, head_len)
    v_heads = values.reshape(frame_n, length, heads_n, head_len)
    scores = (
        jnp.einsum("fshd,gshd->shfg", q_heads, k_heads, preferred_element_type=jnp.float32) * factor
    )
    probs_full = normalize(scores + pair_bias[None])
    probs_low = probs_full.astype(jnp.bfloat16)
    mixed = jnp.einsum("shfg,gshd->fshd", probs_low, v_heads, preferred_element_type=jnp.float32)
    return (probs_full, probs_low, mixed.reshape(frame_n, length, width).astype(jnp.bfloat16))


def time_backward(queries, keys_in, values, d_mixed, probs_full, probs_low):
    frame_n, length, width = queries.shape
    heads_n = probs_full.shape[1]
    head_len = width // heads_n
    factor = 1.0 / math.sqrt(head_len)
    q_heads = queries.reshape(frame_n, length, heads_n, head_len)
    k_heads = keys_in.reshape(frame_n, length, heads_n, head_len)
    v_heads = values.reshape(frame_n, length, heads_n, head_len)
    d_heads = d_mixed.reshape(frame_n, length, heads_n, head_len)
    grad_v = jnp.einsum("shfg,fshd->gshd", probs_low, d_heads, preferred_element_type=jnp.float32)
    grad_p = jnp.einsum("fshd,gshd->shfg", d_heads, v_heads, preferred_element_type=jnp.float32)
    grad_s = probs_full * (grad_p - jnp.sum(probs_full * grad_p, axis=-1, keepdims=True))
    grad_low = grad_s.astype(jnp.bfloat16)
    grad_q = (
        jnp.einsum("shfg,gshd->fshd", grad_low, k_heads, preferred_element_type=jnp.float32)
        * factor
    )
    grad_k = (
        jnp.einsum("shfg,fshd->gshd", grad_low, q_heads, preferred_element_type=jnp.float32)
        * factor
    )
    grads = (
        jnp.stack([grad_q, grad_k, grad_v]).reshape(3, frame_n, length, width).astype(jnp.bfloat16)
    )
    return (grads, jnp.sum(grad_s, axis=0))


def per_device(qkv_time, shard_sizes, bias_time, w_out, cot_out):
    seq_count = lax.axis_size("seq")
    frames_dev = qkv_time.shape[2]
    length = qkv_time.shape[3]
    width = qkv_time.shape[4]
    frame_total = frames_dev * seq_count
    capacity = cot_out.shape[3]
    out_width = cot_out.shape[4]
    counts = shard_sizes[0]
    starts = jnp.cumsum(counts) - counts
    slot_ids = jnp.arange(capacity, dtype=jnp.int32)
    wanted = jnp.minimum(starts[:, None] + slot_ids[None, :], length - 1).reshape(-1)
    picked = jnp.take(qkv_time[:, 0], wanted, axis=2).reshape(
        3, frames_dev, seq_count, capacity, width
    )
    arrived = lax.all_to_all(picked, "seq", split_axis=2, concat_axis=1, tiled=True).reshape(
        3, frame_total, capacity, width
    )
    seq_rank = lax.axis_index("seq")
    shard_ids = jnp.arange(seq_count, dtype=jnp.int32)
    own_count = jnp.sum(jnp.where(shard_ids == seq_rank, counts, 0))
    live_slots = slot_ids < own_count
    upstream = jnp.where(live_slots[None, :, None], cot_out[0, 0], jnp.zeros((), jnp.bfloat16))
    up_rows = upstream.reshape(frame_total * capacity, out_width)
    d_mixed = lax.dot_general(
        up_rows,
        lax.all_gather(w_out, ("dp", "seq"), axis=0, tiled=True),
        (((1,), (1,)), ((), ())),
        preferred_element_type=jnp.float32,
    )
    d_mixed = d_mixed.astype(jnp.bfloat16).reshape(frame_total, capacity, width)
    time_table = offset_table(frame_total)
    pair_bias = jnp.einsum("ho,ofg->hfg", bias_time, time_table, precision=lax.Precision.HIGHEST)
    probs_full, probs_low, mixed = time_forward(arrived[0], arrived[1], arrived[2], pair_bias)
    mixed_rows = mixed.reshape(frame_total * capacity, width)
    grad_w_out = lax.psum_scatter(
        lax.dot_general(
            mixed_rows, up_rows, (((0,), (0,)), ((), ())), preferred_element_type=jnp.float32
        ),
        ("dp", "seq"),
        scatter_dimension=0,
        tiled=True,
    )
    time_grads, pair_sums = time_backward(
        arrived[0], arrived[1], arrived[2], d_mixed, probs_full, probs_low
    )
    leaving = time_grads.reshape(3, seq_count, frames_dev, capacity, width)
    returned = lax.all_to_all(leaving, "seq", split_axis=1, concat_axis=3, tiled=True).reshape(
        3, frames_dev, seq_count * capacity, width
    )
    position = jnp.arange(length, dtype=jnp.int32)
    inside = (position[:, None] >= starts[None, :]) & (
        position[:, None] < (starts + counts)[None, :]
    )
    owners = jnp.sum(jnp.where(inside, shard_ids[None, :], 0), axis=1)
    first_pos = jnp.sum(jnp.where(inside, starts[None, :], 0), axis=1)
    flat_index = owners * capacity + position - first_pos
    grad_qkv_time = jnp.take(returned, flat_index, axis=2)[:, None]
    pair_grand = lax.psum(pair_sums, ("dp", "seq"))
    grad_bias_time = jnp.einsum(
        "hfg,ofg->ho", pair_grand, time_table, precision=lax.Precision.HIGHEST
    )
    return (grad_qkv_time, grad_bias_time, grad_w_out)


def solution(mesh):
    placed = (
        P(None, "dp", "seq", None, None),
        P("dp", None),
        P(),
        P(("dp", "seq"), None),
        P("dp", "seq", None, None, None),
    )
    return jax.shard_map(
        per_device,
        mesh=mesh,
        in_specs=placed,
        out_specs=(P(None, "dp", "seq", None, None), P(), P(("dp", "seq"), None)),
        check_vma=False,
    )
```

profile of v0, /device:TPU:32, one launch (start us, length us, event | category | flops | bytes accessed | tf_op | source)
XLA Modules:
  0.0 1549.7 jit_solution(931333410325470874)
XLA Ops:
  12.5 4.8 gather_fusion
  17.4 4.0 copy_select_fusion
  21.4 4.4 all-to-all-start
  27.9 28.1 %all-to-all-done = bf16[3,1,8,32,1536]{4,3,1,0,2:T(8,128)(2,1)S(1)} async-done(((bf16[3,1,8,32,1536]{4,3,1,0,2:T(8,128)(2,1)}), bf16[3,1,8,32,1536]{4,3,1,0,2:T(8,128)(2,1)S(1)}, u32[]{:S(2)}, u32[]{:S(2)}) %all-to-all-start) | async-done | bytes 2359328 | tf_op jit(solution)/shard_map/all_to_all | solution.py:81
  61.0 2.9 fusion.34
  67.7 6.6 convolution_bitcast_fusion
  74.3 55.1 %all-gather.3.cloned.1.call-done = bf16[256,6,1536]{2,1,0:T(8,128)(2,1)} async-done(((bf16[1,6,1536]{2,1,0:T(8,128)(2,1)}), bf16[256,6,1536]{2,1,0:T(8,128)(2,1)}) %all-gather.3.cloned.1.call-update) | async-done | bytes 4718608 | tf_op jit(solution)/shard_map/all_gather | solution.py:92
  129.4 8.4 reshape.263
  137.8 4.6 convolution_convert_fusion
  156.9 4.4 all-to-all-start.1
  161.3 635.6 %fusion = f32[8,1536]{1,0:T(8,128)S(1)} fusion(f32[1536,1536]{1,0:T(8,128)} %convolution_bitcast_fusion), kind=kCustom, calls=%all-reduce-scatter | all-reduce-scatter fusion | flops 3145729 | bytes 9486336
  801.3 7.1 collective-permute-start.63
  810.2 9.5 collective-permute-start.58
  819.7 17.4 %collective-permute-start.57 = (f32[8,1536]{1,0:T(8,128)S(1)}, f32[8,1536]{1,0:T(8,128)S(1)}, u32[]{:S(2)}, u32[]{:S(2)}) collective-permute-start(f32[8,1536]{1,0:T(8,128)S(1)} %fusion), channel_id=1, source_target_pairs={{0,58},{1,59},{2,60},{3,61},{4,62},{5,63},{6,64},{7,65},{8,66},{9,... | collective-permute-start | bytes 147464
  837.1 15.8 %collective-permute-start.56 = (f32[8,1536]{1,0:T(8,128)S(1)}, f32[8,1536]{1,0:T(8,128)S(1)}, u32[]{:S(2)}, u32[]{:S(2)}) collective-permute-start(f32[8,1536]{1,0:T(8,128)S(1)} %fusion), channel_id=1, source_target_pairs={{0,57},{1,58},{2,59},{3,60},{4,61},{5,62},{6,63},{7,64},{8,65},{9,... | collective-permute-start | bytes 147464
  852.9 10.5 collective-permute-start.55
  863.4 13.6 collective-permute-start.54
  877.0 25.4 %collective-permute-start.53 = (f32[8,1536]{1,0:T(8,128)S(1)}, f32[8,1536]{1,0:T(8,128)S(1)}, u32[]{:S(2)}, u32[]{:S(2)}) collective-permute-start(f32[8,1536]{1,0:T(8,128)S(1)} %fusion), channel_id=1, source_target_pairs={{0,54},{1,55},{2,56},{3,57},{4,58},{5,59},{6,60},{7,61},{8,62},{9,... | collective-permute-start | bytes 147464
  902.5 6.4 collective-permute-start.52
  908.9 4.6 collective-permute-start.51
  919.1 2.5 collective-permute-start.47
  923.9 3.9 collective-permute-start.45
  929.1 2.6 collective-permute-start.43
  935.7 2.8 collective-permute-start.39
  938.5 4.9 collective-permute-start.38
  944.8 3.9 collective-permute-start.36
  948.7 3.0 collective-permute-start.35
  954.4 4.3 collective-permute-start.32
  960.7 4.3 collective-permute-start.30
  965.0 4.9 collective-permute-start.29
  969.9 13.1 collective-permute-start.28
  983.1 13.1 collective-permute-start.27
  996.2 13.1 collective-permute-start.26
  1009.4 13.1 collective-permute-start.25
  1022.5 13.1 collective-permute-start.24
  1035.7 13.1 collective-permute-start.23
  1048.8 13.1 collective-permute-start.22
  1062.0 13.1 collective-permute-start.21
  1075.9 13.1 collective-permute-start.20
  1089.1 13.1 collective-permute-start.19
  1102.2 13.1 collective-permute-start.18
  1115.4 13.1 collective-permute-start.17
  1128.5 13.1 collective-permute-start.16
  1141.7 13.1 collective-permute-start.15
  1154.9 13.1 collective-permute-start.14
  1168.1 13.1 collective-permute-start.13
  1181.2 13.1 collective-permute-start.12
  1194.4 13.1 collective-permute-start.11
  1207.5 13.1 collective-permute-start.10
  1220.7 13.1 collective-permute-start.9
  1233.8 13.1 collective-permute-start.8
  1247.0 13.1 collective-permute-start.7
  1260.1 13.1 collective-permute-start.6
  1273.3 13.1 collective-permute-start.5
  1286.4 13.1 collective-permute-start.4
  1299.6 13.1 collective-permute-start.3
  1312.7 13.1 collective-permute-start.2
  1325.9 13.1 collective-permute-start.1
  1339.0 13.4 collective-permute-start
  1352.7 5.9 collective-permute-done
  1358.5 97.2 %concatenate.9 = f32[518,1536]{1,0:T(8,128)} concatenate(f32[6,1536]{1,0:T(8,128)S(1)} %collective-permute-done.63, f32[8,1536]{1,0:T(8,128)S(1)} %collective-permute-done.62, f32[8,1536]{1,0:T(8,128)S(1)} %collective-permute-done.61, f32[8,1536]{1,0:T(8,128)S(1)} %collective-permute-done.60, f32[8,1536]{1,0:T(8,128)S(1)} %collective-permute-done.59, ...), dimensions={0} | concatenate | bytes 6365184
  1457.4 75.1 %psum.7 = f32[12,8,8]{0,2,1:T(8,128)S(1)} all-reduce(f32[12,8,8]{0,2,1:T(8,128)S(1)} %copy.69), channel_id=1, replica_groups=mesh['dp'=32,'seq'=8] {'dp','seq'}, use_global_device_ids=true, to_apply=%region_8.9 | all-reduce | flops 768 | bytes 6144 | tf_op jit(solution)/shard_map/psum | solution.py:124
  1533.3 3.7 copy.68
  1537.0 3.8 gather_fusion.1
  (227 shorter events, 61.2 us)
Async XLA Ops:
  7.2 122.2 %all-gather.3.cloned.1.call-start = ((), (), s32[]{:S(2)}) async-start(), calls=%async_computation.2 | async-start | bytes 6316032 | tf_op jit(solution)/shard_map/all_gather | solution.py:92
  21.4 34.7 %all-to-all-start = ((bf16[3,1,8,32,1536]{4,3,1,0,2:T(8,128)(2,1)}), bf16[3,1,8,32,1536]{4,3,1,0,2:T(8,128)(2,1)S(1)}, u32[]{:S(2)}, u32[]{:S(2)}) async-start(bf16[3,1,8,32,1536]{4,3,1,0,2:T(8,128)(2,1)} %copy_select_fusion), calls=%async_computation | async-start | bytes 4718592 | tf_op jit(solution)/shard_map/all_to_all | solution.py:81
  156.9 1376.4 %all-to-all-start.1 = ((bf16[3,8,1,32,1536]{4,3,2,0,1:T(8,128)(2,1)}), bf16[3,8,1,32,1536]{4,3,2,0,1:T(8,128)(2,1)S(1)}, u32[]{:S(2)}, u32[]{:S(2)}) async-start(bf16[3,8,1,32,1536]{4,3,2,0,1:T(8,128)(2,1)} %copy.67), calls=%async_computation.1 | async-start | bytes 4718592 | tf_op jit(solution)/shard_map/all_to_all | solution.py:113
  796.9 22.8 %collective-permute-start.62 = (f32[8,1536]{1,0:T(8,128)S(1)}, f32[8,1536]{1,0:T(8,128)S(1)}, u32[]{:S(2)}, u32[]{:S(2)}) collective-permute-start(f32[8,1536]{1,0:T(8,128)S(1)} %fusion), channel_id=1, source_target_pairs={{0,63},{1,64},{2,65},{3,66},{4,67},{5,68},{6,69},{7,70},{8,71},{9,... | collective-permute-start | bytes 147464
  798.7 38.4 %collective-permute-start.61 = (f32[8,1536]{1,0:T(8,128)S(1)}, f32[8,1536]{1,0:T(8,128)S(1)}, u32[]{:S(2)}, u32[]{:S(2)}) collective-permute-start(f32[8,1536]{1,0:T(8,128)S(1)} %fusion), channel_id=1, source_target_pairs={{0,62},{1,63},{2,64},{3,65},{4,66},{5,67},{6,68},{7,69},{8,70},{9,... | collective-permute-start | bytes 147464
  800.0 52.9 %collective-permute-start.60 = (f32[8,1536]{1,0:T(8,128)S(1)}, f32[8,1536]{1,0:T(8,128)S(1)}, u32[]{:S(2)}, u32[]{:S(2)}) collective-permute-start(f32[8,1536]{1,0:T(8,128)S(1)} %fusion), channel_id=1, source_target_pairs={{0,61},{1,62},{2,63},{3,64},{4,65},{5,66},{6,67},{7,68},{8,69},{9,... | collective-permute-start | bytes 147464
  808.5 54.9 %collective-permute-start.59 = (f32[8,1536]{1,0:T(8,128)S(1)}, f32[8,1536]{1,0:T(8,128)S(1)}, u32[]{:S(2)}, u32[]{:S(2)}) collective-permute-start(f32[8,1536]{1,0:T(8,128)S(1)} %fusion), channel_id=1, source_target_pairs={{0,60},{1,61},{2,62},{3,63},{4,64},{5,65},{6,66},{7,67},{8,68},{9,... | collective-permute-start | bytes 147464
  810.2 66.8 %collective-permute-start.58 = (f32[8,1536]{1,0:T(8,128)S(1)}, f32[8,1536]{1,0:T(8,128)S(1)}, u32[]{:S(2)}, u32[]{:S(2)}) collective-permute-start(f32[8,1536]{1,0:T(8,128)S(1)} %fusion), channel_id=1, source_target_pairs={{0,59},{1,60},{2,61},{3,62},{4,63},{5,64},{6,65},{7,66},{8,67},{9,... | collective-permute-start | bytes 147464
  819.7 82.7 %collective-permute-start.57 = (f32[8,1536]{1,0:T(8,128)S(1)}, f32[8,1536]{1,0:T(8,128)S(1)}, u32[]{:S(2)}, u32[]{:S(2)}) collective-permute-start(f32[8,1536]{1,0:T(8,128)S(1)} %fusion), channel_id=1, source_target_pairs={{0,58},{1,59},{2,60},{3,61},{4,62},{5,63},{6,64},{7,65},{8,66},{9,... | collective-permute-start | bytes 147464
  837.1 71.7 %collective-permute-start.56 = (f32[8,1536]{1,0:T(8,128)S(1)}, f32[8,1536]{1,0:T(8,128)S(1)}, u32[]{:S(2)}, u32[]{:S(2)}) collective-permute-start(f32[8,1536]{1,0:T(8,128)S(1)} %fusion), channel_id=1, source_target_pairs={{0,57},{1,58},{2,59},{3,60},{4,61},{5,62},{6,63},{7,64},{8,65},{9,... | collective-permute-start | bytes 147464
  852.9 60.5 %collective-permute-start.55 = (f32[8,1536]{1,0:T(8,128)S(1)}, f32[8,1536]{1,0:T(8,128)S(1)}, u32[]{:S(2)}, u32[]{:S(2)}) collective-permute-start(f32[8,1536]{1,0:T(8,128)S(1)} %fusion), channel_id=1, source_target_pairs={{0,56},{1,57},{2,58},{3,59},{4,60},{5,61},{6,62},{7,63},{8,64},{9,... | collective-permute-start | bytes 147464
  863.4 51.7 %collective-permute-start.54 = (f32[8,1536]{1,0:T(8,128)S(1)}, f32[8,1536]{1,0:T(8,128)S(1)}, u32[]{:S(2)}, u32[]{:S(2)}) collective-permute-start(f32[8,1536]{1,0:T(8,128)S(1)} %fusion), channel_id=1, source_target_pairs={{0,55},{1,56},{2,57},{3,58},{4,59},{5,60},{6,61},{7,62},{8,63},{9,... | collective-permute-start | bytes 147464
  877.0 40.6 %collective-permute-start.53 = (f32[8,1536]{1,0:T(8,128)S(1)}, f32[8,1536]{1,0:T(8,128)S(1)}, u32[]{:S(2)}, u32[]{:S(2)}) collective-permute-start(f32[8,1536]{1,0:T(8,128)S(1)} %fusion), channel_id=1, source_target_pairs={{0,54},{1,55},{2,56},{3,57},{4,58},{5,59},{6,60},{7,61},{8,62},{9,... | collective-permute-start | bytes 147464
  902.5 16.6 %collective-permute-start.52 = (f32[8,1536]{1,0:T(8,128)S(1)}, f32[8,1536]{1,0:T(8,128)S(1)}, u32[]{:S(2)}, u32[]{:S(2)}) collective-permute-start(f32[8,1536]{1,0:T(8,128)S(1)} %fusion), channel_id=1, source_target_pairs={{0,53},{1,54},{2,55},{3,56},{4,57},{5,58},{6,59},{7,60},{8,61},{9,... | collective-permute-start | bytes 147464
  908.9 12.8 collective-permute-start.51
  913.4 10.4 collective-permute-start.50
  915.1 12.7 collective-permute-start.49
  917.6 11.5 collective-permute-start.48
  919.1 12.6 collective-permute-start.47
  921.6 11.4 collective-permute-start.46
  923.9 10.5 collective-permute-start.45
  931.7 11.7 collective-permute-start.42
  933.1 11.7 collective-permute-start.41
  934.4 14.3 collective-permute-start.40
  935.7 16.1 %collective-permute-start.39 = (f32[8,1536]{1,0:T(8,128)S(1)}, f32[8,1536]{1,0:T(8,128)S(1)}, u32[]{:S(2)}, u32[]{:S(2)}) collective-permute-start(f32[8,1536]{1,0:T(8,128)S(1)} %fusion), channel_id=1, source_target_pairs={{0,40},{1,41},{2,42},{3,43},{4,44},{5,45},{6,46},{7,47},{8,48},{9,... | collective-permute-start | bytes 147464
  938.5 14.6 collective-permute-start.38
  943.5 10.9 collective-permute-start.37
  944.8 13.9 collective-permute-start.36
  948.7 11.9 collective-permute-start.35
  951.8 13.2 collective-permute-start.34
  953.1 16.8 %collective-permute-start.33 = (f32[8,1536]{1,0:T(8,128)S(1)}, f32[8,1536]{1,0:T(8,128)S(1)}, u32[]{:S(2)}, u32[]{:S(2)}) collective-permute-start(f32[8,1536]{1,0:T(8,128)S(1)} %fusion), channel_id=1, source_target_pairs={{0,34},{1,35},{2,36},{3,37},{4,38},{5,39},{6,40},{7,41},{8,42},{9,... | collective-permute-start | bytes 147464
  954.4 28.6 %collective-permute-start.32 = (f32[8,1536]{1,0:T(8,128)S(1)}, f32[8,1536]{1,0:T(8,128)S(1)}, u32[]{:S(2)}, u32[]{:S(2)}) collective-permute-start(f32[8,1536]{1,0:T(8,128)S(1)} %fusion), channel_id=1, source_target_pairs={{0,33},{1,34},{2,35},{3,36},{4,37},{5,38},{6,39},{7,40},{8,41},{9,... | collective-permute-start | bytes 147464
  958.7 37.5 %collective-permute-start.31 = (f32[8,1536]{1,0:T(8,128)S(1)}, f32[8,1536]{1,0:T(8,128)S(1)}, u32[]{:S(2)}, u32[]{:S(2)}) collective-permute-start(f32[8,1536]{1,0:T(8,128)S(1)} %fusion), channel_id=1, source_target_pairs={{0,32},{1,33},{2,34},{3,35},{4,36},{5,37},{6,38},{7,39},{8,40},{9,... | collective-permute-start | bytes 147464
  960.7 48.7 %collective-permute-start.30 = (f32[8,1536]{1,0:T(8,128)S(1)}, f32[8,1536]{1,0:T(8,128)S(1)}, u32[]{:S(2)}, u32[]{:S(2)}) collective-permute-start(f32[8,1536]{1,0:T(8,128)S(1)} %fusion), channel_id=1, source_target_pairs={{0,31},{1,32},{2,33},{3,34},{4,35},{5,36},{6,37},{7,38},{8,39},{9,... | collective-permute-start | bytes 147464
  965.0 57.5 %collective-permute-start.29 = (f32[8,1536]{1,0:T(8,128)S(1)}, f32[8,1536]{1,0:T(8,128)S(1)}, u32[]{:S(2)}, u32[]{:S(2)}) collective-permute-start(f32[8,1536]{1,0:T(8,128)S(1)} %fusion), channel_id=1, source_target_pairs={{0,30},{1,31},{2,32},{3,33},{4,34},{5,35},{6,36},{7,37},{8,38},{9,... | collective-permute-start | bytes 147464
  969.9 65.7 %collective-permute-start.28 = (f32[8,1536]{1,0:T(8,128)S(1)}, f32[8,1536]{1,0:T(8,128)S(1)}, u32[]{:S(2)}, u32[]{:S(2)}) collective-permute-start(f32[8,1536]{1,0:T(8,128)S(1)} %fusion), channel_id=1, source_target_pairs={{0,29},{1,30},{2,31},{3,32},{4,33},{5,34},{6,35},{7,36},{8,37},{9,... | collective-permute-start | bytes 147464
  983.1 65.7 %collective-permute-start.27 = (f32[8,1536]{1,0:T(8,128)S(1)}, f32[8,1536]{1,0:T(8,128)S(1)}, u32[]{:S(2)}, u32[]{:S(2)}) collective-permute-start(f32[8,1536]{1,0:T(8,128)S(1)} %fusion), channel_id=1, source_target_pairs={{0,28},{1,29},{2,30},{3,31},{4,32},{5,33},{6,34},{7,35},{8,36},{9,... | collective-permute-start | bytes 147464
  996.2 65.7 %collective-permute-start.26 = (f32[8,1536]{1,0:T(8,128)S(1)}, f32[8,1536]{1,0:T(8,128)S(1)}, u32[]{:S(2)}, u32[]{:S(2)}) collective-permute-start(f32[8,1536]{1,0:T(8,128)S(1)} %fusion), channel_id=1, source_target_pairs={{0,27},{1,28},{2,29},{3,30},{4,31},{5,32},{6,33},{7,34},{8,35},{9,... | collective-permute-start | bytes 147464
  1009.4 65.7 %collective-permute-start.25 = (f32[8,1536]{1,0:T(8,128)S(1)}, f32[8,1536]{1,0:T(8,128)S(1)}, u32[]{:S(2)}, u32[]{:S(2)}) collective-permute-start(f32[8,1536]{1,0:T(8,128)S(1)} %fusion), channel_id=1, source_target_pairs={{0,26},{1,27},{2,28},{3,29},{4,30},{5,31},{6,32},{7,33},{8,34},{9,... | collective-permute-start | bytes 147464
  1022.5 66.5 %collective-permute-start.24 = (f32[8,1536]{1,0:T(8,128)S(1)}, f32[8,1536]{1,0:T(8,128)S(1)}, u32[]{:S(2)}, u32[]{:S(2)}) collective-permute-start(f32[8,1536]{1,0:T(8,128)S(1)} %fusion), channel_id=1, source_target_pairs={{0,25},{1,26},{2,27},{3,28},{4,29},{5,30},{6,31},{7,32},{8,33},{9,... | collective-permute-start | bytes 147464
  1035.7 66.5 %collective-permute-start.23 = (f32[8,1536]{1,0:T(8,128)S(1)}, f32[8,1536]{1,0:T(8,128)S(1)}, u32[]{:S(2)}, u32[]{:S(2)}) collective-permute-start(f32[8,1536]{1,0:T(8,128)S(1)} %fusion), channel_id=1, source_target_pairs={{0,24},{1,25},{2,26},{3,27},{4,28},{5,29},{6,30},{7,31},{8,32},{9,... | collective-permute-start | bytes 147464
  1048.8 66.5 %collective-permute-start.22 = (f32[8,1536]{1,0:T(8,128)S(1)}, f32[8,1536]{1,0:T(8,128)S(1)}, u32[]{:S(2)}, u32[]{:S(2)}) collective-permute-start(f32[8,1536]{1,0:T(8,128)S(1)} %fusion), channel_id=1, source_target_pairs={{0,23},{1,24},{2,25},{3,26},{4,27},{5,28},{6,29},{7,30},{8,31},{9,... | collective-permute-start | bytes 147464
  1062.0 66.5 %collective-permute-start.21 = (f32[8,1536]{1,0:T(8,128)S(1)}, f32[8,1536]{1,0:T(8,128)S(1)}, u32[]{:S(2)}, u32[]{:S(2)}) collective-permute-start(f32[8,1536]{1,0:T(8,128)S(1)} %fusion), channel_id=1, source_target_pairs={{0,22},{1,23},{2,24},{3,25},{4,26},{5,27},{6,28},{7,29},{8,30},{9,... | collective-permute-start | bytes 147464
  1075.9 65.7 %collective-permute-start.20 = (f32[8,1536]{1,0:T(8,128)S(1)}, f32[8,1536]{1,0:T(8,128)S(1)}, u32[]{:S(2)}, u32[]{:S(2)}) collective-permute-start(f32[8,1536]{1,0:T(8,128)S(1)} %fusion), channel_id=1, source_target_pairs={{0,21},{1,22},{2,23},{3,24},{4,25},{5,26},{6,27},{7,28},{8,29},{9,... | collective-permute-start | bytes 147464
  1089.1 65.8 %collective-permute-start.19 = (f32[8,1536]{1,0:T(8,128)S(1)}, f32[8,1536]{1,0:T(8,128)S(1)}, u32[]{:S(2)}, u32[]{:S(2)}) collective-permute-start(f32[8,1536]{1,0:T(8,128)S(1)} %fusion), channel_id=1, source_target_pairs={{0,20},{1,21},{2,22},{3,23},{4,24},{5,25},{6,26},{7,27},{8,28},{9,... | collective-permute-start | bytes 147464
  1102.2 65.8 %collective-permute-start.18 = (f32[8,1536]{1,0:T(8,128)S(1)}, f32[8,1536]{1,0:T(8,128)S(1)}, u32[]{:S(2)}, u32[]{:S(2)}) collective-permute-start(f32[8,1536]{1,0:T(8,128)S(1)} %fusion), channel_id=1, source_target_pairs={{0,19},{1,20},{2,21},{3,22},{4,23},{5,24},{6,25},{7,26},{8,27},{9,... | collective-permute-start | bytes 147464
  1115.4 65.8 %collective-permute-start.17 = (f32[8,1536]{1,0:T(8,128)S(1)}, f32[8,1536]{1,0:T(8,128)S(1)}, u32[]{:S(2)}, u32[]{:S(2)}) collective-permute-start(f32[8,1536]{1,0:T(8,128)S(1)} %fusion), channel_id=1, source_target_pairs={{0,18},{1,19},{2,20},{3,21},{4,22},{5,23},{6,24},{7,25},{8,26},{9,... | collective-permute-start | bytes 147464
  1128.5 65.8 %collective-permute-start.16 = (f32[8,1536]{1,0:T(8,128)S(1)}, f32[8,1536]{1,0:T(8,128)S(1)}, u32[]{:S(2)}, u32[]{:S(2)}) collective-permute-start(f32[8,1536]{1,0:T(8,128)S(1)} %fusion), channel_id=1, source_target_pairs={{0,17},{1,18},{2,19},{3,20},{4,21},{5,22},{6,23},{7,24},{8,25},{9,... | collective-permute-start | bytes 147464
  1141.7 65.8 %collective-permute-start.15 = (f32[8,1536]{1,0:T(8,128)S(1)}, f32[8,1536]{1,0:T(8,128)S(1)}, u32[]{:S(2)}, u32[]{:S(2)}) collective-permute-start(f32[8,1536]{1,0:T(8,128)S(1)} %fusion), channel_id=1, source_target_pairs={{0,16},{1,17},{2,18},{3,19},{4,20},{5,21},{6,22},{7,23},{8,24},{9,... | collective-permute-start | bytes 147464
  1154.9 65.7 %collective-permute-start.14 = (f32[8,1536]{1,0:T(8,128)S(1)}, f32[8,1536]{1,0:T(8,128)S(1)}, u32[]{:S(2)}, u32[]{:S(2)}) collective-permute-start(f32[8,1536]{1,0:T(8,128)S(1)} %fusion), channel_id=1, source_target_pairs={{0,15},{1,16},{2,17},{3,18},{4,19},{5,20},{6,21},{7,22},{8,23},{9,... | collective-permute-start | bytes 147464
  1168.1 65.7 %collective-permute-start.13 = (f32[8,1536]{1,0:T(8,128)S(1)}, f32[8,1536]{1,0:T(8,128)S(1)}, u32[]{:S(2)}, u32[]{:S(2)}) collective-permute-start(f32[8,1536]{1,0:T(8,128)S(1)} %fusion), channel_id=1, source_target_pairs={{0,14},{1,15},{2,16},{3,17},{4,18},{5,19},{6,20},{7,21},{8,22},{9,... | collective-permute-start | bytes 147464
  1181.2 65.7 %collective-permute-start.12 = (f32[8,1536]{1,0:T(8,128)S(1)}, f32[8,1536]{1,0:T(8,128)S(1)}, u32[]{:S(2)}, u32[]{:S(2)}) collective-permute-start(f32[8,1536]{1,0:T(8,128)S(1)} %fusion), channel_id=1, source_target_pairs={{0,13},{1,14},{2,15},{3,16},{4,17},{5,18},{6,19},{7,20},{8,21},{9,... | collective-permute-start | bytes 147464
  1194.4 65.7 %collective-permute-start.11 = (f32[8,1536]{1,0:T(8,128)S(1)}, f32[8,1536]{1,0:T(8,128)S(1)}, u32[]{:S(2)}, u32[]{:S(2)}) collective-permute-start(f32[8,1536]{1,0:T(8,128)S(1)} %fusion), channel_id=1, source_target_pairs={{0,12},{1,13},{2,14},{3,15},{4,16},{5,17},{6,18},{7,19},{8,20},{9,... | collective-permute-start | bytes 147464
  1207.5 65.7 %collective-permute-start.10 = (f32[8,1536]{1,0:T(8,128)S(1)}, f32[8,1536]{1,0:T(8,128)S(1)}, u32[]{:S(2)}, u32[]{:S(2)}) collective-permute-start(f32[8,1536]{1,0:T(8,128)S(1)} %fusion), channel_id=1, source_target_pairs={{0,11},{1,12},{2,13},{3,14},{4,15},{5,16},{6,17},{7,18},{8,19},{9,... | collective-permute-start | bytes 147464
  1220.7 65.7 %collective-permute-start.9 = (f32[8,1536]{1,0:T(8,128)S(1)}, f32[8,1536]{1,0:T(8,128)S(1)}, u32[]{:S(2)}, u32[]{:S(2)}) collective-permute-start(f32[8,1536]{1,0:T(8,128)S(1)} %fusion), channel_id=1, source_target_pairs={{0,10},{1,11},{2,12},{3,13},{4,14},{5,15},{6,16},{7,17},{8,18},{9,... | collective-permute-start | bytes 147464
  1233.8 65.7 %collective-permute-start.8 = (f32[8,1536]{1,0:T(8,128)S(1)}, f32[8,1536]{1,0:T(8,128)S(1)}, u32[]{:S(2)}, u32[]{:S(2)}) collective-permute-start(f32[8,1536]{1,0:T(8,128)S(1)} %fusion), channel_id=1, source_target_pairs={{0,9},{1,10},{2,11},{3,12},{4,13},{5,14},{6,15},{7,16},{8,17},{9,1... | collective-permute-start | bytes 147464
  1247.0 65.8 %collective-permute-start.7 = (f32[8,1536]{1,0:T(8,128)S(1)}, f32[8,1536]{1,0:T(8,128)S(1)}, u32[]{:S(2)}, u32[]{:S(2)}) collective-permute-start(f32[8,1536]{1,0:T(8,128)S(1)} %fusion), channel_id=1, source_target_pairs={{0,8},{1,9},{2,10},{3,11},{4,12},{5,13},{6,14},{7,15},{8,16},{9,17... | collective-permute-start | bytes 147464
  1260.1 65.8 %collective-permute-start.6 = (f32[8,1536]{1,0:T(8,128)S(1)}, f32[8,1536]{1,0:T(8,128)S(1)}, u32[]{:S(2)}, u32[]{:S(2)}) collective-permute-start(f32[8,1536]{1,0:T(8,128)S(1)} %fusion), channel_id=1, source_target_pairs={{0,7},{1,8},{2,9},{3,10},{4,11},{5,12},{6,13},{7,14},{8,15},{9,16}... | collective-permute-start | bytes 147464
  1273.3 65.8 %collective-permute-start.5 = (f32[8,1536]{1,0:T(8,128)S(1)}, f32[8,1536]{1,0:T(8,128)S(1)}, u32[]{:S(2)}, u32[]{:S(2)}) collective-permute-start(f32[8,1536]{1,0:T(8,128)S(1)} %fusion), channel_id=1, source_target_pairs={{0,6},{1,7},{2,8},{3,9},{4,10},{5,11},{6,12},{7,13},{8,14},{9,15},... | collective-permute-start | bytes 147464
  1286.4 66.2 %collective-permute-start.4 = (f32[8,1536]{1,0:T(8,128)S(1)}, f32[8,1536]{1,0:T(8,128)}, u32[]{:S(2)}, u32[]{:S(2)}) collective-permute-start(f32[8,1536]{1,0:T(8,128)S(1)} %fusion), channel_id=1, source_target_pairs={{0,5},{1,6},{2,7},{3,8},{4,9},{5,10},{6,11},{7,12},{8,13},{9,14},{... | collective-permute-start | bytes 147464
  1299.6 53.1 %collective-permute-start.3 = (f32[8,1536]{1,0:T(8,128)S(1)}, f32[8,1536]{1,0:T(8,128)}, u32[]{:S(2)}, u32[]{:S(2)}) collective-permute-start(f32[8,1536]{1,0:T(8,128)S(1)} %fusion), channel_id=1, source_target_pairs={{0,4},{1,5},{2,6},{3,7},{4,8},{5,9},{6,10},{7,11},{8,12},{9,13},{1... | collective-permute-start | bytes 147464
  1312.7 39.9 %collective-permute-start.2 = (f32[8,1536]{1,0:T(8,128)S(1)}, f32[8,1536]{1,0:T(8,128)}, u32[]{:S(2)}, u32[]{:S(2)}) collective-permute-start(f32[8,1536]{1,0:T(8,128)S(1)} %fusion), channel_id=1, source_target_pairs={{0,3},{1,4},{2,5},{3,6},{4,7},{5,8},{6,9},{7,10},{8,11},{9,12},{10... | collective-permute-start | bytes 147464
  1325.9 26.8 %collective-permute-start.1 = (f32[8,1536]{1,0:T(8,128)S(1)}, f32[8,1536]{1,0:T(8,128)}, u32[]{:S(2)}, u32[]{:S(2)}) collective-permute-start(f32[8,1536]{1,0:T(8,128)S(1)} %fusion), channel_id=1, source_target_pairs={{0,2},{1,3},{2,4},{3,5},{4,6},{5,7},{6,8},{7,9},{8,10},{9,11},{10,... | collective-permute-start | bytes 147464
  1339.0 19.5 %collective-permute-start = (f32[8,1536]{1,0:T(8,128)S(1)}, f32[8,1536]{1,0:T(8,128)}, u32[]{:S(2)}, u32[]{:S(2)}) collective-permute-start(f32[8,1536]{1,0:T(8,128)S(1)} %fusion), channel_id=1, source_target_pairs={{0,1},{1,2},{2,3},{3,4},{4,5},{5,6},{6,7},{7,8},{8,9},{9,10},{10,1... | collective-permute-start | bytes 147464
  (52 other events, 5384.3 us)
Sparse Core Ops, SparseCore 0:
  11.7 117.6 all-gather.2
where the time goes:
time: 1560 us; the launch traced here: 1550 us
  blocking collectives  711 us (46%)
  starting transfers between devices  562 us (36%)
  local copies, waits for them, and re-layouts  137 us (9%)
  waiting for transfers between devices  90.4 us (6%)
  matrix products  24.4 us (2%)
  between operations  15.9 us (1%)
    unnamed x1, blocking collectives  636 us
    unnamed x64, starting transfers between devices  553 us
    unnamed x104, local copies, waits for them, and re-layouts  112 us
    psum x1, blocking collectives, per_device(): pair_grand = lax.psum(pair_sums, ('dp', 'seq'))  75.1 us
    all_gather x1, waiting for transfers between devices, per_device(): lax.all_gather(w_out, ('dp', 'seq'), axis=0, tiled=True)  55.1 us
  transfers between devices with their start and end apart: 67, of which 4 were waited for; matrix products, arithmetic and copies ran while one was open for 50% of the time, Pallas kernels for 0%

commit v1 on v0

v1 whole, which is shorter than its diff:
```python
import math

import jax
import jax.numpy as jnp
from jax import lax
from jax.experimental import pallas as pl
from jax.experimental.pallas import tpu as pltpu
from jax.sharding import Mesh, PartitionSpec as P

Z, Y, X, C = 8, 4, 4, 2
SEQ = ("x", "core")
F = 8
POS = 128
HALF = 64
NB = 4
HL = 3
HD = 128
COLS = HL * HD
DW = 1536
CAP = 32
FACTOR = 1.0 / math.sqrt(HD)
NT = (((1,), (1,)), ((), ()))
TN = (((0,), (0,)), ((), ()))


def dot(a, b, dims):
    return lax.dot_general(a, b, dims, preferred_element_type=jnp.float32)


def fwd_kernel(qkv_ref, bias_ref, probs_ref, mixed_ref):
    for h in range(HL):
        cols = slice(h * HD, (h + 1) * HD)
        for b in range(NB):
            rows = slice(b * 16, (b + 1) * 16)
            q = qkv_ref[:, 0, rows, cols].reshape(POS, HD)
            k = qkv_ref[:, 1, rows, cols].reshape(POS, HD)
            v = qkv_ref[:, 2, rows, cols].reshape(POS, HD)
            s = dot(q, k, NT) * FACTOR + bias_ref[h]
            e = jnp.exp(s - jnp.max(s, axis=-1, keepdims=True))
            p = e / jnp.sum(e, axis=-1, keepdims=True)
            probs_ref[h, b] = p
            m = dot(p.astype(jnp.bfloat16), v, (((1,), (0,)), ((), ())))
            mixed_ref[:, rows, cols] = m.astype(jnp.bfloat16).reshape(F, 16, HD)


def bwd_kernel(qkv_ref, probs_ref, up_ref, w_ref, grads_ref, pair_ref, dm_ref):
    up = up_ref[...].reshape(F * HALF, DW)
    dm = dot(up, w_ref[...], NT)
    dm_ref[...] = dm.astype(jnp.bfloat16).reshape(F, HALF, COLS)
    for h in range(HL):
        cols = slice(h * HD, (h + 1) * HD)
        total = jnp.zeros((F, POS), jnp.float32)
        for b in range(NB):
            rows = slice(b * 16, (b + 1) * 16)
            q = qkv_ref[:, 0, rows, cols].reshape(POS, HD)
            k = qkv_ref[:, 1, rows, cols].reshape(POS, HD)
            v = qkv_ref[:, 2, rows, cols].reshape(POS, HD)
            d = dm_ref[:, rows, cols].reshape(POS, HD)
            p = probs_ref[h, b]
            g = dot(d, v, NT)
            ds = p * (g - jnp.sum(p * g, axis=-1, keepdims=True))
            total = total + jnp.sum(ds.reshape(F, 16, POS), axis=1)
            low = ds.astype(jnp.bfloat16)
            gq = dot(low, k, (((1,), (0,)), ((), ()))) * FACTOR
            gk = dot(low, q, TN) * FACTOR
            gv = dot(p.astype(jnp.bfloat16), d, TN)
            for i, val in enumerate((gq, gk, gv)):
                grads_ref[:, i, rows, cols] = val.astype(jnp.bfloat16).reshape(F, 16, HD)
        pair_ref[h] = total


def hop(x, axis, k, n):
    return lax.ppermute(x, axis, [(i, i ^ k) for i in range(n)])


def per_device(qkv_time, shard_sizes, bias_time, w_out, cot_out):
    bf, f32 = jnp.bfloat16, jnp.float32
    xi = lax.axis_index("x")
    core = lax.axis_index("core")

    cot = lax.all_to_all(cot_out[0, 0], SEQ, 0, 0, tiled=True).reshape(F * CAP, DW)

    packed = qkv_time[:, 0, 0].reshape(3, C, HALF, X, COLS).transpose(3, 1, 0, 2, 4)
    qkv = lax.all_to_all(packed.reshape(F, 3, HALF, COLS), SEQ, 0, 0, tiled=True)

    there = [
        ((2 * c + z0) * X + x, (z0 * X + x) * X + c)
        for c in range(X)
        for z0 in range(2)
        for x in range(X)
    ]
    w8 = jnp.pad(w_out, ((0, 2), (0, 0)))
    w8 = lax.ppermute(w8, ("z", "x"), there)
    wz = lax.all_to_all(jnp.broadcast_to(w8, (Z, 8, DW)), "z", 0, 0, tiled=True)
    wy = lax.all_to_all(jnp.broadcast_to(wz.reshape(64, DW), (Y, 64, DW)), "y", 0, 0, tiled=True)
    wo = hop(wy, "core", 1, C)
    held = jnp.concatenate([wy, wo]).reshape(2 * Y * 64, DW)
    r = lax.broadcasted_iota(jnp.int32, (COLS, 512), 0)
    t = lax.broadcasted_iota(jnp.int32, (COLS, 512), 1)
    i, sub = r % 6, r // 6
    rz0, ry, rx, rc = sub // 32, (sub // 8) % 4, (sub // 2) % 4, sub % 2
    spot = (((rc ^ core) * 4 + ry) * 8 + rz0 * 4 + rx) * 8 + i
    w_c = dot((spot == t).astype(bf), held, (((1,), (0,)), ((), ()))).astype(bf)

    counts = shard_sizes[0]
    starts = jnp.cumsum(counts) - counts
    slot = lax.broadcasted_iota(jnp.int32, (POS, F, CAP), 2)
    pos = lax.broadcasted_iota(jnp.int32, (POS, F, CAP), 0)
    pick = (slot < counts[None, :, None]) & (starts[None, :, None] + slot == pos)
    up = dot(pick.reshape(POS, F * CAP).astype(bf), cot, (((1,), (0,)), ((), ()))).astype(bf)
    up = jnp.broadcast_to(up.reshape(1, C, HALF, DW), (X, C, HALF, DW)).reshape(F, HALF, DW)
    up = lax.all_to_all(up, SEQ, 0, 0, tiled=True)

    local_bias = lax.dynamic_slice(bias_time, (xi * HL, 0), (HL, 15))
    pair = jnp.stack([local_bias[:, 7 - f : 15 - f] for f in range(F)], axis=1)
    same = jnp.eye(16, dtype=jnp.bool_)[None, None, :, None, :]
    bias_m = jnp.where(same, pair[:, :, None, :, None], f32(-1e30)).reshape(HL, POS, POS)
    probs, mixed = pl.pallas_call(
        fwd_kernel,
        out_shape=(
            jax.ShapeDtypeStruct((HL, NB, POS, POS), f32),
            jax.ShapeDtypeStruct((F, HALF, COLS), bf),
        ),
        compiler_params=pltpu.CompilerParams(vmem_limit_bytes=32 << 20),
        cost_estimate=pl.CostEstimate(flops=200_000_000, bytes_accessed=4_000_000, transcendentals=200_000),
        name="attn_fwd",
    )(qkv, bias_m)

    mixed_rows = mixed.reshape(F * HALF, COLS)
    q2 = lax.broadcasted_iota(jnp.int32, (COLS, COLS), 1)
    r2 = lax.broadcasted_iota(jnp.int32, (COLS, COLS), 0)
    i2, sub2 = q2 % 6, q2 // 6
    qc, qy, qz0, qx = sub2 // 32, (sub2 // 8) % 4, (sub2 // 4) % 2, sub2 % 4
    src = ((((qz0 * 4 + qy) * 4 + qx) * 2) + qc) * 6 + i2
    mixed_p = dot(mixed_rows, (src == r2).astype(bf), (((1,), (0,)), ((), ()))).astype(bf)
    up_rows = up.reshape(F * HALF, DW)
    gw = dot(mixed_p, up_rows, TN)
    half = COLS // 2
    mine = lax.dynamic_slice(gw, (core * half, 0), (half, DW))
    other = lax.dynamic_slice(gw, ((1 - core) * half, 0), (half, DW))
    gw = mine + hop(other, "core", 1, C)
    gw = gw.reshape(Y, 48, DW).astype(bf)
    gw = jnp.sum(lax.all_to_all(gw, "y", 0, 0, tiled=True).astype(f32), axis=0)
    gw = jnp.pad(gw.reshape(Z, 6, DW), ((0, 0), (0, 2), (0, 0)))
    gw = jnp.sum(lax.all_to_all(gw, "z", 0, 0, tiled=True), axis=0)
    grad_w_out = lax.ppermute(gw, ("z", "x"), [(b, a) for a, b in there])[:6]

    grads, pairs = pl.pallas_call(
        bwd_kernel,
        out_shape=(
            jax.ShapeDtypeStruct((F, 3, HALF, COLS), bf),
            jax.ShapeDtypeStruct((HL, F, POS), f32),
        ),
        scratch_shapes=[pltpu.VMEM((F, HALF, COLS), bf)],
        compiler_params=pltpu.CompilerParams(vmem_limit_bytes=32 << 20),
        cost_estimate=pl.CostEstimate(flops=900_000_000, bytes_accessed=6_000_000, transcendentals=0),
        name="attn_bwd",
    )(qkv, probs, up, w_c)
    back = lax.all_to_all(grads, SEQ, 0, 0, tiled=True).reshape(X, C, 3, HALF, COLS)
    grad_qkv = back.transpose(2, 1, 3, 0, 4).reshape(3, 1, 1, POS, DW)

    pairs = pairs.reshape(HL, F, F, 16).sum(axis=-1)
    offs = jnp.stack([jnp.pad(pairs[:, f], ((0, 0), (7 - f, f))) for f in range(F)]).sum(axis=0)
    offs = lax.dynamic_update_slice(jnp.zeros((16, 128), f32), jnp.pad(offs, ((0, 0), (0, 113))), (xi * HL, 0))
    for axis, n in (("core", C), ("x", X), ("y", Y), ("z", Z)):
        k = 1
        while k < n:
            offs = offs + hop(offs, axis, k, n)
            k *= 2
    return grad_qkv, offs[:12, :15], grad_w_out


def solution(mesh):
    grid = Mesh(mesh.devices.reshape(Z, Y, X, C), ("z", "y", "x", "core"))
    dp, every = ("z", "y"), ("z", "y", "x", "core")
    return jax.shard_map(
        per_device,
        mesh=grid,
        in_specs=(
            P(None, dp, SEQ, None, None),
            P(dp, None),
            P(),
            P(every, None),
            P(dp, SEQ, None, None, None),
        ),
        out_specs=(P(None, dp, SEQ, None, None), P(), P(every, None)),
        check_vma=False,
    )
```

time: 1560 us -> 212 us (0.14)
  blocking collectives: 711 us -> 32.5 us
  starting transfers between devices: 562 us -> 43.6 us
  local copies, waits for them, and re-layouts: 137 us -> 18.3 us
  matrix products: 24.4 us -> 7.34 us
    unnamed x1 -> x0, blocking collectives: 636 us -> none
    unnamed x64 -> x0, starting transfers between devices: 553 us -> none
    unnamed x104 -> x32, local copies, waits for them, and re-layouts: 112 us -> 3.55 us
    psum x1 -> x0, blocking collectives: 75.1 us -> none  [per_device(): pair_grand = lax.psum(pair_sums, ('dp', 'seq'))]
    all_gather x1 -> x0, waiting for transfers between devices: 55.1 us -> none  [per_device(): lax.all_gather(w_out, ('dp', 'seq'), axis=0, tiled=True)]
    ppermute x0 -> x12, waiting for transfers between devices: none -> 35.3 us  [the longest x10 32.8 us: hop(): return lax.ppermute(x, axis, [(i, i ^ k) for i in range(n)])]
    all_to_all x0 -> x2, blocking collectives: none -> 32.5 us  [the longest x1 17.9 us: per_device(): wz = lax.all_to_all(jnp.broadcast_to(w8, (Z, 8, DW)), 'z', 0, 0, tiled=True)]
    all_to_all x2 -> x6, waiting for transfers between devices: 28.1 us -> 52.5 us  [the longest x1 16.7 us: per_device(): lax.all_to_all(packed.reshape(F, 3, HALF, COLS), SEQ, 0, 0, tiled=True)]
  transfers between devices with their start and end apart: 67 -> 18, of which waited for: 4 -> 15; matrix products, arithmetic and copies ran while one was open for 50% -> 10% of each run, Pallas kernels for 0% -> 4%
where the time goes in v1:
time: 212 us; the launch traced here: 209 us
  waiting for transfers between devices  87.8 us (41%)
  starting transfers between devices  43.6 us (21%)
  blocking collectives  32.5 us (15%)
  local copies, waits for them, and re-layouts  18.3 us (9%)
  other arithmetic  10.4 us (5%)
  Pallas kernels  8.51 us (4%)
  matrix products  7.34 us (3%)
    ppermute x10, waiting for transfers between devices, hop(): return lax.ppermute(x, axis, [(i, i ^ k) for i in range(n)])  32.8 us
    all_to_all x1, blocking collectives, per_device(): wz = lax.all_to_all(jnp.broadcast_to(w8, (Z, 8, DW)), 'z', 0, 0, tiled=True)  17.9 us
    all_to_all x1, waiting for transfers between devices, per_device(): lax.all_to_all(packed.reshape(F, 3, HALF, COLS), SEQ, 0, 0, tiled=True)  16.7 us
    all_to_all x1, blocking collectives, per_device(): lax.all_to_all(jnp.broadcast_to(wz.reshape(64, DW), (Y, 64, DW)), 'y', 0,...  14.6 us
    all_to_all x1, waiting for transfers between devices, per_device(): up = lax.all_to_all(up, SEQ, 0, 0, tiled=True)  11.9 us
    all_to_all x1, waiting for transfers between devices, per_device(): lax.all_to_all(cot_out[0, 0], SEQ, 0, 0, tiled=True).reshape(F * CAP, DW)  11.4 us
    ppermute x10, starting transfers between devices, hop(): return lax.ppermute(x, axis, [(i, i ^ k) for i in range(n)])  9.13 us
    all_to_all x1, waiting for transfers between devices, per_device(): gw = jnp.sum(lax.all_to_all(gw, 'y', 0, 0, tiled=True).astype(f32), axis=0)  8.49 us
  transfers between devices with their start and end apart: 18, of which 15 were waited for; matrix products, arithmetic and copies ran while one was open for 10% of the time, Pallas kernels for 4%

profile of v1, /device:TPU:32, one launch (start us, length us, event | category | flops | bytes accessed | tf_op | source)
XLA Modules:
  0.0 209.4 jit_solution(403271333591854609)
XLA Ops:
  0.7 4.4 %all-to-all-start.1 = ((bf16[8,32,1536]{2,1,0:T(8,128)(2,1)}), bf16[8,32,1536]{2,1,0:T(8,128)(2,1)S(1)}, u32[]{:S(2)}, u32[]{:S(2)}) async-start(bf16[8,32,1536]{2,1,0:T(8,128)(2,1)} %bitcast.81), calls=%async_computation.1 | async-start | bytes 1572864 | tf_op jit(solution)/shard_map/all_to_all | solution.py:81
  5.1 0.2 reduce-window.8
  5.3 0.3 reshape_squeeze.3
  5.6 1.2 copy.14
  6.9 11.4 %all-to-all-done.1 = bf16[8,32,1536]{2,1,0:T(8,128)(2,1)S(1)} async-done(((bf16[8,32,1536]{2,1,0:T(8,128)(2,1)}), bf16[8,32,1536]{2,1,0:T(8,128)(2,1)S(1)}, u32[]{:S(2)}, u32[]{:S(2)}) %all-to-all-start.1) | async-done | bytes 786464 | tf_op jit(solution)/shard_map/all_to_all | solution.py:81
  18.3 3.6 %all-to-all-start = ((bf16[8,3,64,384]{3,2,1,0:T(8,128)(2,1)}), bf16[8,3,64,384]{3,2,1,0:T(8,128)(2,1)S(1)}, u32[]{:S(2)}, u32[]{:S(2)}) async-start(bf16[8,3,64,384]{3,2,1,0:T(8,128)(2,1)} %bitcast.1), calls=%async_computation | async-start | bytes 2359296 | tf_op jit(solution)/shard_map/all_to_all | solution.py:84
  22.1 0.4 fusion
  22.5 16.7 %all-to-all-done.qkv_ref = bf16[8,3,64,384]{3,2,1,0:T(8,128)(2,1)S(1)} async-done(((bf16[8,3,64,384]{3,2,1,0:T(8,128)(2,1)}), bf16[8,3,64,384]{3,2,1,0:T(8,128)(2,1)S(1)}, u32[]{:S(2)}, u32[]{:S(2)}) %all-to-all-start) | async-done | bytes 1179680 | tf_op jit(solution)/shard_map/all_to_all | solution.py:84
  39.1 1.3 broadcast_in_dim.52
  40.4 3.6 %all-to-all-start.2 = ((bf16[8,64,1536]{2,1,0:T(8,128)(2,1)}), bf16[8,64,1536]{2,1,0:T(8,128)(2,1)S(1)}, u32[]{:S(2)}, u32[]{:S(2)}) async-start(bf16[8,64,1536]{2,1,0:T(8,128)(2,1)} %bitcast.76), calls=%async_computation.2 | async-start | bytes 3145728 | tf_op jit(solution)/shard_map/all_to_all | solution.py:112
  44.3 0.2 broadcast_in_dim.46
  44.6 1.3 broadcast_in_dim.48
  45.9 1.8 broadcast_in_dim.49
  47.7 0.6 fusion.137
  48.3 0.6 iota_divide_fusion
  48.9 4.0 %attn_fwd.1 = (f32[3,4,128,128]{3,2,1,0:T(8,128)S(1)}, bf16[8,64,384]{2,1,0:T(8,128)(2,1)S(1)}) custom-call(bf16[8,3,64,384]{3,2,1,0:T(8,128)(2,1)S(1)} %all-to-all-done.qkv_ref, f32[3,128,128]{2,1,0:T(8,128)S(1)} %broadcast_select_fusion.bias_ref), custom_call_target="tpu_custom_call" | custom-call | flops 200000000 | bytes 4000000 | tf_op jit(solution)/shard_map/attn_fwd/pallas_call | solution.py:118
  52.9 0.7 copy-done.4
  53.7 11.9 %all-to-all-done.2.up_ref = bf16[8,64,1536]{2,1,0:T(8,128)(2,1)S(1)} async-done(((bf16[8,64,1536]{2,1,0:T(8,128)(2,1)}), bf16[8,64,1536]{2,1,0:T(8,128)(2,1)S(1)}, u32[]{:S(2)}, u32[]{:S(2)}) %all-to-all-start.2) | async-done | bytes 1572896 | tf_op jit(solution)/shard_map/all_to_all | solution.py:112
  65.5 3.7 %fusion.1 = f32[384,1536]{1,0:T(8,128)} fusion(bf16[512,1536]{1,0:T(8,128)(2,1)S(1)} %bitcast.74, bf16[512,384]{1,0:T(8,128)(2,1)} %bitcast.75, s32[384]{0:T(512)} %get-tuple-element.20, s32[384]{0:T(512)S(1)} %get-tuple-element.21, s32[384]{0:T(512)} %get-tuple-element.19, s32[384]{0:T(512)S(1)} %get-tuple-element.22, ...), kind=kOutput, calls=%fused_computation.13 | convolution fusion | flops 765788160 | bytes 4332288 | tf_op jit(solution)/shard_map/dot_general | solution.py:27
  69.2 2.4 %constant_dynamic-slice_fusion = f32[192,1536]{1,0:T(8,128)} fusion(f32[384,1536]{1,0:T(8,128)} %fusion.1, s32[]{:T(128)S(6)} %select_n.108), kind=kLoop, calls=%fused_computation.179 | loop fusion | bytes 2359300 | tf_op jit(solution)/shard_map/dynamic_slice | solution.py:140
  71.6 7.7 %collective-permute-start = (bf16[8,1536]{1,0:T(8,128)(2,1)S(1)}, bf16[8,1536]{1,0:T(8,128)(2,1)S(1)}, u32[]{:S(2)}, u32[]{:S(2)}) collective-permute-start(bf16[8,1536]{1,0:T(8,128)(2,1)S(1)} %pad.44), channel_id=1, source_target_pairs={{0,0},{2,32},{4,64},{6,96},{32,128},{34,160},{36,192},{38,224},{64... | collective-permute-start | bytes 73736 | tf_op jit(solution)/shard_map/ppermute | solution.py:93
  79.4 1.5 collective-permute-done
  80.9 17.9 %all_to_all.40 = bf16[8,8,1536]{2,1,0:T(8,128)(2,1)S(1)} all-to-all(bf16[8,8,1536]{2,1,0:T(8,128)(2,1)S(1)} %broadcast_in_dim.53), channel_id=1, replica_groups=mesh['z'=8,'y'=4,'x'=4,'core'=2] {'z'}, dimensions={0} | all-to-all | bytes 393216 | tf_op jit(solution)/shard_map/all_to_all | solution.py:94
  98.8 14.6 %all_to_all.41 = bf16[4,64,1536]{2,1,0:T(8,128)(2,1)} all-to-all(bf16[4,64,1536]{2,1,0:T(8,128)(2,1)S(1)} %broadcast_in_dim.54), channel_id=1, replica_groups=mesh['z'=8,'y'=4,'x'=4,'core'=2] {'y'}, dimensions={0} | all-to-all | bytes 1572864 | tf_op jit(solution)/shard_map/all_to_all | solution.py:95
  113.5 2.6 %add_convert_fusion = bf16[192,1536]{1,0:T(8,128)(2,1)} fusion(f32[192,1536]{1,0:T(8,128)} %collective-permute-done.10, f32[384,1536]{1,0:T(8,128)} %fusion.1, s32[]{:T(128)S(6)} %select_n.107), kind=kLoop, calls=%fused_computation.31 | loop fusion | flops 589824 | bytes 2949124 | tf_op jit(solution)/shard_map/convert_element_type | solution.py:142
  116.0 4.2 %all-to-all-start.6 = ((bf16[4,48,1536]{2,1,0:T(8,128)(2,1)}), bf16[4,48,1536]{2,1,0:T(8,128)(2,1)}, u32[]{:S(2)}, u32[]{:S(2)}) async-start(bf16[4,48,1536]{2,1,0:T(8,128)(2,1)} %bitcast.78), calls=%async_computation.6 | async-start | bytes 1179648 | tf_op jit(solution)/shard_map/all_to_all | solution.py:143
  120.2 2.7 %pad_maximum_fusion = bf16[8,64,1536]{2,1,0:T(8,128)(2,1)} fusion(bf16[4,64,1536]{2,1,0:T(8,128)(2,1)} %collective-permute-done.1, bf16[4,64,1536]{2,1,0:T(8,128)(2,1)} %all_to_all.41), kind=kLoop, calls=%fused_computation.7 | loop fusion | flops 786432 | bytes 3145728 | tf_op jit(solution)/shard_map/concatenate | solution.py:97
  122.9 8.5 %all-to-all-done.6 = bf16[4,48,1536]{2,1,0:T(8,128)(2,1)} async-done(((bf16[4,48,1536]{2,1,0:T(8,128)(2,1)}), bf16[4,48,1536]{2,1,0:T(8,128)(2,1)}, u32[]{:S(2)}, u32[]{:S(2)}) %all-to-all-start.6) | async-done | bytes 589856 | tf_op jit(solution)/shard_map/all_to_all | solution.py:143
  131.4 1.9 convert_reduce_fusion
  133.3 1.7 reshape.105
  135.0 1.8 pad.54
  136.8 5.1 %all-to-all-start.7 = ((f32[8,8,1536]{2,1,0:T(8,128)}), f32[8,8,1536]{2,1,0:T(8,128)}, u32[]{:S(2)}, u32[]{:S(2)}) async-start(f32[8,8,1536]{2,1,0:T(8,128)} %pad.54), calls=%async_computation.7 | async-start | bytes 786432 | tf_op jit(solution)/shard_map/all_to_all | solution.py:145
  141.9 3.3 %convolution_convert_fusion.w_ref = bf16[384,1536]{1,0:T(8,128)(2,1)S(1)} fusion(bf16[512,1536]{1,0:T(8,128)(2,1)} %bitcast.79, s32[384]{0:T(512)} %get-tuple-element.20, s32[384]{0:T(512)S(1)} %get-tuple-element.21, s32[]{:T(128)S(6)} %axis_index.25, s32[384]{0:T(512)} %get-tuple-element.19, s32[384]{0:T(512)S(1)} %get-tuple-element.22, ...), kind=kOutput, calls=%fused_computation | convolution fusion | flops 618921984 | bytes 2759428 | tf_op jit(solution)/shard_map/dot_general | solution.py:27
  145.2 4.5 %attn_bwd.1 = (bf16[8,3,64,384]{3,2,1,0:T(8,128)(2,1)S(1)}, f32[3,8,128]{2,1,0:T(8,128)S(1)}) custom-call(bf16[8,3,64,384]{3,2,1,0:T(8,128)(2,1)S(1)} %all-to-all-done.qkv_ref, f32[3,4,128,128]{3,2,1,0:T(8,128)S(1)} %get-tuple-element.7.probs_ref, bf16[8,64,1536]{2,1,0:T(8,128)(2,1)S(1)} %all-to-all-done.2.up_ref, ...), custom_call_target="tpu_custom_call" | custom-call | flops 900000000 | bytes 6000000 | tf_op jit(solution)/shard_map/attn_bwd/pallas_call | solution.py:148
  149.7 1.0 copy-done.1
  150.7 0.6 copy-done.2
  151.3 4.1 %all-to-all-done.7 = f32[8,8,1536]{2,1,0:T(8,128)} async-done(((f32[8,8,1536]{2,1,0:T(8,128)}), f32[8,8,1536]{2,1,0:T(8,128)}, u32[]{:S(2)}, u32[]{:S(2)}) %all-to-all-start.7) | async-done | bytes 393248 | tf_op jit(solution)/shard_map/all_to_all | solution.py:145
  155.4 3.7 %all-to-all-start.5 = ((bf16[8,3,64,384]{3,2,1,0:T(8,128)(2,1)}), bf16[8,3,64,384]{3,2,1,0:T(8,128)(2,1)S(1)}, u32[]{:S(2)}, u32[]{:S(2)}) async-start(bf16[8,3,64,384]{3,2,1,0:T(8,128)(2,1)} %copy-done.1), calls=%async_computation.5 | async-start | bytes 2359296 | tf_op jit(solution)/shard_map/all_to_all | solution.py:159
  159.1 0.1 reshape.102
  159.2 0.1 reduce_sum.52
  159.5 0.1 dynamic_update_slice.5
  159.7 0.5 collective-permute-start.2
  160.1 0.8 collective-permute-done.2
  161.0 0.1 add.154
  161.1 2.0 collective-permute-start.3
  163.1 12.0 %collective-permute-done.3 = f32[16,128]{1,0:T(8,128)S(1)} collective-permute-done((f32[16,128]{1,0:T(8,128)S(1)}, f32[16,128]{1,0:T(8,128)S(1)}, u32[]{:S(2)}, u32[]{:S(2)}) %collective-permute-start.3) | collective-permute-done | bytes 8224 | tf_op jit(solution)/shard_map/ppermute | solution.py:73
  175.1 2.7 %collective-permute-start.4 = (f32[16,128]{1,0:T(8,128)S(1)}, f32[16,128]{1,0:T(8,128)S(1)}, u32[]{:S(2)}, u32[]{:S(2)}) collective-permute-start(f32[16,128]{1,0:T(8,128)S(1)} %add.155), channel_id=1, source_target_pairs={{0,4},{2,6},{4,0},{6,2},{1,5},{3,7},{5,1},{7,3},{8,12},{10,14},{12... | collective-permute-start | bytes 24584 | tf_op jit(solution)/shard_map/ppermute | solution.py:73
  177.8 2.5 %collective-permute-done.4 = f32[16,128]{1,0:T(8,128)S(1)} collective-permute-done((f32[16,128]{1,0:T(8,128)S(1)}, f32[16,128]{1,0:T(8,128)S(1)}, u32[]{:S(2)}, u32[]{:S(2)}) %collective-permute-start.4) | collective-permute-done | bytes 8224 | tf_op jit(solution)/shard_map/ppermute | solution.py:73
  180.2 0.6 collective-permute-start.5
  180.8 3.1 %collective-permute-done.5 = f32[16,128]{1,0:T(8,128)S(1)} collective-permute-done((f32[16,128]{1,0:T(8,128)S(1)}, f32[16,128]{1,0:T(8,128)S(1)}, u32[]{:S(2)}, u32[]{:S(2)}) %collective-permute-start.5) | collective-permute-done | bytes 8224 | tf_op jit(solution)/shard_map/ppermute | solution.py:73
  183.9 0.5 collective-permute-start.6
  184.5 4.6 %collective-permute-done.6 = f32[16,128]{1,0:T(8,128)S(1)} collective-permute-done((f32[16,128]{1,0:T(8,128)S(1)}, f32[16,128]{1,0:T(8,128)S(1)}, u32[]{:S(2)}, u32[]{:S(2)}) %collective-permute-start.6) | collective-permute-done | bytes 8224 | tf_op jit(solution)/shard_map/ppermute | solution.py:73
  189.1 1.4 collective-permute-start.7
  190.5 2.2 %collective-permute-done.7 = f32[16,128]{1,0:T(8,128)S(1)} collective-permute-done((f32[16,128]{1,0:T(8,128)S(1)}, f32[16,128]{1,0:T(8,128)S(1)}, u32[]{:S(2)}, u32[]{:S(2)}) %collective-permute-start.7) | collective-permute-done | bytes 8224 | tf_op jit(solution)/shard_map/ppermute | solution.py:73
  192.8 4.6 %collective-permute-done.8 = f32[16,128]{1,0:T(8,128)S(1)} collective-permute-done((f32[16,128]{1,0:T(8,128)S(1)}, f32[16,128]{1,0:T(8,128)S(1)}, u32[]{:S(2)}, u32[]{:S(2)}) %collective-permute-start.8) | collective-permute-done | bytes 8224 | tf_op jit(solution)/shard_map/ppermute | solution.py:73
  197.4 1.4 collective-permute-start.9
  198.7 1.0 reduce_sum.61
  199.8 2.2 %collective-permute-start.11 = (f32[8,1536]{1,0:T(8,128)S(1)}, f32[8,1536]{1,0:T(8,128)S(1)}, u32[]{:S(2)}, u32[]{:S(2)}) collective-permute-start(f32[8,1536]{1,0:T(8,128)S(1)} %reduce_sum.61), channel_id=1, source_target_pairs={{0,0},{32,2},{64,4},{96,6},{128,32},{160,34},{192,36},{224,38},{2,... | collective-permute-start | bytes 147464 | tf_op jit(solution)/shard_map/ppermute | solution.py:146
  202.0 2.9 %collective-permute-done.9 = f32[16,128]{1,0:T(8,128)S(1)} collective-permute-done((f32[16,128]{1,0:T(8,128)S(1)}, f32[16,128]{1,0:T(8,128)S(1)}, u32[]{:S(2)}, u32[]{:S(2)}) %collective-permute-start.9) | collective-permute-done | bytes 8224 | tf_op jit(solution)/shard_map/ppermute | solution.py:73
  204.9 0.6 slice_add_fusion
  205.5 0.9 copy.16
  206.5 1.3 reshape.101
  207.8 1.1 collective-permute-done.11
  208.8 0.6 copy.51
  (56 shorter events, 1.0 us)
Async XLA Ops:
  0.6 6.2 %copy-start = (f32[12,15]{1,0:T(8,128)S(1)}, f32[12,15]{1,0:T(8,128)}, u32[]{:S(2)}) copy-start(f32[12,15]{1,0:T(8,128)} %param.7) | copy-start | bytes 2164
  0.6 4.5 %copy-start.7 = (s32[1,8]{1,0:T(1,128)S(1)}, s32[1,8]{1,0:T(1,128)}, u32[]{:S(2)}) copy-start(s32[1,8]{1,0:T(1,128)} %param.6) | copy-start | bytes 100
  0.7 4.6 %copy-start.5 = (bf16[3,1,1,128,1536]{4,3,2,1,0:T(8,128)(2,1)S(1)}, bf16[3,1,1,128,1536]{4,3,2,1,0:T(8,128)(2,1)}, u32[]{:S(2)}) copy-start(bf16[3,1,1,128,1536]{4,3,2,1,0:T(8,128)(2,1)} %param.5) | copy-start | bytes 3538948
  0.7 17.6 %all-to-all-start.1 = ((bf16[8,32,1536]{2,1,0:T(8,128)(2,1)}), bf16[8,32,1536]{2,1,0:T(8,128)(2,1)S(1)}, u32[]{:S(2)}, u32[]{:S(2)}) async-start(bf16[8,32,1536]{2,1,0:T(8,128)(2,1)} %bitcast.81), calls=%async_computation.1 | async-start | bytes 1572864 | tf_op jit(solution)/shard_map/all_to_all | solution.py:81
  18.3 20.9 %all-to-all-start = ((bf16[8,3,64,384]{3,2,1,0:T(8,128)(2,1)}), bf16[8,3,64,384]{3,2,1,0:T(8,128)(2,1)S(1)}, u32[]{:S(2)}, u32[]{:S(2)}) async-start(bf16[8,3,64,384]{3,2,1,0:T(8,128)(2,1)} %bitcast.1), calls=%async_computation | async-start | bytes 2359296 | tf_op jit(solution)/shard_map/all_to_all | solution.py:84
  40.4 25.1 %all-to-all-start.2 = ((bf16[8,64,1536]{2,1,0:T(8,128)(2,1)}), bf16[8,64,1536]{2,1,0:T(8,128)(2,1)S(1)}, u32[]{:S(2)}, u32[]{:S(2)}) async-start(bf16[8,64,1536]{2,1,0:T(8,128)(2,1)} %bitcast.76), calls=%async_computation.2 | async-start | bytes 3145728 | tf_op jit(solution)/shard_map/all_to_all | solution.py:112
  52.9 0.7 copy-start.4
  69.2 2.4 %copy-start.6 = (bf16[6,1536]{1,0:T(8,128)(2,1)S(1)}, bf16[6,1536]{1,0:T(8,128)(2,1)}, u32[]{:S(2)}) copy-start(bf16[6,1536]{1,0:T(8,128)(2,1)} %param.8) | copy-start | bytes 55300
  71.6 41.9 %collective-permute-start.10 = (f32[192,1536]{1,0:T(8,128)}, f32[192,1536]{1,0:T(8,128)}, u32[]{:S(2)}, u32[]{:S(2)}) collective-permute-start(f32[192,1536]{1,0:T(8,128)} %constant_dynamic-slice_fusion), channel_id=1, source_target_pairs={{0,1},{1,0},{2,3},{3,2},{4,5},{5,4},{6,7},{7,6},{8,9},{9,8},{10,11... | collective-permute-start | bytes 3538952 | tf_op jit(solution)/shard_map/ppermute | solution.py:73
  71.6 9.2 %collective-permute-start = (bf16[8,1536]{1,0:T(8,128)(2,1)S(1)}, bf16[8,1536]{1,0:T(8,128)(2,1)S(1)}, u32[]{:S(2)}, u32[]{:S(2)}) collective-permute-start(bf16[8,1536]{1,0:T(8,128)(2,1)S(1)} %pad.44), channel_id=1, source_target_pairs={{0,0},{2,32},{4,64},{6,96},{32,128},{34,160},{36,192},{38,224},{64... | collective-permute-start | bytes 73736 | tf_op jit(solution)/shard_map/ppermute | solution.py:93
  113.5 6.7 %collective-permute-start.1 = (bf16[4,64,1536]{2,1,0:T(8,128)(2,1)}, bf16[4,64,1536]{2,1,0:T(8,128)(2,1)}, u32[]{:S(2)}, u32[]{:S(2)}) collective-permute-start(bf16[4,64,1536]{2,1,0:T(8,128)(2,1)} %all_to_all.41), channel_id=1, source_target_pairs={{0,1},{1,0},{2,3},{3,2},{4,5},{5,4},{6,7},{7,6},{8,9},{9,8},{10,11... | collective-permute-start | bytes 2359304 | tf_op jit(solution)/shard_map/ppermute | solution.py:73
  116.0 15.3 %all-to-all-start.6 = ((bf16[4,48,1536]{2,1,0:T(8,128)(2,1)}), bf16[4,48,1536]{2,1,0:T(8,128)(2,1)}, u32[]{:S(2)}, u32[]{:S(2)}) async-start(bf16[4,48,1536]{2,1,0:T(8,128)(2,1)} %bitcast.78), calls=%async_computation.6 | async-start | bytes 1179648 | tf_op jit(solution)/shard_map/all_to_all | solution.py:143
  136.8 18.6 %all-to-all-start.7 = ((f32[8,8,1536]{2,1,0:T(8,128)}), f32[8,8,1536]{2,1,0:T(8,128)}, u32[]{:S(2)}, u32[]{:S(2)}) async-start(f32[8,8,1536]{2,1,0:T(8,128)} %pad.54), calls=%async_computation.7 | async-start | bytes 786432 | tf_op jit(solution)/shard_map/all_to_all | solution.py:145
  149.7 1.0 copy-start.1
  150.7 0.6 copy-start.2
  155.4 3.7 %copy-start.3 = (f32[3,8,128]{2,1,0:T(8,128)S(1)}, f32[3,8,128]{2,1,0:T(8,128)}, u32[]{:S(2)}) copy-start(f32[3,8,128]{2,1,0:T(8,128)} %copy-done.2) | copy-start | bytes 36868
  155.4 50.1 %all-to-all-start.5 = ((bf16[8,3,64,384]{3,2,1,0:T(8,128)(2,1)}), bf16[8,3,64,384]{3,2,1,0:T(8,128)(2,1)S(1)}, u32[]{:S(2)}, u32[]{:S(2)}) async-start(bf16[8,3,64,384]{3,2,1,0:T(8,128)(2,1)} %copy-done.1), calls=%async_computation.5 | async-start | bytes 2359296 | tf_op jit(solution)/shard_map/all_to_all | solution.py:159
  159.7 1.3 collective-permute-start.2
  161.1 14.0 %collective-permute-start.3 = (f32[16,128]{1,0:T(8,128)S(1)}, f32[16,128]{1,0:T(8,128)S(1)}, u32[]{:S(2)}, u32[]{:S(2)}) collective-permute-start(f32[16,128]{1,0:T(8,128)S(1)} %add.154), channel_id=1, source_target_pairs={{0,2},{2,0},{4,6},{6,4},{1,3},{3,1},{5,7},{7,5},{8,10},{10,8},{12,... | collective-permute-start | bytes 24584 | tf_op jit(solution)/shard_map/ppermute | solution.py:73
  175.1 5.2 %collective-permute-start.4 = (f32[16,128]{1,0:T(8,128)S(1)}, f32[16,128]{1,0:T(8,128)S(1)}, u32[]{:S(2)}, u32[]{:S(2)}) collective-permute-start(f32[16,128]{1,0:T(8,128)S(1)} %add.155), channel_id=1, source_target_pairs={{0,4},{2,6},{4,0},{6,2},{1,5},{3,7},{5,1},{7,3},{8,12},{10,14},{12... | collective-permute-start | bytes 24584 | tf_op jit(solution)/shard_map/ppermute | solution.py:73
  180.2 3.7 %collective-permute-start.5 = (f32[16,128]{1,0:T(8,128)S(1)}, f32[16,128]{1,0:T(8,128)S(1)}, u32[]{:S(2)}, u32[]{:S(2)}) collective-permute-start(f32[16,128]{1,0:T(8,128)S(1)} %add.156), channel_id=1, source_target_pairs={{0,8},{8,0},{16,24},{24,16},{1,9},{9,1},{17,25},{25,17},{2,10},{10... | collective-permute-start | bytes 24584 | tf_op jit(solution)/shard_map/ppermute | solution.py:73
  183.9 5.2 %collective-permute-start.6 = (f32[16,128]{1,0:T(8,128)S(1)}, f32[16,128]{1,0:T(8,128)S(1)}, u32[]{:S(2)}, u32[]{:S(2)}) collective-permute-start(f32[16,128]{1,0:T(8,128)S(1)} %add.157), channel_id=1, source_target_pairs={{0,16},{8,24},{16,0},{24,8},{1,17},{9,25},{17,1},{25,9},{2,18},{10... | collective-permute-start | bytes 24584 | tf_op jit(solution)/shard_map/ppermute | solution.py:73
  189.1 3.7 %collective-permute-start.7 = (f32[16,128]{1,0:T(8,128)S(1)}, f32[16,128]{1,0:T(8,128)S(1)}, u32[]{:S(2)}, u32[]{:S(2)}) collective-permute-start(f32[16,128]{1,0:T(8,128)S(1)} %add.158), channel_id=1, source_target_pairs={{0,32},{32,0},{64,96},{96,64},{128,160},{160,128},{192,224},{224,1... | collective-permute-start | bytes 24584 | tf_op jit(solution)/shard_map/ppermute | solution.py:73
  192.8 4.6 %collective-permute-start.8 = (f32[16,128]{1,0:T(8,128)S(1)}, f32[16,128]{1,0:T(8,128)S(1)}, u32[]{:S(2)}, u32[]{:S(2)}) collective-permute-start(f32[16,128]{1,0:T(8,128)S(1)} %add.159), channel_id=1, source_target_pairs={{0,64},{32,96},{64,0},{96,32},{128,192},{160,224},{192,128},{224,1... | collective-permute-start | bytes 24584 | tf_op jit(solution)/shard_map/ppermute | solution.py:73
  197.4 7.6 %collective-permute-start.9 = (f32[16,128]{1,0:T(8,128)S(1)}, f32[16,128]{1,0:T(8,128)S(1)}, u32[]{:S(2)}, u32[]{:S(2)}) collective-permute-start(f32[16,128]{1,0:T(8,128)S(1)} %add.160), channel_id=1, source_target_pairs={{0,128},{32,160},{64,192},{96,224},{128,0},{160,32},{192,64},{224,... | collective-permute-start | bytes 24584 | tf_op jit(solution)/shard_map/ppermute | solution.py:73
  199.8 9.0 %collective-permute-start.11 = (f32[8,1536]{1,0:T(8,128)S(1)}, f32[8,1536]{1,0:T(8,128)S(1)}, u32[]{:S(2)}, u32[]{:S(2)}) collective-permute-start(f32[8,1536]{1,0:T(8,128)S(1)} %reduce_sum.61), channel_id=1, source_target_pairs={{0,0},{32,2},{64,4},{96,6},{128,32},{160,34},{192,36},{224,38},{2,... | collective-permute-start | bytes 147464 | tf_op jit(solution)/shard_map/ppermute | solution.py:146

commit v2 on v1

v2 whole, which is shorter than its diff:
```python
import functools
import math

import jax
import jax.numpy as jnp
from jax import lax
from jax.experimental import pallas as pl
from jax.experimental.pallas import tpu as pltpu
from jax.sharding import Mesh, PartitionSpec as P

Z, Y, X, C = 8, 4, 4, 2
SEQ = ("x", "core")
F = 8
POS = 128
HALF = 64
NB = 4
HL = 3
HD = 128
COLS = HL * HD
DW = 1536
CAP = 32
FACTOR = 1.0 / math.sqrt(HD)
NN = (((1,), (0,)), ((), ()))
NT = (((1,), (1,)), ((), ()))
TN = (((0,), (0,)), ((), ()))
bf, f32 = jnp.bfloat16, jnp.float32
CORE, YI, ZI, RANK = 0, 1, 2, 3


def dot(a, b, dims, **kw):
    return lax.dot_general(a, b, dims, preferred_element_type=f32, **kw)


def iota(shape, dim):
    return lax.broadcasted_iota(jnp.int32, shape, dim)


def call(body, name, outs, *ins, smem=0, scratch=(), flops=0):
    total = sum(math.prod(s) * jnp.dtype(d).itemsize for s, d in outs)
    total += sum(a.size * a.dtype.itemsize for a in ins)
    specs = [pl.BlockSpec(memory_space=pltpu.SMEM)] * smem
    specs += [pl.BlockSpec(memory_space=pltpu.VMEM)] * (len(ins) - smem)
    return pl.pallas_call(
        body,
        out_shape=tuple(jax.ShapeDtypeStruct(s, d) for s, d in outs),
        in_specs=specs,
        out_specs=tuple(pl.BlockSpec(memory_space=pltpu.VMEM) for _ in outs),
        scratch_shapes=list(scratch),
        compiler_params=pltpu.CompilerParams(vmem_limit_bytes=32 << 20),
        cost_estimate=pl.CostEstimate(flops=flops, bytes_accessed=total, transcendentals=0),
        name=name,
    )(*ins)


def compact_kernel(place, sizes, cot_ref, same_ref, other_ref):
    shape = (POS, F * CAP)
    row, col = iota(shape, 0), iota(shape, 1)
    pos = row ^ (place[CORE] * HALF)
    start = jnp.int32(0)
    picked = jnp.full(shape, -1, jnp.int32)
    for j in range(F):
        slot = col - j * CAP
        inside = (slot >= 0) & (slot < sizes[0, j])
        picked = jnp.where(inside, slot + start, picked)
        start = start + sizes[0, j]
    hot = (picked == pos).astype(f32).astype(bf)
    up = dot(hot, cot_ref[...].reshape(F * CAP, DW), NN).astype(bf)
    same_ref[...] = up[:HALF]
    other_ref[...] = up[HALF:]


def block(ref, i, b, h):
    return ref[:, i, b * 16 : (b + 1) * 16, h * HD : (h + 1) * HD].reshape(POS, HD)


def fwd_kernel(qkv_ref, bias_ref, order_ref, probs_ref, mixed_ref, raw_ref):
    for h in range(HL):
        for b in range(NB):
            q, k, v = (block(qkv_ref, i, b, h) for i in range(3))
            s = dot(q, k, NT) * FACTOR + bias_ref[h]
            e = jnp.exp(s - jnp.max(s, axis=-1, keepdims=True))
            p = e / jnp.sum(e, axis=-1, keepdims=True)
            probs_ref[h, b] = p
            m = dot(p.astype(bf), v, NN).astype(bf).reshape(F, 16, HD)
            raw_ref[:, b * 16 : (b + 1) * 16, h * HD : (h + 1) * HD] = m
    mixed_ref[...] = dot(raw_ref[...].reshape(F * HALF, COLS), order_ref[...], NN).astype(bf)


def gw_kernel(place, *refs):
    pieces, mixed_ref, up_ref, mine_ref, other_ref = refs[:F], *refs[F:]
    for k in range(F):
        up_ref[place[RANK] ^ k] = pieces[k][...]
    up = up_ref[...].reshape(F * HALF, DW)
    gw = dot(mixed_ref[...], up, TN)
    mine_ref[...] = gw[: COLS // 2]
    other_ref[...] = gw[COLS // 2 :].astype(bf)


def score_kernel(qkv_ref, probs_ref, up_ref, w_ref, dm_ref, ds_ref, sums_ref):
    dm = dot(up_ref[...].reshape(F * HALF, DW), w_ref[...], NT)
    dm_ref[...] = dm.astype(bf).reshape(F, HALF, COLS)
    for h in range(HL):
        cols = slice(h * HD, (h + 1) * HD)
        total = jnp.zeros((F, POS), f32)
        for b in range(NB):
            d = dm_ref[:, b * 16 : (b + 1) * 16, cols].reshape(POS, HD)
            p = probs_ref[h, b]
            g = dot(d, block(qkv_ref, 2, b, h), NT)
            ds = p * (g - jnp.sum(p * g, axis=-1, keepdims=True))
            total = total + jnp.sum(ds.reshape(F, 16, POS), axis=1)
            ds_ref[h, b] = ds.astype(bf)
        sums_ref[:, cols] = total


def grad_kernel(qkv_ref, probs_ref, dm_ref, ds_ref, grads_ref):
    for h in range(HL):
        cols = slice(h * HD, (h + 1) * HD)
        for b in range(NB):
            rows = slice(b * 16, (b + 1) * 16)
            d = dm_ref[:, rows, cols].reshape(POS, HD)
            low = ds_ref[h, b]
            gq = dot(low, block(qkv_ref, 1, b, h), NN) * FACTOR
            gk = dot(low, block(qkv_ref, 0, b, h), TN) * FACTOR
            gv = dot(probs_ref[h, b].astype(bf), d, TN)
            for i, val in enumerate((gq, gk, gv)):
                grads_ref[:, i, rows, cols] = val.astype(bf).reshape(F, 16, HD)


def tiles(x):
    return jnp.concatenate([x[:, a * 128 : (a + 1) * 128] for a in range(HL)], axis=0)


def join_kernel(mine_ref, other_ref, sums_ref, sums2_ref, own_ref, b_ref, m1, m2, m3):
    gw = mine_ref[...] + other_ref[...].astype(f32)
    b = tiles(sums_ref[...] + sums2_ref[...])
    own_ref[...] = gw[:48]
    high = b.astype(bf).astype(f32)
    low = (b - high).astype(bf).astype(f32)
    b_ref[...] = high + low
    ride = jnp.concatenate([high, low], axis=0).astype(bf)
    for k, m in enumerate((m1, m2, m3), 1):
        m[:, :DW] = gw[48 * k : 48 * (k + 1)].astype(bf)
        m[:, DW:] = ride


def ysum_kernel(own_ref, b_ref, m1, m2, m3, keep_ref, send_ref):
    gw = [own_ref[...]] + [m[:, :DW].astype(f32) for m in (m1, m2, m3)]
    rides = [m[:, DW:].astype(f32) for m in (m1, m2, m3)]
    b = [b_ref[...]] + [x[:24] + x[24:] for x in rides]
    gw, b = ((x[0] + x[1]) + (x[2] + x[3]) for x in (gw, b))
    flat = jnp.concatenate([b[2 * a : 2 * a + 2] for a in range(12)], axis=1)
    for ref, part in ((keep_ref, gw[:24]), (send_ref, gw[24:])):
        ref[:24] = part
        ref[24:26] = flat
        ref[26:] = jnp.zeros((6, DW), f32)


def zsum_kernel(keep_ref, recv_ref, first_ref, second_ref):
    n = first_ref.shape[0]
    total = keep_ref[...] + recv_ref[...]
    rows = {16: 12, 8: 6}[n]
    for ref, part in ((first_ref, total[:rows]), (second_ref, total[rows : 2 * rows])):
        ref[:rows] = part
        ref[rows : rows + 2] = total[2 * rows : 2 * rows + 2]
        if n - rows > 2:
            ref[rows + 2 :] = jnp.zeros((n - rows - 2, DW), f32)


def last_kernel(a_ref, b_ref, gw_ref, off_ref):
    total = a_ref[...] + b_ref[...]
    gw_ref[...] = total[:6]
    flat = total[6:8]
    rows = [flat[:, 128 * a : 128 * (a + 1)] for a in range(12)]
    sums = jnp.concatenate(rows, axis=0)
    out = jnp.zeros((16, 128), f32)
    head = iota((16, 24), 0) % HL
    t = iota((16, 24), 1)
    g = iota((128, 128), 0) // 16
    o = iota((128, 128), 1)
    hi = lax.Precision.HIGHEST
    for f in range(F):
        pick = (t == head * F + f).astype(f32)
        row = dot(pick, sums, NN, precision=hi)
        out = out + dot(row, (g - f + 7 == o).astype(f32), NN, precision=hi)
    off_ref[...] = out


def bias_kernel(place, *refs):
    parts, out_ref = refs[:4], refs[4]
    row = iota((16, 128), 0) // HL
    out = jnp.zeros((16, 128), f32)
    for k in range(4):
        out = out + jnp.where(row == ((place[ZI] // 2) ^ k), parts[k][...], 0.0)
    out_ref[...] = out[:12, :15]


def hop(x, axis, k, n):
    return lax.ppermute(x, axis, [(i, i ^ k) for i in range(n)])


def per_device(qkv_time, shard_sizes, bias_time, w_out, cot_out):
    xi, yi, zi = (lax.axis_index(a) for a in ("x", "y", "z"))
    core = lax.axis_index("core")
    place = jnp.stack([core, yi, zi, xi * C + core]).astype(jnp.int32)

    there = [
        ((2 * c + z0) * X + x, (z0 * X + x) * X + c)
        for c in range(X)
        for z0 in range(2)
        for x in range(X)
    ]
    held = lax.ppermute(jnp.pad(w_out, ((0, 2), (0, 0))), ("z", "x"), there)
    for axis, n in (("z", Z), ("y", Y), ("core", C)):
        k = 1
        while k < n:
            held = jnp.concatenate([held, hop(held, axis, k, n)])
            k *= 2

    cot = lax.all_to_all(cot_out[0, 0], SEQ, 0, 0, tiled=True)
    packed = qkv_time[:, 0, 0].reshape(3, C, HALF, X, COLS).transpose(3, 1, 0, 2, 4)
    qkv = lax.all_to_all(packed.reshape(F, 3, HALF, COLS), SEQ, 0, 0, tiled=True)

    same, other = call(
        compact_kernel, "compact", [((HALF, DW), bf)] * 2, place, shard_sizes, cot, smem=2, flops=100_000_000
    )
    pieces = [same] + [hop(other if k & 1 else same, SEQ, k, F) for k in range(1, F)]

    r, t = iota((COLS, 512), 0), iota((COLS, 512), 1)
    i, sub = r % 6, r // 6
    rj, ry, rc = (sub // 32) * 4 + (sub // 2) % 4, (sub // 8) % 4, sub % 2
    spot = (((rc ^ core) * 4 + (ry ^ yi)) * 8 + (rj ^ zi)) * 8 + i
    w_c = dot((spot == t).astype(bf), held, NN).astype(bf)

    local_bias = lax.dynamic_slice(bias_time, (xi * HL, 0), (HL, 15))
    pair = jnp.stack([local_bias[:, 7 - f : 15 - f] for f in range(F)], axis=1)
    alike = jnp.eye(16, dtype=jnp.bool_)[None, None, :, None, :]
    bias_m = jnp.where(alike, pair[:, :, None, :, None], f32(-1e30)).reshape(HL, POS, POS)
    t2, r2 = iota((COLS, COLS), 1), iota((COLS, COLS), 0)
    j = (((t2 // 24) % 2) + ((t2 // 12) % 2) * 2 + ((t2 // 6) % 2) * 4) ^ zi
    oy, oc = ((t2 // 48) % 4) ^ yi, (t2 // 192) ^ core
    src = (((j // 4) * 4 + oy) * 8 + (j % 4) * 2 + oc) * 6 + t2 % 6
    order = (src == r2).astype(bf)
    probs, mixed = call(
        fwd_kernel,
        "attn_fwd",
        [((HL, NB, POS, POS), f32), ((F * HALF, COLS), bf)],
        qkv,
        bias_m,
        order,
        scratch=[pltpu.VMEM((F, HALF, COLS), bf)],
        flops=250_000_000,
    )

    up, mine, theirs = call(
        gw_kernel,
        "grad_w",
        [((F, HALF, DW), bf), ((COLS // 2, DW), f32), ((COLS // 2, DW), bf)],
        place,
        *pieces,
        mixed,
        smem=1,
        flops=604_000_000,
    )
    theirs = hop(theirs, "core", 1, C)

    dm, ds, sums = call(
        score_kernel,
        "scores_bwd",
        [((F, HALF, COLS), bf), ((HL, NB, POS, POS), bf), ((F, COLS), f32)],
        qkv,
        probs,
        up,
        w_c,
        flops=700_000_000,
    )
    sums2 = hop(sums, "core", 1, C)
    (grads,) = call(
        grad_kernel, "grads", [((F, 3, HALF, COLS), bf)], qkv, probs, dm, ds, flops=150_000_000
    )

    wide = ((48, DW + 128), bf)
    own, b, *msgs = call(
        join_kernel, "join", [((48, DW), f32), ((24, 128), f32), wide, wide, wide], mine, theirs, sums, sums2
    )
    msgs = [hop(m, "y", k, Y) for k, m in enumerate(msgs, 1)]
    keep, send = call(ysum_kernel, "ysum", [((32, DW), f32)] * 2, own, b, *msgs)
    keep, send = call(zsum_kernel, "zsum1", [((16, DW), f32)] * 2, keep, hop(send, "z", 1, Z))
    first, second = call(zsum_kernel, "zsum2", [((8, DW), f32)] * 2, keep, hop(send, "z", 2, Z))
    home = [(a, b) for b, a in there]
    cross = [((((a // X) ^ 4) * X + a % X), b) for a, b in home]
    first = lax.ppermute(first, ("z", "x"), home)
    second = lax.ppermute(second, ("z", "x"), cross)
    grad_w_out, off = call(last_kernel, "last", [((6, DW), f32), ((16, 128), f32)], first, second)
    offs = [off] + [hop(off, "z", 2 * k, Z) for k in range(1, 4)]
    (grad_bias,) = call(bias_kernel, "bias", [((12, 15), f32)], place, *offs, smem=1)

    back = lax.all_to_all(grads, SEQ, 0, 0, tiled=True).reshape(X, C, 3, HALF, COLS)
    grad_qkv = back.transpose(2, 1, 3, 0, 4).reshape(3, 1, 1, POS, DW)
    return grad_qkv, grad_bias, grad_w_out


def solution(mesh):
    grid = Mesh(mesh.devices.reshape(Z, Y, X, C), ("z", "y", "x", "core"))
    dp, every = ("z", "y"), ("z", "y", "x", "core")
    return jax.shard_map(
        per_device,
        mesh=grid,
        in_specs=(
            P(None, dp, SEQ, None, None),
            P(dp, None),
            P(),
            P(every, None),
            P(dp, SEQ, None, None, None),
        ),
        out_specs=(P(None, dp, SEQ, None, None), P(), P(every, None)),
        check_vma=False,
    )
```

time: 212 us -> 166 us (0.78)
  blocking collectives: 32.5 us -> 0 us
  waiting for transfers between devices: 87.8 us -> 61 us
  starting transfers between devices: 43.6 us -> 64.5 us
  other arithmetic: 10.4 us -> 1.26 us
  matrix products: 7.34 us -> 1.98 us
  Pallas kernels: 8.51 us -> 13.6 us
    all_to_all x4 -> x1, waiting for transfers between devices: 35.8 us -> 0.01 us  [per_device(): cot = lax.all_to_all(cot_out[0, 0], SEQ, 0, 0, tiled=True)]
    all_to_all x2 -> x0, blocking collectives: 32.5 us -> none  [the longest x1 17.9 us: per_device(): wz = lax.all_to_all(jnp.broadcast_to(w8, (Z, 8, DW)), 'z', 0, 0, tiled=True)]
    ppermute x10 -> x23, starting transfers between devices: 9.13 us -> 39 us  [hop(): return lax.ppermute(x, axis, [(i, i ^ k) for i in range(n)])]
    ppermute x10 -> x23, waiting for transfers between devices: 32.8 us -> 56.8 us  [hop(): return lax.ppermute(x, axis, [(i, i ^ k) for i in range(n)])]
    all_to_all x1, waiting for transfers between devices: 16.7 us -> 0.01 us  [per_device(): lax.all_to_all(packed.reshape(F, 3, HALF, COLS), SEQ, 0, 0, tiled=True)]
    all_to_all x4 -> x1, starting transfers between devices: 17.2 us -> 4.27 us  [per_device(): cot = lax.all_to_all(cot_out[0, 0], SEQ, 0, 0, tiled=True)]
    dot_general x3 -> x1, matrix products: 7.34 us -> 1.98 us  [dot(): return lax.dot_general(a, b, dims, preferred_element_type=f32, **kw)]
    unnamed x32, local copies, waits for them, and re-layouts: 3.55 us -> 8.76 us
  transfers between devices with their start and end apart: 18 -> 29, of which waited for: 15 -> 19; matrix products, arithmetic and copies ran while one was open for 10% -> 9% of each run, Pallas kernels for 4% -> 8%
where the time goes in v2:
time: 166 us; the launch traced here: 163 us
  starting transfers between devices  64.5 us (39%)
  waiting for transfers between devices  61 us (37%)
  local copies, waits for them, and re-layouts  19.6 us (12%)
  Pallas kernels  13.6 us (8%)
  matrix products  1.98 us (1%)
    ppermute x23, waiting for transfers between devices, hop(): return lax.ppermute(x, axis, [(i, i ^ k) for i in range(n)])  56.8 us
    ppermute x23, starting transfers between devices, hop(): return lax.ppermute(x, axis, [(i, i ^ k) for i in range(n)])  39 us
    pallas_call x11, Pallas kernels, call(): pl.pallas_call(body, out_shape=tuple((jax.ShapeDtypeStruct(s, d) for s, d...  13.6 us
    unnamed x32, local copies, waits for them, and re-layouts  8.76 us
    ppermute x1, starting transfers between devices, per_device(): held = lax.ppermute(jnp.pad(w_out, ((0, 2), (0, 0))), ('z', 'x'), there)  7.73 us
    ppermute x1, starting transfers between devices, per_device(): first = lax.ppermute(first, ('z', 'x'), home)  4.96 us
    all_to_all x1, starting transfers between devices, per_device(): lax.all_to_all(packed.reshape(F, 3, HALF, COLS), SEQ, 0, 0, tiled=True)  4.75 us
    all_to_all x1, starting transfers between devices, per_device(): cot = lax.all_to_all(cot_out[0, 0], SEQ, 0, 0, tiled=True)  4.27 us
  transfers between devices with their start and end apart: 29, of which 19 were waited for; matrix products, arithmetic and copies ran while one was open for 9% of the time, Pallas kernels for 8%

profile of v2, /device:TPU:32, one launch (start us, length us, event | category | flops | bytes accessed | tf_op | source)
XLA Modules:
  0.0 162.9 jit_solution(15062093851579412492)
XLA Ops:
  0.7 0.8 pad.4
  1.5 7.7 %collective-permute-start.7 = (bf16[8,1536]{1,0:T(8,128)(2,1)S(1)}, bf16[8,1536]{1,0:T(8,128)(2,1)S(1)}, u32[]{:S(2)}, u32[]{:S(2)}) collective-permute-start(bf16[8,1536]{1,0:T(8,128)(2,1)S(1)} %pad.4), channel_id=1, source_target_pairs={{0,0},{2,32},{4,64},{6,96},{32,128},{34,160},{36,192},{38,224},{64... | collective-permute-start | bytes 73736 | tf_op jit(solution)/shard_map/ppermute | solution.py:212
  9.2 4.3 %all-to-all-start.1 = ((bf16[8,32,1536]{2,1,0:T(8,128)(2,1)}), bf16[8,32,1536]{2,1,0:T(8,128)(2,1)S(1)}, u32[]{:S(2)}, u32[]{:S(2)}) async-start(bf16[8,32,1536]{2,1,0:T(8,128)(2,1)} %bitcast.35), calls=%async_computation.1 | async-start | bytes 1572864 | tf_op jit(solution)/shard_map/all_to_all | solution.py:219
  14.4 1.2 copy.8
  15.7 0.6 constant_dynamic-update-slice_fusion.18
  16.3 3.2 %collective-permute-done.8 = bf16[8,1536]{1,0:T(8,128)(2,1)S(1)} collective-permute-done((bf16[8,1536]{1,0:T(8,128)(2,1)S(1)}, bf16[8,1536]{1,0:T(8,128)(2,1)S(1)}, u32[]{:S(2)}, u32[]{:S(2)}) %collective-permute-start.8) | collective-permute-done | bytes 24608 | tf_op jit(solution)/shard_map/ppermute | solution.py:198
  19.5 2.6 %collective-permute-start.9 = (bf16[16,1536]{1,0:T(8,128)(2,1)S(1)}, bf16[16,1536]{1,0:T(8,128)(2,1)S(1)}, u32[]{:S(2)}, u32[]{:S(2)}) collective-permute-start(bf16[16,1536]{1,0:T(8,128)(2,1)S(1)} %pad_maximum_fusion.2), channel_id=1, source_target_pairs={{0,64},{32,96},{64,0},{96,32},{128,192},{160,224},{192,128},{224,1... | collective-permute-start | bytes 147464 | tf_op jit(solution)/shard_map/ppermute | solution.py:198
  22.0 0.6 constant_dynamic-update-slice_fusion.17
  22.7 1.8 %collective-permute-done.9 = bf16[16,1536]{1,0:T(8,128)(2,1)S(1)} collective-permute-done((bf16[16,1536]{1,0:T(8,128)(2,1)S(1)}, bf16[16,1536]{1,0:T(8,128)(2,1)S(1)}, u32[]{:S(2)}, u32[]{:S(2)}) %collective-permute-start.9) | collective-permute-done | bytes 49184 | tf_op jit(solution)/shard_map/ppermute | solution.py:198
  24.5 3.3 %collective-permute-start.10 = (bf16[32,1536]{1,0:T(8,128)(2,1)S(1)}, bf16[32,1536]{1,0:T(8,128)(2,1)S(1)}, u32[]{:S(2)}, u32[]{:S(2)}) collective-permute-start(bf16[32,1536]{1,0:T(8,128)(2,1)S(1)} %pad_maximum_fusion.1), channel_id=1, source_target_pairs={{0,128},{32,160},{64,192},{96,224},{128,0},{160,32},{192,64},{224,... | collective-permute-start | bytes 294920 | tf_op jit(solution)/shard_map/ppermute | solution.py:198
  27.8 0.6 constant_dynamic-update-slice_fusion.16
  28.5 5.0 %collective-permute-done.10 = bf16[32,1536]{1,0:T(8,128)(2,1)S(1)} collective-permute-done((bf16[32,1536]{1,0:T(8,128)(2,1)S(1)}, bf16[32,1536]{1,0:T(8,128)(2,1)S(1)}, u32[]{:S(2)}, u32[]{:S(2)}) %collective-permute-start.10) | collective-permute-done | bytes 98336 | tf_op jit(solution)/shard_map/ppermute | solution.py:198
  33.5 1.7 %collective-permute-start.11 = (bf16[64,1536]{1,0:T(8,128)(2,1)S(1)}, bf16[64,1536]{1,0:T(8,128)(2,1)S(1)}, u32[]{:S(2)}, u32[]{:S(2)}) collective-permute-start(bf16[64,1536]{1,0:T(8,128)(2,1)S(1)} %pad_maximum_fusion), channel_id=1, source_target_pairs={{0,8},{8,0},{16,24},{24,16},{1,9},{9,1},{17,25},{25,17},{2,10},{10... | collective-permute-start | bytes 589832 | tf_op jit(solution)/shard_map/ppermute | solution.py:198
  35.1 0.7 constant_dynamic-update-slice_fusion.15
  35.9 3.4 %collective-permute-done.11 = bf16[64,1536]{1,0:T(8,128)(2,1)S(1)} collective-permute-done((bf16[64,1536]{1,0:T(8,128)(2,1)S(1)}, bf16[64,1536]{1,0:T(8,128)(2,1)S(1)}, u32[]{:S(2)}, u32[]{:S(2)}) %collective-permute-start.11) | collective-permute-done | bytes 196640 | tf_op jit(solution)/shard_map/ppermute | solution.py:198
  39.2 0.8 constant_dynamic-update-slice_fusion.14
  40.0 3.4 %collective-permute-start.12 = (bf16[128,1536]{1,0:T(8,128)(2,1)S(1)}, bf16[128,1536]{1,0:T(8,128)(2,1)S(1)}, u32[]{:S(2)}, u32[]{:S(2)}) collective-permute-start(bf16[128,1536]{1,0:T(8,128)(2,1)S(1)} %get-tuple-element.53), channel_id=1, source_target_pairs={{0,16},{8,24},{16,0},{24,8},{1,17},{9,25},{17,1},{25,9},{2,18},{10... | collective-permute-start | bytes 1179656 | tf_op jit(solution)/shard_map/ppermute | solution.py:198
  43.5 4.8 %all-to-all-start = ((bf16[8,3,64,384]{3,2,1,0:T(8,128)(2,1)}), bf16[8,3,64,384]{3,2,1,0:T(8,128)(2,1)S(1)}, u32[]{:S(2)}, u32[]{:S(2)}) async-start(bf16[8,3,64,384]{3,2,1,0:T(8,128)(2,1)} %bitcast.1), calls=%async_computation | async-start | bytes 2359296 | tf_op jit(solution)/shard_map/all_to_all | solution.py:221
  48.3 1.8 %collective-permute-done.12 = bf16[128,1536]{1,0:T(8,128)(2,1)S(1)} collective-permute-done((bf16[128,1536]{1,0:T(8,128)(2,1)S(1)}, bf16[128,1536]{1,0:T(8,128)(2,1)S(1)}, u32[]{:S(2)}, u32[]{:S(2)}) %collective-permute-start.12) | collective-permute-done | bytes 393248 | tf_op jit(solution)/shard_map/ppermute | solution.py:198
  50.1 0.9 constant_dynamic-update-slice_fusion.13
  51.2 0.8 compact.1
  52.6 1.9 %collective-permute-start.2 = (bf16[64,1536]{1,0:T(8,128)(2,1)S(1)}, bf16[64,1536]{1,0:T(8,128)(2,1)S(1)}, u32[]{:S(2)}, u32[]{:S(2)}) collective-permute-start(bf16[64,1536]{1,0:T(8,128)(2,1)S(1)} %get-tuple-element.28), channel_id=1, source_target_pairs={{0,3},{1,2},{2,1},{3,0},{4,7},{5,6},{6,5},{7,4},{8,11},{9,10},{10,... | collective-permute-start | bytes 589832 | tf_op jit(solution)/shard_map/ppermute | solution.py:198
  54.9 1.3 broadcast_in_dim.31
  56.2 2.5 %broadcast_in_dim.32 = f32[3,128,128]{2,1,0:T(8,128)} reshape(f32[3,8,16,8,16]{4,3,2,1,0:T(8,128)} %broadcast_in_dim.31) | data formatting | bytes 393216 | tf_op jit(solution)/shard_map/jit(_where)/broadcast_in_dim | solution.py:237
  59.0 2.9 %collective-permute-start.3 = (bf16[64,1536]{1,0:T(8,128)(2,1)S(1)}, bf16[64,1536]{1,0:T(8,128)(2,1)S(1)}, u32[]{:S(2)}, u32[]{:S(2)}) collective-permute-start(bf16[64,1536]{1,0:T(8,128)(2,1)S(1)} %get-tuple-element.27.refs_0_), channel_id=1, source_target_pairs={{0,4},{1,5},{2,6},{3,7},{4,0},{5,1},{6,2},{7,3},{8,12},{9,13},{10,... | collective-permute-start | bytes 589832 | tf_op jit(solution)/shard_map/ppermute | solution.py:198
  62.0 11.1 %collective-permute-done.1.refs_2_ = bf16[64,1536]{1,0:T(8,128)(2,1)S(1)} collective-permute-done((bf16[64,1536]{1,0:T(8,128)(2,1)S(1)}, bf16[64,1536]{1,0:T(8,128)(2,1)S(1)}, u32[]{:S(2)}, u32[]{:S(2)}) %collective-permute-start.1) | collective-permute-done | bytes 196640 | tf_op jit(solution)/shard_map/ppermute | solution.py:198
  73.1 2.1 %collective-permute-start.5 = (bf16[64,1536]{1,0:T(8,128)(2,1)S(1)}, bf16[64,1536]{1,0:T(8,128)(2,1)S(1)}, u32[]{:S(2)}, u32[]{:S(2)}) collective-permute-start(bf16[64,1536]{1,0:T(8,128)(2,1)S(1)} %get-tuple-element.27.refs_0_), channel_id=1, source_target_pairs={{0,6},{1,7},{2,4},{3,5},{4,2},{5,3},{6,0},{7,1},{8,14},{9,15},{10,... | collective-permute-start | bytes 589832 | tf_op jit(solution)/shard_map/ppermute | solution.py:198
  75.1 0.9 broadcast_select_fusion.bias_ref
  76.1 4.3 %attn_fwd.1 = (f32[3,4,128,128]{3,2,1,0:T(8,128)S(1)}, bf16[512,384]{1,0:T(8,128)(2,1)S(1)}) custom-call(bf16[8,3,64,384]{3,2,1,0:T(8,128)(2,1)S(1)} %all-to-all-done.qkv_ref, f32[3,128,128]{2,1,0:T(8,128)S(1)} %broadcast_select_fusion.bias_ref, bf16[384,384]{1,0:T(8,128)(2,1)S(1)} %fusion.57.order_ref), custom_call_target="tpu_custom_call" | custom-call | flops 250000000 | bytes 2850816 | tf_op jit(solution)/shard_map/attn_fwd/pallas_call | solution.py:43
  80.5 0.7 copy-done.2
  81.1 1.0 collective-permute-done.4.refs_5_
  82.1 0.7 copy-done.4
  82.8 4.0 %collective-permute-done.5.refs_6_ = bf16[64,1536]{1,0:T(8,128)(2,1)S(1)} collective-permute-done((bf16[64,1536]{1,0:T(8,128)(2,1)S(1)}, bf16[64,1536]{1,0:T(8,128)(2,1)S(1)}, u32[]{:S(2)}, u32[]{:S(2)}) %collective-permute-start.5) | collective-permute-done | bytes 196640 | tf_op jit(solution)/shard_map/ppermute | solution.py:198
  86.8 0.7 copy-done.6
  87.5 3.5 %collective-permute-done.6.refs_7_ = bf16[64,1536]{1,0:T(8,128)(2,1)} collective-permute-done((bf16[64,1536]{1,0:T(8,128)(2,1)S(1)}, bf16[64,1536]{1,0:T(8,128)(2,1)}, u32[]{:S(2)}, u32[]{:S(2)}) %collective-permute-start.6) | collective-permute-done | bytes 196640 | tf_op jit(solution)/shard_map/ppermute | solution.py:198
  91.0 0.9 copy-done.3
  91.9 0.9 copy-done.5
  92.8 0.9 copy-done.7
  93.7 2.7 %grad_w.1 = (bf16[8,64,1536]{2,1,0:T(8,128)(2,1)S(1)}, f32[192,1536]{1,0:T(8,128)S(1)}, bf16[192,1536]{1,0:T(8,128)(2,1)}) custom-call(s32[4]{0:T(128)S(1)} %pad_add_fusion.place, bf16[64,1536]{1,0:T(8,128)(2,1)S(1)} %get-tuple-element.27.refs_0_, bf16[64,1536]{1,0:T(8,128)(2,1)S(1)} %collective-permute-done.refs_1_, ...), custom_call_target="tpu_custom_call" | custom-call | flops 604000000 | bytes 5308432 | tf_op jit(solution)/shard_map/grad_w/pallas_call | solution.py:43
  96.5 1.2 constant_dynamic-update-slice_fusion.19
  97.7 2.0 %convolution_convert_fusion.w_ref = bf16[384,1536]{1,0:T(8,128)(2,1)S(1)} fusion(bf16[512,1536]{1,0:T(8,128)(2,1)S(1)} %constant_dynamic-update-slice_fusion.19, s32[384]{0:T(512)S(1)} %get-tuple-element.67, s32[384]{0:T(512)S(1)} %get-tuple-element.72, s32[]{:T(128)} %axis_index.46, s32[]{:T(128)} %axis_index.49, s32[]{:T(128)} %axis_index.51, ...), kind=kOutput, calls=%fused_computation | convolution fusion | flops 619315200 | bytes 2759436 | tf_op jit(solution)/shard_map/dot_general | solution.py:31
  99.7 1.5 scores_bwd.1
  101.2 1.5 grads.1
  102.7 3.6 %all-to-all-start.2 = ((bf16[8,3,64,384]{3,2,1,0:T(8,128)(2,1)}), bf16[8,3,64,384]{3,2,1,0:T(8,128)(2,1)S(1)}, u32[]{:S(2)}, u32[]{:S(2)}) async-start(bf16[8,3,64,384]{3,2,1,0:T(8,128)(2,1)} %grads.1), calls=%async_computation.2 | async-start | bytes 2359296 | tf_op jit(solution)/shard_map/all_to_all | solution.py:297
  106.7 0.8 collective-permute-done.15.sums2_ref
  107.7 2.0 %collective-permute-start.16 = (bf16[48,1664]{1,0:T(8,128)(2,1)S(1)}, bf16[48,1664]{1,0:T(8,128)(2,1)S(1)}, u32[]{:S(2)}, u32[]{:S(2)}) collective-permute-start(bf16[48,1664]{1,0:T(8,128)(2,1)S(1)} %get-tuple-element.38), channel_id=1, source_target_pairs={{0,8},{8,0},{16,24},{24,16},{1,9},{9,1},{17,25},{25,17},{2,10},{10... | collective-permute-start | bytes 479240 | tf_op jit(solution)/shard_map/ppermute | solution.py:198
  110.3 2.2 %collective-permute-start.18 = (bf16[48,1664]{1,0:T(8,128)(2,1)S(1)}, bf16[48,1664]{1,0:T(8,128)(2,1)S(1)}, u32[]{:S(2)}, u32[]{:S(2)}) collective-permute-start(bf16[48,1664]{1,0:T(8,128)(2,1)S(1)} %get-tuple-element.40), channel_id=1, source_target_pairs={{0,24},{8,16},{16,8},{24,0},{1,25},{9,17},{17,9},{25,1},{2,26},{10... | collective-permute-start | bytes 479240 | tf_op jit(solution)/shard_map/ppermute | solution.py:198
  112.5 2.2 %collective-permute-done.16.m1 = bf16[48,1664]{1,0:T(8,128)(2,1)S(1)} collective-permute-done((bf16[48,1664]{1,0:T(8,128)(2,1)S(1)}, bf16[48,1664]{1,0:T(8,128)(2,1)S(1)}, u32[]{:S(2)}, u32[]{:S(2)}) %collective-permute-start.16) | collective-permute-done | bytes 159776 | tf_op jit(solution)/shard_map/ppermute | solution.py:198
  114.7 3.4 %collective-permute-done.17.m2 = bf16[48,1664]{1,0:T(8,128)(2,1)S(1)} collective-permute-done((bf16[48,1664]{1,0:T(8,128)(2,1)S(1)}, bf16[48,1664]{1,0:T(8,128)(2,1)S(1)}, u32[]{:S(2)}, u32[]{:S(2)}) %collective-permute-start.17) | collective-permute-done | bytes 159776 | tf_op jit(solution)/shard_map/ppermute | solution.py:198
  118.1 2.6 %collective-permute-done.18.m3 = bf16[48,1664]{1,0:T(8,128)(2,1)S(1)} collective-permute-done((bf16[48,1664]{1,0:T(8,128)(2,1)S(1)}, bf16[48,1664]{1,0:T(8,128)(2,1)S(1)}, u32[]{:S(2)}, u32[]{:S(2)}) %collective-permute-start.18) | collective-permute-done | bytes 159776 | tf_op jit(solution)/shard_map/ppermute | solution.py:198
  120.8 1.6 collective-permute-start.19
  122.3 4.7 %collective-permute-done.19.recv_ref = f32[32,1536]{1,0:T(8,128)S(1)} collective-permute-done((f32[32,1536]{1,0:T(8,128)S(1)}, f32[32,1536]{1,0:T(8,128)S(1)}, u32[]{:S(2)}, u32[]{:S(2)}) %collective-permute-start.19) | collective-permute-done | bytes 196640 | tf_op jit(solution)/shard_map/ppermute | solution.py:198
  127.1 3.2 %collective-permute-start.20 = (f32[16,1536]{1,0:T(8,128)S(1)}, f32[16,1536]{1,0:T(8,128)S(1)}, u32[]{:S(2)}, u32[]{:S(2)}) collective-permute-start(f32[16,1536]{1,0:T(8,128)S(1)} %get-tuple-element.44), channel_id=1, source_target_pairs={{0,64},{32,96},{64,0},{96,32},{128,192},{160,224},{192,128},{224,1... | collective-permute-start | bytes 294920 | tf_op jit(solution)/shard_map/ppermute | solution.py:198
  130.3 3.1 %collective-permute-done.20.recv_ref = f32[16,1536]{1,0:T(8,128)S(1)} collective-permute-done((f32[16,1536]{1,0:T(8,128)S(1)}, f32[16,1536]{1,0:T(8,128)S(1)}, u32[]{:S(2)}, u32[]{:S(2)}) %collective-permute-start.20) | collective-permute-done | bytes 98336 | tf_op jit(solution)/shard_map/ppermute | solution.py:198
  133.3 5.0 %collective-permute-start.21 = (f32[8,1536]{1,0:T(8,128)S(1)}, f32[8,1536]{1,0:T(8,128)S(1)}, u32[]{:S(2)}, u32[]{:S(2)}) collective-permute-start(f32[8,1536]{1,0:T(8,128)S(1)} %get-tuple-element.45), channel_id=1, source_target_pairs={{0,0},{32,2},{64,4},{96,6},{128,32},{160,34},{192,36},{224,38},{2,... | collective-permute-start | bytes 147464 | tf_op jit(solution)/shard_map/ppermute | solution.py:291
  138.6 3.8 %collective-permute-done.21.a_ref = f32[8,1536]{1,0:T(8,128)S(1)} collective-permute-done((f32[8,1536]{1,0:T(8,128)S(1)}, f32[8,1536]{1,0:T(8,128)S(1)}, u32[]{:S(2)}, u32[]{:S(2)}) %collective-permute-start.21) | collective-permute-done | bytes 49184 | tf_op jit(solution)/shard_map/ppermute | solution.py:291
  142.7 1.4 last.1
  144.1 6.3 %collective-permute-start.23 = (f32[16,128]{1,0:T(8,128)S(1)}, f32[16,128]{1,0:T(8,128)S(1)}, u32[]{:S(2)}, u32[]{:S(2)}) collective-permute-start(f32[16,128]{1,0:T(8,128)S(1)} %get-tuple-element.47.refs_0_), channel_id=1, source_target_pairs={{0,64},{32,96},{64,0},{96,32},{128,192},{160,224},{192,128},{224,1... | collective-permute-start | bytes 24584 | tf_op jit(solution)/shard_map/ppermute | solution.py:198
  150.4 3.3 %collective-permute-start.24 = (f32[16,128]{1,0:T(8,128)S(1)}, f32[16,128]{1,0:T(8,128)S(1)}, u32[]{:S(2)}, u32[]{:S(2)}) collective-permute-start(f32[16,128]{1,0:T(8,128)S(1)} %get-tuple-element.47.refs_0_), channel_id=1, source_target_pairs={{0,128},{32,160},{64,192},{96,224},{128,0},{160,32},{192,64},{224,... | collective-permute-start | bytes 24584 | tf_op jit(solution)/shard_map/ppermute | solution.py:198
  154.3 3.7 %collective-permute-done.24.refs_2_ = f32[16,128]{1,0:T(8,128)S(1)} collective-permute-done((f32[16,128]{1,0:T(8,128)S(1)}, f32[16,128]{1,0:T(8,128)S(1)}, u32[]{:S(2)}, u32[]{:S(2)}) %collective-permute-start.24) | collective-permute-done | bytes 8224 | tf_op jit(solution)/shard_map/ppermute | solution.py:198
  158.0 1.5 collective-permute-done.25.refs_3_
  159.5 1.2 bias.1
  160.7 0.9 copy.10
  161.6 1.3 reshape.28
  (68 shorter events, 5.0 us)
Async XLA Ops:
  0.6 13.0 %copy-start = (f32[12,15]{1,0:T(8,128)S(1)}, f32[12,15]{1,0:T(8,128)}, u32[]{:S(2)}) copy-start(f32[12,15]{1,0:T(8,128)} %param.7) | copy-start | bytes 2164
  0.6 13.5 %copy-start.8 = (bf16[3,1,1,128,1536]{4,3,2,1,0:T(8,128)(2,1)S(1)}, bf16[3,1,1,128,1536]{4,3,2,1,0:T(8,128)(2,1)}, u32[]{:S(2)}) copy-start(bf16[3,1,1,128,1536]{4,3,2,1,0:T(8,128)(2,1)} %param.5) | copy-start | bytes 3538948
  1.5 14.2 %collective-permute-start.7 = (bf16[8,1536]{1,0:T(8,128)(2,1)S(1)}, bf16[8,1536]{1,0:T(8,128)(2,1)S(1)}, u32[]{:S(2)}, u32[]{:S(2)}) collective-permute-start(bf16[8,1536]{1,0:T(8,128)(2,1)S(1)} %pad.4), channel_id=1, source_target_pairs={{0,0},{2,32},{4,64},{6,96},{32,128},{34,160},{36,192},{38,224},{64... | collective-permute-start | bytes 73736 | tf_op jit(solution)/shard_map/ppermute | solution.py:212
  9.2 34.3 %all-to-all-start.1 = ((bf16[8,32,1536]{2,1,0:T(8,128)(2,1)}), bf16[8,32,1536]{2,1,0:T(8,128)(2,1)S(1)}, u32[]{:S(2)}, u32[]{:S(2)}) async-start(bf16[8,32,1536]{2,1,0:T(8,128)(2,1)} %bitcast.35), calls=%async_computation.1 | async-start | bytes 1572864 | tf_op jit(solution)/shard_map/all_to_all | solution.py:219
  15.7 3.8 %collective-permute-start.8 = (bf16[8,1536]{1,0:T(8,128)(2,1)S(1)}, bf16[8,1536]{1,0:T(8,128)(2,1)S(1)}, u32[]{:S(2)}, u32[]{:S(2)}) collective-permute-start(bf16[8,1536]{1,0:T(8,128)(2,1)S(1)} %collective-permute-done.7), channel_id=1, source_target_pairs={{0,32},{32,0},{64,96},{96,64},{128,160},{160,128},{192,224},{224,1... | collective-permute-start | bytes 73736 | tf_op jit(solution)/shard_map/ppermute | solution.py:198
  19.5 5.0 %collective-permute-start.9 = (bf16[16,1536]{1,0:T(8,128)(2,1)S(1)}, bf16[16,1536]{1,0:T(8,128)(2,1)S(1)}, u32[]{:S(2)}, u32[]{:S(2)}) collective-permute-start(bf16[16,1536]{1,0:T(8,128)(2,1)S(1)} %pad_maximum_fusion.2), channel_id=1, source_target_pairs={{0,64},{32,96},{64,0},{96,32},{128,192},{160,224},{192,128},{224,1... | collective-permute-start | bytes 147464 | tf_op jit(solution)/shard_map/ppermute | solution.py:198
  24.5 9.0 %collective-permute-start.10 = (bf16[32,1536]{1,0:T(8,128)(2,1)S(1)}, bf16[32,1536]{1,0:T(8,128)(2,1)S(1)}, u32[]{:S(2)}, u32[]{:S(2)}) collective-permute-start(bf16[32,1536]{1,0:T(8,128)(2,1)S(1)} %pad_maximum_fusion.1), channel_id=1, source_target_pairs={{0,128},{32,160},{64,192},{96,224},{128,0},{160,32},{192,64},{224,... | collective-permute-start | bytes 294920 | tf_op jit(solution)/shard_map/ppermute | solution.py:198
  33.5 5.8 %collective-permute-start.11 = (bf16[64,1536]{1,0:T(8,128)(2,1)S(1)}, bf16[64,1536]{1,0:T(8,128)(2,1)S(1)}, u32[]{:S(2)}, u32[]{:S(2)}) collective-permute-start(bf16[64,1536]{1,0:T(8,128)(2,1)S(1)} %pad_maximum_fusion), channel_id=1, source_target_pairs={{0,8},{8,0},{16,24},{24,16},{1,9},{9,1},{17,25},{25,17},{2,10},{10... | collective-permute-start | bytes 589832 | tf_op jit(solution)/shard_map/ppermute | solution.py:198
  40.0 10.1 %collective-permute-start.12 = (bf16[128,1536]{1,0:T(8,128)(2,1)S(1)}, bf16[128,1536]{1,0:T(8,128)(2,1)S(1)}, u32[]{:S(2)}, u32[]{:S(2)}) collective-permute-start(bf16[128,1536]{1,0:T(8,128)(2,1)S(1)} %get-tuple-element.53), channel_id=1, source_target_pairs={{0,16},{8,24},{16,0},{24,8},{1,17},{9,25},{17,1},{25,9},{2,18},{10... | collective-permute-start | bytes 1179656 | tf_op jit(solution)/shard_map/ppermute | solution.py:198
  43.5 7.7 %copy-start.1 = (s32[1,8]{1,0:T(1,128)S(1)}, s32[1,8]{1,0:T(1,128)}, u32[]{:S(2)}) copy-start(s32[1,8]{1,0:T(1,128)} %sizes.1) | copy-start | bytes 100
  43.5 32.5 %all-to-all-start = ((bf16[8,3,64,384]{3,2,1,0:T(8,128)(2,1)}), bf16[8,3,64,384]{3,2,1,0:T(8,128)(2,1)S(1)}, u32[]{:S(2)}, u32[]{:S(2)}) async-start(bf16[8,3,64,384]{3,2,1,0:T(8,128)(2,1)} %bitcast.1), calls=%async_computation | async-start | bytes 2359296 | tf_op jit(solution)/shard_map/all_to_all | solution.py:221
  51.1 45.5 %collective-permute-start.13 = (bf16[256,1536]{1,0:T(8,128)(2,1)}, bf16[256,1536]{1,0:T(8,128)(2,1)}, u32[]{:S(2)}, u32[]{:S(2)}) collective-permute-start(bf16[256,1536]{1,0:T(8,128)(2,1)} %get-tuple-element.49), channel_id=1, source_target_pairs={{0,1},{1,0},{2,3},{3,2},{4,5},{5,4},{6,7},{7,6},{8,9},{9,8},{10,11... | collective-permute-start | bytes 2359304 | tf_op jit(solution)/shard_map/ppermute | solution.py:198
  52.0 9.9 %collective-permute-start = (bf16[64,1536]{1,0:T(8,128)(2,1)S(1)}, bf16[64,1536]{1,0:T(8,128)(2,1)S(1)}, u32[]{:S(2)}, u32[]{:S(2)}) collective-permute-start(bf16[64,1536]{1,0:T(8,128)(2,1)S(1)} %get-tuple-element.28), channel_id=1, source_target_pairs={{0,1},{1,0},{2,3},{3,2},{4,5},{5,4},{6,7},{7,6},{8,9},{9,8},{10,11... | collective-permute-start | bytes 589832 | tf_op jit(solution)/shard_map/ppermute | solution.py:198
  52.6 22.5 %collective-permute-start.2 = (bf16[64,1536]{1,0:T(8,128)(2,1)S(1)}, bf16[64,1536]{1,0:T(8,128)(2,1)S(1)}, u32[]{:S(2)}, u32[]{:S(2)}) collective-permute-start(bf16[64,1536]{1,0:T(8,128)(2,1)S(1)} %get-tuple-element.28), channel_id=1, source_target_pairs={{0,3},{1,2},{2,1},{3,0},{4,7},{5,6},{6,5},{7,4},{8,11},{9,10},{10,... | collective-permute-start | bytes 589832 | tf_op jit(solution)/shard_map/ppermute | solution.py:198
  54.5 18.6 %collective-permute-start.1 = (bf16[64,1536]{1,0:T(8,128)(2,1)S(1)}, bf16[64,1536]{1,0:T(8,128)(2,1)S(1)}, u32[]{:S(2)}, u32[]{:S(2)}) collective-permute-start(bf16[64,1536]{1,0:T(8,128)(2,1)S(1)} %get-tuple-element.27.refs_0_), channel_id=1, source_target_pairs={{0,2},{1,3},{2,0},{3,1},{4,6},{5,7},{6,4},{7,5},{8,10},{9,11},{10,... | collective-permute-start | bytes 589832 | tf_op jit(solution)/shard_map/ppermute | solution.py:198
  59.0 21.5 %collective-permute-start.3 = (bf16[64,1536]{1,0:T(8,128)(2,1)S(1)}, bf16[64,1536]{1,0:T(8,128)(2,1)S(1)}, u32[]{:S(2)}, u32[]{:S(2)}) collective-permute-start(bf16[64,1536]{1,0:T(8,128)(2,1)S(1)} %get-tuple-element.27.refs_0_), channel_id=1, source_target_pairs={{0,4},{1,5},{2,6},{3,7},{4,0},{5,1},{6,2},{7,3},{8,12},{9,13},{10,... | collective-permute-start | bytes 589832 | tf_op jit(solution)/shard_map/ppermute | solution.py:198
  61.9 20.3 %collective-permute-start.4 = (bf16[64,1536]{1,0:T(8,128)(2,1)S(1)}, bf16[64,1536]{1,0:T(8,128)(2,1)S(1)}, u32[]{:S(2)}, u32[]{:S(2)}) collective-permute-start(bf16[64,1536]{1,0:T(8,128)(2,1)S(1)} %get-tuple-element.28), channel_id=1, source_target_pairs={{0,5},{1,4},{2,7},{3,6},{4,1},{5,0},{6,3},{7,2},{8,13},{9,12},{10,... | collective-permute-start | bytes 589832 | tf_op jit(solution)/shard_map/ppermute | solution.py:198
  73.1 13.8 %collective-permute-start.5 = (bf16[64,1536]{1,0:T(8,128)(2,1)S(1)}, bf16[64,1536]{1,0:T(8,128)(2,1)S(1)}, u32[]{:S(2)}, u32[]{:S(2)}) collective-permute-start(bf16[64,1536]{1,0:T(8,128)(2,1)S(1)} %get-tuple-element.27.refs_0_), channel_id=1, source_target_pairs={{0,6},{1,7},{2,4},{3,5},{4,2},{5,3},{6,0},{7,1},{8,14},{9,15},{10,... | collective-permute-start | bytes 589832 | tf_op jit(solution)/shard_map/ppermute | solution.py:198
  75.1 15.8 %collective-permute-start.6 = (bf16[64,1536]{1,0:T(8,128)(2,1)S(1)}, bf16[64,1536]{1,0:T(8,128)(2,1)}, u32[]{:S(2)}, u32[]{:S(2)}) collective-permute-start(bf16[64,1536]{1,0:T(8,128)(2,1)S(1)} %get-tuple-element.28), channel_id=1, source_target_pairs={{0,7},{1,6},{2,5},{3,4},{4,3},{5,2},{6,1},{7,0},{8,15},{9,14},{10,... | collective-permute-start | bytes 589832 | tf_op jit(solution)/shard_map/ppermute | solution.py:198
  76.1 20.4 %copy-start.9 = (bf16[512,1536]{1,0:T(8,128)(2,1)S(1)}, bf16[512,1536]{1,0:T(8,128)(2,1)}, u32[]{:S(2)}) copy-start(bf16[512,1536]{1,0:T(8,128)(2,1)} %get-tuple-element.50) | copy-start | bytes 4718596
  80.5 0.7 copy-start.2
  82.1 0.7 copy-start.4
  86.8 0.7 copy-start.6
  91.0 0.9 copy-start.3
  91.9 0.9 copy-start.5
  92.8 0.9 copy-start.7
  96.4 11.2 %collective-permute-start.14 = (bf16[192,1536]{1,0:T(8,128)(2,1)}, bf16[192,1536]{1,0:T(8,128)(2,1)S(1)}, u32[]{:S(2)}, u32[]{:S(2)}) collective-permute-start(bf16[192,1536]{1,0:T(8,128)(2,1)} %get-tuple-element.34), channel_id=1, source_target_pairs={{0,1},{1,0},{2,3},{3,2},{4,5},{5,4},{6,7},{7,6},{8,9},{9,8},{10,11... | collective-permute-start | bytes 1769480 | tf_op jit(solution)/shard_map/ppermute | solution.py:198
  102.7 57.9 %all-to-all-start.2 = ((bf16[8,3,64,384]{3,2,1,0:T(8,128)(2,1)}), bf16[8,3,64,384]{3,2,1,0:T(8,128)(2,1)S(1)}, u32[]{:S(2)}, u32[]{:S(2)}) async-start(bf16[8,3,64,384]{3,2,1,0:T(8,128)(2,1)} %grads.1), calls=%async_computation.2 | async-start | bytes 2359296 | tf_op jit(solution)/shard_map/all_to_all | solution.py:297
  106.3 1.3 collective-permute-start.15
  107.7 7.0 %collective-permute-start.16 = (bf16[48,1664]{1,0:T(8,128)(2,1)S(1)}, bf16[48,1664]{1,0:T(8,128)(2,1)S(1)}, u32[]{:S(2)}, u32[]{:S(2)}) collective-permute-start(bf16[48,1664]{1,0:T(8,128)(2,1)S(1)} %get-tuple-element.38), channel_id=1, source_target_pairs={{0,8},{8,0},{16,24},{24,16},{1,9},{9,1},{17,25},{25,17},{2,10},{10... | collective-permute-start | bytes 479240 | tf_op jit(solution)/shard_map/ppermute | solution.py:198
  109.7 8.5 %collective-permute-start.17 = (bf16[48,1664]{1,0:T(8,128)(2,1)S(1)}, bf16[48,1664]{1,0:T(8,128)(2,1)S(1)}, u32[]{:S(2)}, u32[]{:S(2)}) collective-permute-start(bf16[48,1664]{1,0:T(8,128)(2,1)S(1)} %get-tuple-element.39), channel_id=1, source_target_pairs={{0,16},{8,24},{16,0},{24,8},{1,17},{9,25},{17,1},{25,9},{2,18},{10... | collective-permute-start | bytes 479240 | tf_op jit(solution)/shard_map/ppermute | solution.py:198
  110.3 10.4 %collective-permute-start.18 = (bf16[48,1664]{1,0:T(8,128)(2,1)S(1)}, bf16[48,1664]{1,0:T(8,128)(2,1)S(1)}, u32[]{:S(2)}, u32[]{:S(2)}) collective-permute-start(bf16[48,1664]{1,0:T(8,128)(2,1)S(1)} %get-tuple-element.40), channel_id=1, source_target_pairs={{0,24},{8,16},{16,8},{24,0},{1,25},{9,17},{17,9},{25,1},{2,26},{10... | collective-permute-start | bytes 479240 | tf_op jit(solution)/shard_map/ppermute | solution.py:198
  120.8 6.3 %collective-permute-start.19 = (f32[32,1536]{1,0:T(8,128)S(1)}, f32[32,1536]{1,0:T(8,128)S(1)}, u32[]{:S(2)}, u32[]{:S(2)}) collective-permute-start(f32[32,1536]{1,0:T(8,128)S(1)} %get-tuple-element.42), channel_id=1, source_target_pairs={{0,32},{32,0},{64,96},{96,64},{128,160},{160,128},{192,224},{224,1... | collective-permute-start | bytes 589832 | tf_op jit(solution)/shard_map/ppermute | solution.py:198
  127.1 6.2 %collective-permute-start.20 = (f32[16,1536]{1,0:T(8,128)S(1)}, f32[16,1536]{1,0:T(8,128)S(1)}, u32[]{:S(2)}, u32[]{:S(2)}) collective-permute-start(f32[16,1536]{1,0:T(8,128)S(1)} %get-tuple-element.44), channel_id=1, source_target_pairs={{0,64},{32,96},{64,0},{96,32},{128,192},{160,224},{192,128},{224,1... | collective-permute-start | bytes 294920 | tf_op jit(solution)/shard_map/ppermute | solution.py:198
  133.3 9.0 %collective-permute-start.21 = (f32[8,1536]{1,0:T(8,128)S(1)}, f32[8,1536]{1,0:T(8,128)S(1)}, u32[]{:S(2)}, u32[]{:S(2)}) collective-permute-start(f32[8,1536]{1,0:T(8,128)S(1)} %get-tuple-element.45), channel_id=1, source_target_pairs={{0,0},{32,2},{64,4},{96,6},{128,32},{160,34},{192,36},{224,38},{2,... | collective-permute-start | bytes 147464 | tf_op jit(solution)/shard_map/ppermute | solution.py:291
  138.3 4.4 %collective-permute-start.22 = (f32[8,1536]{1,0:T(8,128)S(1)}, f32[8,1536]{1,0:T(8,128)S(1)}, u32[]{:S(2)}, u32[]{:S(2)}) collective-permute-start(f32[8,1536]{1,0:T(8,128)S(1)} %get-tuple-element.46), channel_id=1, source_target_pairs={{128,0},{160,2},{192,4},{224,6},{0,32},{32,34},{64,36},{96,38},{13... | collective-permute-start | bytes 147464 | tf_op jit(solution)/shard_map/ppermute | solution.py:292
  144.1 10.1 %collective-permute-start.23 = (f32[16,128]{1,0:T(8,128)S(1)}, f32[16,128]{1,0:T(8,128)S(1)}, u32[]{:S(2)}, u32[]{:S(2)}) collective-permute-start(f32[16,128]{1,0:T(8,128)S(1)} %get-tuple-element.47.refs_0_), channel_id=1, source_target_pairs={{0,64},{32,96},{64,0},{96,32},{128,192},{160,224},{192,128},{224,1... | collective-permute-start | bytes 24584 | tf_op jit(solution)/shard_map/ppermute | solution.py:198
  150.4 7.6 %collective-permute-start.24 = (f32[16,128]{1,0:T(8,128)S(1)}, f32[16,128]{1,0:T(8,128)S(1)}, u32[]{:S(2)}, u32[]{:S(2)}) collective-permute-start(f32[16,128]{1,0:T(8,128)S(1)} %get-tuple-element.47.refs_0_), channel_id=1, source_target_pairs={{0,128},{32,160},{64,192},{96,224},{128,0},{160,32},{192,64},{224,... | collective-permute-start | bytes 24584 | tf_op jit(solution)/shard_map/ppermute | solution.py:198
  153.8 5.8 %collective-permute-start.25 = (f32[16,128]{1,0:T(8,128)S(1)}, f32[16,128]{1,0:T(8,128)S(1)}, u32[]{:S(2)}, u32[]{:S(2)}) collective-permute-start(f32[16,128]{1,0:T(8,128)S(1)} %get-tuple-element.47.refs_0_), channel_id=1, source_target_pairs={{0,192},{32,224},{64,128},{96,160},{128,64},{160,96},{192,0},{224,... | collective-permute-start | bytes 24584 | tf_op jit(solution)/shard_map/ppermute | solution.py:198

commit v3 on v2

--- a/solution.py
+++ b/solution.py
@@ -35,11 +35,12 @@
     return lax.broadcasted_iota(jnp.int32, shape, dim)
 
 
-def call(body, name, outs, *ins, smem=0, scratch=(), flops=0):
+def call(body, name, outs, *ins, smem=0, hbm=0, scratch=(), flops=0):
     total = sum(math.prod(s) * jnp.dtype(d).itemsize for s, d in outs)
     total += sum(a.size * a.dtype.itemsize for a in ins)
     specs = [pl.BlockSpec(memory_space=pltpu.SMEM)] * smem
-    specs += [pl.BlockSpec(memory_space=pltpu.VMEM)] * (len(ins) - smem)
+    specs += [pl.BlockSpec(memory_space=pl.ANY)] * hbm
+    specs += [pl.BlockSpec(memory_space=pltpu.VMEM)] * (len(ins) - smem - hbm)
     return pl.pallas_call(
         body,
         out_shape=tuple(jax.ShapeDtypeStruct(s, d) for s, d in outs),
@@ -87,17 +88,23 @@
 
 
 def gw_kernel(place, *refs):
-    pieces, mixed_ref, up_ref, mine_ref, other_ref = refs[:F], *refs[F:]
-    for k in range(F):
-        up_ref[place[RANK] ^ k] = pieces[k][...]
+    pieces, (mixed_ref, up_ref, mine_ref, other_ref, sems) = refs[:F], refs[F:]
+    copies = [
+        pltpu.make_async_copy(pieces[k], up_ref.at[place[RANK] ^ k], sems.at[k]) for k in range(F)
+    ]
+    for c in copies:
+        c.start()
+    for c in copies:
+        c.wait()
     up = up_ref[...].reshape(F * HALF, DW)
     gw = dot(mixed_ref[...], up, TN)
     mine_ref[...] = gw[: COLS // 2]
     other_ref[...] = gw[COLS // 2 :].astype(bf)
 
 
-def score_kernel(qkv_ref, probs_ref, up_ref, w_ref, dm_ref, ds_ref, sums_ref):
-    dm = dot(up_ref[...].reshape(F * HALF, DW), w_ref[...], NT)
+def score_kernel(qkv_ref, probs_ref, up_ref, w_ref, spot_ref, dm_ref, ds_ref, sums_ref):
+    dm = dot(up_ref[...].reshape(F * HALF, DW), w_ref[...], NT).astype(bf)
+    dm = dot(dm, spot_ref[...], NN)
     dm_ref[...] = dm.astype(bf).reshape(F, HALF, COLS)
     for h in range(HL):
         cols = slice(h * HD, (h + 1) * HD)
@@ -130,12 +137,16 @@
     return jnp.concatenate([x[:, a * 128 : (a + 1) * 128] for a in range(HL)], axis=0)
 
 
-def join_kernel(mine_ref, other_ref, sums_ref, sums2_ref, own_ref, b_ref, m1, m2, m3):
-    gw = mine_ref[...] + other_ref[...].astype(f32)
-    b = tiles(sums_ref[...] + sums2_ref[...])
-    own_ref[...] = gw[:48]
+def split(b):
     high = b.astype(bf).astype(f32)
     low = (b - high).astype(bf).astype(f32)
+    return high, low
+
+
+def join_kernel(mine_ref, other_ref, s0, s1, s2, s3, own_ref, b_ref, m1, m2, m3):
+    gw = mine_ref[...] + other_ref[...].astype(f32)
+    high, low = split(tiles((s0[...] + s1[...]) + (s2[...] + s3[...])))
+    own_ref[...] = gw[:48]
     b_ref[...] = high + low
     ride = jnp.concatenate([high, low], axis=0).astype(bf)
     for k, m in enumerate((m1, m2, m3), 1):
@@ -143,55 +154,44 @@
         m[:, DW:] = ride
 
 
-def ysum_kernel(own_ref, b_ref, m1, m2, m3, keep_ref, send_ref):
+def ysum_kernel(own_ref, b_ref, m1, m2, m3, own_out, b_out, n1, n2, n3):
     gw = [own_ref[...]] + [m[:, :DW].astype(f32) for m in (m1, m2, m3)]
     rides = [m[:, DW:].astype(f32) for m in (m1, m2, m3)]
     b = [b_ref[...]] + [x[:24] + x[24:] for x in rides]
     gw, b = ((x[0] + x[1]) + (x[2] + x[3]) for x in (gw, b))
-    flat = jnp.concatenate([b[2 * a : 2 * a + 2] for a in range(12)], axis=1)
-    for ref, part in ((keep_ref, gw[:24]), (send_ref, gw[24:])):
-        ref[:24] = part
-        ref[24:26] = flat
-        ref[26:] = jnp.zeros((6, DW), f32)
-
-
-def zsum_kernel(keep_ref, recv_ref, first_ref, second_ref):
-    n = first_ref.shape[0]
-    total = keep_ref[...] + recv_ref[...]
-    rows = {16: 12, 8: 6}[n]
-    for ref, part in ((first_ref, total[:rows]), (second_ref, total[rows : 2 * rows])):
-        ref[:rows] = part
-        ref[rows : rows + 2] = total[2 * rows : 2 * rows + 2]
-        if n - rows > 2:
-            ref[rows + 2 :] = jnp.zeros((n - rows - 2, DW), f32)
-
-
-def last_kernel(a_ref, b_ref, gw_ref, off_ref):
-    total = a_ref[...] + b_ref[...]
-    gw_ref[...] = total[:6]
-    flat = total[6:8]
-    rows = [flat[:, 128 * a : 128 * (a + 1)] for a in range(12)]
-    sums = jnp.concatenate(rows, axis=0)
+    high, low = split(jnp.concatenate([b[2 * a : 2 * a + 2] for a in range(12)], axis=1))
+    own_out[...] = gw[:12]
+    b_out[...] = high + low
+    for k, n in enumerate((n1, n2, n3), 1):
+        n[...] = jnp.concatenate([gw[12 * k : 12 * (k + 1)], high, low], axis=0).astype(bf)
+
+
+def zsum_kernel(own_ref, b_ref, n1, n2, n3, first_ref, second_ref, off_ref):
+    parts = [n[...].astype(f32) for n in (n1, n2, n3)]
+    gw = [own_ref[...]] + [x[:12] for x in parts]
+    b = [b_ref[...]] + [x[12:14] + x[14:16] for x in parts]
+    gw, flat = ((x[0] + x[1]) + (x[2] + x[3]) for x in (gw, b))
+    pad = jnp.zeros((2, DW), f32)
+    first_ref[...] = jnp.concatenate([gw[:6], pad], axis=0)
+    second_ref[...] = jnp.concatenate([gw[6:], pad], axis=0)
+    sums = jnp.concatenate([flat[:, 128 * a : 128 * (a + 1)] for a in range(12)], axis=0)
     out = jnp.zeros((16, 128), f32)
-    head = iota((16, 24), 0) % HL
-    t = iota((16, 24), 1)
-    g = iota((128, 128), 0) // 16
-    o = iota((128, 128), 1)
+    head, t = iota((16, 24), 0) % HL, iota((16, 24), 1)
+    g, o = iota((128, 128), 0) // 16, iota((128, 128), 1)
     hi = lax.Precision.HIGHEST
     for f in range(F):
-        pick = (t == head * F + f).astype(f32)
-        row = dot(pick, sums, NN, precision=hi)
+        row = dot((t == head * F + f).astype(f32), sums, NN, precision=hi)
         out = out + dot(row, (g - f + 7 == o).astype(f32), NN, precision=hi)
     off_ref[...] = out
 
 
-def bias_kernel(place, *refs):
-    parts, out_ref = refs[:4], refs[4]
+def last_kernel(place, a_ref, b_ref, o0, o1, o2, o3, gw_ref, bias_ref):
+    gw_ref[...] = (a_ref[...] + b_ref[...])[:6]
     row = iota((16, 128), 0) // HL
     out = jnp.zeros((16, 128), f32)
-    for k in range(4):
-        out = out + jnp.where(row == ((place[ZI] // 2) ^ k), parts[k][...], 0.0)
-    out_ref[...] = out[:12, :15]
+    for k, o in enumerate((o0, o1, o2, o3)):
+        out = out + jnp.where(row == ((place[RANK] // C) ^ k), o[...], 0.0)
+    bias_ref[...] = out[:12, :15]
 
 
 def hop(x, axis, k, n):
@@ -209,12 +209,10 @@
         for z0 in range(2)
         for x in range(X)
     ]
-    held = lax.ppermute(jnp.pad(w_out, ((0, 2), (0, 0))), ("z", "x"), there)
-    for axis, n in (("z", Z), ("y", Y), ("core", C)):
-        k = 1
-        while k < n:
-            held = jnp.concatenate([held, hop(held, axis, k, n)])
-            k *= 2
+    near = [(a, b ^ X) for a, b in there]
+    rows8 = jnp.pad(w_out, ((0, 2), (0, 0)))
+    held = jnp.concatenate([lax.ppermute(rows8, ("z", "x"), p) for p in (there, near)])
+    held = jnp.concatenate([held, hop(held, "z", 2, Z)])
 
     cot = lax.all_to_all(cot_out[0, 0], SEQ, 0, 0, tiled=True)
     packed = qkv_time[:, 0, 0].reshape(3, C, HALF, X, COLS).transpose(3, 1, 0, 2, 4)
@@ -223,20 +221,22 @@
     same, other = call(
         compact_kernel, "compact", [((HALF, DW), bf)] * 2, place, shard_sizes, cot, smem=2, flops=100_000_000
     )
+    held, same = lax.optimization_barrier((held, same))
+    held = jnp.concatenate([held, hop(held, "z", 4, Z)])
+    held = lax.all_gather(held, ("y", "core"), axis=0, tiled=True)
     pieces = [same] + [hop(other if k & 1 else same, SEQ, k, F) for k in range(1, F)]
 
-    r, t = iota((COLS, 512), 0), iota((COLS, 512), 1)
+    t, r = iota((512, COLS), 0), iota((512, COLS), 1)
     i, sub = r % 6, r // 6
     rj, ry, rc = (sub // 32) * 4 + (sub // 2) % 4, (sub // 8) % 4, sub % 2
-    spot = (((rc ^ core) * 4 + (ry ^ yi)) * 8 + (rj ^ zi)) * 8 + i
-    w_c = dot((spot == t).astype(bf), held, NN).astype(bf)
+    spot = ((((ry * C + rc) * Z + (rj ^ zi)) * 8 + i) == t).astype(bf)
 
     local_bias = lax.dynamic_slice(bias_time, (xi * HL, 0), (HL, 15))
     pair = jnp.stack([local_bias[:, 7 - f : 15 - f] for f in range(F)], axis=1)
     alike = jnp.eye(16, dtype=jnp.bool_)[None, None, :, None, :]
     bias_m = jnp.where(alike, pair[:, :, None, :, None], f32(-1e30)).reshape(HL, POS, POS)
     t2, r2 = iota((COLS, COLS), 1), iota((COLS, COLS), 0)
-    j = (((t2 // 24) % 2) + ((t2 // 12) % 2) * 2 + ((t2 // 6) % 2) * 4) ^ zi
+    j = ((t2 // 12) % 4 + ((t2 // 6) % 2) * 4) ^ zi
     oy, oc = ((t2 // 48) % 4) ^ yi, (t2 // 192) ^ core
     src = (((j // 4) * 4 + oy) * 8 + (j % 4) * 2 + oc) * 6 + t2 % 6
     order = (src == r2).astype(bf)
@@ -259,6 +259,8 @@
         *pieces,
         mixed,
         smem=1,
+        hbm=F,
+        scratch=[pltpu.SemaphoreType.DMA((F,))],
         flops=604_000_000,
     )
     theirs = hop(theirs, "core", 1, C)
@@ -270,32 +272,41 @@
         qkv,
         probs,
         up,
-        w_c,
-        flops=700_000_000,
-    )
-    sums2 = hop(sums, "core", 1, C)
+        held,
+        spot,
+        flops=900_000_000,
+    )
+    both = lax.ppermute(sums, ("z", "core"), [(i, i ^ 9) for i in range(Z * C)])
+    sums = [sums, hop(sums, "core", 1, C), hop(sums, "z", 4, Z), both]
     (grads,) = call(
         grad_kernel, "grads", [((F, 3, HALF, COLS), bf)], qkv, probs, dm, ds, flops=150_000_000
     )
 
     wide = ((48, DW + 128), bf)
     own, b, *msgs = call(
-        join_kernel, "join", [((48, DW), f32), ((24, 128), f32), wide, wide, wide], mine, theirs, sums, sums2
+        join_kernel, "join", [((48, DW), f32), ((24, 128), f32), wide, wide, wide], mine, theirs, *sums
     )
     msgs = [hop(m, "y", k, Y) for k, m in enumerate(msgs, 1)]
-    keep, send = call(ysum_kernel, "ysum", [((32, DW), f32)] * 2, own, b, *msgs)
-    keep, send = call(zsum_kernel, "zsum1", [((16, DW), f32)] * 2, keep, hop(send, "z", 1, Z))
-    first, second = call(zsum_kernel, "zsum2", [((8, DW), f32)] * 2, keep, hop(send, "z", 2, Z))
+    part = ((16, DW), bf)
+    own, b, *msgs = call(
+        ysum_kernel, "ysum", [((12, DW), f32), ((2, DW), f32), part, part, part], own, b, *msgs
+    )
+    msgs = [hop(m, "z", k, Z) for k, m in enumerate(msgs, 1)]
+    first, second, off = call(
+        zsum_kernel, "zsum", [((8, DW), f32), ((8, DW), f32), ((16, 128), f32)], own, b, *msgs
+    )
     home = [(a, b) for b, a in there]
     cross = [((((a // X) ^ 4) * X + a % X), b) for a, b in home]
     first = lax.ppermute(first, ("z", "x"), home)
     second = lax.ppermute(second, ("z", "x"), cross)
-    grad_w_out, off = call(last_kernel, "last", [((6, DW), f32), ((16, 128), f32)], first, second)
-    offs = [off] + [hop(off, "z", 2 * k, Z) for k in range(1, 4)]
-    (grad_bias,) = call(bias_kernel, "bias", [((12, 15), f32)], place, *offs, smem=1)
+    offs = [off] + [hop(off, "x", k, X) for k in range(1, X)]
 
     back = lax.all_to_all(grads, SEQ, 0, 0, tiled=True).reshape(X, C, 3, HALF, COLS)
     grad_qkv = back.transpose(2, 1, 3, 0, 4).reshape(3, 1, 1, POS, DW)
+    first, grad_qkv = lax.optimization_barrier((first, grad_qkv))
+    grad_w_out, grad_bias = call(
+        last_kernel, "last", [((6, DW), f32), ((12, 15), f32)], place, first, second, *offs, smem=1
+    )
     return grad_qkv, grad_bias, grad_w_out
 
 

time: 166 us -> 165 us (level); the launches traced: 163 us -> 165 us
  waiting for transfers between devices: 61 us -> 47.4 us
  between operations: 0.9 us -> 14.4 us
  starting transfers between devices: 64.5 us -> 67.5 us
  matrix products: 1.98 us -> 0 us
    ppermute x23 -> x21, waiting for transfers between devices: 56.8 us -> 40.1 us  [hop(): return lax.ppermute(x, axis, [(i, i ^ k) for i in range(n)])]
    all_to_all x1, waiting for transfers between devices: 0.01 us -> 7.23 us  [per_device(): cot = lax.all_to_all(cot_out[0, 0], SEQ, 0, 0, tiled=True)]
    ppermute x1 -> x3, starting transfers between devices: 7.73 us -> 14.6 us  [the longest x2 9.39 us: per_device(): lax.ppermute(rows8, ('z', 'x'), p)]
    ppermute x1, waiting for transfers between devices: 3.8 us -> 0.01 us  [per_device(): first = lax.ppermute(first, ('z', 'x'), home)]
    ppermute x23 -> x21, starting transfers between devices: 39 us -> 35.3 us  [hop(): return lax.ppermute(x, axis, [(i, i ^ k) for i in range(n)])]
    concatenate x2 -> x0, local copies, waits for them, and re-layouts: 2.12 us -> none  [per_device(): held = jnp.concatenate([held, hop(held, axis, k, n)])]
    dot_general x1 -> x0, matrix products: 1.98 us -> none  [dot(): return lax.dot_general(a, b, dims, preferred_element_type=f32, **kw)]
    pallas_call x11 -> x9, Pallas kernels: 13.6 us -> 15.1 us  [call(): pl.pallas_call(body, out_shape=tuple((jax.ShapeDtypeStruct(s, d) for s, d...]
  transfers between devices with their start and end apart: 29 -> 30, of which waited for: 19 -> 15; matrix products, arithmetic and copies ran while one was open for 9% -> 6% of each run, Pallas kernels for 8% -> 6%
where the time goes in v3:
time: 165 us
  starting transfers between devices  67.5 us (41%)
  waiting for transfers between devices  47.4 us (29%)
  local copies, waits for them, and re-layouts  18.2 us (11%)
  Pallas kernels  15.1 us (9%)
  between operations  14.4 us (9%)
  other arithmetic  1.92 us (1%)
    ppermute x21, waiting for transfers between devices, hop(): return lax.ppermute(x, axis, [(i, i ^ k) for i in range(n)])  40.1 us
    ppermute x21, starting transfers between devices, hop(): return lax.ppermute(x, axis, [(i, i ^ k) for i in range(n)])  35.3 us
    pallas_call x9, Pallas kernels, call(): pl.pallas_call(body, out_shape=tuple((jax.ShapeDtypeStruct(s, d) for s, d...  15.1 us
    unnamed x49, local copies, waits for them, and re-layouts  10.2 us
    ppermute x2, starting transfers between devices, per_device(): lax.ppermute(rows8, ('z', 'x'), p)  9.39 us
    all_to_all x1, waiting for transfers between devices, per_device(): cot = lax.all_to_all(cot_out[0, 0], SEQ, 0, 0, tiled=True)  7.23 us
    all_to_all x1, starting transfers between devices, per_device(): cot = lax.all_to_all(cot_out[0, 0], SEQ, 0, 0, tiled=True)  5.52 us
    ppermute x1, starting transfers between devices, per_device(): both = lax.ppermute(sums, ('z', 'core'), [(i, i ^ 9) for i in range(Z * C)])  5.24 us
  transfers between devices with their start and end apart: 30, of which 15 were waited for; matrix products, arithmetic and copies ran while one was open for 6% of the time, Pallas kernels for 6%

profile of v3, /device:TPU:32, one launch (start us, length us, event | category | flops | bytes accessed | tf_op | source)
XLA Modules:
  0.0 164.5 jit_solution(15682275710244416295)
XLA Ops:
  7.2 0.8 pad.4
  8.0 6.3 %collective-permute-start.1 = (bf16[8,1536]{1,0:T(8,128)(2,1)S(1)}, bf16[8,1536]{1,0:T(8,128)(2,1)S(1)}, u32[]{:S(2)}, u32[]{:S(2)}) collective-permute-start(bf16[8,1536]{1,0:T(8,128)(2,1)S(1)} %pad.4), channel_id=1, source_target_pairs={{0,32},{2,0},{4,96},{6,64},{32,160},{34,128},{36,224},{38,192},{64... | collective-permute-start | bytes 73736 | tf_op jit(solution)/shard_map/ppermute | solution.py:214
  14.3 3.1 %collective-permute-start = (bf16[8,1536]{1,0:T(8,128)(2,1)S(1)}, bf16[8,1536]{1,0:T(8,128)(2,1)S(1)}, u32[]{:S(2)}, u32[]{:S(2)}) collective-permute-start(bf16[8,1536]{1,0:T(8,128)(2,1)S(1)} %pad.4), channel_id=1, source_target_pairs={{0,0},{2,32},{4,64},{6,96},{32,128},{34,160},{36,192},{38,224},{64... | collective-permute-start | bytes 73736 | tf_op jit(solution)/shard_map/ppermute | solution.py:214
  17.4 5.5 %all-to-all-start = ((bf16[8,32,1536]{2,1,0:T(8,128)(2,1)}), bf16[8,32,1536]{2,1,0:T(8,128)(2,1)S(1)}, u32[]{:S(2)}, u32[]{:S(2)}) async-start(bf16[8,32,1536]{2,1,0:T(8,128)(2,1)} %bitcast.34), calls=%async_computation | async-start | bytes 1572864 | tf_op jit(solution)/shard_map/all_to_all | solution.py:217
  23.3 3.2 %collective-permute-start.2 = (bf16[16,1536]{1,0:T(8,128)(2,1)S(1)}, bf16[16,1536]{1,0:T(8,128)(2,1)S(1)}, u32[]{:S(2)}, u32[]{:S(2)}) collective-permute-start(bf16[16,1536]{1,0:T(8,128)(2,1)S(1)} %pad_maximum_fusion.2), channel_id=1, source_target_pairs={{0,64},{32,96},{64,0},{96,32},{128,192},{160,224},{192,128},{224,1... | collective-permute-start | bytes 147464 | tf_op jit(solution)/shard_map/ppermute | solution.py:198
  26.5 0.3 reshape_squeeze.3
  26.8 1.2 copy.8
  28.1 0.8 collective-permute-done.2
  28.9 7.2 %all-to-all-done.cot_ref = bf16[8,32,1536]{2,1,0:T(8,128)(2,1)S(1)} async-done(((bf16[8,32,1536]{2,1,0:T(8,128)(2,1)}), bf16[8,32,1536]{2,1,0:T(8,128)(2,1)S(1)}, u32[]{:S(2)}, u32[]{:S(2)}) %all-to-all-start) | async-done | bytes 786464 | tf_op jit(solution)/shard_map/all_to_all | solution.py:217
  36.1 3.7 %all-to-all-start.1 = ((bf16[8,3,64,384]{3,2,1,0:T(8,128)(2,1)}), bf16[8,3,64,384]{3,2,1,0:T(8,128)(2,1)S(1)}, u32[]{:S(2)}, u32[]{:S(2)}) async-start(bf16[8,3,64,384]{3,2,1,0:T(8,128)(2,1)} %bitcast.6), calls=%async_computation.1 | async-start | bytes 2359296 | tf_op jit(solution)/shard_map/all_to_all | solution.py:219
  39.9 0.8 compact.1
  40.7 0.4 collective-permute-start.11
  41.1 8.6 %collective-permute-done.11 = bf16[32,1536]{1,0:T(8,128)(2,1)S(1)} collective-permute-done((bf16[32,1536]{1,0:T(8,128)(2,1)S(1)}, bf16[32,1536]{1,0:T(8,128)(2,1)S(1)}, u32[]{:S(2)}, u32[]{:S(2)}) %collective-permute-start.11) | collective-permute-done | bytes 98336 | tf_op jit(solution)/shard_map/ppermute | solution.py:198
  49.8 0.7 pad_maximum_fusion
  50.8 0.9 fusion.23.spot_ref
  52.0 1.8 %collective-permute-start.4 = (bf16[64,1536]{1,0:T(8,128)(2,1)S(1)}, bf16[64,1536]{1,0:T(8,128)(2,1)S(1)}, u32[]{:S(2)}, u32[]{:S(2)}) collective-permute-start(bf16[64,1536]{1,0:T(8,128)(2,1)S(1)} %get-tuple-element.33.refs_0_), channel_id=1, source_target_pairs={{0,2},{1,3},{2,0},{3,1},{4,6},{5,7},{6,4},{7,5},{8,10},{9,11},{10,... | collective-permute-start | bytes 589832 | tf_op jit(solution)/shard_map/ppermute | solution.py:198
  53.7 1.3 broadcast_in_dim.31
  55.0 1.8 %broadcast_in_dim.32 = f32[3,128,128]{2,1,0:T(8,128)S(1)} reshape(f32[3,8,16,8,16]{4,3,2,1,0:T(8,128)} %broadcast_in_dim.31) | data formatting | bytes 393216 | tf_op jit(solution)/shard_map/jit(_where)/broadcast_in_dim | solution.py:237
  57.4 3.2 %collective-permute-start.6 = (bf16[64,1536]{1,0:T(8,128)(2,1)S(1)}, bf16[64,1536]{1,0:T(8,128)(2,1)S(1)}, u32[]{:S(2)}, u32[]{:S(2)}) collective-permute-start(bf16[64,1536]{1,0:T(8,128)(2,1)S(1)} %get-tuple-element.33.refs_0_), channel_id=1, source_target_pairs={{0,4},{1,5},{2,6},{3,7},{4,0},{5,1},{6,2},{7,3},{8,12},{9,13},{10,... | collective-permute-start | bytes 589832 | tf_op jit(solution)/shard_map/ppermute | solution.py:198
  60.6 0.7 copy-done.12
  61.3 2.9 %collective-permute-start.8 = (bf16[64,1536]{1,0:T(8,128)(2,1)S(1)}, bf16[64,1536]{1,0:T(8,128)(2,1)}, u32[]{:S(2)}, u32[]{:S(2)}) collective-permute-start(bf16[64,1536]{1,0:T(8,128)(2,1)S(1)} %get-tuple-element.33.refs_0_), channel_id=1, source_target_pairs={{0,6},{1,7},{2,4},{3,5},{4,2},{5,3},{6,0},{7,1},{8,14},{9,15},{10,... | collective-permute-start | bytes 589832 | tf_op jit(solution)/shard_map/ppermute | solution.py:198
  64.2 0.3 collective-permute-start.9
  64.6 4.3 %attn_fwd.1 = (f32[3,4,128,128]{3,2,1,0:T(8,128)S(1)}, bf16[512,384]{1,0:T(8,128)(2,1)S(1)}) custom-call(bf16[8,3,64,384]{3,2,1,0:T(8,128)(2,1)S(1)} %all-to-all-done.1.qkv_ref, f32[3,128,128]{2,1,0:T(8,128)S(1)} %broadcast_select_fusion.bias_ref, bf16[384,384]{1,0:T(8,128)(2,1)S(1)} %fusion.44.order_ref), custom_call_target="tpu_custom_call" | custom-call | flops 250000000 | bytes 2850816 | tf_op jit(solution)/shard_map/attn_fwd/pallas_call | solution.py:44
  68.9 0.7 copy-done.16
  69.6 1.0 collective-permute-done.6.refs_4_
  70.6 0.7 copy-done.18
  71.3 3.0 %collective-permute-done.7.refs_5_ = bf16[64,1536]{1,0:T(8,128)(2,1)} collective-permute-done((bf16[64,1536]{1,0:T(8,128)(2,1)S(1)}, bf16[64,1536]{1,0:T(8,128)(2,1)}, u32[]{:S(2)}, u32[]{:S(2)}) %collective-permute-start.7) | collective-permute-done | bytes 196640 | tf_op jit(solution)/shard_map/ppermute | solution.py:198
  74.3 4.3 %collective-permute-done.8.refs_6_ = bf16[64,1536]{1,0:T(8,128)(2,1)} collective-permute-done((bf16[64,1536]{1,0:T(8,128)(2,1)S(1)}, bf16[64,1536]{1,0:T(8,128)(2,1)}, u32[]{:S(2)}, u32[]{:S(2)}) %collective-permute-start.8) | collective-permute-done | bytes 196640 | tf_op jit(solution)/shard_map/ppermute | solution.py:198
  78.6 3.6 %collective-permute-done.9.refs_7_ = bf16[64,1536]{1,0:T(8,128)(2,1)} collective-permute-done((bf16[64,1536]{1,0:T(8,128)(2,1)S(1)}, bf16[64,1536]{1,0:T(8,128)(2,1)}, u32[]{:S(2)}, u32[]{:S(2)}) %collective-permute-start.9) | collective-permute-done | bytes 196640 | tf_op jit(solution)/shard_map/ppermute | solution.py:198
  82.2 0.9 copy-done.15
  83.1 0.9 copy-done.17
  84.0 0.9 copy-done.19
  85.0 3.8 %grad_w.1 = (bf16[8,64,1536]{2,1,0:T(8,128)(2,1)S(1)}, f32[192,1536]{1,0:T(8,128)S(1)}, bf16[192,1536]{1,0:T(8,128)(2,1)S(1)}) custom-call(s32[4]{0:T(128)S(1)} %pad_add_fusion.place, bf16[64,1536]{1,0:T(8,128)(2,1)S(1)} %copy-done.11, bf16[64,1536]{1,0:T(8,128)(2,1)S(1)} %copy-done.13, bf16[64,1536]{1,0:T(8,128)(2,1)S(1)} %copy-done.15, ...), custom_call_target="tpu_custom_call" | custom-call | flops 604000000 | bytes 5308432 | tf_op jit(solution)/shard_map/grad_w/pallas_call | solution.py:44
  88.8 1.0 copy-done.3
  89.8 0.8 copy-done.8
  90.6 1.4 copy-done.1
  92.0 1.0 copy-done.2
  93.0 1.7 %scores_bwd.1 = (bf16[8,64,384]{2,1,0:T(8,128)(2,1)S(1)}, bf16[3,4,128,128]{3,2,1,0:T(8,128)(2,1)S(1)}, f32[8,384]{1,0:T(8,128)S(1)}) custom-call(bf16[8,3,64,384]{3,2,1,0:T(8,128)(2,1)S(1)} %all-to-all-done.1.qkv_ref, f32[3,4,128,128]{3,2,1,0:T(8,128)S(1)} %get-tuple-element.38.probs_ref, bf16[8,64,1536]{2,1,0:T(8,128)(2,1)S(1)} %get-tuple-element.39.up_ref, ...), custom_call_target="tpu_custom_call" | custom-call | flops 900000000 | bytes 6303744 | tf_op jit(solution)/shard_map/scores_bwd/pallas_call | solution.py:44
  94.8 0.6 copy-done.5
  95.4 1.5 grads.1
  96.9 3.7 %all-to-all-start.2 = ((bf16[8,3,64,384]{3,2,1,0:T(8,128)(2,1)}), bf16[8,3,64,384]{3,2,1,0:T(8,128)(2,1)S(1)}, u32[]{:S(2)}, u32[]{:S(2)}) async-start(bf16[8,3,64,384]{3,2,1,0:T(8,128)(2,1)} %grads.1), calls=%async_computation.2 | async-start | bytes 2359296 | tf_op jit(solution)/shard_map/all_to_all | solution.py:304
  100.6 0.4 collective-permute-start.10
  101.2 0.3 collective-permute-start.13
  101.6 5.2 %collective-permute-start.14 = (f32[8,384]{1,0:T(8,128)S(1)}, f32[8,384]{1,0:T(8,128)S(1)}, u32[]{:S(2)}, u32[]{:S(2)}) collective-permute-start(f32[8,384]{1,0:T(8,128)S(1)} %copy-done.6), channel_id=1, source_target_pairs={{0,129},{1,128},{32,161},{33,160},{64,193},{65,192},{96,225},{97,2... | collective-permute-start | bytes 36872 | tf_op jit(solution)/shard_map/ppermute | solution.py:279
  106.8 2.0 %collective-permute-done.13.s2 = f32[8,384]{1,0:T(8,128)S(1)} collective-permute-done((f32[8,384]{1,0:T(8,128)S(1)}, f32[8,384]{1,0:T(8,128)S(1)}, u32[]{:S(2)}, u32[]{:S(2)}) %collective-permute-start.13) | collective-permute-done | bytes 12320 | tf_op jit(solution)/shard_map/ppermute | solution.py:198
  109.0 1.7 %collective-permute-start.15 = (bf16[48,1664]{1,0:T(8,128)(2,1)S(1)}, bf16[48,1664]{1,0:T(8,128)(2,1)S(1)}, u32[]{:S(2)}, u32[]{:S(2)}) collective-permute-start(bf16[48,1664]{1,0:T(8,128)(2,1)S(1)} %get-tuple-element.44), channel_id=1, source_target_pairs={{0,8},{8,0},{16,24},{24,16},{1,9},{9,1},{17,25},{25,17},{2,10},{10... | collective-permute-start | bytes 479240 | tf_op jit(solution)/shard_map/ppermute | solution.py:198
  110.7 2.9 %collective-permute-start.16 = (bf16[48,1664]{1,0:T(8,128)(2,1)S(1)}, bf16[48,1664]{1,0:T(8,128)(2,1)S(1)}, u32[]{:S(2)}, u32[]{:S(2)}) collective-permute-start(bf16[48,1664]{1,0:T(8,128)(2,1)S(1)} %get-tuple-element.45), channel_id=1, source_target_pairs={{0,16},{8,24},{16,0},{24,8},{1,17},{9,25},{17,1},{25,9},{2,18},{10... | collective-permute-start | bytes 479240 | tf_op jit(solution)/shard_map/ppermute | solution.py:198
  113.8 2.3 %collective-permute-done.15.m1 = bf16[48,1664]{1,0:T(8,128)(2,1)S(1)} collective-permute-done((bf16[48,1664]{1,0:T(8,128)(2,1)S(1)}, bf16[48,1664]{1,0:T(8,128)(2,1)S(1)}, u32[]{:S(2)}, u32[]{:S(2)}) %collective-permute-start.15) | collective-permute-done | bytes 159776 | tf_op jit(solution)/shard_map/ppermute | solution.py:198
  116.1 5.1 %collective-permute-done.16.m2 = bf16[48,1664]{1,0:T(8,128)(2,1)S(1)} collective-permute-done((bf16[48,1664]{1,0:T(8,128)(2,1)S(1)}, bf16[48,1664]{1,0:T(8,128)(2,1)S(1)}, u32[]{:S(2)}, u32[]{:S(2)}) %collective-permute-start.16) | collective-permute-done | bytes 159776 | tf_op jit(solution)/shard_map/ppermute | solution.py:198
  121.2 2.5 %collective-permute-done.17.m3 = bf16[48,1664]{1,0:T(8,128)(2,1)S(1)} collective-permute-done((bf16[48,1664]{1,0:T(8,128)(2,1)S(1)}, bf16[48,1664]{1,0:T(8,128)(2,1)S(1)}, u32[]{:S(2)}, u32[]{:S(2)}) %collective-permute-start.17) | collective-permute-done | bytes 159776 | tf_op jit(solution)/shard_map/ppermute | solution.py:198
  123.8 4.9 %collective-permute-start.18 = (bf16[16,1536]{1,0:T(8,128)(2,1)S(1)}, bf16[16,1536]{1,0:T(8,128)(2,1)S(1)}, u32[]{:S(2)}, u32[]{:S(2)}) collective-permute-start(bf16[16,1536]{1,0:T(8,128)(2,1)S(1)} %get-tuple-element.49), channel_id=1, source_target_pairs={{0,32},{32,0},{64,96},{96,64},{128,160},{160,128},{192,224},{224,1... | collective-permute-start | bytes 147464 | tf_op jit(solution)/shard_map/ppermute | solution.py:198
  128.8 0.4 collective-permute-start.19
  129.1 1.2 collective-permute-start.20
  130.3 0.5 collective-permute-done.18.n1
  130.8 3.0 %collective-permute-done.19.n2 = bf16[16,1536]{1,0:T(8,128)(2,1)S(1)} collective-permute-done((bf16[16,1536]{1,0:T(8,128)(2,1)S(1)}, bf16[16,1536]{1,0:T(8,128)(2,1)S(1)}, u32[]{:S(2)}, u32[]{:S(2)}) %collective-permute-start.19) | collective-permute-done | bytes 49184 | tf_op jit(solution)/shard_map/ppermute | solution.py:198
  133.9 0.6 collective-permute-done.20.n3
  134.5 1.5 zsum.1
  136.0 4.6 %collective-permute-start.21 = (f32[8,1536]{1,0:T(8,128)S(1)}, f32[8,1536]{1,0:T(8,128)S(1)}, u32[]{:S(2)}, u32[]{:S(2)}) collective-permute-start(f32[8,1536]{1,0:T(8,128)S(1)} %get-tuple-element.52), channel_id=1, source_target_pairs={{0,0},{32,2},{64,4},{96,6},{128,32},{160,34},{192,36},{224,38},{2,... | collective-permute-start | bytes 147464 | tf_op jit(solution)/shard_map/ppermute | solution.py:300
  140.7 2.6 %collective-permute-start.23 = (f32[16,128]{1,0:T(8,128)S(1)}, f32[16,128]{1,0:T(8,128)S(1)}, u32[]{:S(2)}, u32[]{:S(2)}) collective-permute-start(f32[16,128]{1,0:T(8,128)S(1)} %get-tuple-element.58.o0), channel_id=1, source_target_pairs={{0,2},{2,0},{4,6},{6,4},{1,3},{3,1},{5,7},{7,5},{8,10},{10,8},{12,... | collective-permute-start | bytes 24584 | tf_op jit(solution)/shard_map/ppermute | solution.py:198
  143.3 8.3 %collective-permute-start.24 = (f32[16,128]{1,0:T(8,128)S(1)}, f32[16,128]{1,0:T(8,128)S(1)}, u32[]{:S(2)}, u32[]{:S(2)}) collective-permute-start(f32[16,128]{1,0:T(8,128)S(1)} %get-tuple-element.58.o0), channel_id=1, source_target_pairs={{0,4},{2,6},{4,0},{6,2},{1,5},{3,7},{5,1},{7,3},{8,12},{10,14},{12... | collective-permute-start | bytes 24584 | tf_op jit(solution)/shard_map/ppermute | solution.py:198
  151.6 0.9 copy.10
  152.6 1.3 reshape.28
  153.9 2.6 %collective-permute-done.25.o3 = f32[16,128]{1,0:T(8,128)S(1)} collective-permute-done((f32[16,128]{1,0:T(8,128)S(1)}, f32[16,128]{1,0:T(8,128)S(1)}, u32[]{:S(2)}, u32[]{:S(2)}) %collective-permute-start.25) | collective-permute-done | bytes 8224 | tf_op jit(solution)/shard_map/ppermute | solution.py:198
  156.5 1.2 last.1
  (83 shorter events, 2.4 us)
Async XLA Ops:
  7.2 15.8 %copy-start = (f32[12,15]{1,0:T(8,128)S(1)}, f32[12,15]{1,0:T(8,128)}, u32[]{:S(2)}) copy-start(f32[12,15]{1,0:T(8,128)} %param.7) | copy-start | bytes 2164
  7.2 19.4 %copy-start.20 = (bf16[3,1,1,128,1536]{4,3,2,1,0:T(8,128)(2,1)S(1)}, bf16[3,1,1,128,1536]{4,3,2,1,0:T(8,128)(2,1)}, u32[]{:S(2)}) copy-start(bf16[3,1,1,128,1536]{4,3,2,1,0:T(8,128)(2,1)} %param.5) | copy-start | bytes 3538948
  8.0 15.2 %collective-permute-start.1 = (bf16[8,1536]{1,0:T(8,128)(2,1)S(1)}, bf16[8,1536]{1,0:T(8,128)(2,1)S(1)}, u32[]{:S(2)}, u32[]{:S(2)}) collective-permute-start(bf16[8,1536]{1,0:T(8,128)(2,1)S(1)} %pad.4), channel_id=1, source_target_pairs={{0,32},{2,0},{4,96},{6,64},{32,160},{34,128},{36,224},{38,192},{64... | collective-permute-start | bytes 73736 | tf_op jit(solution)/shard_map/ppermute | solution.py:214
  14.3 8.9 %collective-permute-start = (bf16[8,1536]{1,0:T(8,128)(2,1)S(1)}, bf16[8,1536]{1,0:T(8,128)(2,1)S(1)}, u32[]{:S(2)}, u32[]{:S(2)}) collective-permute-start(bf16[8,1536]{1,0:T(8,128)(2,1)S(1)} %pad.4), channel_id=1, source_target_pairs={{0,0},{2,32},{4,64},{6,96},{32,128},{34,160},{36,192},{38,224},{64... | collective-permute-start | bytes 73736 | tf_op jit(solution)/shard_map/ppermute | solution.py:214
  17.4 18.7 %all-to-all-start = ((bf16[8,32,1536]{2,1,0:T(8,128)(2,1)}), bf16[8,32,1536]{2,1,0:T(8,128)(2,1)S(1)}, u32[]{:S(2)}, u32[]{:S(2)}) async-start(bf16[8,32,1536]{2,1,0:T(8,128)(2,1)} %bitcast.34), calls=%async_computation | async-start | bytes 1572864 | tf_op jit(solution)/shard_map/all_to_all | solution.py:217
  23.3 5.6 %collective-permute-start.2 = (bf16[16,1536]{1,0:T(8,128)(2,1)S(1)}, bf16[16,1536]{1,0:T(8,128)(2,1)S(1)}, u32[]{:S(2)}, u32[]{:S(2)}) collective-permute-start(bf16[16,1536]{1,0:T(8,128)(2,1)S(1)} %pad_maximum_fusion.2), channel_id=1, source_target_pairs={{0,64},{32,96},{64,0},{96,32},{128,192},{160,224},{192,128},{224,1... | collective-permute-start | bytes 147464 | tf_op jit(solution)/shard_map/ppermute | solution.py:198
  36.1 3.8 %copy-start.7 = (s32[1,8]{1,0:T(1,128)S(1)}, s32[1,8]{1,0:T(1,128)}, u32[]{:S(2)}) copy-start(s32[1,8]{1,0:T(1,128)} %sizes.1) | copy-start | bytes 100
  36.1 28.4 %all-to-all-start.1 = ((bf16[8,3,64,384]{3,2,1,0:T(8,128)(2,1)}), bf16[8,3,64,384]{3,2,1,0:T(8,128)(2,1)S(1)}, u32[]{:S(2)}, u32[]{:S(2)}) async-start(bf16[8,3,64,384]{3,2,1,0:T(8,128)(2,1)} %bitcast.6), calls=%async_computation.1 | async-start | bytes 2359296 | tf_op jit(solution)/shard_map/all_to_all | solution.py:219
  39.8 50.8 %all-gather.2.cloned.1.call-start = ((), (), s32[]{:S(2)}) async-start(), calls=%async_computation.3 | async-start | bytes 1769472 | tf_op jit(solution)/shard_map/all_gather | solution.py:226
  40.7 19.9 %copy-start.10 = (bf16[64,1536]{1,0:T(8,128)(2,1)}, bf16[64,1536]{1,0:T(8,128)(2,1)S(1)}, u32[]{:S(2)}) copy-start(bf16[64,1536]{1,0:T(8,128)(2,1)S(1)} %get-tuple-element.33.refs_0_) | copy-start | bytes 589828
  40.7 9.1 %collective-permute-start.11 = (bf16[32,1536]{1,0:T(8,128)(2,1)S(1)}, bf16[32,1536]{1,0:T(8,128)(2,1)S(1)}, u32[]{:S(2)}, u32[]{:S(2)}) collective-permute-start(bf16[32,1536]{1,0:T(8,128)(2,1)S(1)} %pad_maximum_fusion.1), channel_id=1, source_target_pairs={{0,128},{32,160},{64,192},{96,224},{128,0},{160,32},{192,64},{224,... | collective-permute-start | bytes 294920 | tf_op jit(solution)/shard_map/ppermute | solution.py:198
  51.9 8.8 %collective-permute-start.3 = (bf16[64,1536]{1,0:T(8,128)(2,1)S(1)}, bf16[64,1536]{1,0:T(8,128)(2,1)S(1)}, u32[]{:S(2)}, u32[]{:S(2)}) collective-permute-start(bf16[64,1536]{1,0:T(8,128)(2,1)S(1)} %get-tuple-element.34), channel_id=1, source_target_pairs={{0,1},{1,0},{2,3},{3,2},{4,5},{5,4},{6,7},{7,6},{8,9},{9,8},{10,11... | collective-permute-start | bytes 589832 | tf_op jit(solution)/shard_map/ppermute | solution.py:198
  52.0 12.2 %collective-permute-start.4 = (bf16[64,1536]{1,0:T(8,128)(2,1)S(1)}, bf16[64,1536]{1,0:T(8,128)(2,1)S(1)}, u32[]{:S(2)}, u32[]{:S(2)}) collective-permute-start(bf16[64,1536]{1,0:T(8,128)(2,1)S(1)} %get-tuple-element.33.refs_0_), channel_id=1, source_target_pairs={{0,2},{1,3},{2,0},{3,1},{4,6},{5,7},{6,4},{7,5},{8,10},{9,11},{10,... | collective-permute-start | bytes 589832 | tf_op jit(solution)/shard_map/ppermute | solution.py:198
  57.2 11.7 %collective-permute-start.5 = (bf16[64,1536]{1,0:T(8,128)(2,1)S(1)}, bf16[64,1536]{1,0:T(8,128)(2,1)S(1)}, u32[]{:S(2)}, u32[]{:S(2)}) collective-permute-start(bf16[64,1536]{1,0:T(8,128)(2,1)S(1)} %get-tuple-element.34), channel_id=1, source_target_pairs={{0,3},{1,2},{2,1},{3,0},{4,7},{5,6},{6,5},{7,4},{8,11},{9,10},{10,... | collective-permute-start | bytes 589832 | tf_op jit(solution)/shard_map/ppermute | solution.py:198
  57.4 13.2 %collective-permute-start.6 = (bf16[64,1536]{1,0:T(8,128)(2,1)S(1)}, bf16[64,1536]{1,0:T(8,128)(2,1)S(1)}, u32[]{:S(2)}, u32[]{:S(2)}) collective-permute-start(bf16[64,1536]{1,0:T(8,128)(2,1)S(1)} %get-tuple-element.33.refs_0_), channel_id=1, source_target_pairs={{0,4},{1,5},{2,6},{3,7},{4,0},{5,1},{6,2},{7,3},{8,12},{9,13},{10,... | collective-permute-start | bytes 589832 | tf_op jit(solution)/shard_map/ppermute | solution.py:198
  60.6 13.7 %collective-permute-start.7 = (bf16[64,1536]{1,0:T(8,128)(2,1)S(1)}, bf16[64,1536]{1,0:T(8,128)(2,1)}, u32[]{:S(2)}, u32[]{:S(2)}) collective-permute-start(bf16[64,1536]{1,0:T(8,128)(2,1)S(1)} %get-tuple-element.34), channel_id=1, source_target_pairs={{0,5},{1,4},{2,7},{3,6},{4,1},{5,0},{6,3},{7,2},{8,13},{9,12},{10,... | collective-permute-start | bytes 589832 | tf_op jit(solution)/shard_map/ppermute | solution.py:198
  60.6 0.7 copy-start.12
  61.3 17.3 %collective-permute-start.8 = (bf16[64,1536]{1,0:T(8,128)(2,1)S(1)}, bf16[64,1536]{1,0:T(8,128)(2,1)}, u32[]{:S(2)}, u32[]{:S(2)}) collective-permute-start(bf16[64,1536]{1,0:T(8,128)(2,1)S(1)} %get-tuple-element.33.refs_0_), channel_id=1, source_target_pairs={{0,6},{1,7},{2,4},{3,5},{4,2},{5,3},{6,0},{7,1},{8,14},{9,15},{10,... | collective-permute-start | bytes 589832 | tf_op jit(solution)/shard_map/ppermute | solution.py:198
  64.2 18.0 %copy-start.14 = (bf16[64,1536]{1,0:T(8,128)(2,1)}, bf16[64,1536]{1,0:T(8,128)(2,1)S(1)}, u32[]{:S(2)}) copy-start(bf16[64,1536]{1,0:T(8,128)(2,1)S(1)} %collective-permute-done.4.refs_2_) | copy-start | bytes 589828
  64.2 18.0 %collective-permute-start.9 = (bf16[64,1536]{1,0:T(8,128)(2,1)S(1)}, bf16[64,1536]{1,0:T(8,128)(2,1)}, u32[]{:S(2)}, u32[]{:S(2)}) collective-permute-start(bf16[64,1536]{1,0:T(8,128)(2,1)S(1)} %get-tuple-element.34), channel_id=1, source_target_pairs={{0,7},{1,6},{2,5},{3,4},{4,3},{5,2},{6,1},{7,0},{8,15},{9,14},{10,... | collective-permute-start | bytes 589832 | tf_op jit(solution)/shard_map/ppermute | solution.py:198
  64.6 17.6 %copy-start.11 = (bf16[64,1536]{1,0:T(8,128)(2,1)S(1)}, bf16[64,1536]{1,0:T(8,128)(2,1)}, u32[]{:S(2)}) copy-start(bf16[64,1536]{1,0:T(8,128)(2,1)} %copy-done.10) | copy-start | bytes 589828
  64.6 17.6 %copy-start.13 = (bf16[64,1536]{1,0:T(8,128)(2,1)S(1)}, bf16[64,1536]{1,0:T(8,128)(2,1)}, u32[]{:S(2)}) copy-start(bf16[64,1536]{1,0:T(8,128)(2,1)} %copy-done.12) | copy-start | bytes 589828
  68.9 0.7 copy-start.16
  70.6 0.7 copy-start.18
  82.2 0.9 copy-start.15
  83.1 0.9 copy-start.17
  84.0 0.9 copy-start.19
  88.8 1.0 copy-start.3
  89.8 0.8 copy-start.8
  90.6 1.4 copy-start.1
  92.0 1.0 copy-start.2
  94.8 0.6 copy-start.5
  96.9 3.7 %copy-start.9 = (bf16[192,1536]{1,0:T(8,128)(2,1)S(1)}, bf16[192,1536]{1,0:T(8,128)(2,1)}, u32[]{:S(2)}) copy-start(bf16[192,1536]{1,0:T(8,128)(2,1)} %copy-done.8) | copy-start | bytes 1769476
  96.9 4.1 %copy-start.6 = (f32[8,384]{1,0:T(8,128)S(1)}, f32[8,384]{1,0:T(8,128)}, u32[]{:S(2)}) copy-start(f32[8,384]{1,0:T(8,128)} %copy-done.5) | copy-start | bytes 36868
  96.9 11.9 %copy-start.4 = (f32[192,1536]{1,0:T(8,128)S(1)}, f32[192,1536]{1,0:T(8,128)}, u32[]{:S(2)}) copy-start(f32[192,1536]{1,0:T(8,128)} %copy-done.3) | copy-start | bytes 3538948
  96.9 54.7 %all-to-all-start.2 = ((bf16[8,3,64,384]{3,2,1,0:T(8,128)(2,1)}), bf16[8,3,64,384]{3,2,1,0:T(8,128)(2,1)S(1)}, u32[]{:S(2)}, u32[]{:S(2)}) async-start(bf16[8,3,64,384]{3,2,1,0:T(8,128)(2,1)} %grads.1), calls=%async_computation.2 | async-start | bytes 2359296 | tf_op jit(solution)/shard_map/all_to_all | solution.py:304
  100.6 6.2 %collective-permute-start.10 = (bf16[192,1536]{1,0:T(8,128)(2,1)S(1)}, bf16[192,1536]{1,0:T(8,128)(2,1)S(1)}, u32[]{:S(2)}, u32[]{:S(2)}) collective-permute-start(bf16[192,1536]{1,0:T(8,128)(2,1)S(1)} %copy-done.9), channel_id=1, source_target_pairs={{0,1},{1,0},{2,3},{3,2},{4,5},{5,4},{6,7},{7,6},{8,9},{9,8},{10,11... | collective-permute-start | bytes 1769480 | tf_op jit(solution)/shard_map/ppermute | solution.py:198
  101.0 5.8 %collective-permute-start.12 = (f32[8,384]{1,0:T(8,128)S(1)}, f32[8,384]{1,0:T(8,128)S(1)}, u32[]{:S(2)}, u32[]{:S(2)}) collective-permute-start(f32[8,384]{1,0:T(8,128)S(1)} %copy-done.6), channel_id=1, source_target_pairs={{0,1},{1,0},{2,3},{3,2},{4,5},{5,4},{6,7},{7,6},{8,9},{9,8},{10,11... | collective-permute-start | bytes 36872 | tf_op jit(solution)/shard_map/ppermute | solution.py:198
  101.2 7.6 %collective-permute-start.13 = (f32[8,384]{1,0:T(8,128)S(1)}, f32[8,384]{1,0:T(8,128)S(1)}, u32[]{:S(2)}, u32[]{:S(2)}) collective-permute-start(f32[8,384]{1,0:T(8,128)S(1)} %copy-done.6), channel_id=1, source_target_pairs={{0,128},{32,160},{64,192},{96,224},{128,0},{160,32},{192,64},{224,... | collective-permute-start | bytes 36872 | tf_op jit(solution)/shard_map/ppermute | solution.py:198
  101.6 7.3 %collective-permute-start.14 = (f32[8,384]{1,0:T(8,128)S(1)}, f32[8,384]{1,0:T(8,128)S(1)}, u32[]{:S(2)}, u32[]{:S(2)}) collective-permute-start(f32[8,384]{1,0:T(8,128)S(1)} %copy-done.6), channel_id=1, source_target_pairs={{0,129},{1,128},{32,161},{33,160},{64,193},{65,192},{96,225},{97,2... | collective-permute-start | bytes 36872 | tf_op jit(solution)/shard_map/ppermute | solution.py:279
  109.0 7.0 %collective-permute-start.15 = (bf16[48,1664]{1,0:T(8,128)(2,1)S(1)}, bf16[48,1664]{1,0:T(8,128)(2,1)S(1)}, u32[]{:S(2)}, u32[]{:S(2)}) collective-permute-start(bf16[48,1664]{1,0:T(8,128)(2,1)S(1)} %get-tuple-element.44), channel_id=1, source_target_pairs={{0,8},{8,0},{16,24},{24,16},{1,9},{9,1},{17,25},{25,17},{2,10},{10... | collective-permute-start | bytes 479240 | tf_op jit(solution)/shard_map/ppermute | solution.py:198
  110.7 10.5 %collective-permute-start.16 = (bf16[48,1664]{1,0:T(8,128)(2,1)S(1)}, bf16[48,1664]{1,0:T(8,128)(2,1)S(1)}, u32[]{:S(2)}, u32[]{:S(2)}) collective-permute-start(bf16[48,1664]{1,0:T(8,128)(2,1)S(1)} %get-tuple-element.45), channel_id=1, source_target_pairs={{0,16},{8,24},{16,0},{24,8},{1,17},{9,25},{17,1},{25,9},{2,18},{10... | collective-permute-start | bytes 479240 | tf_op jit(solution)/shard_map/ppermute | solution.py:198
  113.6 10.2 %collective-permute-start.17 = (bf16[48,1664]{1,0:T(8,128)(2,1)S(1)}, bf16[48,1664]{1,0:T(8,128)(2,1)S(1)}, u32[]{:S(2)}, u32[]{:S(2)}) collective-permute-start(bf16[48,1664]{1,0:T(8,128)(2,1)S(1)} %get-tuple-element.46), channel_id=1, source_target_pairs={{0,24},{8,16},{16,8},{24,0},{1,25},{9,17},{17,9},{25,1},{2,26},{10... | collective-permute-start | bytes 479240 | tf_op jit(solution)/shard_map/ppermute | solution.py:198
  123.8 7.0 %collective-permute-start.18 = (bf16[16,1536]{1,0:T(8,128)(2,1)S(1)}, bf16[16,1536]{1,0:T(8,128)(2,1)S(1)}, u32[]{:S(2)}, u32[]{:S(2)}) collective-permute-start(bf16[16,1536]{1,0:T(8,128)(2,1)S(1)} %get-tuple-element.49), channel_id=1, source_target_pairs={{0,32},{32,0},{64,96},{96,64},{128,160},{160,128},{192,224},{224,1... | collective-permute-start | bytes 147464 | tf_op jit(solution)/shard_map/ppermute | solution.py:198
  128.8 5.1 %collective-permute-start.19 = (bf16[16,1536]{1,0:T(8,128)(2,1)S(1)}, bf16[16,1536]{1,0:T(8,128)(2,1)S(1)}, u32[]{:S(2)}, u32[]{:S(2)}) collective-permute-start(bf16[16,1536]{1,0:T(8,128)(2,1)S(1)} %get-tuple-element.50), channel_id=1, source_target_pairs={{0,64},{32,96},{64,0},{96,32},{128,192},{160,224},{192,128},{224,1... | collective-permute-start | bytes 147464 | tf_op jit(solution)/shard_map/ppermute | solution.py:198
  129.1 5.4 %collective-permute-start.20 = (bf16[16,1536]{1,0:T(8,128)(2,1)S(1)}, bf16[16,1536]{1,0:T(8,128)(2,1)S(1)}, u32[]{:S(2)}, u32[]{:S(2)}) collective-permute-start(bf16[16,1536]{1,0:T(8,128)(2,1)S(1)} %get-tuple-element.51), channel_id=1, source_target_pairs={{0,96},{32,64},{64,32},{96,0},{128,224},{160,192},{192,160},{224,1... | collective-permute-start | bytes 147464 | tf_op jit(solution)/shard_map/ppermute | solution.py:198
  136.0 17.9 %collective-permute-start.21 = (f32[8,1536]{1,0:T(8,128)S(1)}, f32[8,1536]{1,0:T(8,128)S(1)}, u32[]{:S(2)}, u32[]{:S(2)}) collective-permute-start(f32[8,1536]{1,0:T(8,128)S(1)} %get-tuple-element.52), channel_id=1, source_target_pairs={{0,0},{32,2},{64,4},{96,6},{128,32},{160,34},{192,36},{224,38},{2,... | collective-permute-start | bytes 147464 | tf_op jit(solution)/shard_map/ppermute | solution.py:300
  140.6 15.9 %collective-permute-start.22 = (f32[8,1536]{1,0:T(8,128)S(1)}, f32[8,1536]{1,0:T(8,128)S(1)}, u32[]{:S(2)}, u32[]{:S(2)}) collective-permute-start(f32[8,1536]{1,0:T(8,128)S(1)} %get-tuple-element.57), channel_id=1, source_target_pairs={{128,0},{160,2},{192,4},{224,6},{0,32},{32,34},{64,36},{96,38},{13... | collective-permute-start | bytes 147464 | tf_op jit(solution)/shard_map/ppermute | solution.py:301
  140.7 13.2 %collective-permute-start.23 = (f32[16,128]{1,0:T(8,128)S(1)}, f32[16,128]{1,0:T(8,128)S(1)}, u32[]{:S(2)}, u32[]{:S(2)}) collective-permute-start(f32[16,128]{1,0:T(8,128)S(1)} %get-tuple-element.58.o0), channel_id=1, source_target_pairs={{0,2},{2,0},{4,6},{6,4},{1,3},{3,1},{5,7},{7,5},{8,10},{10,8},{12,... | collective-permute-start | bytes 24584 | tf_op jit(solution)/shard_map/ppermute | solution.py:198
  143.3 10.5 %collective-permute-start.24 = (f32[16,128]{1,0:T(8,128)S(1)}, f32[16,128]{1,0:T(8,128)S(1)}, u32[]{:S(2)}, u32[]{:S(2)}) collective-permute-start(f32[16,128]{1,0:T(8,128)S(1)} %get-tuple-element.58.o0), channel_id=1, source_target_pairs={{0,4},{2,6},{4,0},{6,2},{1,5},{3,7},{5,1},{7,3},{8,12},{10,14},{12... | collective-permute-start | bytes 24584 | tf_op jit(solution)/shard_map/ppermute | solution.py:198
  151.6 4.9 %collective-permute-start.25 = (f32[16,128]{1,0:T(8,128)S(1)}, f32[16,128]{1,0:T(8,128)S(1)}, u32[]{:S(2)}, u32[]{:S(2)}) collective-permute-start(f32[16,128]{1,0:T(8,128)S(1)} %get-tuple-element.58.o0), channel_id=1, source_target_pairs={{0,6},{2,4},{4,2},{6,0},{1,7},{3,5},{5,3},{7,1},{8,14},{10,12},{12... | collective-permute-start | bytes 24584 | tf_op jit(solution)/shard_map/ppermute | solution.py:198
Sparse Core Ops, SparseCore 0:
  50.6 27.7 all-gather.1

commit v4 on v3

--- a/solution.py
+++ b/solution.py
@@ -1,4 +1,3 @@
-import functools
 import math
 
 import jax
@@ -24,7 +23,6 @@
 NT = (((1,), (1,)), ((), ()))
 TN = (((0,), (0,)), ((), ()))
 bf, f32 = jnp.bfloat16, jnp.float32
-CORE, YI, ZI, RANK = 0, 1, 2, 3
 
 
 def dot(a, b, dims, **kw):
@@ -35,28 +33,41 @@
     return lax.broadcasted_iota(jnp.int32, shape, dim)
 
 
-def call(body, name, outs, *ins, smem=0, hbm=0, scratch=(), flops=0):
+def call(body, name, outs, *ins, smem=0, scratch=(), flops=0, space=pltpu.VMEM, vmem=16):
     total = sum(math.prod(s) * jnp.dtype(d).itemsize for s, d in outs)
     total += sum(a.size * a.dtype.itemsize for a in ins)
     specs = [pl.BlockSpec(memory_space=pltpu.SMEM)] * smem
-    specs += [pl.BlockSpec(memory_space=pl.ANY)] * hbm
-    specs += [pl.BlockSpec(memory_space=pltpu.VMEM)] * (len(ins) - smem - hbm)
+    specs += [pl.BlockSpec(memory_space=space)] * (len(ins) - smem)
     return pl.pallas_call(
         body,
         out_shape=tuple(jax.ShapeDtypeStruct(s, d) for s, d in outs),
         in_specs=specs,
-        out_specs=tuple(pl.BlockSpec(memory_space=pltpu.VMEM) for _ in outs),
+        out_specs=tuple(pl.BlockSpec(memory_space=space) for _ in outs),
         scratch_shapes=list(scratch),
-        compiler_params=pltpu.CompilerParams(vmem_limit_bytes=32 << 20),
+        compiler_params=pltpu.CompilerParams(vmem_limit_bytes=vmem << 20),
         cost_estimate=pl.CostEstimate(flops=flops, bytes_accessed=total, transcendentals=0),
         name=name,
     )(*ins)
 
 
-def compact_kernel(place, sizes, cot_ref, same_ref, other_ref):
+def pack_kernel(qkv_ref, cot_ref, out_ref, sems):
+    copies = []
+    for d in range(F):
+        rows, cols = pl.ds((d % C) * HALF, HALF), pl.ds((d // C) * COLS, COLS)
+        copies.append((qkv_ref.at[:, rows, cols], out_ref.at[d, pl.ds(0, 3)]))
+    for j in range(X):
+        dst = out_ref.at[:, 3 + j // 2, pl.ds((j % 2) * CAP, CAP)]
+        copies.append((cot_ref.at[:, :, pl.ds(j * COLS, COLS)], dst))
+    copies = [pltpu.make_async_copy(src, dst, sems.at[n]) for n, (src, dst) in enumerate(copies)]
+    for c in copies:
+        c.start()
+    for c in copies:
+        c.wait()
+
+
+def compact_kernel(sizes, recv_ref, out_ref):
     shape = (POS, F * CAP)
-    row, col = iota(shape, 0), iota(shape, 1)
-    pos = row ^ (place[CORE] * HALF)
+    pos, col = iota(shape, 0), iota(shape, 1)
     start = jnp.int32(0)
     picked = jnp.full(shape, -1, jnp.int32)
     for j in range(F):
@@ -65,9 +76,12 @@
         picked = jnp.where(inside, slot + start, picked)
         start = start + sizes[0, j]
     hot = (picked == pos).astype(f32).astype(bf)
-    up = dot(hot, cot_ref[...].reshape(F * CAP, DW), NN).astype(bf)
-    same_ref[...] = up[:HALF]
-    other_ref[...] = up[HALF:]
+    for j in range(X):
+        slots = recv_ref[:, 3 + j // 2, (j % 2) * CAP : (j % 2 + 1) * CAP, :]
+        up = dot(hot, slots.reshape(F * CAP, COLS), NN).astype(bf)
+        for d in range(F):
+            r = (d % C) * HALF
+            out_ref[d, :, j * COLS : (j + 1) * COLS] = up[r : r + HALF]
 
 
 def block(ref, i, b, h):
@@ -87,23 +101,15 @@
     mixed_ref[...] = dot(raw_ref[...].reshape(F * HALF, COLS), order_ref[...], NN).astype(bf)
 
 
-def gw_kernel(place, *refs):
-    pieces, (mixed_ref, up_ref, mine_ref, other_ref, sems) = refs[:F], refs[F:]
-    copies = [
-        pltpu.make_async_copy(pieces[k], up_ref.at[place[RANK] ^ k], sems.at[k]) for k in range(F)
-    ]
-    for c in copies:
-        c.start()
-    for c in copies:
-        c.wait()
-    up = up_ref[...].reshape(F * HALF, DW)
-    gw = dot(mixed_ref[...], up, TN)
+def gw_kernel(up_ref, mixed_ref, mine_ref, other_ref):
+    gw = dot(mixed_ref[...], up_ref[...].reshape(F * HALF, DW), TN)
     mine_ref[...] = gw[: COLS // 2]
     other_ref[...] = gw[COLS // 2 :].astype(bf)
 
 
-def score_kernel(qkv_ref, probs_ref, up_ref, w_ref, spot_ref, dm_ref, ds_ref, sums_ref):
-    dm = dot(up_ref[...].reshape(F * HALF, DW), w_ref[...], NT).astype(bf)
+def score_kernel(qkv_ref, probs_ref, up_ref, w0_ref, w1_ref, spot_ref, dm_ref, ds_ref, sums_ref):
+    up = up_ref[...].reshape(F * HALF, DW)
+    dm = jnp.concatenate([dot(up, w[...], NT).astype(bf) for w in (w0_ref, w1_ref)], axis=1)
     dm = dot(dm, spot_ref[...], NN)
     dm_ref[...] = dm.astype(bf).reshape(F, HALF, COLS)
     for h in range(HL):
@@ -143,9 +149,9 @@
     return high, low
 
 
-def join_kernel(mine_ref, other_ref, s0, s1, s2, s3, own_ref, b_ref, m1, m2, m3):
+def join_kernel(mine_ref, other_ref, s0, s1, own_ref, b_ref, m1, m2, m3):
     gw = mine_ref[...] + other_ref[...].astype(f32)
-    high, low = split(tiles((s0[...] + s1[...]) + (s2[...] + s3[...])))
+    high, low = split(tiles(s0[...] + s1[...]))
     own_ref[...] = gw[:48]
     b_ref[...] = high + low
     ride = jnp.concatenate([high, low], axis=0).astype(bf)
@@ -166,14 +172,19 @@
         n[...] = jnp.concatenate([gw[12 * k : 12 * (k + 1)], high, low], axis=0).astype(bf)
 
 
-def zsum_kernel(own_ref, b_ref, n1, n2, n3, first_ref, second_ref, off_ref):
+def zsum_kernel(own_ref, b_ref, n1, n2, n3, keep_ref, send_ref):
     parts = [n[...].astype(f32) for n in (n1, n2, n3)]
     gw = [own_ref[...]] + [x[:12] for x in parts]
     b = [b_ref[...]] + [x[12:14] + x[14:16] for x in parts]
-    gw, flat = ((x[0] + x[1]) + (x[2] + x[3]) for x in (gw, b))
-    pad = jnp.zeros((2, DW), f32)
-    first_ref[...] = jnp.concatenate([gw[:6], pad], axis=0)
-    second_ref[...] = jnp.concatenate([gw[6:], pad], axis=0)
+    gw, b = ((x[0] + x[1]) + (x[2] + x[3]) for x in (gw, b))
+    keep_ref[...] = jnp.concatenate([gw[:6], b], axis=0)
+    send_ref[...] = jnp.concatenate([gw[6:], b], axis=0)
+
+
+def total_kernel(keep_ref, recv_ref, sum_ref, off_ref):
+    total = keep_ref[...] + recv_ref[...]
+    sum_ref[...] = total
+    flat = total[6:]
     sums = jnp.concatenate([flat[:, 128 * a : 128 * (a + 1)] for a in range(12)], axis=0)
     out = jnp.zeros((16, 128), f32)
     head, t = iota((16, 24), 0) % HL, iota((16, 24), 1)
@@ -185,12 +196,12 @@
     off_ref[...] = out
 
 
-def last_kernel(place, a_ref, b_ref, o0, o1, o2, o3, gw_ref, bias_ref):
-    gw_ref[...] = (a_ref[...] + b_ref[...])[:6]
+def last_kernel(place, home_ref, o0, o1, o2, o3, gw_ref, bias_ref):
+    gw_ref[...] = home_ref[:6]
     row = iota((16, 128), 0) // HL
     out = jnp.zeros((16, 128), f32)
     for k, o in enumerate((o0, o1, o2, o3)):
-        out = out + jnp.where(row == ((place[RANK] // C) ^ k), o[...], 0.0)
+        out = out + jnp.where(row == ((place[0]) ^ k), o[...], 0.0)
     bias_ref[...] = out[:12, :15]
 
 
@@ -201,7 +212,19 @@
 def per_device(qkv_time, shard_sizes, bias_time, w_out, cot_out):
     xi, yi, zi = (lax.axis_index(a) for a in ("x", "y", "z"))
     core = lax.axis_index("core")
-    place = jnp.stack([core, yi, zi, xi * C + core]).astype(jnp.int32)
+
+    block5 = ((F, 5, HALF, COLS), bf)
+    (packed,) = call(
+        pack_kernel,
+        "pack",
+        [block5],
+        qkv_time[:, 0, 0],
+        cot_out[0, 0],
+        scratch=[pltpu.SemaphoreType.DMA((F + X,))],
+        space=pltpu.HBM,
+        vmem=56,
+    )
+    recv = lax.all_to_all(packed, SEQ, 0, 0, tiled=True)
 
     there = [
         ((2 * c + z0) * X + x, (z0 * X + x) * X + c)
@@ -211,25 +234,24 @@
     ]
     near = [(a, b ^ X) for a, b in there]
     rows8 = jnp.pad(w_out, ((0, 2), (0, 0)))
+    rows8, _ = lax.optimization_barrier((rows8, packed))
     held = jnp.concatenate([lax.ppermute(rows8, ("z", "x"), p) for p in (there, near)])
     held = jnp.concatenate([held, hop(held, "z", 2, Z)])
-
-    cot = lax.all_to_all(cot_out[0, 0], SEQ, 0, 0, tiled=True)
-    packed = qkv_time[:, 0, 0].reshape(3, C, HALF, X, COLS).transpose(3, 1, 0, 2, 4)
-    qkv = lax.all_to_all(packed.reshape(F, 3, HALF, COLS), SEQ, 0, 0, tiled=True)
-
-    same, other = call(
-        compact_kernel, "compact", [((HALF, DW), bf)] * 2, place, shard_sizes, cot, smem=2, flops=100_000_000
-    )
-    held, same = lax.optimization_barrier((held, same))
     held = jnp.concatenate([held, hop(held, "z", 4, Z)])
-    held = lax.all_gather(held, ("y", "core"), axis=0, tiled=True)
-    pieces = [same] + [hop(other if k & 1 else same, SEQ, k, F) for k in range(1, F)]
+
+    (up,) = call(
+        compact_kernel, "compact", [((F, HALF, DW), bf)], shard_sizes, recv, smem=1, flops=100_000_000
+    )
+    held, up = lax.optimization_barrier((held, up))
+    up = lax.all_to_all(up, SEQ, 0, 0, tiled=True)
+    held = jnp.concatenate([held] + [hop(held, "y", k, Y) for k in range(1, Y)])
+    recv, held = lax.optimization_barrier((recv, held))
+    held2 = hop(held, "core", 1, C)
 
     t, r = iota((512, COLS), 0), iota((512, COLS), 1)
     i, sub = r % 6, r // 6
     rj, ry, rc = (sub // 32) * 4 + (sub // 2) % 4, (sub // 8) % 4, sub % 2
-    spot = ((((ry * C + rc) * Z + (rj ^ zi)) * 8 + i) == t).astype(bf)
+    spot = (((((rc ^ core) * Y + (ry ^ yi)) * Z + (rj ^ zi)) * 8 + i) == t).astype(bf)
 
     local_bias = lax.dynamic_slice(bias_time, (xi * HL, 0), (HL, 15))
     pair = jnp.stack([local_bias[:, 7 - f : 15 - f] for f in range(F)], axis=1)
@@ -244,68 +266,64 @@
         fwd_kernel,
         "attn_fwd",
         [((HL, NB, POS, POS), f32), ((F * HALF, COLS), bf)],
-        qkv,
+        recv,
         bias_m,
         order,
         scratch=[pltpu.VMEM((F, HALF, COLS), bf)],
         flops=250_000_000,
     )
 
-    up, mine, theirs = call(
+    mine, theirs = call(
         gw_kernel,
         "grad_w",
-        [((F, HALF, DW), bf), ((COLS // 2, DW), f32), ((COLS // 2, DW), bf)],
-        place,
-        *pieces,
+        [((COLS // 2, DW), f32), ((COLS // 2, DW), bf)],
+        up,
         mixed,
-        smem=1,
-        hbm=F,
-        scratch=[pltpu.SemaphoreType.DMA((F,))],
         flops=604_000_000,
     )
     theirs = hop(theirs, "core", 1, C)
+    up, theirs = lax.optimization_barrier((up, theirs))
 
     dm, ds, sums = call(
         score_kernel,
         "scores_bwd",
         [((F, HALF, COLS), bf), ((HL, NB, POS, POS), bf), ((F, COLS), f32)],
-        qkv,
+        recv,
         probs,
         up,
         held,
+        held2,
         spot,
         flops=900_000_000,
     )
-    both = lax.ppermute(sums, ("z", "core"), [(i, i ^ 9) for i in range(Z * C)])
-    sums = [sums, hop(sums, "core", 1, C), hop(sums, "z", 4, Z), both]
-    (grads,) = call(
-        grad_kernel, "grads", [((F, 3, HALF, COLS), bf)], qkv, probs, dm, ds, flops=150_000_000
-    )
+    sums2 = hop(sums, "core", 1, C)
 
     wide = ((48, DW + 128), bf)
     own, b, *msgs = call(
-        join_kernel, "join", [((48, DW), f32), ((24, 128), f32), wide, wide, wide], mine, theirs, *sums
+        join_kernel, "join", [((48, DW), f32), ((24, 128), f32), wide, wide, wide], mine, theirs, sums, sums2
     )
     msgs = [hop(m, "y", k, Y) for k, m in enumerate(msgs, 1)]
+    dm, msgs[1], msgs[2] = lax.optimization_barrier((dm, msgs[1], msgs[2]))
+    (grads,) = call(
+        grad_kernel, "grads", [((F, 3, HALF, COLS), bf)], recv, probs, dm, ds, flops=150_000_000
+    )
     part = ((16, DW), bf)
     own, b, *msgs = call(
         ysum_kernel, "ysum", [((12, DW), f32), ((2, DW), f32), part, part, part], own, b, *msgs
     )
     msgs = [hop(m, "z", k, Z) for k, m in enumerate(msgs, 1)]
-    first, second, off = call(
-        zsum_kernel, "zsum", [((8, DW), f32), ((8, DW), f32), ((16, 128), f32)], own, b, *msgs
-    )
-    home = [(a, b) for b, a in there]
-    cross = [((((a // X) ^ 4) * X + a % X), b) for a, b in home]
-    first = lax.ppermute(first, ("z", "x"), home)
-    second = lax.ppermute(second, ("z", "x"), cross)
+    keep, send = call(zsum_kernel, "zsum", [((8, DW), f32)] * 2, own, b, *msgs)
+    total, off = call(
+        total_kernel, "total", [((8, DW), f32), ((16, 128), f32)], keep, hop(send, "z", 4, Z)
+    )
+    home = lax.ppermute(total, ("z", "x"), [(b, a) for a, b in there])
     offs = [off] + [hop(off, "x", k, X) for k in range(1, X)]
 
     back = lax.all_to_all(grads, SEQ, 0, 0, tiled=True).reshape(X, C, 3, HALF, COLS)
     grad_qkv = back.transpose(2, 1, 3, 0, 4).reshape(3, 1, 1, POS, DW)
-    first, grad_qkv = lax.optimization_barrier((first, grad_qkv))
+    home, grad_qkv = lax.optimization_barrier((home, grad_qkv))
     grad_w_out, grad_bias = call(
-        last_kernel, "last", [((6, DW), f32), ((12, 15), f32)], place, first, second, *offs, smem=1
+        last_kernel, "last", [((6, DW), f32), ((12, 15), f32)], xi.reshape(1), home, *offs, smem=1
     )
     return grad_qkv, grad_bias, grad_w_out
 

time: 165 us -> 198 us (1.20)
  Pallas kernels: 15.1 us -> 73.7 us
  between operations: 14.4 us -> 0.86 us
  starting transfers between devices: 67.5 us -> 55.6 us
  other arithmetic: 1.92 us -> 8.75 us
  waiting for transfers between devices: 47.4 us -> 42.6 us
  local copies, waits for them, and re-layouts: 18.2 us -> 15 us
    pallas_call x9 -> x11, Pallas kernels: 15.1 us -> 73.7 us  [call(): pl.pallas_call(body, out_shape=tuple((jax.ShapeDtypeStruct(s, d) for s, d...]
    ppermute x21 -> x18, starting transfers between devices: 35.3 us -> 26.3 us  [hop(): return lax.ppermute(x, axis, [(i, i ^ k) for i in range(n)])]
    unnamed x49 -> x39, local copies, waits for them, and re-layouts: 10.2 us -> 4.44 us
    ppermute x3 -> x1, starting transfers between devices: 9.94 us -> 6.27 us  [per_device(): home = lax.ppermute(total, ('z', 'x'), [(b, a) for a, b in there])]
    ppermute x21 -> x18, waiting for transfers between devices: 40.1 us -> 37 us  [hop(): return lax.ppermute(x, axis, [(i, i ^ k) for i in range(n)])]
    broadcast_in_dim x4, local copies, waits for them, and re-layouts: 3.43 us -> 6.26 us  [per_device(): jnp.where(alike, pair[:, :, None, :, None], f32(-1e+30))]
    concatenate x0 -> x1, other arithmetic: none -> 2.15 us  [per_device(): held = jnp.concatenate([held] + [hop(held, 'y', k, Y) for k in range(1, Y)])]
  transfers between devices with their start and end apart: 30 -> 24, of which waited for: 15 -> 15; matrix products, arithmetic and copies ran while one was open for 6% -> 10% of each run, Pallas kernels for 6% -> 3%
where the time goes in v4:
time: 198 us; the launch traced here: 196 us
  Pallas kernels  73.7 us (37%)
  starting transfers between devices  55.6 us (28%)
  waiting for transfers between devices  42.6 us (22%)
  local copies, waits for them, and re-layouts  15 us (8%)
  other arithmetic  8.75 us (4%)
    pallas_call x11, Pallas kernels, call(): pl.pallas_call(body, out_shape=tuple((jax.ShapeDtypeStruct(s, d) for s, d...  73.7 us
    ppermute x18, waiting for transfers between devices, hop(): return lax.ppermute(x, axis, [(i, i ^ k) for i in range(n)])  37 us
    ppermute x18, starting transfers between devices, hop(): return lax.ppermute(x, axis, [(i, i ^ k) for i in range(n)])  26.3 us
    ppermute x2, starting transfers between devices, per_device(): lax.ppermute(rows8, ('z', 'x'), p)  9.47 us
    ppermute x1, starting transfers between devices, per_device(): home = lax.ppermute(total, ('z', 'x'), [(b, a) for a, b in there])  6.27 us
    broadcast_in_dim x4, local copies, waits for them, and re-layouts, per_device(): jnp.where(alike, pair[:, :, None, :, None], f32(-1e+30))  6.26 us
    all_to_all x1, waiting for transfers between devices, per_device(): recv = lax.all_to_all(packed, SEQ, 0, 0, tiled=True)  5.52 us
    all_to_all x1, starting transfers between devices, per_device(): recv = lax.all_to_all(packed, SEQ, 0, 0, tiled=True)  5.52 us
  transfers between devices with their start and end apart: 24, of which 15 were waited for; matrix products, arithmetic and copies ran while one was open for 10% of the time, Pallas kernels for 3%

profile of v4, /device:TPU:32, one launch (start us, length us, event | category | flops | bytes accessed | tf_op | source)
XLA Modules:
  0.0 196.4 jit_solution(13725442444899236956)
XLA Ops:
  0.6 0.8 pad.4
  1.4 60.8 %pack.1 = bf16[8,5,64,384]{3,2,1,0:T(8,128)(2,1)} custom-call(bf16[3,128,1536]{2,1,0:T(8,128)(2,1)} %bitcast.27, bf16[8,32,1536]{2,1,0:T(8,128)(2,1)} %bitcast.28), custom_call_target="tpu_custom_call" | custom-call | bytes 3932160 | tf_op jit(solution)/shard_map/pack/pallas_call | solution.py:41
  62.2 6.4 %collective-permute-start.1 = (bf16[8,1536]{1,0:T(8,128)(2,1)S(1)}, bf16[8,1536]{1,0:T(8,128)(2,1)S(1)}, u32[]{:S(2)}, u32[]{:S(2)}) collective-permute-start(bf16[8,1536]{1,0:T(8,128)(2,1)S(1)} %pad.4), channel_id=1, source_target_pairs={{0,32},{2,0},{4,96},{6,64},{32,160},{34,128},{36,224},{38,192},{64... | collective-permute-start | bytes 73736 | tf_op jit(solution)/shard_map/ppermute | solution.py:238
  68.5 3.1 %collective-permute-start = (bf16[8,1536]{1,0:T(8,128)(2,1)S(1)}, bf16[8,1536]{1,0:T(8,128)(2,1)S(1)}, u32[]{:S(2)}, u32[]{:S(2)}) collective-permute-start(bf16[8,1536]{1,0:T(8,128)(2,1)S(1)} %pad.4), channel_id=1, source_target_pairs={{0,0},{2,32},{4,64},{6,96},{32,128},{34,160},{36,192},{38,224},{64... | collective-permute-start | bytes 73736 | tf_op jit(solution)/shard_map/ppermute | solution.py:238
  71.7 5.5 %all-to-all-start = ((bf16[8,5,64,384]{3,2,1,0:T(8,128)(2,1)}), bf16[8,5,64,384]{3,2,1,0:T(8,128)(2,1)S(1)}, u32[]{:S(2)}, u32[]{:S(2)}) async-start(bf16[8,5,64,384]{3,2,1,0:T(8,128)(2,1)} %pack.1), calls=%async_computation | async-start | bytes 3932160 | tf_op jit(solution)/shard_map/all_to_all | solution.py:227
  77.2 0.6 iota_divide_fusion
  77.8 0.6 fusion.47
  78.3 0.6 iota_divide_fusion.1
  79.2 0.6 iota_divide_fusion.3
  80.1 0.6 broadcast_add_fusion.1
  80.7 3.2 %collective-permute-start.2 = (bf16[16,1536]{1,0:T(8,128)(2,1)S(1)}, bf16[16,1536]{1,0:T(8,128)(2,1)S(1)}, u32[]{:S(2)}, u32[]{:S(2)}) collective-permute-start(bf16[16,1536]{1,0:T(8,128)(2,1)S(1)} %pad_maximum_fusion.3), channel_id=1, source_target_pairs={{0,64},{32,96},{64,0},{96,32},{128,192},{160,224},{192,128},{224,1... | collective-permute-start | bytes 147464 | tf_op jit(solution)/shard_map/ppermute | solution.py:209
  83.9 0.6 fusion.57
  84.5 1.8 collective-permute-done.2
  86.3 1.1 collective-permute-start.3
  87.4 0.6 fusion.54
  88.0 8.8 %collective-permute-done.3 = bf16[32,1536]{1,0:T(8,128)(2,1)S(1)} collective-permute-done((bf16[32,1536]{1,0:T(8,128)(2,1)S(1)}, bf16[32,1536]{1,0:T(8,128)(2,1)S(1)}, u32[]{:S(2)}, u32[]{:S(2)}) %collective-permute-start.3) | collective-permute-done | bytes 98336 | tf_op jit(solution)/shard_map/ppermute | solution.py:209
  96.8 0.7 pad_maximum_fusion.1
  97.4 5.5 %all-to-all-done.recv_ref.qkv_ref = bf16[8,5,64,384]{3,2,1,0:T(8,128)(2,1)S(1)} async-done(((bf16[8,5,64,384]{3,2,1,0:T(8,128)(2,1)}), bf16[8,5,64,384]{3,2,1,0:T(8,128)(2,1)S(1)}, u32[]{:S(2)}, u32[]{:S(2)}) %all-to-all-start) | async-done | bytes 1966112 | tf_op jit(solution)/shard_map/all_to_all | solution.py:227
  103.0 0.8 compact.1
  103.8 1.2 copy-done.1
  105.0 3.6 %all-to-all-start.1 = ((bf16[8,64,1536]{2,1,0:T(8,128)(2,1)}), bf16[8,64,1536]{2,1,0:T(8,128)(2,1)S(1)}, u32[]{:S(2)}, u32[]{:S(2)}) async-start(bf16[8,64,1536]{2,1,0:T(8,128)(2,1)} %copy-done.1), calls=%async_computation.1 | async-start | bytes 3145728 | tf_op jit(solution)/shard_map/all_to_all | solution.py:246
  108.6 1.6 fusion.46.order_ref
  110.2 3.0 %collective-permute-start.6 = (bf16[64,1536]{1,0:T(8,128)(2,1)}, bf16[64,1536]{1,0:T(8,128)(2,1)}, u32[]{:S(2)}, u32[]{:S(2)}) collective-permute-start(bf16[64,1536]{1,0:T(8,128)(2,1)} %pad_maximum_fusion.1), channel_id=1, source_target_pairs={{0,24},{8,16},{16,8},{24,0},{1,25},{9,17},{17,9},{25,1},{2,26},{10... | collective-permute-start | bytes 589832 | tf_op jit(solution)/shard_map/ppermute | solution.py:209
  113.2 0.6 collective-permute-start.5
  114.3 0.6 constant_dynamic-update-slice_fusion
  114.9 0.7 copy.8
  115.6 1.3 broadcast_in_dim.31
  116.9 2.5 %broadcast_in_dim.32 = f32[3,128,128]{2,1,0:T(8,128)} reshape(f32[3,8,16,8,16]{4,3,2,1,0:T(8,128)} %broadcast_in_dim.31) | data formatting | bytes 393216 | tf_op jit(solution)/shard_map/jit(_where)/broadcast_in_dim | solution.py:259
  119.4 0.7 broadcast_in_dim.28
  120.1 1.7 broadcast_in_dim.29
  121.9 1.3 collective-permute-done.6
  123.2 0.6 collective-permute-done.4
  123.8 2.1 %pad_maximum_fusion.w0_ref = bf16[256,1536]{1,0:T(8,128)(2,1)} fusion(bf16[64,1536]{1,0:T(8,128)(2,1)} %collective-permute-done.6, bf16[64,1536]{1,0:T(8,128)(2,1)} %collective-permute-done.5, bf16[64,1536]{1,0:T(8,128)(2,1)} %collective-permute-done.4, bf16[64,1536]{1,0:T(8,128)(2,1)} %pad_maximum_fusion.1), kind=kLoop, calls=%fused_computation.63 | loop fusion | flops 3145728 | bytes 1572864 | tf_op jit(solution)/shard_map/concatenate | solution.py:247
  126.0 4.3 %attn_fwd.1 = (f32[3,4,128,128]{3,2,1,0:T(8,128)S(1)}, bf16[512,384]{1,0:T(8,128)(2,1)S(1)}) custom-call(bf16[8,5,64,384]{3,2,1,0:T(8,128)(2,1)S(1)} %all-to-all-done.recv_ref.qkv_ref, f32[3,128,128]{2,1,0:T(8,128)S(1)} %broadcast_select_fusion.bias_ref, bf16[384,384]{1,0:T(8,128)(2,1)S(1)} %copy-done.4), custom_call_target="tpu_custom_call" | custom-call | flops 250000000 | bytes 3637248 | tf_op jit(solution)/shard_map/attn_fwd/pallas_call | solution.py:41
  130.4 0.9 copy-done.2
  131.2 0.7 copy-done.6
  132.0 1.1 copy-done.7
  133.1 0.8 grad_w.1
  133.9 0.6 collective-permute-start.7
  134.6 1.5 collective-permute-done.7.other_ref
  136.1 3.1 %scores_bwd.1 = (bf16[8,64,384]{2,1,0:T(8,128)(2,1)S(1)}, bf16[3,4,128,128]{3,2,1,0:T(8,128)(2,1)S(1)}, f32[8,384]{1,0:T(8,128)S(1)}) custom-call(bf16[8,5,64,384]{3,2,1,0:T(8,128)(2,1)S(1)} %all-to-all-done.recv_ref.qkv_ref, f32[3,4,128,128]{3,2,1,0:T(8,128)S(1)} %copy-done.3, bf16[8,64,1536]{2,1,0:T(8,128)(2,1)S(1)} %all-to-all-done.1.up_ref, ...), custom_call_target="tpu_custom_call" | custom-call | flops 900000000 | bytes 7090176 | tf_op jit(solution)/shard_map/scores_bwd/pallas_call | solution.py:41
  139.2 0.5 collective-permute-start.9
  139.7 0.8 collective-permute-done.9.s1
  140.6 3.2 %collective-permute-start.11 = (bf16[48,1664]{1,0:T(8,128)(2,1)S(1)}, bf16[48,1664]{1,0:T(8,128)(2,1)S(1)}, u32[]{:S(2)}, u32[]{:S(2)}) collective-permute-start(bf16[48,1664]{1,0:T(8,128)(2,1)S(1)} %get-tuple-element.54), channel_id=1, source_target_pairs={{0,16},{8,24},{16,0},{24,8},{1,17},{9,25},{17,1},{25,9},{2,18},{10... | collective-permute-start | bytes 479240 | tf_op jit(solution)/shard_map/ppermute | solution.py:209
  143.9 1.1 collective-permute-start.12
  144.9 3.7 %collective-permute-done.11.m2 = bf16[48,1664]{1,0:T(8,128)(2,1)S(1)} collective-permute-done((bf16[48,1664]{1,0:T(8,128)(2,1)S(1)}, bf16[48,1664]{1,0:T(8,128)(2,1)S(1)}, u32[]{:S(2)}, u32[]{:S(2)}) %collective-permute-start.11) | collective-permute-done | bytes 159776 | tf_op jit(solution)/shard_map/ppermute | solution.py:209
  148.7 3.3 %collective-permute-done.12.m3 = bf16[48,1664]{1,0:T(8,128)(2,1)S(1)} collective-permute-done((bf16[48,1664]{1,0:T(8,128)(2,1)S(1)}, bf16[48,1664]{1,0:T(8,128)(2,1)S(1)}, u32[]{:S(2)}, u32[]{:S(2)}) %collective-permute-start.12) | collective-permute-done | bytes 159776 | tf_op jit(solution)/shard_map/ppermute | solution.py:209
  152.0 1.5 grads.1
  153.5 4.5 %all-to-all-start.2 = ((bf16[8,3,64,384]{3,2,1,0:T(8,128)(2,1)}), bf16[8,3,64,384]{3,2,1,0:T(8,128)(2,1)S(1)}, u32[]{:S(2)}, u32[]{:S(2)}) async-start(bf16[8,3,64,384]{3,2,1,0:T(8,128)(2,1)} %grads.1), calls=%async_computation.2 | async-start | bytes 2359296 | tf_op jit(solution)/shard_map/all_to_all | solution.py:322
  158.0 1.5 collective-permute-start.10
  159.5 5.0 %collective-permute-done.10.m1 = bf16[48,1664]{1,0:T(8,128)(2,1)S(1)} collective-permute-done((bf16[48,1664]{1,0:T(8,128)(2,1)S(1)}, bf16[48,1664]{1,0:T(8,128)(2,1)S(1)}, u32[]{:S(2)}, u32[]{:S(2)}) %collective-permute-start.10) | collective-permute-done | bytes 159776 | tf_op jit(solution)/shard_map/ppermute | solution.py:209
  164.9 3.0 %collective-permute-start.14 = (bf16[16,1536]{1,0:T(8,128)(2,1)S(1)}, bf16[16,1536]{1,0:T(8,128)(2,1)S(1)}, u32[]{:S(2)}, u32[]{:S(2)}) collective-permute-start(bf16[16,1536]{1,0:T(8,128)(2,1)S(1)} %get-tuple-element.61), channel_id=1, source_target_pairs={{0,64},{32,96},{64,0},{96,32},{128,192},{160,224},{192,128},{224,1... | collective-permute-start | bytes 147464 | tf_op jit(solution)/shard_map/ppermute | solution.py:209
  167.9 0.5 collective-permute-start.15
  168.8 1.7 collective-permute-done.14.n2
  170.5 1.5 collective-permute-done.15.n3
  172.1 2.6 %collective-permute-start.16 = (f32[8,1536]{1,0:T(8,128)S(1)}, f32[8,1536]{1,0:T(8,128)S(1)}, u32[]{:S(2)}, u32[]{:S(2)}) collective-permute-start(f32[8,1536]{1,0:T(8,128)S(1)} %get-tuple-element.64), channel_id=1, source_target_pairs={{0,128},{32,160},{64,192},{96,224},{128,0},{160,32},{192,64},{224,... | collective-permute-start | bytes 147464 | tf_op jit(solution)/shard_map/ppermute | solution.py:209
  174.6 6.0 %collective-permute-done.16.recv_ref = f32[8,1536]{1,0:T(8,128)S(1)} collective-permute-done((f32[8,1536]{1,0:T(8,128)S(1)}, f32[8,1536]{1,0:T(8,128)S(1)}, u32[]{:S(2)}, u32[]{:S(2)}) %collective-permute-start.16) | collective-permute-done | bytes 49184 | tf_op jit(solution)/shard_map/ppermute | solution.py:209
  180.6 1.4 total.1
  182.1 6.3 %collective-permute-start.17 = (f32[8,1536]{1,0:T(8,128)S(1)}, f32[8,1536]{1,0:T(8,128)S(1)}, u32[]{:S(2)}, u32[]{:S(2)}) collective-permute-start(f32[8,1536]{1,0:T(8,128)S(1)} %get-tuple-element.65), channel_id=1, source_target_pairs={{0,0},{32,2},{64,4},{96,6},{128,32},{160,34},{192,36},{224,38},{2,... | collective-permute-start | bytes 147464 | tf_op jit(solution)/shard_map/ppermute | solution.py:319
  188.4 2.5 %collective-permute-start.19 = (f32[16,128]{1,0:T(8,128)S(1)}, f32[16,128]{1,0:T(8,128)S(1)}, u32[]{:S(2)}, u32[]{:S(2)}) collective-permute-start(f32[16,128]{1,0:T(8,128)S(1)} %get-tuple-element.70.o0), channel_id=1, source_target_pairs={{0,4},{2,6},{4,0},{6,2},{1,5},{3,7},{5,1},{7,3},{8,12},{10,14},{12... | collective-permute-start | bytes 24584 | tf_op jit(solution)/shard_map/ppermute | solution.py:209
  190.9 2.2 %collective-permute-start.20 = (f32[16,128]{1,0:T(8,128)S(1)}, f32[16,128]{1,0:T(8,128)S(1)}, u32[]{:S(2)}, u32[]{:S(2)}) collective-permute-start(f32[16,128]{1,0:T(8,128)S(1)} %get-tuple-element.70.o0), channel_id=1, source_target_pairs={{0,6},{2,4},{4,2},{6,0},{1,7},{3,5},{5,3},{7,1},{8,14},{10,12},{12... | collective-permute-start | bytes 24584 | tf_op jit(solution)/shard_map/ppermute | solution.py:209
  193.1 0.9 copy.9
  194.1 1.3 reshape.27
  195.8 0.6 last.1
  (60 shorter events, 2.8 us)
Async XLA Ops:
  0.6 78.3 %copy-start = (f32[12,15]{1,0:T(8,128)S(1)}, f32[12,15]{1,0:T(8,128)}, u32[]{:S(2)}) copy-start(f32[12,15]{1,0:T(8,128)} %param.7) | copy-start | bytes 2164
  62.2 40.8 %copy-start.5 = (s32[1,8]{1,0:T(1,128)S(1)}, s32[1,8]{1,0:T(1,128)}, u32[]{:S(2)}) copy-start(s32[1,8]{1,0:T(1,128)} %sizes.1) | copy-start | bytes 100
  62.2 18.5 %collective-permute-start.1 = (bf16[8,1536]{1,0:T(8,128)(2,1)S(1)}, bf16[8,1536]{1,0:T(8,128)(2,1)S(1)}, u32[]{:S(2)}, u32[]{:S(2)}) collective-permute-start(bf16[8,1536]{1,0:T(8,128)(2,1)S(1)} %pad.4), channel_id=1, source_target_pairs={{0,32},{2,0},{4,96},{6,64},{32,160},{34,128},{36,224},{38,192},{64... | collective-permute-start | bytes 73736 | tf_op jit(solution)/shard_map/ppermute | solution.py:238
  68.5 12.1 %collective-permute-start = (bf16[8,1536]{1,0:T(8,128)(2,1)S(1)}, bf16[8,1536]{1,0:T(8,128)(2,1)S(1)}, u32[]{:S(2)}, u32[]{:S(2)}) collective-permute-start(bf16[8,1536]{1,0:T(8,128)(2,1)S(1)} %pad.4), channel_id=1, source_target_pairs={{0,0},{2,32},{4,64},{6,96},{32,128},{34,160},{36,192},{38,224},{64... | collective-permute-start | bytes 73736 | tf_op jit(solution)/shard_map/ppermute | solution.py:238
  71.7 31.3 %all-to-all-start = ((bf16[8,5,64,384]{3,2,1,0:T(8,128)(2,1)}), bf16[8,5,64,384]{3,2,1,0:T(8,128)(2,1)S(1)}, u32[]{:S(2)}, u32[]{:S(2)}) async-start(bf16[8,5,64,384]{3,2,1,0:T(8,128)(2,1)} %pack.1), calls=%async_computation | async-start | bytes 3932160 | tf_op jit(solution)/shard_map/all_to_all | solution.py:227
  80.1 0.6 copy-start.10
  80.7 5.6 %collective-permute-start.2 = (bf16[16,1536]{1,0:T(8,128)(2,1)S(1)}, bf16[16,1536]{1,0:T(8,128)(2,1)S(1)}, u32[]{:S(2)}, u32[]{:S(2)}) collective-permute-start(bf16[16,1536]{1,0:T(8,128)(2,1)S(1)} %pad_maximum_fusion.3), channel_id=1, source_target_pairs={{0,64},{32,96},{64,0},{96,32},{128,192},{160,224},{192,128},{224,1... | collective-permute-start | bytes 147464 | tf_op jit(solution)/shard_map/ppermute | solution.py:209
  86.3 10.5 %collective-permute-start.3 = (bf16[32,1536]{1,0:T(8,128)(2,1)S(1)}, bf16[32,1536]{1,0:T(8,128)(2,1)S(1)}, u32[]{:S(2)}, u32[]{:S(2)}) collective-permute-start(bf16[32,1536]{1,0:T(8,128)(2,1)S(1)} %pad_maximum_fusion.2), channel_id=1, source_target_pairs={{0,128},{32,160},{64,192},{96,224},{128,0},{160,32},{192,64},{224,... | collective-permute-start | bytes 294920 | tf_op jit(solution)/shard_map/ppermute | solution.py:209
  103.8 1.2 copy-start.1
  105.0 27.0 %all-to-all-start.1 = ((bf16[8,64,1536]{2,1,0:T(8,128)(2,1)}), bf16[8,64,1536]{2,1,0:T(8,128)(2,1)S(1)}, u32[]{:S(2)}, u32[]{:S(2)}) async-start(bf16[8,64,1536]{2,1,0:T(8,128)(2,1)} %copy-done.1), calls=%async_computation.1 | async-start | bytes 3145728 | tf_op jit(solution)/shard_map/all_to_all | solution.py:246
  110.2 13.0 %collective-permute-start.6 = (bf16[64,1536]{1,0:T(8,128)(2,1)}, bf16[64,1536]{1,0:T(8,128)(2,1)}, u32[]{:S(2)}, u32[]{:S(2)}) collective-permute-start(bf16[64,1536]{1,0:T(8,128)(2,1)} %pad_maximum_fusion.1), channel_id=1, source_target_pairs={{0,24},{8,16},{16,8},{24,0},{1,25},{9,17},{17,9},{25,1},{2,26},{10... | collective-permute-start | bytes 589832 | tf_op jit(solution)/shard_map/ppermute | solution.py:209
  113.2 10.0 %collective-permute-start.5 = (bf16[64,1536]{1,0:T(8,128)(2,1)}, bf16[64,1536]{1,0:T(8,128)(2,1)}, u32[]{:S(2)}, u32[]{:S(2)}) collective-permute-start(bf16[64,1536]{1,0:T(8,128)(2,1)} %pad_maximum_fusion.1), channel_id=1, source_target_pairs={{0,16},{8,24},{16,0},{24,8},{1,17},{9,25},{17,1},{25,9},{2,18},{10... | collective-permute-start | bytes 589832 | tf_op jit(solution)/shard_map/ppermute | solution.py:209
  113.8 10.0 %collective-permute-start.4 = (bf16[64,1536]{1,0:T(8,128)(2,1)}, bf16[64,1536]{1,0:T(8,128)(2,1)}, u32[]{:S(2)}, u32[]{:S(2)}) collective-permute-start(bf16[64,1536]{1,0:T(8,128)(2,1)} %pad_maximum_fusion.1), channel_id=1, source_target_pairs={{0,8},{8,0},{16,24},{24,16},{1,9},{9,1},{17,25},{25,17},{2,10},{10... | collective-permute-start | bytes 589832 | tf_op jit(solution)/shard_map/ppermute | solution.py:209
  121.8 4.1 %copy-start.8 = (f32[3,128,128]{2,1,0:T(8,128)S(1)}, f32[3,128,128]{2,1,0:T(8,128)}, u32[]{:S(2)}) copy-start(f32[3,128,128]{2,1,0:T(8,128)} %broadcast_in_dim.32) | copy-start | bytes 589828
  121.8 4.1 %copy-start.9 = (pred[128,128]{1,0:T(8,128)(4,1)S(1)}, pred[128,128]{1,0:T(8,128)(4,1)}, u32[]{:S(2)}) copy-start(pred[128,128]{1,0:T(8,128)(4,1)} %broadcast_in_dim.29) | copy-start | bytes 49156
  121.8 4.2 %copy-start.4 = (bf16[384,384]{1,0:T(8,128)(2,1)S(1)}, bf16[384,384]{1,0:T(8,128)(2,1)}, u32[]{:S(2)}) copy-start(bf16[384,384]{1,0:T(8,128)(2,1)} %fusion.46.order_ref) | copy-start | bytes 884740
  126.0 10.1 %collective-permute-start.8 = (bf16[256,1536]{1,0:T(8,128)(2,1)}, bf16[256,1536]{1,0:T(8,128)(2,1)}, u32[]{:S(2)}, u32[]{:S(2)}) collective-permute-start(bf16[256,1536]{1,0:T(8,128)(2,1)} %pad_maximum_fusion.w0_ref), channel_id=1, source_target_pairs={{0,1},{1,0},{2,3},{3,2},{4,5},{5,4},{6,7},{7,6},{8,9},{9,8},{10,11... | collective-permute-start | bytes 2359304 | tf_op jit(solution)/shard_map/ppermute | solution.py:209
  126.0 8.5 %copy-start.11 = (s32[384]{0:T(512)S(1)}, s32[384]{0:T(512)}, u32[]{:S(2)}) copy-start(s32[384]{0:T(512)} %get-tuple-element.74) | copy-start | bytes 4612
  130.4 0.9 copy-start.2
  131.2 0.7 copy-start.6
  132.0 4.1 %copy-start.3 = (f32[3,4,128,128]{3,2,1,0:T(8,128)S(1)}, f32[3,4,128,128]{3,2,1,0:T(8,128)}, u32[]{:S(2)}) copy-start(f32[3,4,128,128]{3,2,1,0:T(8,128)} %copy-done.2) | copy-start | bytes 2359300
  132.0 1.1 copy-start.7
  133.1 1.4 copy-start.12
  133.1 1.4 copy-start.13
  133.1 1.4 copy-start.14
  133.1 1.4 copy-start.15
  133.9 2.2 %collective-permute-start.7 = (bf16[192,1536]{1,0:T(8,128)(2,1)S(1)}, bf16[192,1536]{1,0:T(8,128)(2,1)S(1)}, u32[]{:S(2)}, u32[]{:S(2)}) collective-permute-start(bf16[192,1536]{1,0:T(8,128)(2,1)S(1)} %get-tuple-element.44), channel_id=1, source_target_pairs={{0,1},{1,0},{2,3},{3,2},{4,5},{5,4},{6,7},{7,6},{8,9},{9,8},{10,11... | collective-permute-start | bytes 1769480 | tf_op jit(solution)/shard_map/ppermute | solution.py:209
  139.2 1.3 collective-permute-start.9
  140.6 8.0 %collective-permute-start.11 = (bf16[48,1664]{1,0:T(8,128)(2,1)S(1)}, bf16[48,1664]{1,0:T(8,128)(2,1)S(1)}, u32[]{:S(2)}, u32[]{:S(2)}) collective-permute-start(bf16[48,1664]{1,0:T(8,128)(2,1)S(1)} %get-tuple-element.54), channel_id=1, source_target_pairs={{0,16},{8,24},{16,0},{24,8},{1,17},{9,25},{17,1},{25,9},{2,18},{10... | collective-permute-start | bytes 479240 | tf_op jit(solution)/shard_map/ppermute | solution.py:209
  143.9 8.1 %collective-permute-start.12 = (bf16[48,1664]{1,0:T(8,128)(2,1)S(1)}, bf16[48,1664]{1,0:T(8,128)(2,1)S(1)}, u32[]{:S(2)}, u32[]{:S(2)}) collective-permute-start(bf16[48,1664]{1,0:T(8,128)(2,1)S(1)} %get-tuple-element.55), channel_id=1, source_target_pairs={{0,24},{8,16},{16,8},{24,0},{1,25},{9,17},{17,9},{25,1},{2,26},{10... | collective-permute-start | bytes 479240 | tf_op jit(solution)/shard_map/ppermute | solution.py:209
  153.5 39.6 %all-to-all-start.2 = ((bf16[8,3,64,384]{3,2,1,0:T(8,128)(2,1)}), bf16[8,3,64,384]{3,2,1,0:T(8,128)(2,1)S(1)}, u32[]{:S(2)}, u32[]{:S(2)}) async-start(bf16[8,3,64,384]{3,2,1,0:T(8,128)(2,1)} %grads.1), calls=%async_computation.2 | async-start | bytes 2359296 | tf_op jit(solution)/shard_map/all_to_all | solution.py:322
  158.0 6.5 %collective-permute-start.10 = (bf16[48,1664]{1,0:T(8,128)(2,1)S(1)}, bf16[48,1664]{1,0:T(8,128)(2,1)S(1)}, u32[]{:S(2)}, u32[]{:S(2)}) collective-permute-start(bf16[48,1664]{1,0:T(8,128)(2,1)S(1)} %get-tuple-element.52), channel_id=1, source_target_pairs={{0,8},{8,0},{16,24},{24,16},{1,9},{9,1},{17,25},{25,17},{2,10},{10... | collective-permute-start | bytes 479240 | tf_op jit(solution)/shard_map/ppermute | solution.py:209
  164.6 4.2 %collective-permute-start.13 = (bf16[16,1536]{1,0:T(8,128)(2,1)S(1)}, bf16[16,1536]{1,0:T(8,128)(2,1)S(1)}, u32[]{:S(2)}, u32[]{:S(2)}) collective-permute-start(bf16[16,1536]{1,0:T(8,128)(2,1)S(1)} %get-tuple-element.60), channel_id=1, source_target_pairs={{0,32},{32,0},{64,96},{96,64},{128,160},{160,128},{192,224},{224,1... | collective-permute-start | bytes 147464 | tf_op jit(solution)/shard_map/ppermute | solution.py:209
  164.9 5.6 %collective-permute-start.14 = (bf16[16,1536]{1,0:T(8,128)(2,1)S(1)}, bf16[16,1536]{1,0:T(8,128)(2,1)S(1)}, u32[]{:S(2)}, u32[]{:S(2)}) collective-permute-start(bf16[16,1536]{1,0:T(8,128)(2,1)S(1)} %get-tuple-element.61), channel_id=1, source_target_pairs={{0,64},{32,96},{64,0},{96,32},{128,192},{160,224},{192,128},{224,1... | collective-permute-start | bytes 147464 | tf_op jit(solution)/shard_map/ppermute | solution.py:209
  167.9 4.1 %collective-permute-start.15 = (bf16[16,1536]{1,0:T(8,128)(2,1)S(1)}, bf16[16,1536]{1,0:T(8,128)(2,1)S(1)}, u32[]{:S(2)}, u32[]{:S(2)}) collective-permute-start(bf16[16,1536]{1,0:T(8,128)(2,1)S(1)} %get-tuple-element.62), channel_id=1, source_target_pairs={{0,96},{32,64},{64,32},{96,0},{128,224},{160,192},{192,160},{224,1... | collective-permute-start | bytes 147464 | tf_op jit(solution)/shard_map/ppermute | solution.py:209
  172.1 8.6 %collective-permute-start.16 = (f32[8,1536]{1,0:T(8,128)S(1)}, f32[8,1536]{1,0:T(8,128)S(1)}, u32[]{:S(2)}, u32[]{:S(2)}) collective-permute-start(f32[8,1536]{1,0:T(8,128)S(1)} %get-tuple-element.64), channel_id=1, source_target_pairs={{0,128},{32,160},{64,192},{96,224},{128,0},{160,32},{192,64},{224,... | collective-permute-start | bytes 147464 | tf_op jit(solution)/shard_map/ppermute | solution.py:209
  182.1 13.3 %collective-permute-start.17 = (f32[8,1536]{1,0:T(8,128)S(1)}, f32[8,1536]{1,0:T(8,128)S(1)}, u32[]{:S(2)}, u32[]{:S(2)}) collective-permute-start(f32[8,1536]{1,0:T(8,128)S(1)} %get-tuple-element.65), channel_id=1, source_target_pairs={{0,0},{32,2},{64,4},{96,6},{128,32},{160,34},{192,36},{224,38},{2,... | collective-permute-start | bytes 147464 | tf_op jit(solution)/shard_map/ppermute | solution.py:319
  188.3 7.0 %collective-permute-start.18 = (f32[16,128]{1,0:T(8,128)S(1)}, f32[16,128]{1,0:T(8,128)S(1)}, u32[]{:S(2)}, u32[]{:S(2)}) collective-permute-start(f32[16,128]{1,0:T(8,128)S(1)} %get-tuple-element.70.o0), channel_id=1, source_target_pairs={{0,2},{2,0},{4,6},{6,4},{1,3},{3,1},{5,7},{7,5},{8,10},{10,8},{12,... | collective-permute-start | bytes 24584 | tf_op jit(solution)/shard_map/ppermute | solution.py:209
  188.4 6.9 %collective-permute-start.19 = (f32[16,128]{1,0:T(8,128)S(1)}, f32[16,128]{1,0:T(8,128)S(1)}, u32[]{:S(2)}, u32[]{:S(2)}) collective-permute-start(f32[16,128]{1,0:T(8,128)S(1)} %get-tuple-element.70.o0), channel_id=1, source_target_pairs={{0,4},{2,6},{4,0},{6,2},{1,5},{3,7},{5,1},{7,3},{8,12},{10,14},{12... | collective-permute-start | bytes 24584 | tf_op jit(solution)/shard_map/ppermute | solution.py:209
  190.9 4.9 %collective-permute-start.20 = (f32[16,128]{1,0:T(8,128)S(1)}, f32[16,128]{1,0:T(8,128)S(1)}, u32[]{:S(2)}, u32[]{:S(2)}) collective-permute-start(f32[16,128]{1,0:T(8,128)S(1)} %get-tuple-element.70.o0), channel_id=1, source_target_pairs={{0,6},{2,4},{4,2},{6,0},{1,7},{3,5},{5,3},{7,1},{8,14},{10,12},{12... | collective-permute-start | bytes 24584 | tf_op jit(solution)/shard_map/ppermute | solution.py:209

commit v5 on v4

v5 whole, which is shorter than its diff:
```python
import math

import jax
import jax.numpy as jnp
import numpy as np
from jax import lax
from jax.experimental import pallas as pl
from jax.experimental.pallas import tpu as pltpu
from jax.sharding import Mesh, PartitionSpec as P

Z, Y, X, C = 8, 4, 4, 2
SEQ = ("x", "core")
F = 8
POS = 128
HALF = 64
NB = 4
HL = 3
HD = 128
COLS = HL * HD
DW = 1536
CAP = 32
FACTOR = 1.0 / math.sqrt(HD)
NN = (((1,), (0,)), ((), ()))
NT = (((1,), (1,)), ((), ()))
TN = (((0,), (0,)), ((), ()))
bf, f32 = jnp.bfloat16, jnp.float32
CORE, YI, ZI, XI, RANK = range(5)

ROW = np.arange(COLS)
ROWS_OF = np.zeros((8, COLS), np.int32)
ROWS_OF[0] = ROW // 6 % 2
ROWS_OF[1] = ROW // 48 % 4
ROWS_OF[2] = ROW // 192 * 4 + ROW // 12 % 4
ROWS_OF[3] = ROW % 6
LEAVE = np.zeros((8, COLS), np.int32)
LEAVE[0] = ROW // 192
LEAVE[1] = (((ROW % 48 // 24) * 4 + ROW // 48 % 4) * 8 + ROW % 24 // 6 * 2) * 6 + ROW % 6


def dot(a, b, dims, **kw):
    return lax.dot_general(a, b, dims, preferred_element_type=f32, **kw)


def iota(shape, dim):
    return lax.broadcasted_iota(jnp.int32, shape, dim)


def call(body, name, outs, *ins, smem=0, scratch=(), flops=0, space=pltpu.VMEM, vmem=16):
    total = sum(math.prod(s) * jnp.dtype(d).itemsize for s, d in outs)
    total += sum(a.size * a.dtype.itemsize for a in ins)
    specs = [pl.BlockSpec(memory_space=pltpu.SMEM)] * smem
    specs += [pl.BlockSpec(memory_space=space)] * (len(ins) - smem)
    return pl.pallas_call(
        body,
        out_shape=tuple(jax.ShapeDtypeStruct(s, d) for s, d in outs),
        in_specs=specs,
        out_specs=tuple(pl.BlockSpec(memory_space=space) for _ in outs),
        scratch_shapes=list(scratch),
        compiler_params=pltpu.CompilerParams(vmem_limit_bytes=vmem << 20),
        cost_estimate=pl.CostEstimate(flops=flops, bytes_accessed=total, transcendentals=0),
        name=name,
    )(*ins)


def pack_kernel(qkv_ref, cot_ref, out_ref):
    for d in range(F):
        r, c = d % C * HALF, d // C * COLS
        out_ref[d, :3] = qkv_ref[:, r : r + HALF, c : c + COLS]
    for j in range(X):
        r = j % 2 * CAP
        out_ref[:, 3 + j // 2, r : r + CAP, :] = cot_ref[:, :, j * COLS : (j + 1) * COLS]


def compact_kernel(sizes, recv_ref, out_ref):
    shape = (POS, F * CAP)
    pos, col = iota(shape, 0), iota(shape, 1)
    start = jnp.int32(0)
    picked = jnp.full(shape, -1, jnp.int32)
    for j in range(F):
        slot = col - j * CAP
        inside = (slot >= 0) & (slot < sizes[0, j])
        picked = jnp.where(inside, slot + start, picked)
        start = start + sizes[0, j]
    hot = (picked == pos).astype(f32).astype(bf)
    for j in range(X):
        slots = recv_ref[:, 3 + j // 2, (j % 2) * CAP : (j % 2 + 1) * CAP, :]
        up = dot(hot, slots.reshape(F * CAP, COLS), NN).astype(bf)
        for d in range(F):
            r = (d % C) * HALF
            out_ref[d, :, j * COLS : (j + 1) * COLS] = up[r : r + HALF]


def block(ref, i, b, h):
    return ref[:, i, b * 16 : (b + 1) * 16, h * HD : (h + 1) * HD].reshape(POS, HD)


def fwd_kernel(place, bias, leave_ref, qkv_ref, probs_ref, mixed_ref, raw_ref):
    row, col = iota((POS, POS), 0), iota((POS, POS), 1)
    alike = (row & 15) == (col & 15)
    offset = (col >> 4) - (row >> 4) + 7
    for h in range(HL):
        pair = jnp.full((POS, POS), -1e30, f32)
        for o in range(15):
            pair = jnp.where(alike & (offset == o), bias[place[XI] * HL + h, o], pair)
        for b in range(NB):
            q, k, v = (block(qkv_ref, i, b, h) for i in range(3))
            s = dot(q, k, NT) * FACTOR + pair
            e = jnp.exp(s - jnp.max(s, axis=-1, keepdims=True))
            p = e / jnp.sum(e, axis=-1, keepdims=True)
            probs_ref[h, b] = p
            m = dot(p.astype(bf), v, NN).astype(bf).reshape(F, 16, HD)
            raw_ref[:, b * 16 : (b + 1) * 16, h * HD : (h + 1) * HD] = m
    source = leave_ref[1:2] + (leave_ref[0:1] ^ place[CORE]) * 6
    order = (iota((COLS, COLS), 0) == source).astype(f32).astype(bf)
    mixed_ref[...] = dot(raw_ref[...].reshape(F * HALF, COLS), order, NN).astype(bf)


def gw_kernel(up_ref, mixed_ref, mine_ref, other_ref):
    gw = dot(mixed_ref[...], up_ref[...].reshape(F * HALF, DW), TN)
    mine_ref[...] = gw[: COLS // 2]
    other_ref[...] = gw[COLS // 2 :].astype(bf)


def score_kernel(place, rows_ref, qkv_ref, probs_ref, up_ref, w0_ref, w1_ref, dm_ref, ds_ref, sums_ref):
    up = up_ref[...].reshape(F * HALF, DW)
    dm = jnp.concatenate([dot(up, w[...], NT).astype(bf) for w in (w0_ref, w1_ref)], axis=1)
    c, y, j = (rows_ref[n : n + 1] ^ place[n] for n in (CORE, YI, ZI))
    spot = ((c * Y + y) * Z + j) * 8 + rows_ref[3:4]
    spot = (iota((512, COLS), 0) == spot).astype(f32).astype(bf)
    dm = dot(dm, spot, NN)
    dm_ref[...] = dm.astype(bf).reshape(F, HALF, COLS)
    for h in range(HL):
        cols = slice(h * HD, (h + 1) * HD)
        total = jnp.zeros((F, POS), f32)
        for b in range(NB):
            d = dm_ref[:, b * 16 : (b + 1) * 16, cols].reshape(POS, HD)
            p = probs_ref[h, b]
            g = dot(d, block(qkv_ref, 2, b, h), NT)
            ds = p * (g - jnp.sum(p * g, axis=-1, keepdims=True))
            total = total + jnp.sum(ds.reshape(F, 16, POS), axis=1)
            ds_ref[h, b] = ds.astype(bf)
        sums_ref[:, cols] = total


def grad_kernel(place, qkv_ref, probs_ref, dm_ref, ds_ref, *refs):
    pieces, nat_ref = refs[:F], refs[F]
    for h in range(HL):
        cols = slice(h * HD, (h + 1) * HD)
        for b in range(NB):
            rows = slice(b * 16, (b + 1) * 16)
            d = dm_ref[:, rows, cols].reshape(POS, HD)
            low = ds_ref[h, b]
            gq = dot(low, block(qkv_ref, 1, b, h), NN) * FACTOR
            gk = dot(low, block(qkv_ref, 0, b, h), TN) * FACTOR
            gv = dot(probs_ref[h, b].astype(bf), d, TN)
            for i, val in enumerate((gq, gk, gv)):
                nat_ref[:, i, rows, cols] = val.astype(bf).reshape(F, 16, HD)
    for k in range(F):
        pieces[k][...] = nat_ref[place[RANK] ^ k]


def unpack_kernel(place, *refs):
    pieces, out_ref, nat_ref = refs[:F], refs[F], refs[F + 1]
    for k in range(F):
        nat_ref[place[RANK] ^ k] = pieces[k][...]
    for d in range(F):
        r, c = d % C * HALF, d // C * COLS
        out_ref[:, r : r + HALF, c : c + COLS] = nat_ref[d]


def split(b):
    high = b.astype(bf).astype(f32)
    low = (b - high).astype(bf).astype(f32)
    return high, low


def join_kernel(mine_ref, other_ref, s0, s1, out_ref):
    gw = mine_ref[...] + other_ref[...].astype(f32)
    hot = ((iota((COLS, 128), 0) >> 4) == iota((COLS, 128), 1)).astype(f32)
    b = dot(s0[...] + s1[...], hot, NN, precision=lax.Precision.HIGHEST)
    high, low = split(b)
    ride = jnp.concatenate([high, low, jnp.zeros((32, 128), f32)], axis=0).astype(bf)
    for y in range(Y):
        out_ref[y, :, :DW] = gw[48 * y : 48 * (y + 1)].astype(bf)
        out_ref[y, :, DW:] = ride


def ysum_kernel(in_ref, out_ref):
    gw = jnp.sum(in_ref[:, :, :DW].astype(f32), axis=0)
    ride = jnp.sum(in_ref[:, :, DW:].astype(f32), axis=0)
    high, low = split(ride[:8] + ride[8:16])
    pad = jnp.zeros((1, DW - F * 128), f32)
    flat = [jnp.concatenate([x[f : f + 1] for f in range(F)] + [pad], axis=1) for x in (high, low)]
    for j in range(Z):
        out_ref[j] = jnp.concatenate([gw[6 * j : 6 * j + 6]] + flat, axis=0).astype(bf)


def total_kernel(in_ref, sum_ref, off_ref):
    total = jnp.sum(in_ref[...].astype(f32), axis=0)
    sum_ref[...] = total
    flat = total[6:7] + total[7:8]
    head, lane = iota((16, 128), 0) % HL, iota((16, 128), 1)
    g, o = iota((128, 128), 0) & 7, iota((128, 128), 1)
    out = jnp.zeros((16, 128), f32)
    for f in range(F):
        row = jnp.where((lane >> 3) == head, flat[:, 128 * f : 128 * (f + 1)], 0.0)
        out = out + dot(row, (g - f + 7 == o).astype(f32), NN, precision=lax.Precision.HIGHEST)
    off_ref[...] = out


def last_kernel(place, home_ref, o0, o1, o2, o3, gw_ref, bias_ref):
    gw_ref[...] = home_ref[:6]
    row = iota((16, 128), 0) // HL
    out = jnp.zeros((16, 128), f32)
    for k, o in enumerate((o0, o1, o2, o3)):
        out = out + jnp.where(row == (place[XI] ^ k), o[...], 0.0)
    bias_ref[...] = out[:12, :15]


def hop(x, axis, k, n):
    return lax.ppermute(x, axis, [(i, i ^ k) for i in range(n)])


def per_device(qkv_time, shard_sizes, bias_time, w_out, cot_out):
    xi, yi, zi, core = (lax.axis_index(a) for a in ("x", "y", "z", "core"))
    place = jnp.stack([core, yi, zi, xi, xi * C + core]).astype(jnp.int32)

    block5 = ((F, 5, HALF, COLS), bf)
    (packed,) = call(
        pack_kernel,
        "pack",
        [block5],
        qkv_time[:, 0, 0],
        cot_out[0, 0],
    )
    recv = lax.all_to_all(packed, SEQ, 0, 0, tiled=True)

    there = [
        ((2 * c + z0) * X + x, (z0 * X + x) * X + c)
        for c in range(X)
        for z0 in range(2)
        for x in range(X)
    ]
    near = [(a, b ^ X) for a, b in there]
    rows8 = jnp.pad(w_out, ((0, 2), (0, 0)))
    rows8, _ = lax.optimization_barrier((rows8, packed))
    held = jnp.concatenate([lax.ppermute(rows8, ("z", "x"), p) for p in (there, near)])
    held = jnp.concatenate([held, hop(held, "z", 2, Z)])
    held = jnp.concatenate([held, hop(held, "z", 4, Z)])

    (up,) = call(
        compact_kernel, "compact", [((F, HALF, DW), bf)], shard_sizes, recv, smem=1, flops=100_000_000
    )
    held, up = lax.optimization_barrier((held, up))
    up = lax.all_to_all(up, SEQ, 0, 0, tiled=True)
    held = jnp.concatenate([held] + [hop(held, "y", k, Y) for k in range(1, Y)])
    recv, held = lax.optimization_barrier((recv, held))
    held2 = hop(held, "core", 1, C)

    probs, mixed = call(
        fwd_kernel,
        "attn_fwd",
        [((HL, NB, POS, POS), f32), ((F * HALF, COLS), bf)],
        place,
        bias_time,
        LEAVE,
        recv,
        smem=2,
        scratch=[pltpu.VMEM((F, HALF, COLS), bf)],
        flops=250_000_000,
    )

    mine, theirs = call(
        gw_kernel,
        "grad_w",
        [((COLS // 2, DW), f32), ((COLS // 2, DW), bf)],
        up,
        mixed,
        flops=604_000_000,
    )
    theirs = hop(theirs, "core", 1, C)
    up, theirs = lax.optimization_barrier((up, theirs))

    dm, ds, sums = call(
        score_kernel,
        "scores_bwd",
        [((F, HALF, COLS), bf), ((HL, NB, POS, POS), bf), ((F, COLS), f32)],
        place,
        ROWS_OF,
        recv,
        probs,
        up,
        held,
        held2,
        smem=1,
        flops=900_000_000,
    )
    sums2 = hop(sums, "core", 1, C)

    pieces = call(
        grad_kernel,
        "grads",
        [((3, HALF, COLS), bf)] * F,
        place,
        recv,
        probs,
        dm,
        ds,
        smem=1,
        scratch=[pltpu.VMEM((F, 3, HALF, COLS), bf)],
        flops=150_000_000,
    )

    (msgs,) = call(join_kernel, "join", [((Y, 48, DW + 128), bf)], mine, theirs, sums, sums2)
    msgs, *pieces = lax.optimization_barrier((msgs, *pieces))
    msgs = lax.all_to_all(msgs, "y", 0, 0, tiled=True)
    pieces = pieces[:1] + [hop(p, SEQ, k, F) for k, p in enumerate(pieces[1:], 1)]
    msgs, *pieces[2:6] = lax.optimization_barrier((msgs, *pieces[2:6]))
    (msgs,) = call(ysum_kernel, "ysum", [((Z, 8, DW), bf)], msgs)
    msgs = lax.all_to_all(msgs, "z", 0, 0, tiled=True)
    total, off = call(total_kernel, "total", [((8, DW), f32), ((16, 128), f32)], msgs)
    home = lax.ppermute(total, ("z", "x"), [(b, a) for a, b in there])
    offs = [off] + [hop(off, "x", k, X) for k in range(1, X)]

    (grad_qkv,) = call(
        unpack_kernel,
        "unpack",
        [((3, POS, DW), bf)],
        place,
        *pieces,
        smem=1,
        scratch=[pltpu.VMEM((F, 3, HALF, COLS), bf)],
    )
    grad_qkv = grad_qkv.reshape(3, 1, 1, POS, DW)
    home, grad_qkv = lax.optimization_barrier((home, grad_qkv))
    grad_w_out, grad_bias = call(
        last_kernel, "last", [((6, DW), f32), ((12, 15), f32)], place, home, *offs, smem=1
    )
    return grad_qkv, grad_bias, grad_w_out


def solution(mesh):
    grid = Mesh(mesh.devices.reshape(Z, Y, X, C), ("z", "y", "x", "core"))
    dp, every = ("z", "y"), ("z", "y", "x", "core")
    return jax.shard_map(
        per_device,
        mesh=grid,
        in_specs=(
            P(None, dp, SEQ, None, None),
            P(dp, None),
            P(),
            P(every, None),
            P(dp, SEQ, None, None, None),
        ),
        out_specs=(P(None, dp, SEQ, None, None), P(), P(every, None)),
        check_vma=False,
    )
```

time: 198 us -> 145 us (0.73)
  Pallas kernels: 73.7 us -> 16.7 us
  starting transfers between devices: 55.6 us -> 74.3 us
  local copies, waits for them, and re-layouts: 15 us -> 8.37 us
  other arithmetic: 8.75 us -> 2.58 us
    pallas_call x11, Pallas kernels: 73.7 us -> 16.7 us  [call(): pl.pallas_call(body, out_shape=tuple((jax.ShapeDtypeStruct(s, d) for s, d...]
    ppermute x18, starting transfers between devices: 26.3 us -> 37.6 us  [hop(): return lax.ppermute(x, axis, [(i, i ^ k) for i in range(n)])]
    all_to_all x1 -> x2, starting transfers between devices: 4.47 us -> 13.3 us  [the longest x1 8.93 us: per_device(): msgs = lax.all_to_all(msgs, 'z', 0, 0, tiled=True)]
    all_to_all x1 -> x2, waiting for transfers between devices: 0.01 us -> 7.07 us  [the longest x1 7.07 us: per_device(): msgs = lax.all_to_all(msgs, 'z', 0, 0, tiled=True)]
    ppermute x18, waiting for transfers between devices: 37 us -> 30.7 us  [hop(): return lax.ppermute(x, axis, [(i, i ^ k) for i in range(n)])]
    broadcast_in_dim x4 -> x0, local copies, waits for them, and re-layouts: 6.26 us -> none  [per_device(): jnp.where(alike, pair[:, :, None, :, None], f32(-1e+30))]
    all_to_all x1, waiting for transfers between devices: 5.52 us -> 0.01 us  [per_device(): recv = lax.all_to_all(packed, SEQ, 0, 0, tiled=True)]
    unnamed x39 -> x26, local copies, waits for them, and re-layouts: 4.44 us -> 8.28 us
  transfers between devices with their start and end apart: 24 -> 25, of which waited for: 15 -> 12; matrix products, arithmetic and copies ran while one was open for 10% -> 2% of each run, Pallas kernels for 3% -> 6%
where the time goes in v5:
time: 145 us; the launch traced here: 144 us
  starting transfers between devices  74.3 us (51%)
  waiting for transfers between devices  40.9 us (28%)
  Pallas kernels  16.7 us (12%)
  local copies, waits for them, and re-layouts  8.37 us (6%)
  other arithmetic  2.58 us (2%)
    ppermute x18, starting transfers between devices, hop(): return lax.ppermute(x, axis, [(i, i ^ k) for i in range(n)])  37.6 us
    ppermute x18, waiting for transfers between devices, hop(): return lax.ppermute(x, axis, [(i, i ^ k) for i in range(n)])  30.7 us
    pallas_call x11, Pallas kernels, call(): pl.pallas_call(body, out_shape=tuple((jax.ShapeDtypeStruct(s, d) for s, d...  16.7 us
    ppermute x2, starting transfers between devices, per_device(): lax.ppermute(rows8, ('z', 'x'), p)  9.96 us
    all_to_all x1, starting transfers between devices, per_device(): msgs = lax.all_to_all(msgs, 'z', 0, 0, tiled=True)  8.93 us
    unnamed x26, local copies, waits for them, and re-layouts  8.28 us
    all_to_all x1, waiting for transfers between devices, per_device(): msgs = lax.all_to_all(msgs, 'z', 0, 0, tiled=True)  7.07 us
    all_to_all x1, starting transfers between devices, per_device(): up = lax.all_to_all(up, SEQ, 0, 0, tiled=True)  6 us
  transfers between devices with their start and end apart: 25, of which 12 were waited for; matrix products, arithmetic and copies ran while one was open for 2% of the time, Pallas kernels for 6%

profile of v5, /device:TPU:32, one launch (start us, length us, event | category | flops | bytes accessed | tf_op | source)
XLA Modules:
  0.0 143.6 jit_solution(12939453334997484778)
XLA Ops:
  0.6 1.3 copy-done.4
  1.9 1.1 copy-done.5
  3.0 0.2 pack.1
  3.2 1.3 copy-done
  4.5 4.4 %all-to-all-start = ((bf16[8,5,64,384]{3,2,1,0:T(8,128)(2,1)}), bf16[8,5,64,384]{3,2,1,0:T(8,128)(2,1)S(1)}, u32[]{:S(2)}, u32[]{:S(2)}) async-start(bf16[8,5,64,384]{3,2,1,0:T(8,128)(2,1)} %copy-done), calls=%async_computation | async-start | bytes 3932160 | tf_op jit(solution)/shard_map/all_to_all | solution.py:236
  9.0 6.4 %collective-permute-start.1 = (bf16[8,1536]{1,0:T(8,128)(2,1)S(1)}, bf16[8,1536]{1,0:T(8,128)(2,1)S(1)}, u32[]{:S(2)}, u32[]{:S(2)}) collective-permute-start(bf16[8,1536]{1,0:T(8,128)(2,1)S(1)} %pad.4), channel_id=1, source_target_pairs={{0,32},{2,0},{4,96},{6,64},{32,160},{34,128},{36,224},{38,192},{64... | collective-permute-start | bytes 73736 | tf_op jit(solution)/shard_map/ppermute | solution.py:247
  15.4 3.6 %collective-permute-start = (bf16[8,1536]{1,0:T(8,128)(2,1)S(1)}, bf16[8,1536]{1,0:T(8,128)(2,1)S(1)}, u32[]{:S(2)}, u32[]{:S(2)}) collective-permute-start(bf16[8,1536]{1,0:T(8,128)(2,1)S(1)} %pad.4), channel_id=1, source_target_pairs={{0,0},{2,32},{4,64},{6,96},{32,128},{34,160},{36,192},{38,224},{64... | collective-permute-start | bytes 73736 | tf_op jit(solution)/shard_map/ppermute | solution.py:247
  19.0 0.0 collective-permute-done.1
  19.0 3.0 %collective-permute-done = bf16[8,1536]{1,0:T(8,128)(2,1)S(1)} collective-permute-done((bf16[8,1536]{1,0:T(8,128)(2,1)S(1)}, bf16[8,1536]{1,0:T(8,128)(2,1)S(1)}, u32[]{:S(2)}, u32[]{:S(2)}) %collective-permute-start) | collective-permute-done | bytes 24608 | tf_op jit(solution)/shard_map/ppermute | solution.py:247
  22.0 5.0 %collective-permute-start.2 = (bf16[16,1536]{1,0:T(8,128)(2,1)S(1)}, bf16[16,1536]{1,0:T(8,128)(2,1)S(1)}, u32[]{:S(2)}, u32[]{:S(2)}) collective-permute-start(bf16[16,1536]{1,0:T(8,128)(2,1)S(1)} %pad_maximum_fusion.3), channel_id=1, source_target_pairs={{0,64},{32,96},{64,0},{96,32},{128,192},{160,224},{192,128},{224,1... | collective-permute-start | bytes 147464 | tf_op jit(solution)/shard_map/ppermute | solution.py:221
  27.0 2.1 %collective-permute-done.2 = bf16[16,1536]{1,0:T(8,128)(2,1)S(1)} collective-permute-done((bf16[16,1536]{1,0:T(8,128)(2,1)S(1)}, bf16[16,1536]{1,0:T(8,128)(2,1)S(1)}, u32[]{:S(2)}, u32[]{:S(2)}) %collective-permute-start.2) | collective-permute-done | bytes 49184 | tf_op jit(solution)/shard_map/ppermute | solution.py:221
  29.1 14.5 %collective-permute-start.3 = (bf16[32,1536]{1,0:T(8,128)(2,1)S(1)}, bf16[32,1536]{1,0:T(8,128)(2,1)S(1)}, u32[]{:S(2)}, u32[]{:S(2)}) collective-permute-start(bf16[32,1536]{1,0:T(8,128)(2,1)S(1)} %pad_maximum_fusion.2), channel_id=1, source_target_pairs={{0,128},{32,160},{64,192},{96,224},{128,0},{160,32},{192,64},{224,... | collective-permute-start | bytes 294920 | tf_op jit(solution)/shard_map/ppermute | solution.py:221
  43.6 3.9 %collective-permute-done.3 = bf16[32,1536]{1,0:T(8,128)(2,1)S(1)} collective-permute-done((bf16[32,1536]{1,0:T(8,128)(2,1)S(1)}, bf16[32,1536]{1,0:T(8,128)(2,1)S(1)}, u32[]{:S(2)}, u32[]{:S(2)}) %collective-permute-start.3) | collective-permute-done | bytes 98336 | tf_op jit(solution)/shard_map/ppermute | solution.py:221
  47.5 0.7 pad_maximum_fusion.1
  48.2 0.0 all-to-all-done.recv_ref.qkv_ref
  48.2 0.8 compact.1
  49.1 1.2 copy-done.1
  50.2 6.0 %all-to-all-start.1 = ((bf16[8,64,1536]{2,1,0:T(8,128)(2,1)}), bf16[8,64,1536]{2,1,0:T(8,128)(2,1)S(1)}, u32[]{:S(2)}, u32[]{:S(2)}) async-start(bf16[8,64,1536]{2,1,0:T(8,128)(2,1)} %copy-done.1), calls=%async_computation.1 | async-start | bytes 3145728 | tf_op jit(solution)/shard_map/all_to_all | solution.py:255
  56.3 3.1 %collective-permute-start.6 = (bf16[64,1536]{1,0:T(8,128)(2,1)}, bf16[64,1536]{1,0:T(8,128)(2,1)S(1)}, u32[]{:S(2)}, u32[]{:S(2)}) collective-permute-start(bf16[64,1536]{1,0:T(8,128)(2,1)} %pad_maximum_fusion.1), channel_id=1, source_target_pairs={{0,24},{8,16},{16,8},{24,0},{1,25},{9,17},{17,9},{25,1},{2,26},{10... | collective-permute-start | bytes 589832 | tf_op jit(solution)/shard_map/ppermute | solution.py:221
  59.4 0.6 collective-permute-start.5
  60.0 0.5 collective-permute-start.4
  60.4 8.8 %collective-permute-done.6 = bf16[64,1536]{1,0:T(8,128)(2,1)S(1)} collective-permute-done((bf16[64,1536]{1,0:T(8,128)(2,1)}, bf16[64,1536]{1,0:T(8,128)(2,1)S(1)}, u32[]{:S(2)}, u32[]{:S(2)}) %collective-permute-start.6) | collective-permute-done | bytes 196640 | tf_op jit(solution)/shard_map/ppermute | solution.py:221
  69.3 0.7 collective-permute-done.4
  70.0 1.9 %pad_maximum_fusion.w0_ref = bf16[256,1536]{1,0:T(8,128)(2,1)} fusion(bf16[64,1536]{1,0:T(8,128)(2,1)S(1)} %collective-permute-done.6, bf16[64,1536]{1,0:T(8,128)(2,1)S(1)} %collective-permute-done.5, bf16[64,1536]{1,0:T(8,128)(2,1)S(1)} %collective-permute-done.4, bf16[64,1536]{1,0:T(8,128)(2,1)} %pad_maximum_fusion.1), kind=kLoop, calls=%fused_computation | loop fusion | flops 3145728 | bytes 1572864 | tf_op jit(solution)/shard_map/concatenate | solution.py:256
  71.8 0.1 stack.23.place
  71.9 0.7 copy-done.8
  72.6 5.0 %attn_fwd.1 = (f32[3,4,128,128]{3,2,1,0:T(8,128)S(1)}, bf16[512,384]{1,0:T(8,128)(2,1)S(1)}) custom-call(s32[5]{0:T(128)S(1)} %stack.23.place, f32[12,15]{1,0:T(8,128)S(1)} %copy-done.8, s32[8,384]{1,0:T(8,128)S(1)} %copy-done.6, bf16[8,5,64,384]{3,2,1,0:T(8,128)(2,1)S(1)} %all-to-all-done.recv_ref.qkv_ref), custom_call_target="tpu_custom_call" | custom-call | flops 250000000 | bytes 3158756 | tf_op jit(solution)/shard_map/attn_fwd/pallas_call | solution.py:53
  77.7 0.0 copy-start.2
  77.7 0.9 copy-done.2
  78.6 0.7 copy-done.10
  79.3 1.1 copy-done.11
  80.4 0.8 grad_w.1
  81.2 0.6 collective-permute-start.7
  81.8 1.6 %collective-permute-done.7.other_ref = bf16[192,1536]{1,0:T(8,128)(2,1)S(1)} collective-permute-done((bf16[192,1536]{1,0:T(8,128)(2,1)S(1)}, bf16[192,1536]{1,0:T(8,128)(2,1)S(1)}, u32[]{:S(2)}, u32[]{:S(2)}) %collective-permute-start.7) | collective-permute-done | bytes 589856 | tf_op jit(solution)/shard_map/ppermute | solution.py:221
  83.4 3.1 %scores_bwd.1 = (bf16[8,64,384]{2,1,0:T(8,128)(2,1)S(1)}, bf16[3,4,128,128]{3,2,1,0:T(8,128)(2,1)S(1)}, f32[8,384]{1,0:T(8,128)S(1)}) custom-call(s32[5]{0:T(128)S(1)} %stack.23.place, s32[8,384]{1,0:T(8,128)S(1)} %copy-done.7, bf16[8,5,64,384]{3,2,1,0:T(8,128)(2,1)S(1)} %all-to-all-done.recv_ref.qkv_ref, f32[3,4,128,128]{3,2,1,0:T(8,128)S(1)} %copy-done.3, ...), custom_call_target="tpu_custom_call" | custom-call | flops 900000000 | bytes 6709268 | tf_op jit(solution)/shard_map/scores_bwd/pallas_call | solution.py:53
  86.6 0.5 collective-permute-start.9
  87.0 1.2 grads.1
  88.2 0.0 collective-permute-done.9.s1
  88.2 1.3 join.1
  89.5 4.3 %all-to-all-start.2 = ((bf16[4,48,1664]{2,1,0:T(8,128)(2,1)}), bf16[4,48,1664]{2,1,0:T(8,128)(2,1)S(1)}, u32[]{:S(2)}, u32[]{:S(2)}) async-start(bf16[4,48,1664]{2,1,0:T(8,128)(2,1)} %join.1), calls=%async_computation.2 | async-start | bytes 1277952 | tf_op jit(solution)/shard_map/all_to_all | solution.py:316
  93.8 1.6 %collective-permute-start.10 = (bf16[3,64,384]{2,1,0:T(8,128)(2,1)S(1)}, bf16[3,64,384]{2,1,0:T(8,128)(2,1)S(1)}, u32[]{:S(2)}, u32[]{:S(2)}) collective-permute-start(bf16[3,64,384]{2,1,0:T(8,128)(2,1)S(1)} %get-tuple-element.68), channel_id=1, source_target_pairs={{0,2},{1,3},{2,0},{3,1},{4,6},{5,7},{6,4},{7,5},{8,10},{9,11},{10,... | collective-permute-start | bytes 442376 | tf_op jit(solution)/shard_map/ppermute | solution.py:221
  95.5 2.7 %collective-permute-start.12 = (bf16[3,64,384]{2,1,0:T(8,128)(2,1)S(1)}, bf16[3,64,384]{2,1,0:T(8,128)(2,1)S(1)}, u32[]{:S(2)}, u32[]{:S(2)}) collective-permute-start(bf16[3,64,384]{2,1,0:T(8,128)(2,1)S(1)} %get-tuple-element.70), channel_id=1, source_target_pairs={{0,4},{1,5},{2,6},{3,7},{4,0},{5,1},{6,2},{7,3},{8,12},{9,13},{10,... | collective-permute-start | bytes 442376 | tf_op jit(solution)/shard_map/ppermute | solution.py:221
  98.2 0.6 collective-permute-start.13
  98.8 1.6 %collective-permute-done.10.refs_2_ = bf16[3,64,384]{2,1,0:T(8,128)(2,1)S(1)} collective-permute-done((bf16[3,64,384]{2,1,0:T(8,128)(2,1)S(1)}, bf16[3,64,384]{2,1,0:T(8,128)(2,1)S(1)}, u32[]{:S(2)}, u32[]{:S(2)}) %collective-permute-start.10) | collective-permute-done | bytes 147488 | tf_op jit(solution)/shard_map/ppermute | solution.py:221
  100.4 2.5 %collective-permute-done.11.refs_3_ = bf16[3,64,384]{2,1,0:T(8,128)(2,1)S(1)} collective-permute-done((bf16[3,64,384]{2,1,0:T(8,128)(2,1)S(1)}, bf16[3,64,384]{2,1,0:T(8,128)(2,1)S(1)}, u32[]{:S(2)}, u32[]{:S(2)}) %collective-permute-start.11) | collective-permute-done | bytes 147488 | tf_op jit(solution)/shard_map/ppermute | solution.py:221
  102.9 6.3 %collective-permute-done.12.refs_4_ = bf16[3,64,384]{2,1,0:T(8,128)(2,1)S(1)} collective-permute-done((bf16[3,64,384]{2,1,0:T(8,128)(2,1)S(1)}, bf16[3,64,384]{2,1,0:T(8,128)(2,1)S(1)}, u32[]{:S(2)}, u32[]{:S(2)}) %collective-permute-start.12) | collective-permute-done | bytes 147488 | tf_op jit(solution)/shard_map/ppermute | solution.py:221
  109.2 0.9 collective-permute-done.13.refs_5_
  110.1 0.0 all-to-all-done.2.in_ref
  110.1 0.8 ysum.1
  110.9 8.9 %all-to-all-start.3 = ((bf16[8,8,1536]{2,1,0:T(8,128)(2,1)}), bf16[8,8,1536]{2,1,0:T(8,128)(2,1)S(1)}, u32[]{:S(2)}, u32[]{:S(2)}) async-start(bf16[8,8,1536]{2,1,0:T(8,128)(2,1)} %ysum.1), calls=%async_computation.3 | async-start | bytes 393216 | tf_op jit(solution)/shard_map/all_to_all | solution.py:320
  119.8 0.4 collective-permute-start.15
  120.2 0.4 collective-permute-start.16
  120.6 2.3 %collective-permute-start.17 = (bf16[3,64,384]{2,1,0:T(8,128)(2,1)S(1)}, bf16[3,64,384]{2,1,0:T(8,128)(2,1)S(1)}, u32[]{:S(2)}, u32[]{:S(2)}) collective-permute-start(bf16[3,64,384]{2,1,0:T(8,128)(2,1)S(1)} %get-tuple-element.81), channel_id=1, source_target_pairs={{0,7},{1,6},{2,5},{3,4},{4,3},{5,2},{6,1},{7,0},{8,15},{9,14},{10,... | collective-permute-start | bytes 442376 | tf_op jit(solution)/shard_map/ppermute | solution.py:221
  122.9 7.1 %all-to-all-done.3.in_ref = bf16[8,8,1536]{2,1,0:T(8,128)(2,1)S(1)} async-done(((bf16[8,8,1536]{2,1,0:T(8,128)(2,1)}), bf16[8,8,1536]{2,1,0:T(8,128)(2,1)S(1)}, u32[]{:S(2)}, u32[]{:S(2)}) %all-to-all-start.3) | async-done | bytes 196640 | tf_op jit(solution)/shard_map/all_to_all | solution.py:320
  130.0 0.6 total.1
  130.5 3.1 %collective-permute-start.14 = (f32[8,1536]{1,0:T(8,128)S(1)}, f32[8,1536]{1,0:T(8,128)S(1)}, u32[]{:S(2)}, u32[]{:S(2)}) collective-permute-start(f32[8,1536]{1,0:T(8,128)S(1)} %get-tuple-element.73), channel_id=1, source_target_pairs={{0,0},{32,2},{64,4},{96,6},{128,32},{160,34},{192,36},{224,38},{2,... | collective-permute-start | bytes 147464 | tf_op jit(solution)/shard_map/ppermute | solution.py:322
  133.6 0.1 collective-permute-start.18
  133.7 3.9 %collective-permute-start.19 = (f32[16,128]{1,0:T(8,128)S(1)}, f32[16,128]{1,0:T(8,128)S(1)}, u32[]{:S(2)}, u32[]{:S(2)}) collective-permute-start(f32[16,128]{1,0:T(8,128)S(1)} %get-tuple-element.84.o0), channel_id=1, source_target_pairs={{0,4},{2,6},{4,0},{6,2},{1,5},{3,7},{5,1},{7,3},{8,12},{10,14},{12... | collective-permute-start | bytes 24584 | tf_op jit(solution)/shard_map/ppermute | solution.py:221
  137.6 0.0 collective-permute-done.16.refs_6_
  137.6 0.8 collective-permute-start.20
  138.4 1.8 %unpack.1 = bf16[3,128,1536]{2,1,0:T(8,128)(2,1)} custom-call(s32[5]{0:T(128)S(1)} %stack.23.place, bf16[3,64,384]{2,1,0:T(8,128)(2,1)S(1)} %get-tuple-element.74.refs_0_, bf16[3,64,384]{2,1,0:T(8,128)(2,1)S(1)} %collective-permute-done.15.refs_1_, bf16[3,64,384]{2,1,0:T(8,128)(2,1)S(1)} %collective-permute-done.10.refs_2_, ...), custom_call_target="tpu_custom_call" | custom-call | bytes 2359316 | tf_op jit(solution)/shard_map/unpack/pallas_call | solution.py:53
  140.2 0.0 collective-permute-done.14.home_ref
  140.2 2.3 %collective-permute-done.20.o3 = f32[16,128]{1,0:T(8,128)S(1)} collective-permute-done((f32[16,128]{1,0:T(8,128)S(1)}, f32[16,128]{1,0:T(8,128)S(1)}, u32[]{:S(2)}, u32[]{:S(2)}) %collective-permute-start.20) | collective-permute-done | bytes 8224 | tf_op jit(solution)/shard_map/ppermute | solution.py:221
  142.5 1.2 last.1
  (29 shorter events, 0.1 us)
Async XLA Ops:
  0.6 1.3 copy-start.4
  1.9 1.1 copy-start.5
  3.2 1.3 copy-start
  4.5 4.4 %copy-start.12 = (bf16[6,1536]{1,0:T(8,128)(2,1)S(1)}, bf16[6,1536]{1,0:T(8,128)(2,1)}, u32[]{:S(2)}) copy-start(bf16[6,1536]{1,0:T(8,128)(2,1)} %param.10) | copy-start | bytes 55300
  4.5 43.7 %copy-start.9 = (s32[1,8]{1,0:T(1,128)S(1)}, s32[1,8]{1,0:T(1,128)}, u32[]{:S(2)}) copy-start(s32[1,8]{1,0:T(1,128)} %sizes.1) | copy-start | bytes 100
  4.5 43.7 %all-to-all-start = ((bf16[8,5,64,384]{3,2,1,0:T(8,128)(2,1)}), bf16[8,5,64,384]{3,2,1,0:T(8,128)(2,1)S(1)}, u32[]{:S(2)}, u32[]{:S(2)}) async-start(bf16[8,5,64,384]{3,2,1,0:T(8,128)(2,1)} %copy-done), calls=%async_computation | async-start | bytes 3932160 | tf_op jit(solution)/shard_map/all_to_all | solution.py:236
  9.0 10.0 %collective-permute-start.1 = (bf16[8,1536]{1,0:T(8,128)(2,1)S(1)}, bf16[8,1536]{1,0:T(8,128)(2,1)S(1)}, u32[]{:S(2)}, u32[]{:S(2)}) collective-permute-start(bf16[8,1536]{1,0:T(8,128)(2,1)S(1)} %pad.4), channel_id=1, source_target_pairs={{0,32},{2,0},{4,96},{6,64},{32,160},{34,128},{36,224},{38,192},{64... | collective-permute-start | bytes 73736 | tf_op jit(solution)/shard_map/ppermute | solution.py:247
  15.4 6.6 %collective-permute-start = (bf16[8,1536]{1,0:T(8,128)(2,1)S(1)}, bf16[8,1536]{1,0:T(8,128)(2,1)S(1)}, u32[]{:S(2)}, u32[]{:S(2)}) collective-permute-start(bf16[8,1536]{1,0:T(8,128)(2,1)S(1)} %pad.4), channel_id=1, source_target_pairs={{0,0},{2,32},{4,64},{6,96},{32,128},{34,160},{36,192},{38,224},{64... | collective-permute-start | bytes 73736 | tf_op jit(solution)/shard_map/ppermute | solution.py:247
  22.0 7.1 %collective-permute-start.2 = (bf16[16,1536]{1,0:T(8,128)(2,1)S(1)}, bf16[16,1536]{1,0:T(8,128)(2,1)S(1)}, u32[]{:S(2)}, u32[]{:S(2)}) collective-permute-start(bf16[16,1536]{1,0:T(8,128)(2,1)S(1)} %pad_maximum_fusion.3), channel_id=1, source_target_pairs={{0,64},{32,96},{64,0},{96,32},{128,192},{160,224},{192,128},{224,1... | collective-permute-start | bytes 147464 | tf_op jit(solution)/shard_map/ppermute | solution.py:221
  29.1 18.4 %collective-permute-start.3 = (bf16[32,1536]{1,0:T(8,128)(2,1)S(1)}, bf16[32,1536]{1,0:T(8,128)(2,1)S(1)}, u32[]{:S(2)}, u32[]{:S(2)}) collective-permute-start(bf16[32,1536]{1,0:T(8,128)(2,1)S(1)} %pad_maximum_fusion.2), channel_id=1, source_target_pairs={{0,128},{32,160},{64,192},{96,224},{128,0},{160,32},{192,64},{224,... | collective-permute-start | bytes 294920 | tf_op jit(solution)/shard_map/ppermute | solution.py:221
  49.1 1.2 copy-start.1
  50.2 29.1 %all-to-all-start.1 = ((bf16[8,64,1536]{2,1,0:T(8,128)(2,1)}), bf16[8,64,1536]{2,1,0:T(8,128)(2,1)S(1)}, u32[]{:S(2)}, u32[]{:S(2)}) async-start(bf16[8,64,1536]{2,1,0:T(8,128)(2,1)} %copy-done.1), calls=%async_computation.1 | async-start | bytes 3145728 | tf_op jit(solution)/shard_map/all_to_all | solution.py:255
  56.3 15.7 %copy-start.6 = (s32[8,384]{1,0:T(8,128)S(1)}, s32[8,384]{1,0:T(8,128)}, u32[]{:S(2)}) copy-start(s32[8,384]{1,0:T(8,128)} %constant.25.clone.leave_ref) | copy-start | bytes 36868
  56.3 13.0 %collective-permute-start.6 = (bf16[64,1536]{1,0:T(8,128)(2,1)}, bf16[64,1536]{1,0:T(8,128)(2,1)S(1)}, u32[]{:S(2)}, u32[]{:S(2)}) collective-permute-start(bf16[64,1536]{1,0:T(8,128)(2,1)} %pad_maximum_fusion.1), channel_id=1, source_target_pairs={{0,24},{8,16},{16,8},{24,0},{1,25},{9,17},{17,9},{25,1},{2,26},{10... | collective-permute-start | bytes 589832 | tf_op jit(solution)/shard_map/ppermute | solution.py:221
  59.4 9.9 %collective-permute-start.5 = (bf16[64,1536]{1,0:T(8,128)(2,1)}, bf16[64,1536]{1,0:T(8,128)(2,1)S(1)}, u32[]{:S(2)}, u32[]{:S(2)}) collective-permute-start(bf16[64,1536]{1,0:T(8,128)(2,1)} %pad_maximum_fusion.1), channel_id=1, source_target_pairs={{0,16},{8,24},{16,0},{24,8},{1,17},{9,25},{17,1},{25,9},{2,18},{10... | collective-permute-start | bytes 589832 | tf_op jit(solution)/shard_map/ppermute | solution.py:221
  60.0 10.0 %collective-permute-start.4 = (bf16[64,1536]{1,0:T(8,128)(2,1)}, bf16[64,1536]{1,0:T(8,128)(2,1)S(1)}, u32[]{:S(2)}, u32[]{:S(2)}) collective-permute-start(bf16[64,1536]{1,0:T(8,128)(2,1)} %pad_maximum_fusion.1), channel_id=1, source_target_pairs={{0,8},{8,0},{16,24},{24,16},{1,9},{9,1},{17,25},{25,17},{2,10},{10... | collective-permute-start | bytes 589832 | tf_op jit(solution)/shard_map/ppermute | solution.py:221
  71.8 11.6 %collective-permute-start.8 = (bf16[256,1536]{1,0:T(8,128)(2,1)}, bf16[256,1536]{1,0:T(8,128)(2,1)}, u32[]{:S(2)}, u32[]{:S(2)}) collective-permute-start(bf16[256,1536]{1,0:T(8,128)(2,1)} %pad_maximum_fusion.w0_ref), channel_id=1, source_target_pairs={{0,1},{1,0},{2,3},{3,2},{4,5},{5,4},{6,7},{7,6},{8,9},{9,8},{10,11... | collective-permute-start | bytes 2359304 | tf_op jit(solution)/shard_map/ppermute | solution.py:221
  71.9 0.7 copy-start.8
  77.7 0.9 copy-start.2
  78.6 0.7 copy-start.10
  79.3 4.1 %copy-start.7 = (s32[8,384]{1,0:T(8,128)S(1)}, s32[8,384]{1,0:T(8,128)}, u32[]{:S(2)}) copy-start(s32[8,384]{1,0:T(8,128)} %constant.26.clone.rows_ref) | copy-start | bytes 36868
  79.3 4.1 %copy-start.3 = (f32[3,4,128,128]{3,2,1,0:T(8,128)S(1)}, f32[3,4,128,128]{3,2,1,0:T(8,128)}, u32[]{:S(2)}) copy-start(f32[3,4,128,128]{3,2,1,0:T(8,128)} %copy-done.2) | copy-start | bytes 2359300
  79.3 1.1 copy-start.11
  81.2 2.2 %collective-permute-start.7 = (bf16[192,1536]{1,0:T(8,128)(2,1)S(1)}, bf16[192,1536]{1,0:T(8,128)(2,1)S(1)}, u32[]{:S(2)}, u32[]{:S(2)}) collective-permute-start(bf16[192,1536]{1,0:T(8,128)(2,1)S(1)} %get-tuple-element.51), channel_id=1, source_target_pairs={{0,1},{1,0},{2,3},{3,2},{4,5},{5,4},{6,7},{7,6},{8,9},{9,8},{10,11... | collective-permute-start | bytes 1769480 | tf_op jit(solution)/shard_map/ppermute | solution.py:221
  86.6 1.6 %collective-permute-start.9 = (f32[8,384]{1,0:T(8,128)S(1)}, f32[8,384]{1,0:T(8,128)S(1)}, u32[]{:S(2)}, u32[]{:S(2)}) collective-permute-start(f32[8,384]{1,0:T(8,128)S(1)} %get-tuple-element.56.s0), channel_id=1, source_target_pairs={{0,1},{1,0},{2,3},{3,2},{4,5},{5,4},{6,7},{7,6},{8,9},{9,8},{10,11... | collective-permute-start | bytes 36872 | tf_op jit(solution)/shard_map/ppermute | solution.py:221
  89.5 20.6 %all-to-all-start.2 = ((bf16[4,48,1664]{2,1,0:T(8,128)(2,1)}), bf16[4,48,1664]{2,1,0:T(8,128)(2,1)S(1)}, u32[]{:S(2)}, u32[]{:S(2)}) async-start(bf16[4,48,1664]{2,1,0:T(8,128)(2,1)} %join.1), calls=%async_computation.2 | async-start | bytes 1277952 | tf_op jit(solution)/shard_map/all_to_all | solution.py:316
  93.8 6.6 %collective-permute-start.10 = (bf16[3,64,384]{2,1,0:T(8,128)(2,1)S(1)}, bf16[3,64,384]{2,1,0:T(8,128)(2,1)S(1)}, u32[]{:S(2)}, u32[]{:S(2)}) collective-permute-start(bf16[3,64,384]{2,1,0:T(8,128)(2,1)S(1)} %get-tuple-element.68), channel_id=1, source_target_pairs={{0,2},{1,3},{2,0},{3,1},{4,6},{5,7},{6,4},{7,5},{8,10},{9,11},{10,... | collective-permute-start | bytes 442376 | tf_op jit(solution)/shard_map/ppermute | solution.py:221
  95.5 7.4 %collective-permute-start.11 = (bf16[3,64,384]{2,1,0:T(8,128)(2,1)S(1)}, bf16[3,64,384]{2,1,0:T(8,128)(2,1)S(1)}, u32[]{:S(2)}, u32[]{:S(2)}) collective-permute-start(bf16[3,64,384]{2,1,0:T(8,128)(2,1)S(1)} %get-tuple-element.69), channel_id=1, source_target_pairs={{0,3},{1,2},{2,1},{3,0},{4,7},{5,6},{6,5},{7,4},{8,11},{9,10},{10,... | collective-permute-start | bytes 442376 | tf_op jit(solution)/shard_map/ppermute | solution.py:221
  95.5 13.7 %collective-permute-start.12 = (bf16[3,64,384]{2,1,0:T(8,128)(2,1)S(1)}, bf16[3,64,384]{2,1,0:T(8,128)(2,1)S(1)}, u32[]{:S(2)}, u32[]{:S(2)}) collective-permute-start(bf16[3,64,384]{2,1,0:T(8,128)(2,1)S(1)} %get-tuple-element.70), channel_id=1, source_target_pairs={{0,4},{1,5},{2,6},{3,7},{4,0},{5,1},{6,2},{7,3},{8,12},{9,13},{10,... | collective-permute-start | bytes 442376 | tf_op jit(solution)/shard_map/ppermute | solution.py:221
  98.2 11.9 %collective-permute-start.13 = (bf16[3,64,384]{2,1,0:T(8,128)(2,1)S(1)}, bf16[3,64,384]{2,1,0:T(8,128)(2,1)S(1)}, u32[]{:S(2)}, u32[]{:S(2)}) collective-permute-start(bf16[3,64,384]{2,1,0:T(8,128)(2,1)S(1)} %get-tuple-element.71), channel_id=1, source_target_pairs={{0,5},{1,4},{2,7},{3,6},{4,1},{5,0},{6,3},{7,2},{8,13},{9,12},{10,... | collective-permute-start | bytes 442376 | tf_op jit(solution)/shard_map/ppermute | solution.py:221
  110.9 19.1 %all-to-all-start.3 = ((bf16[8,8,1536]{2,1,0:T(8,128)(2,1)}), bf16[8,8,1536]{2,1,0:T(8,128)(2,1)S(1)}, u32[]{:S(2)}, u32[]{:S(2)}) async-start(bf16[8,8,1536]{2,1,0:T(8,128)(2,1)} %ysum.1), calls=%async_computation.3 | async-start | bytes 393216 | tf_op jit(solution)/shard_map/all_to_all | solution.py:320
  119.8 13.9 %collective-permute-start.15 = (bf16[3,64,384]{2,1,0:T(8,128)(2,1)S(1)}, bf16[3,64,384]{2,1,0:T(8,128)(2,1)S(1)}, u32[]{:S(2)}, u32[]{:S(2)}) collective-permute-start(bf16[3,64,384]{2,1,0:T(8,128)(2,1)S(1)} %get-tuple-element.75), channel_id=1, source_target_pairs={{0,1},{1,0},{2,3},{3,2},{4,5},{5,4},{6,7},{7,6},{8,9},{9,8},{10,11... | collective-permute-start | bytes 442376 | tf_op jit(solution)/shard_map/ppermute | solution.py:221
  120.2 17.4 %collective-permute-start.16 = (bf16[3,64,384]{2,1,0:T(8,128)(2,1)S(1)}, bf16[3,64,384]{2,1,0:T(8,128)(2,1)S(1)}, u32[]{:S(2)}, u32[]{:S(2)}) collective-permute-start(bf16[3,64,384]{2,1,0:T(8,128)(2,1)S(1)} %get-tuple-element.80), channel_id=1, source_target_pairs={{0,6},{1,7},{2,4},{3,5},{4,2},{5,3},{6,0},{7,1},{8,14},{9,15},{10,... | collective-permute-start | bytes 442376 | tf_op jit(solution)/shard_map/ppermute | solution.py:221
  120.6 17.8 %collective-permute-start.17 = (bf16[3,64,384]{2,1,0:T(8,128)(2,1)S(1)}, bf16[3,64,384]{2,1,0:T(8,128)(2,1)S(1)}, u32[]{:S(2)}, u32[]{:S(2)}) collective-permute-start(bf16[3,64,384]{2,1,0:T(8,128)(2,1)S(1)} %get-tuple-element.81), channel_id=1, source_target_pairs={{0,7},{1,6},{2,5},{3,4},{4,3},{5,2},{6,1},{7,0},{8,15},{9,14},{10,... | collective-permute-start | bytes 442376 | tf_op jit(solution)/shard_map/ppermute | solution.py:221
  130.5 9.6 %collective-permute-start.14 = (f32[8,1536]{1,0:T(8,128)S(1)}, f32[8,1536]{1,0:T(8,128)S(1)}, u32[]{:S(2)}, u32[]{:S(2)}) collective-permute-start(f32[8,1536]{1,0:T(8,128)S(1)} %get-tuple-element.73), channel_id=1, source_target_pairs={{0,0},{32,2},{64,4},{96,6},{128,32},{160,34},{192,36},{224,38},{2,... | collective-permute-start | bytes 147464 | tf_op jit(solution)/shard_map/ppermute | solution.py:322
  133.6 6.6 %collective-permute-start.18 = (f32[16,128]{1,0:T(8,128)S(1)}, f32[16,128]{1,0:T(8,128)S(1)}, u32[]{:S(2)}, u32[]{:S(2)}) collective-permute-start(f32[16,128]{1,0:T(8,128)S(1)} %get-tuple-element.84.o0), channel_id=1, source_target_pairs={{0,2},{2,0},{4,6},{6,4},{1,3},{3,1},{5,7},{7,5},{8,10},{10,8},{12,... | collective-permute-start | bytes 24584 | tf_op jit(solution)/shard_map/ppermute | solution.py:221
  133.7 6.5 %collective-permute-start.19 = (f32[16,128]{1,0:T(8,128)S(1)}, f32[16,128]{1,0:T(8,128)S(1)}, u32[]{:S(2)}, u32[]{:S(2)}) collective-permute-start(f32[16,128]{1,0:T(8,128)S(1)} %get-tuple-element.84.o0), channel_id=1, source_target_pairs={{0,4},{2,6},{4,0},{6,2},{1,5},{3,7},{5,1},{7,3},{8,12},{10,14},{12... | collective-permute-start | bytes 24584 | tf_op jit(solution)/shard_map/ppermute | solution.py:221
  137.6 4.9 %collective-permute-start.20 = (f32[16,128]{1,0:T(8,128)S(1)}, f32[16,128]{1,0:T(8,128)S(1)}, u32[]{:S(2)}, u32[]{:S(2)}) collective-permute-start(f32[16,128]{1,0:T(8,128)S(1)} %get-tuple-element.84.o0), channel_id=1, source_target_pairs={{0,6},{2,4},{4,2},{6,0},{1,7},{3,5},{5,3},{7,1},{8,14},{10,12},{12... | collective-permute-start | bytes 24584 | tf_op jit(solution)/shard_map/ppermute | solution.py:221

commit v6 on v5

--- a/solution.py
+++ b/solution.py
@@ -34,7 +34,8 @@
 ROWS_OF[3] = ROW % 6
 LEAVE = np.zeros((8, COLS), np.int32)
 LEAVE[0] = ROW // 192
-LEAVE[1] = (((ROW % 48 // 24) * 4 + ROW // 48 % 4) * 8 + ROW % 24 // 6 * 2) * 6 + ROW % 6
+SUB = ROW % 192 // 6
+LEAVE[1] = ((SUB // 16 * 4 + SUB % 4) * 8 + SUB // 4 % 4 * 2) * 6 + ROW % 6
 
 
 def dot(a, b, dims, **kw):
@@ -115,14 +116,12 @@
     mixed_ref[...] = dot(raw_ref[...].reshape(F * HALF, COLS), order, NN).astype(bf)
 
 
-def gw_kernel(up_ref, mixed_ref, mine_ref, other_ref):
-    gw = dot(mixed_ref[...], up_ref[...].reshape(F * HALF, DW), TN)
+def score_kernel(place, rows_ref, recv_ref, probs_ref, mixed_ref, up_ref, w0_ref, w1_ref, *outs):
+    mine_ref, other_ref, dm_ref, ds_ref, sums_ref = outs
+    up = up_ref[...].reshape(F * HALF, DW)
+    gw = dot(mixed_ref[...], up, TN)
     mine_ref[...] = gw[: COLS // 2]
     other_ref[...] = gw[COLS // 2 :].astype(bf)
-
-
-def score_kernel(place, rows_ref, qkv_ref, probs_ref, up_ref, w0_ref, w1_ref, dm_ref, ds_ref, sums_ref):
-    up = up_ref[...].reshape(F * HALF, DW)
     dm = jnp.concatenate([dot(up, w[...], NT).astype(bf) for w in (w0_ref, w1_ref)], axis=1)
     c, y, j = (rows_ref[n : n + 1] ^ place[n] for n in (CORE, YI, ZI))
     spot = ((c * Y + y) * Z + j) * 8 + rows_ref[3:4]
@@ -135,7 +134,7 @@
         for b in range(NB):
             d = dm_ref[:, b * 16 : (b + 1) * 16, cols].reshape(POS, HD)
             p = probs_ref[h, b]
-            g = dot(d, block(qkv_ref, 2, b, h), NT)
+            g = dot(d, block(recv_ref, 2, b, h), NT)
             ds = p * (g - jnp.sum(p * g, axis=-1, keepdims=True))
             total = total + jnp.sum(ds.reshape(F, 16, POS), axis=1)
             ds_ref[h, b] = ds.astype(bf)
@@ -178,21 +177,10 @@
     gw = mine_ref[...] + other_ref[...].astype(f32)
     hot = ((iota((COLS, 128), 0) >> 4) == iota((COLS, 128), 1)).astype(f32)
     b = dot(s0[...] + s1[...], hot, NN, precision=lax.Precision.HIGHEST)
-    high, low = split(b)
-    ride = jnp.concatenate([high, low, jnp.zeros((32, 128), f32)], axis=0).astype(bf)
-    for y in range(Y):
-        out_ref[y, :, :DW] = gw[48 * y : 48 * (y + 1)].astype(bf)
-        out_ref[y, :, DW:] = ride
-
-
-def ysum_kernel(in_ref, out_ref):
-    gw = jnp.sum(in_ref[:, :, :DW].astype(f32), axis=0)
-    ride = jnp.sum(in_ref[:, :, DW:].astype(f32), axis=0)
-    high, low = split(ride[:8] + ride[8:16])
     pad = jnp.zeros((1, DW - F * 128), f32)
-    flat = [jnp.concatenate([x[f : f + 1] for f in range(F)] + [pad], axis=1) for x in (high, low)]
-    for j in range(Z):
-        out_ref[j] = jnp.concatenate([gw[6 * j : 6 * j + 6]] + flat, axis=0).astype(bf)
+    flat = [jnp.concatenate([x[f : f + 1] for f in range(F)] + [pad], axis=1) for x in split(b)]
+    for d in range(Z * Y):
+        out_ref[d] = jnp.concatenate([gw[6 * d : 6 * d + 6]] + flat, axis=0).astype(bf)
 
 
 def total_kernel(in_ref, sum_ref, off_ref):
@@ -208,12 +196,12 @@
     off_ref[...] = out
 
 
-def last_kernel(place, home_ref, o0, o1, o2, o3, gw_ref, bias_ref):
+def last_kernel(home_ref, off_ref, gw_ref, bias_ref):
     gw_ref[...] = home_ref[:6]
     row = iota((16, 128), 0) // HL
     out = jnp.zeros((16, 128), f32)
-    for k, o in enumerate((o0, o1, o2, o3)):
-        out = out + jnp.where(row == (place[XI] ^ k), o[...], 0.0)
+    for c in range(X):
+        out = out + jnp.where(row == c, off_ref[c], 0.0)
     bias_ref[...] = out[:12, :15]
 
 
@@ -233,8 +221,6 @@
         qkv_time[:, 0, 0],
         cot_out[0, 0],
     )
-    recv = lax.all_to_all(packed, SEQ, 0, 0, tiled=True)
-
     there = [
         ((2 * c + z0) * X + x, (z0 * X + x) * X + c)
         for c in range(X)
@@ -243,8 +229,10 @@
     ]
     near = [(a, b ^ X) for a, b in there]
     rows8 = jnp.pad(w_out, ((0, 2), (0, 0)))
-    rows8, _ = lax.optimization_barrier((rows8, packed))
-    held = jnp.concatenate([lax.ppermute(rows8, ("z", "x"), p) for p in (there, near)])
+    held = [lax.ppermute(rows8, ("z", "x"), p) for p in (there, near)]
+    packed, *held = lax.optimization_barrier((packed, *held))
+    recv = lax.all_to_all(packed, SEQ, 0, 0, tiled=True)
+    held = jnp.concatenate(held)
     held = jnp.concatenate([held, hop(held, "z", 2, Z)])
     held = jnp.concatenate([held, hop(held, "z", 4, Z)])
 
@@ -270,31 +258,28 @@
         flops=250_000_000,
     )
 
-    mine, theirs = call(
-        gw_kernel,
-        "grad_w",
-        [((COLS // 2, DW), f32), ((COLS // 2, DW), bf)],
-        up,
-        mixed,
-        flops=604_000_000,
-    )
-    theirs = hop(theirs, "core", 1, C)
-    up, theirs = lax.optimization_barrier((up, theirs))
-
-    dm, ds, sums = call(
+    mine, theirs, dm, ds, sums = call(
         score_kernel,
         "scores_bwd",
-        [((F, HALF, COLS), bf), ((HL, NB, POS, POS), bf), ((F, COLS), f32)],
+        [
+            ((COLS // 2, DW), f32),
+            ((COLS // 2, DW), bf),
+            ((F, HALF, COLS), bf),
+            ((HL, NB, POS, POS), bf),
+            ((F, COLS), f32),
+        ],
         place,
         ROWS_OF,
         recv,
         probs,
+        mixed,
         up,
         held,
         held2,
         smem=1,
-        flops=900_000_000,
-    )
+        flops=1_500_000_000,
+    )
+    theirs = hop(theirs, "core", 1, C)
     sums2 = hop(sums, "core", 1, C)
 
     pieces = call(
@@ -311,17 +296,14 @@
         flops=150_000_000,
     )
 
-    (msgs,) = call(join_kernel, "join", [((Y, 48, DW + 128), bf)], mine, theirs, sums, sums2)
+    (msgs,) = call(join_kernel, "join", [((Z * Y, 8, DW), bf)], mine, theirs, sums, sums2)
     msgs, *pieces = lax.optimization_barrier((msgs, *pieces))
-    msgs = lax.all_to_all(msgs, "y", 0, 0, tiled=True)
+    msgs = lax.all_to_all(msgs, ("z", "y"), 0, 0, tiled=True)
     pieces = pieces[:1] + [hop(p, SEQ, k, F) for k, p in enumerate(pieces[1:], 1)]
-    msgs, *pieces[2:6] = lax.optimization_barrier((msgs, *pieces[2:6]))
-    (msgs,) = call(ysum_kernel, "ysum", [((Z, 8, DW), bf)], msgs)
-    msgs = lax.all_to_all(msgs, "z", 0, 0, tiled=True)
+    msgs, *pieces = lax.optimization_barrier((msgs, *pieces))
     total, off = call(total_kernel, "total", [((8, DW), f32), ((16, 128), f32)], msgs)
     home = lax.ppermute(total, ("z", "x"), [(b, a) for a, b in there])
-    offs = [off] + [hop(off, "x", k, X) for k in range(1, X)]
-
+    off = lax.all_to_all(jnp.broadcast_to(off, (X, 16, 128)), "x", 0, 0, tiled=True)
     (grad_qkv,) = call(
         unpack_kernel,
         "unpack",
@@ -334,7 +316,7 @@
     grad_qkv = grad_qkv.reshape(3, 1, 1, POS, DW)
     home, grad_qkv = lax.optimization_barrier((home, grad_qkv))
     grad_w_out, grad_bias = call(
-        last_kernel, "last", [((6, DW), f32), ((12, 15), f32)], place, home, *offs, smem=1
+        last_kernel, "last", [((6, DW), f32), ((12, 15), f32)], home, off
     )
     return grad_qkv, grad_bias, grad_w_out
 

time: 145 us -> 136 us (0.938)
  the two profiles are of different devices: /device:TPU:32 before, /device:TPU:8 now
where the time goes in v6:
time: 136 us; the launch traced here: 135 us
  starting transfers between devices  53.3 us (39%)
  waiting for transfers between devices  51.4 us (38%)
  Pallas kernels  15.5 us (11%)
  local copies, waits for them, and re-layouts  11.5 us (8%)
  other arithmetic  2.56 us (2%)
    ppermute x15, waiting for transfers between devices, hop(): return lax.ppermute(x, axis, [(i, i ^ k) for i in range(n)])  35.7 us
    pallas_call x9, Pallas kernels, call(): pl.pallas_call(body, out_shape=tuple((jax.ShapeDtypeStruct(s, d) for s, d...  15.5 us
    ppermute x15, starting transfers between devices, hop(): return lax.ppermute(x, axis, [(i, i ^ k) for i in range(n)])  14.8 us
    all_to_all x1, starting transfers between devices, per_device(): recv = lax.all_to_all(packed, SEQ, 0, 0, tiled=True)  14.4 us
    all_to_all x1, waiting for transfers between devices, per_device(): recv = lax.all_to_all(packed, SEQ, 0, 0, tiled=True)  10.6 us
    unnamed x26, local copies, waits for them, and re-layouts  10 us
    all_to_all x1, starting transfers between devices, per_device(): lax.all_to_all(jnp.broadcast_to(off, (X, 16, 128)), 'x', 0, 0, tiled=True)  9.44 us
    all_to_all x1, starting transfers between devices, per_device(): msgs = lax.all_to_all(msgs, ('z', 'y'), 0, 0, tiled=True)  7.73 us
  transfers between devices with their start and end apart: 22, of which 13 were waited for; matrix products, arithmetic and copies ran while one was open for 2% of the time, Pallas kernels for 6%

profile of v6, /device:TPU:8, one launch (start us, length us, event | category | flops | bytes accessed | tf_op | source)
XLA Modules:
  0.0 135.0 jit_solution(17736110682285528929)
XLA Ops:
  0.6 0.7 pad.4
  1.4 1.9 %collective-permute-start.1 = (bf16[8,1536]{1,0:T(8,128)(2,1)S(1)}, bf16[8,1536]{1,0:T(8,128)(2,1)S(1)}, u32[]{:S(2)}, u32[]{:S(2)}) collective-permute-start(bf16[8,1536]{1,0:T(8,128)(2,1)S(1)} %pad.4), channel_id=1, source_target_pairs={{0,32},{2,0},{4,96},{6,64},{32,160},{34,128},{36,224},{38,192},{64... | collective-permute-start | bytes 73736 | tf_op jit(solution)/shard_map/ppermute | solution.py:232
  3.3 0.7 collective-permute-start
  4.0 0.0 copy-start.5
  4.0 1.3 copy-done.5
  5.2 1.1 copy-done.6
  6.4 0.2 pack.1
  6.5 1.3 copy-done
  7.8 0.0 collective-permute-done
  7.9 14.4 %all-to-all-start = ((bf16[8,5,64,384]{3,2,1,0:T(8,128)(2,1)}), bf16[8,5,64,384]{3,2,1,0:T(8,128)(2,1)S(1)}, u32[]{:S(2)}, u32[]{:S(2)}) async-start(bf16[8,5,64,384]{3,2,1,0:T(8,128)(2,1)} %copy-done), calls=%async_computation | async-start | bytes 3932160 | tf_op jit(solution)/shard_map/all_to_all | solution.py:234
  22.3 0.1 collective-permute-start.2
  22.4 5.0 %collective-permute-done.2 = bf16[16,1536]{1,0:T(8,128)(2,1)S(1)} collective-permute-done((bf16[16,1536]{1,0:T(8,128)(2,1)S(1)}, bf16[16,1536]{1,0:T(8,128)(2,1)S(1)}, u32[]{:S(2)}, u32[]{:S(2)}) %collective-permute-start.2) | collective-permute-done | bytes 49184 | tf_op jit(solution)/shard_map/ppermute | solution.py:209
  27.4 1.6 %collective-permute-start.3 = (bf16[32,1536]{1,0:T(8,128)(2,1)S(1)}, bf16[32,1536]{1,0:T(8,128)(2,1)S(1)}, u32[]{:S(2)}, u32[]{:S(2)}) collective-permute-start(bf16[32,1536]{1,0:T(8,128)(2,1)S(1)} %pad_maximum_fusion.2), channel_id=1, source_target_pairs={{0,128},{32,160},{64,192},{96,224},{128,0},{160,32},{192,64},{224,... | collective-permute-start | bytes 294920 | tf_op jit(solution)/shard_map/ppermute | solution.py:209
  29.0 7.8 %collective-permute-done.3 = bf16[32,1536]{1,0:T(8,128)(2,1)S(1)} collective-permute-done((bf16[32,1536]{1,0:T(8,128)(2,1)S(1)}, bf16[32,1536]{1,0:T(8,128)(2,1)S(1)}, u32[]{:S(2)}, u32[]{:S(2)}) %collective-permute-start.3) | collective-permute-done | bytes 98336 | tf_op jit(solution)/shard_map/ppermute | solution.py:209
  36.8 0.7 pad_maximum_fusion.1
  37.4 10.6 %all-to-all-done.recv_ref.qkv_ref = bf16[8,5,64,384]{3,2,1,0:T(8,128)(2,1)S(1)} async-done(((bf16[8,5,64,384]{3,2,1,0:T(8,128)(2,1)}), bf16[8,5,64,384]{3,2,1,0:T(8,128)(2,1)S(1)}, u32[]{:S(2)}, u32[]{:S(2)}) %all-to-all-start) | async-done | bytes 1966112 | tf_op jit(solution)/shard_map/all_to_all | solution.py:234
  48.1 0.8 compact.1
  48.9 1.2 copy-done.1
  50.1 3.6 %all-to-all-start.1 = ((bf16[8,64,1536]{2,1,0:T(8,128)(2,1)}), bf16[8,64,1536]{2,1,0:T(8,128)(2,1)S(1)}, u32[]{:S(2)}, u32[]{:S(2)}) async-start(bf16[8,64,1536]{2,1,0:T(8,128)(2,1)} %copy-done.1), calls=%async_computation.1 | async-start | bytes 3145728 | tf_op jit(solution)/shard_map/all_to_all | solution.py:243
  53.7 0.0 copy-start.9
  53.7 1.7 %collective-permute-start.6 = (bf16[64,1536]{1,0:T(8,128)(2,1)}, bf16[64,1536]{1,0:T(8,128)(2,1)S(1)}, u32[]{:S(2)}, u32[]{:S(2)}) collective-permute-start(bf16[64,1536]{1,0:T(8,128)(2,1)} %pad_maximum_fusion.1), channel_id=1, source_target_pairs={{0,24},{8,16},{16,8},{24,0},{1,25},{9,17},{17,9},{25,1},{2,26},{10... | collective-permute-start | bytes 589832 | tf_op jit(solution)/shard_map/ppermute | solution.py:209
  55.3 0.9 collective-permute-start.5
  56.3 1.6 %collective-permute-start.4 = (bf16[64,1536]{1,0:T(8,128)(2,1)}, bf16[64,1536]{1,0:T(8,128)(2,1)S(1)}, u32[]{:S(2)}, u32[]{:S(2)}) collective-permute-start(bf16[64,1536]{1,0:T(8,128)(2,1)} %pad_maximum_fusion.1), channel_id=1, source_target_pairs={{0,8},{8,0},{16,24},{24,16},{1,9},{9,1},{17,25},{25,17},{2,10},{10... | collective-permute-start | bytes 589832 | tf_op jit(solution)/shard_map/ppermute | solution.py:209
  57.9 7.4 %collective-permute-done.6 = bf16[64,1536]{1,0:T(8,128)(2,1)S(1)} collective-permute-done((bf16[64,1536]{1,0:T(8,128)(2,1)}, bf16[64,1536]{1,0:T(8,128)(2,1)S(1)}, u32[]{:S(2)}, u32[]{:S(2)}) %collective-permute-start.6) | collective-permute-done | bytes 196640 | tf_op jit(solution)/shard_map/ppermute | solution.py:209
  65.3 0.0 collective-permute-done.5
  65.3 1.8 %collective-permute-done.4 = bf16[64,1536]{1,0:T(8,128)(2,1)S(1)} collective-permute-done((bf16[64,1536]{1,0:T(8,128)(2,1)}, bf16[64,1536]{1,0:T(8,128)(2,1)S(1)}, u32[]{:S(2)}, u32[]{:S(2)}) %collective-permute-start.4) | collective-permute-done | bytes 196640 | tf_op jit(solution)/shard_map/ppermute | solution.py:209
  67.1 1.9 %pad_maximum_fusion.w0_ref = bf16[256,1536]{1,0:T(8,128)(2,1)} fusion(bf16[64,1536]{1,0:T(8,128)(2,1)S(1)} %collective-permute-done.6, bf16[64,1536]{1,0:T(8,128)(2,1)S(1)} %collective-permute-done.5, bf16[64,1536]{1,0:T(8,128)(2,1)S(1)} %collective-permute-done.4, bf16[64,1536]{1,0:T(8,128)(2,1)} %pad_maximum_fusion.1), kind=kLoop, calls=%fused_computation | loop fusion | flops 3145728 | bytes 1572864 | tf_op jit(solution)/shard_map/concatenate | solution.py:244
  69.0 0.1 stack.23.place
  69.1 0.7 copy-done.11
  69.8 5.0 %attn_fwd.1 = (f32[3,4,128,128]{3,2,1,0:T(8,128)S(1)}, bf16[512,384]{1,0:T(8,128)(2,1)S(1)}) custom-call(s32[5]{0:T(128)S(1)} %stack.23.place, f32[12,15]{1,0:T(8,128)S(1)} %copy-done.11, s32[8,384]{1,0:T(8,128)S(1)} %copy-done.9, bf16[8,5,64,384]{3,2,1,0:T(8,128)(2,1)S(1)} %all-to-all-done.recv_ref.qkv_ref), custom_call_target="tpu_custom_call" | custom-call | flops 250000000 | bytes 3158756 | tf_op jit(solution)/shard_map/attn_fwd/pallas_call | solution.py:54
  74.8 0.0 copy-start.2
  74.9 0.9 copy-done.2
  75.7 0.7 copy-done.7
  76.5 1.1 copy-done.3
  77.6 1.0 copy-done.8
  78.6 0.7 copy-done.10
  79.3 3.8 %scores_bwd.1 = (f32[192,1536]{1,0:T(8,128)S(1)}, bf16[192,1536]{1,0:T(8,128)(2,1)S(1)}, bf16[8,64,384]{2,1,0:T(8,128)(2,1)S(1)}, bf16[3,4,128,128]{3,2,1,0:T(8,128)(2,1)S(1)}, f32[8,384]{1,0:T(8,128)S(1)}) custom-call(s32[5]{0:T(128)S(1)} %stack.23.place, s32[8,384]{1,0:T(8,128)S(1)} %copy-done.10, ...), custom_call_target="tpu_custom_call" | custom-call | flops 1500000000 | bytes 8871956 | tf_op jit(solution)/shard_map/scores_bwd/pallas_call | solution.py:54
  83.1 0.6 collective-permute-start.8
  83.7 0.1 collective-permute-start.9
  83.8 1.2 grads.1
  85.0 0.4 collective-permute-done.9.s1
  85.4 0.0 collective-permute-done.8.other_ref
  85.4 1.5 %join.1 = bf16[32,8,1536]{2,1,0:T(8,128)(2,1)} custom-call(f32[192,1536]{1,0:T(8,128)S(1)} %get-tuple-element.58.mine_ref, bf16[192,1536]{1,0:T(8,128)(2,1)S(1)} %collective-permute-done.8.other_ref, f32[8,384]{1,0:T(8,128)S(1)} %get-tuple-element.60.s0, f32[8,384]{1,0:T(8,128)S(1)} %collective-permute-done.9.s1), custom_call_target="tpu_custom_call" | custom-call | bytes 2580480 | tf_op jit(solution)/shard_map/join/pallas_call | solution.py:54
  86.9 7.7 %all-to-all-start.2 = ((bf16[32,8,1536]{2,1,0:T(8,128)(2,1)}), bf16[32,8,1536]{2,1,0:T(8,128)(2,1)S(1)}, u32[]{:S(2)}, u32[]{:S(2)}) async-start(bf16[32,8,1536]{2,1,0:T(8,128)(2,1)} %join.1), calls=%async_computation.2 | async-start | bytes 1572864 | tf_op jit(solution)/shard_map/all_to_all | solution.py:301
  94.6 0.1 collective-permute-start.10
  94.7 1.9 %collective-permute-start.11 = (bf16[3,64,384]{2,1,0:T(8,128)(2,1)S(1)}, bf16[3,64,384]{2,1,0:T(8,128)(2,1)S(1)}, u32[]{:S(2)}, u32[]{:S(2)}) collective-permute-start(bf16[3,64,384]{2,1,0:T(8,128)(2,1)S(1)} %get-tuple-element.74), channel_id=1, source_target_pairs={{0,2},{1,3},{2,0},{3,1},{4,6},{5,7},{6,4},{7,5},{8,10},{9,11},{10,... | collective-permute-start | bytes 442376 | tf_op jit(solution)/shard_map/ppermute | solution.py:209
  96.6 3.1 %collective-permute-start.13 = (bf16[3,64,384]{2,1,0:T(8,128)(2,1)S(1)}, bf16[3,64,384]{2,1,0:T(8,128)(2,1)S(1)}, u32[]{:S(2)}, u32[]{:S(2)}) collective-permute-start(bf16[3,64,384]{2,1,0:T(8,128)(2,1)S(1)} %get-tuple-element.76), channel_id=1, source_target_pairs={{0,4},{1,5},{2,6},{3,7},{4,0},{5,1},{6,2},{7,3},{8,12},{9,13},{10,... | collective-permute-start | bytes 442376 | tf_op jit(solution)/shard_map/ppermute | solution.py:209
  99.7 0.2 collective-permute-start.14
  100.0 2.9 %collective-permute-start.15 = (bf16[3,64,384]{2,1,0:T(8,128)(2,1)S(1)}, bf16[3,64,384]{2,1,0:T(8,128)(2,1)S(1)}, u32[]{:S(2)}, u32[]{:S(2)}) collective-permute-start(bf16[3,64,384]{2,1,0:T(8,128)(2,1)S(1)} %get-tuple-element.78), channel_id=1, source_target_pairs={{0,6},{1,7},{2,4},{3,5},{4,2},{5,3},{6,0},{7,1},{8,14},{9,15},{10,... | collective-permute-start | bytes 442376 | tf_op jit(solution)/shard_map/ppermute | solution.py:209
  102.9 0.0 collective-permute-done.11.refs_2_
  102.9 0.0 collective-permute-start.16
  102.9 1.1 collective-permute-done.12.refs_3_
  104.0 6.4 %collective-permute-done.13.refs_4_ = bf16[3,64,384]{2,1,0:T(8,128)(2,1)S(1)} collective-permute-done((bf16[3,64,384]{2,1,0:T(8,128)(2,1)S(1)}, bf16[3,64,384]{2,1,0:T(8,128)(2,1)S(1)}, u32[]{:S(2)}, u32[]{:S(2)}) %collective-permute-start.13) | collective-permute-done | bytes 147488 | tf_op jit(solution)/shard_map/ppermute | solution.py:209
  110.4 1.8 %collective-permute-done.14.refs_5_ = bf16[3,64,384]{2,1,0:T(8,128)(2,1)S(1)} collective-permute-done((bf16[3,64,384]{2,1,0:T(8,128)(2,1)S(1)}, bf16[3,64,384]{2,1,0:T(8,128)(2,1)S(1)}, u32[]{:S(2)}, u32[]{:S(2)}) %collective-permute-start.14) | collective-permute-done | bytes 147488 | tf_op jit(solution)/shard_map/ppermute | solution.py:209
  112.2 2.0 %collective-permute-done.15.refs_6_ = bf16[3,64,384]{2,1,0:T(8,128)(2,1)S(1)} collective-permute-done((bf16[3,64,384]{2,1,0:T(8,128)(2,1)S(1)}, bf16[3,64,384]{2,1,0:T(8,128)(2,1)S(1)}, u32[]{:S(2)}, u32[]{:S(2)}) %collective-permute-start.15) | collective-permute-done | bytes 147488 | tf_op jit(solution)/shard_map/ppermute | solution.py:209
  114.2 2.0 %collective-permute-done.16.refs_7_ = bf16[3,64,384]{2,1,0:T(8,128)(2,1)S(1)} collective-permute-done((bf16[3,64,384]{2,1,0:T(8,128)(2,1)S(1)}, bf16[3,64,384]{2,1,0:T(8,128)(2,1)S(1)}, u32[]{:S(2)}, u32[]{:S(2)}) %collective-permute-start.16) | collective-permute-done | bytes 147488 | tf_op jit(solution)/shard_map/ppermute | solution.py:209
  116.1 1.4 %all-to-all-done.2.in_ref = bf16[32,8,1536]{2,1,0:T(8,128)(2,1)S(1)} async-done(((bf16[32,8,1536]{2,1,0:T(8,128)(2,1)}), bf16[32,8,1536]{2,1,0:T(8,128)(2,1)S(1)}, u32[]{:S(2)}, u32[]{:S(2)}) %all-to-all-start.2) | async-done | bytes 786464 | tf_op jit(solution)/shard_map/all_to_all | solution.py:301
  117.6 0.6 total.1
  118.2 0.7 collective-permute-start.17
  118.9 0.6 broadcast_in_dim.3
  119.5 9.4 %all-to-all-start.3 = ((f32[4,16,128]{2,1,0:T(8,128)}), f32[4,16,128]{2,1,0:T(8,128)S(1)}, u32[]{:S(2)}, u32[]{:S(2)}) async-start(f32[4,16,128]{2,1,0:T(8,128)} %broadcast_in_dim.3), calls=%async_computation.3 | async-start | bytes 65536 | tf_op jit(solution)/shard_map/all_to_all | solution.py:306
  128.9 1.8 %unpack.1 = bf16[3,128,1536]{2,1,0:T(8,128)(2,1)} custom-call(s32[5]{0:T(128)S(1)} %stack.23.place, bf16[3,64,384]{2,1,0:T(8,128)(2,1)S(1)} %get-tuple-element.82.refs_0_, bf16[3,64,384]{2,1,0:T(8,128)(2,1)S(1)} %collective-permute-done.10.refs_1_, bf16[3,64,384]{2,1,0:T(8,128)(2,1)S(1)} %collective-permute-done.11.refs_2_, ...), custom_call_target="tpu_custom_call" | custom-call | bytes 2359316 | tf_op jit(solution)/shard_map/unpack/pallas_call | solution.py:54
  130.7 3.7 %all-to-all-done.3.off_ref = f32[4,16,128]{2,1,0:T(8,128)S(1)} async-done(((f32[4,16,128]{2,1,0:T(8,128)}), f32[4,16,128]{2,1,0:T(8,128)S(1)}, u32[]{:S(2)}, u32[]{:S(2)}) %all-to-all-start.3) | async-done | bytes 32800 | tf_op jit(solution)/shard_map/all_to_all | solution.py:306
  134.4 0.6 last.1
  (22 shorter events, 0.1 us)
Async XLA Ops:
  1.4 6.5 %collective-permute-start.1 = (bf16[8,1536]{1,0:T(8,128)(2,1)S(1)}, bf16[8,1536]{1,0:T(8,128)(2,1)S(1)}, u32[]{:S(2)}, u32[]{:S(2)}) collective-permute-start(bf16[8,1536]{1,0:T(8,128)(2,1)S(1)} %pad.4), channel_id=1, source_target_pairs={{0,32},{2,0},{4,96},{6,64},{32,160},{34,128},{36,224},{38,192},{64... | collective-permute-start | bytes 73736 | tf_op jit(solution)/shard_map/ppermute | solution.py:232
  3.3 4.6 %collective-permute-start = (bf16[8,1536]{1,0:T(8,128)(2,1)S(1)}, bf16[8,1536]{1,0:T(8,128)(2,1)S(1)}, u32[]{:S(2)}, u32[]{:S(2)}) collective-permute-start(bf16[8,1536]{1,0:T(8,128)(2,1)S(1)} %pad.4), channel_id=1, source_target_pairs={{0,0},{2,32},{4,64},{6,96},{32,128},{34,160},{36,192},{38,224},{64... | collective-permute-start | bytes 73736 | tf_op jit(solution)/shard_map/ppermute | solution.py:232
  4.0 1.3 copy-start.5
  5.2 1.1 copy-start.6
  6.5 1.3 copy-start
  7.8 40.2 %copy-start.12 = (s32[1,8]{1,0:T(1,128)S(1)}, s32[1,8]{1,0:T(1,128)}, u32[]{:S(2)}) copy-start(s32[1,8]{1,0:T(1,128)} %sizes.1) | copy-start | bytes 100
  7.9 40.2 %all-to-all-start = ((bf16[8,5,64,384]{3,2,1,0:T(8,128)(2,1)}), bf16[8,5,64,384]{3,2,1,0:T(8,128)(2,1)S(1)}, u32[]{:S(2)}, u32[]{:S(2)}) async-start(bf16[8,5,64,384]{3,2,1,0:T(8,128)(2,1)} %copy-done), calls=%async_computation | async-start | bytes 3932160 | tf_op jit(solution)/shard_map/all_to_all | solution.py:234
  22.3 5.1 %collective-permute-start.2 = (bf16[16,1536]{1,0:T(8,128)(2,1)S(1)}, bf16[16,1536]{1,0:T(8,128)(2,1)S(1)}, u32[]{:S(2)}, u32[]{:S(2)}) collective-permute-start(bf16[16,1536]{1,0:T(8,128)(2,1)S(1)} %pad_maximum_fusion.3), channel_id=1, source_target_pairs={{0,64},{32,96},{64,0},{96,32},{128,192},{160,224},{192,128},{224,1... | collective-permute-start | bytes 147464 | tf_op jit(solution)/shard_map/ppermute | solution.py:209
  27.4 9.3 %collective-permute-start.3 = (bf16[32,1536]{1,0:T(8,128)(2,1)S(1)}, bf16[32,1536]{1,0:T(8,128)(2,1)S(1)}, u32[]{:S(2)}, u32[]{:S(2)}) collective-permute-start(bf16[32,1536]{1,0:T(8,128)(2,1)S(1)} %pad_maximum_fusion.2), channel_id=1, source_target_pairs={{0,128},{32,160},{64,192},{96,224},{128,0},{160,32},{192,64},{224,... | collective-permute-start | bytes 294920 | tf_op jit(solution)/shard_map/ppermute | solution.py:209
  48.9 1.2 copy-start.1
  50.1 26.4 %all-to-all-start.1 = ((bf16[8,64,1536]{2,1,0:T(8,128)(2,1)}), bf16[8,64,1536]{2,1,0:T(8,128)(2,1)S(1)}, u32[]{:S(2)}, u32[]{:S(2)}) async-start(bf16[8,64,1536]{2,1,0:T(8,128)(2,1)} %copy-done.1), calls=%async_computation.1 | async-start | bytes 3145728 | tf_op jit(solution)/shard_map/all_to_all | solution.py:243
  53.7 15.4 %copy-start.9 = (s32[8,384]{1,0:T(8,128)S(1)}, s32[8,384]{1,0:T(8,128)}, u32[]{:S(2)}) copy-start(s32[8,384]{1,0:T(8,128)} %constant.25.clone.leave_ref) | copy-start | bytes 36868
  53.7 11.6 %collective-permute-start.6 = (bf16[64,1536]{1,0:T(8,128)(2,1)}, bf16[64,1536]{1,0:T(8,128)(2,1)S(1)}, u32[]{:S(2)}, u32[]{:S(2)}) collective-permute-start(bf16[64,1536]{1,0:T(8,128)(2,1)} %pad_maximum_fusion.1), channel_id=1, source_target_pairs={{0,24},{8,16},{16,8},{24,0},{1,25},{9,17},{17,9},{25,1},{2,26},{10... | collective-permute-start | bytes 589832 | tf_op jit(solution)/shard_map/ppermute | solution.py:209
  55.3 10.0 %collective-permute-start.5 = (bf16[64,1536]{1,0:T(8,128)(2,1)}, bf16[64,1536]{1,0:T(8,128)(2,1)S(1)}, u32[]{:S(2)}, u32[]{:S(2)}) collective-permute-start(bf16[64,1536]{1,0:T(8,128)(2,1)} %pad_maximum_fusion.1), channel_id=1, source_target_pairs={{0,16},{8,24},{16,0},{24,8},{1,17},{9,25},{17,1},{25,9},{2,18},{10... | collective-permute-start | bytes 589832 | tf_op jit(solution)/shard_map/ppermute | solution.py:209
  56.3 10.8 %collective-permute-start.4 = (bf16[64,1536]{1,0:T(8,128)(2,1)}, bf16[64,1536]{1,0:T(8,128)(2,1)S(1)}, u32[]{:S(2)}, u32[]{:S(2)}) collective-permute-start(bf16[64,1536]{1,0:T(8,128)(2,1)} %pad_maximum_fusion.1), channel_id=1, source_target_pairs={{0,8},{8,0},{16,24},{24,16},{1,9},{9,1},{17,25},{25,17},{2,10},{10... | collective-permute-start | bytes 589832 | tf_op jit(solution)/shard_map/ppermute | solution.py:209
  69.0 7.5 %collective-permute-start.7 = (bf16[256,1536]{1,0:T(8,128)(2,1)}, bf16[256,1536]{1,0:T(8,128)(2,1)}, u32[]{:S(2)}, u32[]{:S(2)}) collective-permute-start(bf16[256,1536]{1,0:T(8,128)(2,1)} %pad_maximum_fusion.w0_ref), channel_id=1, source_target_pairs={{0,1},{1,0},{2,3},{3,2},{4,5},{5,4},{6,7},{7,6},{8,9},{9,8},{10,11... | collective-permute-start | bytes 2359304 | tf_op jit(solution)/shard_map/ppermute | solution.py:209
  69.1 0.7 copy-start.11
  74.8 0.9 copy-start.2
  75.7 0.7 copy-start.7
  76.5 1.1 copy-start.3
  77.6 1.0 copy-start.8
  78.6 0.7 copy-start.10
  79.3 4.5 %copy-start.4 = (f32[3,4,128,128]{3,2,1,0:T(8,128)S(1)}, f32[3,4,128,128]{3,2,1,0:T(8,128)}, u32[]{:S(2)}) copy-start(f32[3,4,128,128]{3,2,1,0:T(8,128)} %copy-done.2) | copy-start | bytes 2359300
  83.1 2.2 %collective-permute-start.8 = (bf16[192,1536]{1,0:T(8,128)(2,1)S(1)}, bf16[192,1536]{1,0:T(8,128)(2,1)S(1)}, u32[]{:S(2)}, u32[]{:S(2)}) collective-permute-start(bf16[192,1536]{1,0:T(8,128)(2,1)S(1)} %get-tuple-element.59), channel_id=1, source_target_pairs={{0,1},{1,0},{2,3},{3,2},{4,5},{5,4},{6,7},{7,6},{8,9},{9,8},{10,11... | collective-permute-start | bytes 1769480 | tf_op jit(solution)/shard_map/ppermute | solution.py:209
  83.7 1.6 %collective-permute-start.9 = (f32[8,384]{1,0:T(8,128)S(1)}, f32[8,384]{1,0:T(8,128)S(1)}, u32[]{:S(2)}, u32[]{:S(2)}) collective-permute-start(f32[8,384]{1,0:T(8,128)S(1)} %get-tuple-element.60.s0), channel_id=1, source_target_pairs={{0,1},{1,0},{2,3},{3,2},{4,5},{5,4},{6,7},{7,6},{8,9},{9,8},{10,11... | collective-permute-start | bytes 36872 | tf_op jit(solution)/shard_map/ppermute | solution.py:209
  86.9 30.7 %all-to-all-start.2 = ((bf16[32,8,1536]{2,1,0:T(8,128)(2,1)}), bf16[32,8,1536]{2,1,0:T(8,128)(2,1)S(1)}, u32[]{:S(2)}, u32[]{:S(2)}) async-start(bf16[32,8,1536]{2,1,0:T(8,128)(2,1)} %join.1), calls=%async_computation.2 | async-start | bytes 1572864 | tf_op jit(solution)/shard_map/all_to_all | solution.py:301
  94.6 5.4 %collective-permute-start.10 = (bf16[3,64,384]{2,1,0:T(8,128)(2,1)S(1)}, bf16[3,64,384]{2,1,0:T(8,128)(2,1)S(1)}, u32[]{:S(2)}, u32[]{:S(2)}) collective-permute-start(bf16[3,64,384]{2,1,0:T(8,128)(2,1)S(1)} %get-tuple-element.73), channel_id=1, source_target_pairs={{0,1},{1,0},{2,3},{3,2},{4,5},{5,4},{6,7},{7,6},{8,9},{9,8},{10,11... | collective-permute-start | bytes 442376 | tf_op jit(solution)/shard_map/ppermute | solution.py:209
  94.7 8.2 %collective-permute-start.11 = (bf16[3,64,384]{2,1,0:T(8,128)(2,1)S(1)}, bf16[3,64,384]{2,1,0:T(8,128)(2,1)S(1)}, u32[]{:S(2)}, u32[]{:S(2)}) collective-permute-start(bf16[3,64,384]{2,1,0:T(8,128)(2,1)S(1)} %get-tuple-element.74), channel_id=1, source_target_pairs={{0,2},{1,3},{2,0},{3,1},{4,6},{5,7},{6,4},{7,5},{8,10},{9,11},{10,... | collective-permute-start | bytes 442376 | tf_op jit(solution)/shard_map/ppermute | solution.py:209
  96.6 7.4 %collective-permute-start.12 = (bf16[3,64,384]{2,1,0:T(8,128)(2,1)S(1)}, bf16[3,64,384]{2,1,0:T(8,128)(2,1)S(1)}, u32[]{:S(2)}, u32[]{:S(2)}) collective-permute-start(bf16[3,64,384]{2,1,0:T(8,128)(2,1)S(1)} %get-tuple-element.75), channel_id=1, source_target_pairs={{0,3},{1,2},{2,1},{3,0},{4,7},{5,6},{6,5},{7,4},{8,11},{9,10},{10,... | collective-permute-start | bytes 442376 | tf_op jit(solution)/shard_map/ppermute | solution.py:209
  96.6 13.8 %collective-permute-start.13 = (bf16[3,64,384]{2,1,0:T(8,128)(2,1)S(1)}, bf16[3,64,384]{2,1,0:T(8,128)(2,1)S(1)}, u32[]{:S(2)}, u32[]{:S(2)}) collective-permute-start(bf16[3,64,384]{2,1,0:T(8,128)(2,1)S(1)} %get-tuple-element.76), channel_id=1, source_target_pairs={{0,4},{1,5},{2,6},{3,7},{4,0},{5,1},{6,2},{7,3},{8,12},{9,13},{10,... | collective-permute-start | bytes 442376 | tf_op jit(solution)/shard_map/ppermute | solution.py:209
  99.7 12.4 %collective-permute-start.14 = (bf16[3,64,384]{2,1,0:T(8,128)(2,1)S(1)}, bf16[3,64,384]{2,1,0:T(8,128)(2,1)S(1)}, u32[]{:S(2)}, u32[]{:S(2)}) collective-permute-start(bf16[3,64,384]{2,1,0:T(8,128)(2,1)S(1)} %get-tuple-element.77), channel_id=1, source_target_pairs={{0,5},{1,4},{2,7},{3,6},{4,1},{5,0},{6,3},{7,2},{8,13},{9,12},{10,... | collective-permute-start | bytes 442376 | tf_op jit(solution)/shard_map/ppermute | solution.py:209
  100.0 14.2 %collective-permute-start.15 = (bf16[3,64,384]{2,1,0:T(8,128)(2,1)S(1)}, bf16[3,64,384]{2,1,0:T(8,128)(2,1)S(1)}, u32[]{:S(2)}, u32[]{:S(2)}) collective-permute-start(bf16[3,64,384]{2,1,0:T(8,128)(2,1)S(1)} %get-tuple-element.78), channel_id=1, source_target_pairs={{0,6},{1,7},{2,4},{3,5},{4,2},{5,3},{6,0},{7,1},{8,14},{9,15},{10,... | collective-permute-start | bytes 442376 | tf_op jit(solution)/shard_map/ppermute | solution.py:209
  102.9 13.3 %collective-permute-start.16 = (bf16[3,64,384]{2,1,0:T(8,128)(2,1)S(1)}, bf16[3,64,384]{2,1,0:T(8,128)(2,1)S(1)}, u32[]{:S(2)}, u32[]{:S(2)}) collective-permute-start(bf16[3,64,384]{2,1,0:T(8,128)(2,1)S(1)} %get-tuple-element.79), channel_id=1, source_target_pairs={{0,7},{1,6},{2,5},{3,4},{4,3},{5,2},{6,1},{7,0},{8,15},{9,14},{10,... | collective-permute-start | bytes 442376 | tf_op jit(solution)/shard_map/ppermute | solution.py:209
  118.2 12.5 %collective-permute-start.17 = (f32[8,1536]{1,0:T(8,128)S(1)}, f32[8,1536]{1,0:T(8,128)S(1)}, u32[]{:S(2)}, u32[]{:S(2)}) collective-permute-start(f32[8,1536]{1,0:T(8,128)S(1)} %get-tuple-element.81), channel_id=1, source_target_pairs={{0,0},{32,2},{64,4},{96,6},{128,32},{160,34},{192,36},{224,38},{2,... | collective-permute-start | bytes 147464 | tf_op jit(solution)/shard_map/ppermute | solution.py:305
  119.5 14.9 %all-to-all-start.3 = ((f32[4,16,128]{2,1,0:T(8,128)}), f32[4,16,128]{2,1,0:T(8,128)S(1)}, u32[]{:S(2)}, u32[]{:S(2)}) async-start(f32[4,16,128]{2,1,0:T(8,128)} %broadcast_in_dim.3), calls=%async_computation.3 | async-start | bytes 65536 | tf_op jit(solution)/shard_map/all_to_all | solution.py:306

commit v7 on v6

--- a/solution.py
+++ b/solution.py
@@ -63,18 +63,27 @@
     )(*ins)
 
 
-def pack_kernel(qkv_ref, cot_ref, out_ref):
+def stack_kernel(*refs):
+    out_ref, row = refs[-1], 0
+    for ref in refs[:-1]:
+        out_ref[row : row + HALF] = ref[...]
+        row += HALF
+
+
+def stack(parts):
+    return call(stack_kernel, "stack", [((len(parts) * HALF, DW), bf)], *parts)[0]
+
+
+def pack_kernel(qkv_ref, out_ref):
     for d in range(F):
         r, c = d % C * HALF, d // C * COLS
-        out_ref[d, :3] = qkv_ref[:, r : r + HALF, c : c + COLS]
-    for j in range(X):
-        r = j % 2 * CAP
-        out_ref[:, 3 + j // 2, r : r + CAP, :] = cot_ref[:, :, j * COLS : (j + 1) * COLS]
-
-
-def compact_kernel(sizes, recv_ref, out_ref):
+        out_ref[d] = qkv_ref[:, r : r + HALF, c : c + COLS]
+
+
+def compact_kernel(place, sizes, cot_ref, same_ref, other_ref):
     shape = (POS, F * CAP)
-    pos, col = iota(shape, 0), iota(shape, 1)
+    row, col = iota(shape, 0), iota(shape, 1)
+    pos = row ^ (place[CORE] * HALF)
     start = jnp.int32(0)
     picked = jnp.full(shape, -1, jnp.int32)
     for j in range(F):
@@ -83,12 +92,9 @@
         picked = jnp.where(inside, slot + start, picked)
         start = start + sizes[0, j]
     hot = (picked == pos).astype(f32).astype(bf)
-    for j in range(X):
-        slots = recv_ref[:, 3 + j // 2, (j % 2) * CAP : (j % 2 + 1) * CAP, :]
-        up = dot(hot, slots.reshape(F * CAP, COLS), NN).astype(bf)
-        for d in range(F):
-            r = (d % C) * HALF
-            out_ref[d, :, j * COLS : (j + 1) * COLS] = up[r : r + HALF]
+    up = dot(hot, cot_ref[...].reshape(F * CAP, DW), NN).astype(bf)
+    same_ref[...] = up[:HALF]
+    other_ref[...] = up[HALF:]
 
 
 def block(ref, i, b, h):
@@ -116,8 +122,14 @@
     mixed_ref[...] = dot(raw_ref[...].reshape(F * HALF, COLS), order, NN).astype(bf)
 
 
-def score_kernel(place, rows_ref, recv_ref, probs_ref, mixed_ref, up_ref, w0_ref, w1_ref, *outs):
-    mine_ref, other_ref, dm_ref, ds_ref, sums_ref = outs
+def score_kernel(place, rows_ref, recv_ref, probs_ref, mixed_ref, u0, u1, u3, q1, q3, w0_ref, w1_ref, *outs):
+    mine_ref, other_ref, dm_ref, ds_ref, sums_ref, up_ref = outs
+    halves = [(0, u0[:HALF], u0[HALF:]), (1, u1[:HALF], u1[HALF:])]
+    halves += [(2, q1[...], q3[...]), (3, u3[:HALF], u3[HALF:])]
+    for k, same, other in halves:
+        chip = (place[XI] ^ k) * C
+        up_ref[chip + place[CORE]] = same
+        up_ref[chip + 1 - place[CORE]] = other
     up = up_ref[...].reshape(F * HALF, DW)
     gw = dot(mixed_ref[...], up, TN)
     mine_ref[...] = gw[: COLS // 2]
@@ -177,31 +189,38 @@
     gw = mine_ref[...] + other_ref[...].astype(f32)
     hot = ((iota((COLS, 128), 0) >> 4) == iota((COLS, 128), 1)).astype(f32)
     b = dot(s0[...] + s1[...], hot, NN, precision=lax.Precision.HIGHEST)
-    pad = jnp.zeros((1, DW - F * 128), f32)
-    flat = [jnp.concatenate([x[f : f + 1] for f in range(F)] + [pad], axis=1) for x in split(b)]
+    ride = jnp.concatenate([x[:, :64] for x in split(b)], axis=1)
     for d in range(Z * Y):
-        out_ref[d] = jnp.concatenate([gw[6 * d : 6 * d + 6]] + flat, axis=0).astype(bf)
+        part = gw[6 * d : 6 * d + 6]
+        ends = [
+            jnp.concatenate([part[r + i : r + i + 1, 1152:] for i in range(3)], axis=1) for r in (0, 3)
+        ]
+        part = jnp.concatenate([part[:, :1152]] + ends, axis=0)
+        out_ref[d] = jnp.concatenate([part, ride], axis=1).astype(bf)
 
 
 def total_kernel(in_ref, sum_ref, off_ref):
     total = jnp.sum(in_ref[...].astype(f32), axis=0)
-    sum_ref[...] = total
-    flat = total[6:7] + total[7:8]
-    head, lane = iota((16, 128), 0) % HL, iota((16, 128), 1)
-    g, o = iota((128, 128), 0) & 7, iota((128, 128), 1)
+    sum_ref[:, :1152] = total[:, :1152]
+    for r in range(6):
+        sum_ref[r : r + 1, 1152:] = total[6 + r // 3 : 7 + r // 3, r % 3 * 384 : (r % 3 + 1) * 384]
+    sum_ref[6:, 1152:] = jnp.zeros((2, 384), f32)
+    sums = total[:, 1152:1216] + total[:, 1216:]
+    head, lane = iota((16, 64), 0) % HL, iota((16, 64), 1)
+    g, o = iota((64, 128), 0) & 7, iota((64, 128), 1)
     out = jnp.zeros((16, 128), f32)
     for f in range(F):
-        row = jnp.where((lane >> 3) == head, flat[:, 128 * f : 128 * (f + 1)], 0.0)
+        row = jnp.where((lane >> 3) == head, sums[f : f + 1], 0.0)
         out = out + dot(row, (g - f + 7 == o).astype(f32), NN, precision=lax.Precision.HIGHEST)
     off_ref[...] = out
 
 
-def last_kernel(home_ref, off_ref, gw_ref, bias_ref):
+def last_kernel(place, home_ref, o0, o1, o2, o3, gw_ref, bias_ref):
     gw_ref[...] = home_ref[:6]
     row = iota((16, 128), 0) // HL
     out = jnp.zeros((16, 128), f32)
-    for c in range(X):
-        out = out + jnp.where(row == c, off_ref[c], 0.0)
+    for k, o in enumerate((o0, o1, o2, o3)):
+        out = out + jnp.where(row == (place[XI] ^ k), o[...], 0.0)
     bias_ref[...] = out[:12, :15]
 
 
@@ -213,14 +232,6 @@
     xi, yi, zi, core = (lax.axis_index(a) for a in ("x", "y", "z", "core"))
     place = jnp.stack([core, yi, zi, xi, xi * C + core]).astype(jnp.int32)
 
-    block5 = ((F, 5, HALF, COLS), bf)
-    (packed,) = call(
-        pack_kernel,
-        "pack",
-        [block5],
-        qkv_time[:, 0, 0],
-        cot_out[0, 0],
-    )
     there = [
         ((2 * c + z0) * X + x, (z0 * X + x) * X + c)
         for c in range(X)
@@ -230,19 +241,35 @@
     near = [(a, b ^ X) for a, b in there]
     rows8 = jnp.pad(w_out, ((0, 2), (0, 0)))
     held = [lax.ppermute(rows8, ("z", "x"), p) for p in (there, near)]
-    packed, *held = lax.optimization_barrier((packed, *held))
-    recv = lax.all_to_all(packed, SEQ, 0, 0, tiled=True)
+    cot, *held = lax.optimization_barrier((cot_out[0, 0], *held))
+
+    cot = lax.all_to_all(cot, SEQ, 0, 0, tiled=True)
+    (packed,) = call(pack_kernel, "pack", [((F, 3, HALF, COLS), bf)], qkv_time[:, 0, 0])
     held = jnp.concatenate(held)
     held = jnp.concatenate([held, hop(held, "z", 2, Z)])
     held = jnp.concatenate([held, hop(held, "z", 4, Z)])
-
-    (up,) = call(
-        compact_kernel, "compact", [((F, HALF, DW), bf)], shard_sizes, recv, smem=1, flops=100_000_000
-    )
-    held, up = lax.optimization_barrier((held, up))
-    up = lax.all_to_all(up, SEQ, 0, 0, tiled=True)
-    held = jnp.concatenate([held] + [hop(held, "y", k, Y) for k in range(1, Y)])
-    recv, held = lax.optimization_barrier((recv, held))
+    packed, held = lax.optimization_barrier((packed, held))
+    recv = lax.all_to_all(packed, SEQ, 0, 0, tiled=True)
+
+    same, other = call(
+        compact_kernel,
+        "compact",
+        [((HALF, DW), bf)] * 2,
+        place,
+        shard_sizes,
+        cot,
+        smem=2,
+        flops=100_000_000,
+    )
+    u0 = stack([same, hop(other, "core", 1, C)])
+    held, u0 = lax.optimization_barrier((held, u0))
+    u1, u3 = hop(u0, "x", 1, X), hop(u0, "x", 3, X)
+    held = [held] + [hop(held, "y", k, Y) for k in range(1, Y)]
+
+    far = u3[:HALF], u1[HALF:]
+    held, far = lax.optimization_barrier((held, far))
+    q1, q3 = hop(far[0], "x", 1, X), hop(far[1], "x", 3, X)
+    held = stack(held)
     held2 = hop(held, "core", 1, C)
 
     probs, mixed = call(
@@ -255,7 +282,7 @@
         recv,
         smem=2,
         scratch=[pltpu.VMEM((F, HALF, COLS), bf)],
-        flops=250_000_000,
+        flops=20_000_000_000,
     )
 
     mine, theirs, dm, ds, sums = call(
@@ -273,10 +300,15 @@
         recv,
         probs,
         mixed,
-        up,
+        u0,
+        u1,
+        u3,
+        q1,
+        q3,
         held,
         held2,
         smem=1,
+        scratch=[pltpu.VMEM((F, HALF, DW), bf)],
         flops=1_500_000_000,
     )
     theirs = hop(theirs, "core", 1, C)
@@ -296,14 +328,14 @@
         flops=150_000_000,
     )
 
-    (msgs,) = call(join_kernel, "join", [((Z * Y, 8, DW), bf)], mine, theirs, sums, sums2)
+    (msgs,) = call(join_kernel, "join", [((Z * Y, 8, 1280), bf)], mine, theirs, sums, sums2)
     msgs, *pieces = lax.optimization_barrier((msgs, *pieces))
     msgs = lax.all_to_all(msgs, ("z", "y"), 0, 0, tiled=True)
     pieces = pieces[:1] + [hop(p, SEQ, k, F) for k, p in enumerate(pieces[1:], 1)]
-    msgs, *pieces = lax.optimization_barrier((msgs, *pieces))
+    msgs, *pieces[1:6] = lax.optimization_barrier((msgs, *pieces[1:6]))
     total, off = call(total_kernel, "total", [((8, DW), f32), ((16, 128), f32)], msgs)
     home = lax.ppermute(total, ("z", "x"), [(b, a) for a, b in there])
-    off = lax.all_to_all(jnp.broadcast_to(off, (X, 16, 128)), "x", 0, 0, tiled=True)
+    offs = [off] + [hop(off, "x", k, X) for k in range(1, X)]
     (grad_qkv,) = call(
         unpack_kernel,
         "unpack",
@@ -316,7 +348,7 @@
     grad_qkv = grad_qkv.reshape(3, 1, 1, POS, DW)
     home, grad_qkv = lax.optimization_barrier((home, grad_qkv))
     grad_w_out, grad_bias = call(
-        last_kernel, "last", [((6, DW), f32), ((12, 15), f32)], home, off
+        last_kernel, "last", [((6, DW), f32), ((12, 15), f32)], place, home, *offs, smem=1
     )
     return grad_qkv, grad_bias, grad_w_out
 

time: 136 us -> 126 us (0.926)
  the two profiles are of different devices: /device:TPU:8 before, /device:TPU:32 now
where the time goes in v7:
time: 126 us; the launch traced here: 125 us
  starting transfers between devices  57.2 us (45%)
  waiting for transfers between devices  47 us (37%)
  Pallas kernels  16.9 us (13%)
  local copies, waits for them, and re-layouts  3.03 us (2%)
    ppermute x23, waiting for transfers between devices, hop(): return lax.ppermute(x, axis, [(i, i ^ k) for i in range(n)])  39.5 us
    ppermute x23, starting transfers between devices, hop(): return lax.ppermute(x, axis, [(i, i ^ k) for i in range(n)])  25.3 us
    pallas_call x11, Pallas kernels, call(): pl.pallas_call(body, out_shape=tuple((jax.ShapeDtypeStruct(s, d) for s, d...  16.9 us
    ppermute x2, starting transfers between devices, per_device(): held = [lax.ppermute(rows8, ('z', 'x'), p) for p in (there, near)]  9.39 us
    all_to_all x1, starting transfers between devices, per_device(): cot = lax.all_to_all(cot, SEQ, 0, 0, tiled=True)  8.02 us
    all_to_all x1, starting transfers between devices, per_device(): msgs = lax.all_to_all(msgs, ('z', 'y'), 0, 0, tiled=True)  7.65 us
    all_to_all x1, starting transfers between devices, per_device(): recv = lax.all_to_all(packed, SEQ, 0, 0, tiled=True)  4.32 us
    all_to_all x1, waiting for transfers between devices, per_device(): msgs = lax.all_to_all(msgs, ('z', 'y'), 0, 0, tiled=True)  3.73 us
  transfers between devices with their start and end apart: 29, of which 14 were waited for; matrix products, arithmetic and copies ran while one was open for 1% of the time, Pallas kernels for 8%

profile of v7, /device:TPU:32, one launch (start us, length us, event | category | flops | bytes accessed | tf_op | source)
XLA Modules:
  0.0 124.9 jit_solution(6105340012750779244)
XLA Ops:
  0.6 0.8 pad.4
  1.5 6.3 %collective-permute-start.1 = (bf16[8,1536]{1,0:T(8,128)(2,1)S(1)}, bf16[8,1536]{1,0:T(8,128)(2,1)S(1)}, u32[]{:S(2)}, u32[]{:S(2)}) collective-permute-start(bf16[8,1536]{1,0:T(8,128)(2,1)S(1)} %pad.4), channel_id=1, source_target_pairs={{0,32},{2,0},{4,96},{6,64},{32,160},{34,128},{36,224},{38,192},{64... | collective-permute-start | bytes 73736 | tf_op jit(solution)/shard_map/ppermute | solution.py:243
  7.8 3.1 %collective-permute-start = (bf16[8,1536]{1,0:T(8,128)(2,1)S(1)}, bf16[8,1536]{1,0:T(8,128)(2,1)S(1)}, u32[]{:S(2)}, u32[]{:S(2)}) collective-permute-start(bf16[8,1536]{1,0:T(8,128)(2,1)S(1)} %pad.4), channel_id=1, source_target_pairs={{0,0},{2,32},{4,64},{6,96},{32,128},{34,160},{36,192},{38,224},{64... | collective-permute-start | bytes 73736 | tf_op jit(solution)/shard_map/ppermute | solution.py:243
  10.9 0.0 collective-permute-done.1
  10.9 3.5 %collective-permute-done = bf16[8,1536]{1,0:T(8,128)(2,1)S(1)} collective-permute-done((bf16[8,1536]{1,0:T(8,128)(2,1)S(1)}, bf16[8,1536]{1,0:T(8,128)(2,1)S(1)}, u32[]{:S(2)}, u32[]{:S(2)}) %collective-permute-start) | collective-permute-done | bytes 24608 | tf_op jit(solution)/shard_map/ppermute | solution.py:243
  14.4 8.0 %all-to-all-start.1 = ((bf16[8,32,1536]{2,1,0:T(8,128)(2,1)}), bf16[8,32,1536]{2,1,0:T(8,128)(2,1)S(1)}, u32[]{:S(2)}, u32[]{:S(2)}) async-start(bf16[8,32,1536]{2,1,0:T(8,128)(2,1)} %bitcast.11), calls=%async_computation.1 | async-start | bytes 1572864 | tf_op jit(solution)/shard_map/all_to_all | solution.py:246
  22.4 0.1 collective-permute-start.2
  22.5 5.0 %collective-permute-done.2 = bf16[16,1536]{1,0:T(8,128)(2,1)S(1)} collective-permute-done((bf16[16,1536]{1,0:T(8,128)(2,1)S(1)}, bf16[16,1536]{1,0:T(8,128)(2,1)S(1)}, u32[]{:S(2)}, u32[]{:S(2)}) %collective-permute-start.2) | collective-permute-done | bytes 49184 | tf_op jit(solution)/shard_map/ppermute | solution.py:228
  27.5 2.5 %collective-permute-start.3 = (bf16[32,1536]{1,0:T(8,128)(2,1)S(1)}, bf16[32,1536]{1,0:T(8,128)(2,1)S(1)}, u32[]{:S(2)}, u32[]{:S(2)}) collective-permute-start(bf16[32,1536]{1,0:T(8,128)(2,1)S(1)} %pad_maximum_fusion.1), channel_id=1, source_target_pairs={{0,128},{32,160},{64,192},{96,224},{128,0},{160,32},{192,64},{224,... | collective-permute-start | bytes 294920 | tf_op jit(solution)/shard_map/ppermute | solution.py:228
  30.1 1.1 pack.1
  31.2 6.3 %collective-permute-done.3 = bf16[32,1536]{1,0:T(8,128)(2,1)S(1)} collective-permute-done((bf16[32,1536]{1,0:T(8,128)(2,1)S(1)}, bf16[32,1536]{1,0:T(8,128)(2,1)S(1)}, u32[]{:S(2)}, u32[]{:S(2)}) %collective-permute-start.3) | collective-permute-done | bytes 98336 | tf_op jit(solution)/shard_map/ppermute | solution.py:228
  37.5 0.0 copy-start.1
  37.5 0.0 all-to-all-done.1.cot_ref
  37.5 4.3 %all-to-all-start = ((bf16[8,3,64,384]{3,2,1,0:T(8,128)(2,1)}), bf16[8,3,64,384]{3,2,1,0:T(8,128)(2,1)S(1)}, u32[]{:S(2)}, u32[]{:S(2)}) async-start(bf16[8,3,64,384]{3,2,1,0:T(8,128)(2,1)} %pack.1), calls=%async_computation | async-start | bytes 2359296 | tf_op jit(solution)/shard_map/all_to_all | solution.py:252
  41.8 0.1 stack.25.place
  41.9 0.8 compact.1
  42.7 0.6 collective-permute-start.4
  43.3 1.1 collective-permute-done.4.refs_1_
  44.4 0.0 copy-start.2
  44.4 3.2 %collective-permute-start.6 = (bf16[128,1536]{1,0:T(8,128)(2,1)S(1)}, bf16[128,1536]{1,0:T(8,128)(2,1)S(1)}, u32[]{:S(2)}, u32[]{:S(2)}) collective-permute-start(bf16[128,1536]{1,0:T(8,128)(2,1)S(1)} %stack.26.u0), channel_id=1, source_target_pairs={{0,6},{2,4},{4,2},{6,0},{1,7},{3,5},{5,3},{7,1},{8,14},{10,12},{12... | collective-permute-start | bytes 1179656 | tf_op jit(solution)/shard_map/ppermute | solution.py:228
  47.6 0.2 collective-permute-start.5
  47.9 3.0 %collective-permute-start.9 = (bf16[64,1536]{1,0:T(8,128)(2,1)S(1)}, bf16[64,1536]{1,0:T(8,128)(2,1)S(1)}, u32[]{:S(2)}, u32[]{:S(2)}) collective-permute-start(bf16[64,1536]{1,0:T(8,128)(2,1)S(1)} %pad_maximum_fusion.refs_0_), channel_id=1, source_target_pairs={{0,24},{8,16},{16,8},{24,0},{1,25},{9,17},{17,9},{25,1},{2,26},{10... | collective-permute-start | bytes 589832 | tf_op jit(solution)/shard_map/ppermute | solution.py:228
  50.9 0.6 collective-permute-start.8
  51.5 0.5 collective-permute-start.7
  52.0 15.4 %collective-permute-done.6.u3 = bf16[128,1536]{1,0:T(8,128)(2,1)S(1)} collective-permute-done((bf16[128,1536]{1,0:T(8,128)(2,1)S(1)}, bf16[128,1536]{1,0:T(8,128)(2,1)S(1)}, u32[]{:S(2)}, u32[]{:S(2)}) %collective-permute-start.6) | collective-permute-done | bytes 393248 | tf_op jit(solution)/shard_map/ppermute | solution.py:228
  67.3 0.7 slice.8
  68.0 0.7 slice.9
  68.7 0.0 collective-permute-done.9.refs_3_
  68.7 0.3 collective-permute-start.10
  69.1 1.1 collective-permute-start.11
  70.2 0.1 stack.27.w0_ref
  70.3 0.0 copy-start.3
  70.3 0.1 collective-permute-start.12
  70.4 0.0 copy-start.4
  70.4 0.7 copy-done.4
  71.1 5.0 %attn_fwd.1 = (f32[3,4,128,128]{3,2,1,0:T(8,128)S(1)}, bf16[512,384]{1,0:T(8,128)(2,1)S(1)}) custom-call(s32[5]{0:T(128)S(1)} %stack.25.place, f32[12,15]{1,0:T(8,128)S(1)} %copy-done.2, s32[8,384]{1,0:T(8,128)S(1)} %copy-done.4, bf16[8,3,64,384]{3,2,1,0:T(8,128)(2,1)S(1)} %all-to-all-done.qkv_ref.recv_ref), custom_call_target="tpu_custom_call" | custom-call | flops 20000000000 | bytes 2372324 | tf_op jit(solution)/shard_map/attn_fwd/pallas_call | solution.py:54
  76.2 0.9 collective-permute-done.11.q3
  77.0 3.7 %scores_bwd.1 = (f32[192,1536]{1,0:T(8,128)S(1)}, bf16[192,1536]{1,0:T(8,128)(2,1)S(1)}, bf16[8,64,384]{2,1,0:T(8,128)(2,1)S(1)}, bf16[3,4,128,128]{3,2,1,0:T(8,128)(2,1)S(1)}, f32[8,384]{1,0:T(8,128)S(1)}) custom-call(s32[5]{0:T(128)S(1)} %stack.25.place, s32[8,384]{1,0:T(8,128)S(1)} %copy-done.3, ...), custom_call_target="tpu_custom_call" | custom-call | flops 1500000000 | bytes 8085524 | tf_op jit(solution)/shard_map/scores_bwd/pallas_call | solution.py:54
  80.7 0.1 collective-permute-start.13
  80.8 0.5 collective-permute-start.14
  81.3 1.2 grads.1
  82.5 0.3 collective-permute-done.14.s1
  82.9 1.5 %join.1 = bf16[32,8,1280]{2,1,0:T(8,128)(2,1)} custom-call(f32[192,1536]{1,0:T(8,128)S(1)} %get-tuple-element.71.mine_ref, bf16[192,1536]{1,0:T(8,128)(2,1)S(1)} %collective-permute-done.13.other_ref, f32[8,384]{1,0:T(8,128)S(1)} %get-tuple-element.73.s0, f32[8,384]{1,0:T(8,128)S(1)} %collective-permute-done.14.s1), custom_call_target="tpu_custom_call" | custom-call | bytes 2449408 | tf_op jit(solution)/shard_map/join/pallas_call | solution.py:54
  84.4 7.7 %all-to-all-start.2 = ((bf16[32,8,1280]{2,1,0:T(8,128)(2,1)}), bf16[32,8,1280]{2,1,0:T(8,128)(2,1)S(1)}, u32[]{:S(2)}, u32[]{:S(2)}) async-start(bf16[32,8,1280]{2,1,0:T(8,128)(2,1)} %join.1), calls=%async_computation.2 | async-start | bytes 1310720 | tf_op jit(solution)/shard_map/all_to_all | solution.py:333
  92.1 0.1 collective-permute-start.15
  92.2 0.5 collective-permute-start.16
  92.7 1.3 %collective-permute-start.17 = (bf16[3,64,384]{2,1,0:T(8,128)(2,1)S(1)}, bf16[3,64,384]{2,1,0:T(8,128)(2,1)S(1)}, u32[]{:S(2)}, u32[]{:S(2)}) collective-permute-start(bf16[3,64,384]{2,1,0:T(8,128)(2,1)S(1)} %get-tuple-element.87), channel_id=1, source_target_pairs={{0,3},{1,2},{2,1},{3,0},{4,7},{5,6},{6,5},{7,4},{8,11},{9,10},{10,... | collective-permute-start | bytes 442376 | tf_op jit(solution)/shard_map/ppermute | solution.py:228
  94.0 2.0 %collective-permute-start.18 = (bf16[3,64,384]{2,1,0:T(8,128)(2,1)S(1)}, bf16[3,64,384]{2,1,0:T(8,128)(2,1)S(1)}, u32[]{:S(2)}, u32[]{:S(2)}) collective-permute-start(bf16[3,64,384]{2,1,0:T(8,128)(2,1)S(1)} %get-tuple-element.88), channel_id=1, source_target_pairs={{0,4},{1,5},{2,6},{3,7},{4,0},{5,1},{6,2},{7,3},{8,12},{9,13},{10,... | collective-permute-start | bytes 442376 | tf_op jit(solution)/shard_map/ppermute | solution.py:228
  96.0 1.2 collective-permute-start.19
  97.3 1.4 %collective-permute-start.21 = (bf16[3,64,384]{2,1,0:T(8,128)(2,1)S(1)}, bf16[3,64,384]{2,1,0:T(8,128)(2,1)S(1)}, u32[]{:S(2)}, u32[]{:S(2)}) collective-permute-start(bf16[3,64,384]{2,1,0:T(8,128)(2,1)S(1)} %get-tuple-element.98), channel_id=1, source_target_pairs={{0,6},{1,7},{2,4},{3,5},{4,2},{5,3},{6,0},{7,1},{8,14},{9,15},{10,... | collective-permute-start | bytes 442376 | tf_op jit(solution)/shard_map/ppermute | solution.py:228
  98.6 0.3 collective-permute-done.16.refs_2_
  98.9 1.4 %collective-permute-start.22 = (bf16[3,64,384]{2,1,0:T(8,128)(2,1)S(1)}, bf16[3,64,384]{2,1,0:T(8,128)(2,1)S(1)}, u32[]{:S(2)}, u32[]{:S(2)}) collective-permute-start(bf16[3,64,384]{2,1,0:T(8,128)(2,1)S(1)} %get-tuple-element.99), channel_id=1, source_target_pairs={{0,7},{1,6},{2,5},{3,4},{4,3},{5,2},{6,1},{7,0},{8,15},{9,14},{10,... | collective-permute-start | bytes 442376 | tf_op jit(solution)/shard_map/ppermute | solution.py:228
  100.3 0.9 collective-permute-done.17.refs_3_
  101.1 5.0 %collective-permute-done.18.refs_4_ = bf16[3,64,384]{2,1,0:T(8,128)(2,1)S(1)} collective-permute-done((bf16[3,64,384]{2,1,0:T(8,128)(2,1)S(1)}, bf16[3,64,384]{2,1,0:T(8,128)(2,1)S(1)}, u32[]{:S(2)}, u32[]{:S(2)}) %collective-permute-start.18) | collective-permute-done | bytes 147488 | tf_op jit(solution)/shard_map/ppermute | solution.py:228
  106.2 2.2 %collective-permute-done.19.refs_5_ = bf16[3,64,384]{2,1,0:T(8,128)(2,1)S(1)} collective-permute-done((bf16[3,64,384]{2,1,0:T(8,128)(2,1)S(1)}, bf16[3,64,384]{2,1,0:T(8,128)(2,1)S(1)}, u32[]{:S(2)}, u32[]{:S(2)}) %collective-permute-start.19) | collective-permute-done | bytes 147488 | tf_op jit(solution)/shard_map/ppermute | solution.py:228
  108.4 3.7 %all-to-all-done.2.in_ref = bf16[32,8,1280]{2,1,0:T(8,128)(2,1)S(1)} async-done(((bf16[32,8,1280]{2,1,0:T(8,128)(2,1)}), bf16[32,8,1280]{2,1,0:T(8,128)(2,1)S(1)}, u32[]{:S(2)}, u32[]{:S(2)}) %all-to-all-start.2) | async-done | bytes 655392 | tf_op jit(solution)/shard_map/all_to_all | solution.py:333
  112.1 0.5 total.1
  112.6 2.5 %collective-permute-start.20 = (f32[8,1536]{1,0:T(8,128)S(1)}, f32[8,1536]{1,0:T(8,128)S(1)}, u32[]{:S(2)}, u32[]{:S(2)}) collective-permute-start(f32[8,1536]{1,0:T(8,128)S(1)} %get-tuple-element.91), channel_id=1, source_target_pairs={{0,0},{32,2},{64,4},{96,6},{128,32},{160,34},{192,36},{224,38},{2,... | collective-permute-start | bytes 147464 | tf_op jit(solution)/shard_map/ppermute | solution.py:337
  115.1 3.5 %collective-permute-start.25 = (f32[16,128]{1,0:T(8,128)S(1)}, f32[16,128]{1,0:T(8,128)S(1)}, u32[]{:S(2)}, u32[]{:S(2)}) collective-permute-start(f32[16,128]{1,0:T(8,128)S(1)} %get-tuple-element.102.o0), channel_id=1, source_target_pairs={{0,6},{2,4},{4,2},{6,0},{1,7},{3,5},{5,3},{7,1},{8,14},{10,12},{12... | collective-permute-start | bytes 24584 | tf_op jit(solution)/shard_map/ppermute | solution.py:228
  118.6 1.0 collective-permute-start.23
  119.6 1.8 %unpack.1 = bf16[3,128,1536]{2,1,0:T(8,128)(2,1)} custom-call(s32[5]{0:T(128)S(1)} %stack.25.place, bf16[3,64,384]{2,1,0:T(8,128)(2,1)S(1)} %get-tuple-element.92.refs_0_, bf16[3,64,384]{2,1,0:T(8,128)(2,1)S(1)} %collective-permute-done.15.refs_1_, bf16[3,64,384]{2,1,0:T(8,128)(2,1)S(1)} %collective-permute-done.16.refs_2_, ...), custom_call_target="tpu_custom_call" | custom-call | bytes 2359316 | tf_op jit(solution)/shard_map/unpack/pallas_call | solution.py:54
  121.3 0.3 collective-permute-done.20.home_ref
  121.6 2.2 %collective-permute-done.24.o2 = f32[16,128]{1,0:T(8,128)S(1)} collective-permute-done((f32[16,128]{1,0:T(8,128)S(1)}, f32[16,128]{1,0:T(8,128)S(1)}, u32[]{:S(2)}, u32[]{:S(2)}) %collective-permute-start.24) | collective-permute-done | bytes 8224 | tf_op jit(solution)/shard_map/ppermute | solution.py:228
  123.8 1.2 last.1
  (22 shorter events, 0.1 us)
Async XLA Ops:
  0.6 29.5 %copy-start = (bf16[3,1,1,128,1536]{4,3,2,1,0:T(8,128)(2,1)S(1)}, bf16[3,1,1,128,1536]{4,3,2,1,0:T(8,128)(2,1)}, u32[]{:S(2)}) copy-start(bf16[3,1,1,128,1536]{4,3,2,1,0:T(8,128)(2,1)} %param.7) | copy-start | bytes 3538948
  1.5 9.4 %collective-permute-start.1 = (bf16[8,1536]{1,0:T(8,128)(2,1)S(1)}, bf16[8,1536]{1,0:T(8,128)(2,1)S(1)}, u32[]{:S(2)}, u32[]{:S(2)}) collective-permute-start(bf16[8,1536]{1,0:T(8,128)(2,1)S(1)} %pad.4), channel_id=1, source_target_pairs={{0,32},{2,0},{4,96},{6,64},{32,160},{34,128},{36,224},{38,192},{64... | collective-permute-start | bytes 73736 | tf_op jit(solution)/shard_map/ppermute | solution.py:243
  7.8 6.6 %collective-permute-start = (bf16[8,1536]{1,0:T(8,128)(2,1)S(1)}, bf16[8,1536]{1,0:T(8,128)(2,1)S(1)}, u32[]{:S(2)}, u32[]{:S(2)}) collective-permute-start(bf16[8,1536]{1,0:T(8,128)(2,1)S(1)} %pad.4), channel_id=1, source_target_pairs={{0,0},{2,32},{4,64},{6,96},{32,128},{34,160},{36,192},{38,224},{64... | collective-permute-start | bytes 73736 | tf_op jit(solution)/shard_map/ppermute | solution.py:243
  14.4 23.1 %all-to-all-start.1 = ((bf16[8,32,1536]{2,1,0:T(8,128)(2,1)}), bf16[8,32,1536]{2,1,0:T(8,128)(2,1)S(1)}, u32[]{:S(2)}, u32[]{:S(2)}) async-start(bf16[8,32,1536]{2,1,0:T(8,128)(2,1)} %bitcast.11), calls=%async_computation.1 | async-start | bytes 1572864 | tf_op jit(solution)/shard_map/all_to_all | solution.py:246
  22.4 5.1 %collective-permute-start.2 = (bf16[16,1536]{1,0:T(8,128)(2,1)S(1)}, bf16[16,1536]{1,0:T(8,128)(2,1)S(1)}, u32[]{:S(2)}, u32[]{:S(2)}) collective-permute-start(bf16[16,1536]{1,0:T(8,128)(2,1)S(1)} %pad_maximum_fusion.2), channel_id=1, source_target_pairs={{0,64},{32,96},{64,0},{96,32},{128,192},{160,224},{192,128},{224,1... | collective-permute-start | bytes 147464 | tf_op jit(solution)/shard_map/ppermute | solution.py:228
  27.5 9.9 %collective-permute-start.3 = (bf16[32,1536]{1,0:T(8,128)(2,1)S(1)}, bf16[32,1536]{1,0:T(8,128)(2,1)S(1)}, u32[]{:S(2)}, u32[]{:S(2)}) collective-permute-start(bf16[32,1536]{1,0:T(8,128)(2,1)S(1)} %pad_maximum_fusion.1), channel_id=1, source_target_pairs={{0,128},{32,160},{64,192},{96,224},{128,0},{160,32},{192,64},{224,... | collective-permute-start | bytes 294920 | tf_op jit(solution)/shard_map/ppermute | solution.py:228
  37.5 4.4 %copy-start.1 = (s32[1,8]{1,0:T(1,128)S(1)}, s32[1,8]{1,0:T(1,128)}, u32[]{:S(2)}) copy-start(s32[1,8]{1,0:T(1,128)} %sizes.1) | copy-start | bytes 100
  37.5 32.9 %all-to-all-start = ((bf16[8,3,64,384]{3,2,1,0:T(8,128)(2,1)}), bf16[8,3,64,384]{3,2,1,0:T(8,128)(2,1)S(1)}, u32[]{:S(2)}, u32[]{:S(2)}) async-start(bf16[8,3,64,384]{3,2,1,0:T(8,128)(2,1)} %pack.1), calls=%async_computation | async-start | bytes 2359296 | tf_op jit(solution)/shard_map/all_to_all | solution.py:252
  42.7 1.7 %collective-permute-start.4 = (bf16[64,1536]{1,0:T(8,128)(2,1)S(1)}, bf16[64,1536]{1,0:T(8,128)(2,1)S(1)}, u32[]{:S(2)}, u32[]{:S(2)}) collective-permute-start(bf16[64,1536]{1,0:T(8,128)(2,1)S(1)} %get-tuple-element.62), channel_id=1, source_target_pairs={{0,1},{1,0},{2,3},{3,2},{4,5},{5,4},{6,7},{7,6},{8,9},{9,8},{10,11... | collective-permute-start | bytes 589832 | tf_op jit(solution)/shard_map/ppermute | solution.py:228
  44.4 26.0 %copy-start.2 = (f32[12,15]{1,0:T(8,128)S(1)}, f32[12,15]{1,0:T(8,128)}, u32[]{:S(2)}) copy-start(f32[12,15]{1,0:T(8,128)} %bias.1) | copy-start | bytes 2164
  44.4 22.9 %collective-permute-start.6 = (bf16[128,1536]{1,0:T(8,128)(2,1)S(1)}, bf16[128,1536]{1,0:T(8,128)(2,1)S(1)}, u32[]{:S(2)}, u32[]{:S(2)}) collective-permute-start(bf16[128,1536]{1,0:T(8,128)(2,1)S(1)} %stack.26.u0), channel_id=1, source_target_pairs={{0,6},{2,4},{4,2},{6,0},{1,7},{3,5},{5,3},{7,1},{8,14},{10,12},{12... | collective-permute-start | bytes 1179656 | tf_op jit(solution)/shard_map/ppermute | solution.py:228
  47.6 20.4 %collective-permute-start.5 = (bf16[128,1536]{1,0:T(8,128)(2,1)S(1)}, bf16[128,1536]{1,0:T(8,128)(2,1)S(1)}, u32[]{:S(2)}, u32[]{:S(2)}) collective-permute-start(bf16[128,1536]{1,0:T(8,128)(2,1)S(1)} %stack.26.u0), channel_id=1, source_target_pairs={{0,2},{2,0},{4,6},{6,4},{1,3},{3,1},{5,7},{7,5},{8,10},{10,8},{12,... | collective-permute-start | bytes 1179656 | tf_op jit(solution)/shard_map/ppermute | solution.py:228
  47.9 20.8 %collective-permute-start.9 = (bf16[64,1536]{1,0:T(8,128)(2,1)S(1)}, bf16[64,1536]{1,0:T(8,128)(2,1)S(1)}, u32[]{:S(2)}, u32[]{:S(2)}) collective-permute-start(bf16[64,1536]{1,0:T(8,128)(2,1)S(1)} %pad_maximum_fusion.refs_0_), channel_id=1, source_target_pairs={{0,24},{8,16},{16,8},{24,0},{1,25},{9,17},{17,9},{25,1},{2,26},{10... | collective-permute-start | bytes 589832 | tf_op jit(solution)/shard_map/ppermute | solution.py:228
  50.9 17.8 %collective-permute-start.8 = (bf16[64,1536]{1,0:T(8,128)(2,1)S(1)}, bf16[64,1536]{1,0:T(8,128)(2,1)S(1)}, u32[]{:S(2)}, u32[]{:S(2)}) collective-permute-start(bf16[64,1536]{1,0:T(8,128)(2,1)S(1)} %pad_maximum_fusion.refs_0_), channel_id=1, source_target_pairs={{0,16},{8,24},{16,0},{24,8},{1,17},{9,25},{17,1},{25,9},{2,18},{10... | collective-permute-start | bytes 589832 | tf_op jit(solution)/shard_map/ppermute | solution.py:228
  51.5 17.2 %collective-permute-start.7 = (bf16[64,1536]{1,0:T(8,128)(2,1)S(1)}, bf16[64,1536]{1,0:T(8,128)(2,1)S(1)}, u32[]{:S(2)}, u32[]{:S(2)}) collective-permute-start(bf16[64,1536]{1,0:T(8,128)(2,1)S(1)} %pad_maximum_fusion.refs_0_), channel_id=1, source_target_pairs={{0,8},{8,0},{16,24},{24,16},{1,9},{9,1},{17,25},{25,17},{2,10},{10... | collective-permute-start | bytes 589832 | tf_op jit(solution)/shard_map/ppermute | solution.py:228
  68.7 7.4 %collective-permute-start.10 = (bf16[64,1536]{1,0:T(8,128)(2,1)}, bf16[64,1536]{1,0:T(8,128)(2,1)S(1)}, u32[]{:S(2)}, u32[]{:S(2)}) collective-permute-start(bf16[64,1536]{1,0:T(8,128)(2,1)} %slice.8), channel_id=1, source_target_pairs={{0,2},{2,0},{4,6},{6,4},{1,3},{3,1},{5,7},{7,5},{8,10},{10,8},{12,... | collective-permute-start | bytes 589832 | tf_op jit(solution)/shard_map/ppermute | solution.py:228
  69.1 8.0 %collective-permute-start.11 = (bf16[64,1536]{1,0:T(8,128)(2,1)}, bf16[64,1536]{1,0:T(8,128)(2,1)}, u32[]{:S(2)}, u32[]{:S(2)}) collective-permute-start(bf16[64,1536]{1,0:T(8,128)(2,1)} %slice.9), channel_id=1, source_target_pairs={{0,6},{2,4},{4,2},{6,0},{1,7},{3,5},{5,3},{7,1},{8,14},{10,12},{12... | collective-permute-start | bytes 589832 | tf_op jit(solution)/shard_map/ppermute | solution.py:228
  70.3 6.8 %copy-start.3 = (s32[8,384]{1,0:T(8,128)S(1)}, s32[8,384]{1,0:T(8,128)}, u32[]{:S(2)}) copy-start(s32[8,384]{1,0:T(8,128)} %constant.26.clone.rows_ref) | copy-start | bytes 36868
  70.3 6.8 %collective-permute-start.12 = (bf16[256,1536]{1,0:T(8,128)(2,1)S(1)}, bf16[256,1536]{1,0:T(8,128)(2,1)}, u32[]{:S(2)}, u32[]{:S(2)}) collective-permute-start(bf16[256,1536]{1,0:T(8,128)(2,1)S(1)} %stack.27.w0_ref), channel_id=1, source_target_pairs={{0,1},{1,0},{2,3},{3,2},{4,5},{5,4},{6,7},{7,6},{8,9},{9,8},{10,11... | collective-permute-start | bytes 2359304 | tf_op jit(solution)/shard_map/ppermute | solution.py:228
  70.4 0.7 copy-start.4
  80.7 2.1 %collective-permute-start.13 = (bf16[192,1536]{1,0:T(8,128)(2,1)S(1)}, bf16[192,1536]{1,0:T(8,128)(2,1)S(1)}, u32[]{:S(2)}, u32[]{:S(2)}) collective-permute-start(bf16[192,1536]{1,0:T(8,128)(2,1)S(1)} %get-tuple-element.72), channel_id=1, source_target_pairs={{0,1},{1,0},{2,3},{3,2},{4,5},{5,4},{6,7},{7,6},{8,9},{9,8},{10,11... | collective-permute-start | bytes 1769480 | tf_op jit(solution)/shard_map/ppermute | solution.py:228
  80.8 2.0 %collective-permute-start.14 = (f32[8,384]{1,0:T(8,128)S(1)}, f32[8,384]{1,0:T(8,128)S(1)}, u32[]{:S(2)}, u32[]{:S(2)}) collective-permute-start(f32[8,384]{1,0:T(8,128)S(1)} %get-tuple-element.73.s0), channel_id=1, source_target_pairs={{0,1},{1,0},{2,3},{3,2},{4,5},{5,4},{6,7},{7,6},{8,9},{9,8},{10,11... | collective-permute-start | bytes 36872 | tf_op jit(solution)/shard_map/ppermute | solution.py:228
  84.4 27.7 %all-to-all-start.2 = ((bf16[32,8,1280]{2,1,0:T(8,128)(2,1)}), bf16[32,8,1280]{2,1,0:T(8,128)(2,1)S(1)}, u32[]{:S(2)}, u32[]{:S(2)}) async-start(bf16[32,8,1280]{2,1,0:T(8,128)(2,1)} %join.1), calls=%async_computation.2 | async-start | bytes 1310720 | tf_op jit(solution)/shard_map/all_to_all | solution.py:333
  92.1 5.2 %collective-permute-start.15 = (bf16[3,64,384]{2,1,0:T(8,128)(2,1)S(1)}, bf16[3,64,384]{2,1,0:T(8,128)(2,1)S(1)}, u32[]{:S(2)}, u32[]{:S(2)}) collective-permute-start(bf16[3,64,384]{2,1,0:T(8,128)(2,1)S(1)} %get-tuple-element.85), channel_id=1, source_target_pairs={{0,1},{1,0},{2,3},{3,2},{4,5},{5,4},{6,7},{7,6},{8,9},{9,8},{10,11... | collective-permute-start | bytes 442376 | tf_op jit(solution)/shard_map/ppermute | solution.py:228
  92.2 6.7 %collective-permute-start.16 = (bf16[3,64,384]{2,1,0:T(8,128)(2,1)S(1)}, bf16[3,64,384]{2,1,0:T(8,128)(2,1)S(1)}, u32[]{:S(2)}, u32[]{:S(2)}) collective-permute-start(bf16[3,64,384]{2,1,0:T(8,128)(2,1)S(1)} %get-tuple-element.86), channel_id=1, source_target_pairs={{0,2},{1,3},{2,0},{3,1},{4,6},{5,7},{6,4},{7,5},{8,10},{9,11},{10,... | collective-permute-start | bytes 442376 | tf_op jit(solution)/shard_map/ppermute | solution.py:228
  92.7 8.4 %collective-permute-start.17 = (bf16[3,64,384]{2,1,0:T(8,128)(2,1)S(1)}, bf16[3,64,384]{2,1,0:T(8,128)(2,1)S(1)}, u32[]{:S(2)}, u32[]{:S(2)}) collective-permute-start(bf16[3,64,384]{2,1,0:T(8,128)(2,1)S(1)} %get-tuple-element.87), channel_id=1, source_target_pairs={{0,3},{1,2},{2,1},{3,0},{4,7},{5,6},{6,5},{7,4},{8,11},{9,10},{10,... | collective-permute-start | bytes 442376 | tf_op jit(solution)/shard_map/ppermute | solution.py:228
  94.0 12.1 %collective-permute-start.18 = (bf16[3,64,384]{2,1,0:T(8,128)(2,1)S(1)}, bf16[3,64,384]{2,1,0:T(8,128)(2,1)S(1)}, u32[]{:S(2)}, u32[]{:S(2)}) collective-permute-start(bf16[3,64,384]{2,1,0:T(8,128)(2,1)S(1)} %get-tuple-element.88), channel_id=1, source_target_pairs={{0,4},{1,5},{2,6},{3,7},{4,0},{5,1},{6,2},{7,3},{8,12},{9,13},{10,... | collective-permute-start | bytes 442376 | tf_op jit(solution)/shard_map/ppermute | solution.py:228
  96.0 12.3 %collective-permute-start.19 = (bf16[3,64,384]{2,1,0:T(8,128)(2,1)S(1)}, bf16[3,64,384]{2,1,0:T(8,128)(2,1)S(1)}, u32[]{:S(2)}, u32[]{:S(2)}) collective-permute-start(bf16[3,64,384]{2,1,0:T(8,128)(2,1)S(1)} %get-tuple-element.89), channel_id=1, source_target_pairs={{0,5},{1,4},{2,7},{3,6},{4,1},{5,0},{6,3},{7,2},{8,13},{9,12},{10,... | collective-permute-start | bytes 442376 | tf_op jit(solution)/shard_map/ppermute | solution.py:228
  97.3 21.3 %collective-permute-start.21 = (bf16[3,64,384]{2,1,0:T(8,128)(2,1)S(1)}, bf16[3,64,384]{2,1,0:T(8,128)(2,1)S(1)}, u32[]{:S(2)}, u32[]{:S(2)}) collective-permute-start(bf16[3,64,384]{2,1,0:T(8,128)(2,1)S(1)} %get-tuple-element.98), channel_id=1, source_target_pairs={{0,6},{1,7},{2,4},{3,5},{4,2},{5,3},{6,0},{7,1},{8,14},{9,15},{10,... | collective-permute-start | bytes 442376 | tf_op jit(solution)/shard_map/ppermute | solution.py:228
  98.9 20.7 %collective-permute-start.22 = (bf16[3,64,384]{2,1,0:T(8,128)(2,1)S(1)}, bf16[3,64,384]{2,1,0:T(8,128)(2,1)S(1)}, u32[]{:S(2)}, u32[]{:S(2)}) collective-permute-start(bf16[3,64,384]{2,1,0:T(8,128)(2,1)S(1)} %get-tuple-element.99), channel_id=1, source_target_pairs={{0,7},{1,6},{2,5},{3,4},{4,3},{5,2},{6,1},{7,0},{8,15},{9,14},{10,... | collective-permute-start | bytes 442376 | tf_op jit(solution)/shard_map/ppermute | solution.py:228
  112.6 9.0 %collective-permute-start.20 = (f32[8,1536]{1,0:T(8,128)S(1)}, f32[8,1536]{1,0:T(8,128)S(1)}, u32[]{:S(2)}, u32[]{:S(2)}) collective-permute-start(f32[8,1536]{1,0:T(8,128)S(1)} %get-tuple-element.91), channel_id=1, source_target_pairs={{0,0},{32,2},{64,4},{96,6},{128,32},{160,34},{192,36},{224,38},{2,... | collective-permute-start | bytes 147464 | tf_op jit(solution)/shard_map/ppermute | solution.py:337
  115.1 6.5 %collective-permute-start.25 = (f32[16,128]{1,0:T(8,128)S(1)}, f32[16,128]{1,0:T(8,128)S(1)}, u32[]{:S(2)}, u32[]{:S(2)}) collective-permute-start(f32[16,128]{1,0:T(8,128)S(1)} %get-tuple-element.102.o0), channel_id=1, source_target_pairs={{0,6},{2,4},{4,2},{6,0},{1,7},{3,5},{5,3},{7,1},{8,14},{10,12},{12... | collective-permute-start | bytes 24584 | tf_op jit(solution)/shard_map/ppermute | solution.py:228
  118.6 5.2 %collective-permute-start.24 = (f32[16,128]{1,0:T(8,128)S(1)}, f32[16,128]{1,0:T(8,128)S(1)}, u32[]{:S(2)}, u32[]{:S(2)}) collective-permute-start(f32[16,128]{1,0:T(8,128)S(1)} %get-tuple-element.102.o0), channel_id=1, source_target_pairs={{0,4},{2,6},{4,0},{6,2},{1,5},{3,7},{5,1},{7,3},{8,12},{10,14},{12... | collective-permute-start | bytes 24584 | tf_op jit(solution)/shard_map/ppermute | solution.py:228
  118.6 5.2 %collective-permute-start.23 = (f32[16,128]{1,0:T(8,128)S(1)}, f32[16,128]{1,0:T(8,128)S(1)}, u32[]{:S(2)}, u32[]{:S(2)}) collective-permute-start(f32[16,128]{1,0:T(8,128)S(1)} %get-tuple-element.102.o0), channel_id=1, source_target_pairs={{0,2},{2,0},{4,6},{6,4},{1,3},{3,1},{5,7},{7,5},{8,10},{10,8},{12,... | collective-permute-start | bytes 24584 | tf_op jit(solution)/shard_map/ppermute | solution.py:228

commit v8 on v7

--- a/solution.py
+++ b/solution.py
@@ -122,18 +122,18 @@
     mixed_ref[...] = dot(raw_ref[...].reshape(F * HALF, COLS), order, NN).astype(bf)
 
 
-def score_kernel(place, rows_ref, recv_ref, probs_ref, mixed_ref, u0, u1, u3, q1, q3, w0_ref, w1_ref, *outs):
-    mine_ref, other_ref, dm_ref, ds_ref, sums_ref, up_ref = outs
-    halves = [(0, u0[:HALF], u0[HALF:]), (1, u1[:HALF], u1[HALF:])]
-    halves += [(2, q1[...], q3[...]), (3, u3[:HALF], u3[HALF:])]
-    for k, same, other in halves:
+def gw_kernel(place, mixed_ref, u0, u1, u2, u3, mine_ref, other_ref, up_ref):
+    for k, ref in enumerate((u0, u1, u2, u3)):
         chip = (place[XI] ^ k) * C
-        up_ref[chip + place[CORE]] = same
-        up_ref[chip + 1 - place[CORE]] = other
-    up = up_ref[...].reshape(F * HALF, DW)
-    gw = dot(mixed_ref[...], up, TN)
+        up_ref[chip + place[CORE]] = ref[:HALF]
+        up_ref[chip + 1 - place[CORE]] = ref[HALF:]
+    gw = dot(mixed_ref[...], up_ref[...].reshape(F * HALF, DW), TN)
     mine_ref[...] = gw[: COLS // 2]
     other_ref[...] = gw[COLS // 2 :].astype(bf)
+
+
+def score_kernel(place, rows_ref, recv_ref, probs_ref, up_ref, w0_ref, w1_ref, dm_ref, ds_ref, sums_ref):
+    up = up_ref[...].reshape(F * HALF, DW)
     dm = jnp.concatenate([dot(up, w[...], NT).astype(bf) for w in (w0_ref, w1_ref)], axis=1)
     c, y, j = (rows_ref[n : n + 1] ^ place[n] for n in (CORE, YI, ZI))
     spot = ((c * Y + y) * Z + j) * 8 + rows_ref[3:4]
@@ -239,15 +239,12 @@
         for x in range(X)
     ]
     near = [(a, b ^ X) for a, b in there]
-    rows8 = jnp.pad(w_out, ((0, 2), (0, 0)))
+    cot = lax.all_to_all(cot_out[0, 0], SEQ, 0, 0, tiled=True)
+    (packed,) = call(pack_kernel, "pack", [((F, 3, HALF, COLS), bf)], qkv_time[:, 0, 0])
+    rows8, packed = lax.optimization_barrier((jnp.pad(w_out, ((0, 2), (0, 0))), packed))
     held = [lax.ppermute(rows8, ("z", "x"), p) for p in (there, near)]
-    cot, *held = lax.optimization_barrier((cot_out[0, 0], *held))
-
-    cot = lax.all_to_all(cot, SEQ, 0, 0, tiled=True)
-    (packed,) = call(pack_kernel, "pack", [((F, 3, HALF, COLS), bf)], qkv_time[:, 0, 0])
     held = jnp.concatenate(held)
     held = jnp.concatenate([held, hop(held, "z", 2, Z)])
-    held = jnp.concatenate([held, hop(held, "z", 4, Z)])
     packed, held = lax.optimization_barrier((packed, held))
     recv = lax.all_to_all(packed, SEQ, 0, 0, tiled=True)
 
@@ -261,14 +258,13 @@
         smem=2,
         flops=100_000_000,
     )
+    held, same = lax.optimization_barrier((held, same))
+    held = jnp.concatenate([held, hop(held, "z", 4, Z)])
     u0 = stack([same, hop(other, "core", 1, C)])
     held, u0 = lax.optimization_barrier((held, u0))
-    u1, u3 = hop(u0, "x", 1, X), hop(u0, "x", 3, X)
+    ups = [u0] + [hop(u0, "x", k, X) for k in range(1, X)]
     held = [held] + [hop(held, "y", k, Y) for k in range(1, Y)]
-
-    far = u3[:HALF], u1[HALF:]
-    held, far = lax.optimization_barrier((held, far))
-    q1, q3 = hop(far[0], "x", 1, X), hop(far[1], "x", 3, X)
+    held, ups[1], ups[3] = lax.optimization_barrier((held, ups[1], ups[3]))
     held = stack(held)
     held2 = hop(held, "core", 1, C)
 
@@ -285,31 +281,29 @@
         flops=20_000_000_000,
     )
 
-    mine, theirs, dm, ds, sums = call(
+    mine, theirs, up = call(
+        gw_kernel,
+        "grad_w",
+        [((COLS // 2, DW), f32), ((COLS // 2, DW), bf), ((F, HALF, DW), bf)],
+        place,
+        mixed,
+        *ups,
+        smem=1,
+        flops=20_000_000_000,
+    )
+    dm, ds, sums = call(
         score_kernel,
         "scores_bwd",
-        [
-            ((COLS // 2, DW), f32),
-            ((COLS // 2, DW), bf),
-            ((F, HALF, COLS), bf),
-            ((HL, NB, POS, POS), bf),
-            ((F, COLS), f32),
-        ],
+        [((F, HALF, COLS), bf), ((HL, NB, POS, POS), bf), ((F, COLS), f32)],
         place,
         ROWS_OF,
         recv,
         probs,
-        mixed,
-        u0,
-        u1,
-        u3,
-        q1,
-        q3,
+        up,
         held,
         held2,
         smem=1,
-        scratch=[pltpu.VMEM((F, HALF, DW), bf)],
-        flops=1_500_000_000,
+        flops=900_000_000,
     )
     theirs = hop(theirs, "core", 1, C)
     sums2 = hop(sums, "core", 1, C)

time: 126 us -> 119 us (0.944)
  waiting for transfers between devices: 47 us -> 37.1 us
  starting transfers between devices: 57.2 us -> 61.3 us
  local copies, waits for them, and re-layouts: 3.03 us -> 0.83 us
    ppermute x23 -> x22, waiting for transfers between devices: 39.5 us -> 30.3 us  [hop(): return lax.ppermute(x, axis, [(i, i ^ k) for i in range(n)])]
    ppermute x23 -> x22, starting transfers between devices: 25.3 us -> 33.1 us  [hop(): return lax.ppermute(x, axis, [(i, i ^ k) for i in range(n)])]
    all_to_all x1, starting transfers between devices: 8.02 us -> 4.44 us  [per_device(): cot = lax.all_to_all(cot_out[0, 0], SEQ, 0, 0, tiled=True)]
    all_to_all x1, starting transfers between devices: 7.65 us -> 5.86 us  [per_device(): msgs = lax.all_to_all(msgs, ('z', 'y'), 0, 0, tiled=True)]
    all_to_all x1, starting transfers between devices: 4.32 us -> 6.03 us  [per_device(): recv = lax.all_to_all(packed, SEQ, 0, 0, tiled=True)]
    slice x2 -> x0, local copies, waits for them, and re-layouts: 1.37 us -> none  [per_device(): far = (u3[:HALF], u1[HALF:])]
    pallas_call x11 -> x12, Pallas kernels: 16.9 us -> 16.9 us  [call(): pl.pallas_call(body, out_shape=tuple((jax.ShapeDtypeStruct(s, d) for s, d...]
  transfers between devices with their start and end apart: 29 -> 28, of which waited for: 14 -> 11; matrix products, arithmetic and copies ran while one was open for 1% -> 0% of each run, Pallas kernels for 8% -> 12%
where the time goes in v8:
time: 119 us; the launch traced here: 117 us
  starting transfers between devices  61.3 us (52%)
  waiting for transfers between devices  37.1 us (31%)
  Pallas kernels  16.9 us (14%)
    ppermute x22, starting transfers between devices, hop(): return lax.ppermute(x, axis, [(i, i ^ k) for i in range(n)])  33.1 us
    ppermute x22, waiting for transfers between devices, hop(): return lax.ppermute(x, axis, [(i, i ^ k) for i in range(n)])  30.3 us
    pallas_call x12, Pallas kernels, call(): pl.pallas_call(body, out_shape=tuple((jax.ShapeDtypeStruct(s, d) for s, d...  16.9 us
    ppermute x2, starting transfers between devices, per_device(): held = [lax.ppermute(rows8, ('z', 'x'), p) for p in (there, near)]  9.96 us
    all_to_all x1, starting transfers between devices, per_device(): recv = lax.all_to_all(packed, SEQ, 0, 0, tiled=True)  6.03 us
    all_to_all x1, starting transfers between devices, per_device(): msgs = lax.all_to_all(msgs, ('z', 'y'), 0, 0, tiled=True)  5.86 us
    all_to_all x1, starting transfers between devices, per_device(): cot = lax.all_to_all(cot_out[0, 0], SEQ, 0, 0, tiled=True)  4.44 us
    ppermute x2, waiting for transfers between devices, per_device(): held = [lax.ppermute(rows8, ('z', 'x'), p) for p in (there, near)]  3 us
  transfers between devices with their start and end apart: 28, of which 11 were waited for; matrix products, arithmetic and copies ran while one was open for 0% of the time, Pallas kernels for 12%

profile of v8, /device:TPU:32, one launch (start us, length us, event | category | flops | bytes accessed | tf_op | source)
XLA Modules:
  0.0 117.1 jit_solution(4936787414932294563)
XLA Ops:
  0.6 4.4 %all-to-all-start.1 = ((bf16[8,32,1536]{2,1,0:T(8,128)(2,1)}), bf16[8,32,1536]{2,1,0:T(8,128)(2,1)S(1)}, u32[]{:S(2)}, u32[]{:S(2)}) async-start(bf16[8,32,1536]{2,1,0:T(8,128)(2,1)} %bitcast.11), calls=%async_computation.1 | async-start | bytes 1572864 | tf_op jit(solution)/shard_map/all_to_all | solution.py:242
  5.1 0.0 copy-start.5
  5.1 1.1 pack.1
  6.2 6.4 %collective-permute-start.1 = (bf16[8,1536]{1,0:T(8,128)(2,1)S(1)}, bf16[8,1536]{1,0:T(8,128)(2,1)S(1)}, u32[]{:S(2)}, u32[]{:S(2)}) collective-permute-start(bf16[8,1536]{1,0:T(8,128)(2,1)S(1)} %pad.4), channel_id=1, source_target_pairs={{0,32},{2,0},{4,96},{6,64},{32,160},{34,128},{36,224},{38,192},{64... | collective-permute-start | bytes 73736 | tf_op jit(solution)/shard_map/ppermute | solution.py:245
  12.6 3.6 %collective-permute-start = (bf16[8,1536]{1,0:T(8,128)(2,1)S(1)}, bf16[8,1536]{1,0:T(8,128)(2,1)S(1)}, u32[]{:S(2)}, u32[]{:S(2)}) collective-permute-start(bf16[8,1536]{1,0:T(8,128)(2,1)S(1)} %pad.4), channel_id=1, source_target_pairs={{0,0},{2,32},{4,64},{6,96},{32,128},{34,160},{36,192},{38,224},{64... | collective-permute-start | bytes 73736 | tf_op jit(solution)/shard_map/ppermute | solution.py:245
  16.2 0.0 collective-permute-done.1
  16.2 3.0 %collective-permute-done = bf16[8,1536]{1,0:T(8,128)(2,1)S(1)} collective-permute-done((bf16[8,1536]{1,0:T(8,128)(2,1)S(1)}, bf16[8,1536]{1,0:T(8,128)(2,1)S(1)}, u32[]{:S(2)}, u32[]{:S(2)}) %collective-permute-start) | collective-permute-done | bytes 24608 | tf_op jit(solution)/shard_map/ppermute | solution.py:245
  19.2 5.0 %collective-permute-start.2 = (bf16[16,1536]{1,0:T(8,128)(2,1)S(1)}, bf16[16,1536]{1,0:T(8,128)(2,1)S(1)}, u32[]{:S(2)}, u32[]{:S(2)}) collective-permute-start(bf16[16,1536]{1,0:T(8,128)(2,1)S(1)} %pad_maximum_fusion.2), channel_id=1, source_target_pairs={{0,64},{32,96},{64,0},{96,32},{128,192},{160,224},{192,128},{224,1... | collective-permute-start | bytes 147464 | tf_op jit(solution)/shard_map/ppermute | solution.py:228
  24.2 2.1 %collective-permute-done.2 = bf16[16,1536]{1,0:T(8,128)(2,1)S(1)} collective-permute-done((bf16[16,1536]{1,0:T(8,128)(2,1)S(1)}, bf16[16,1536]{1,0:T(8,128)(2,1)S(1)}, u32[]{:S(2)}, u32[]{:S(2)}) %collective-permute-start.2) | collective-permute-done | bytes 49184 | tf_op jit(solution)/shard_map/ppermute | solution.py:228
  26.3 0.0 copy-start.2
  26.3 6.0 %all-to-all-start = ((bf16[8,3,64,384]{3,2,1,0:T(8,128)(2,1)}), bf16[8,3,64,384]{3,2,1,0:T(8,128)(2,1)S(1)}, u32[]{:S(2)}, u32[]{:S(2)}) async-start(bf16[8,3,64,384]{3,2,1,0:T(8,128)(2,1)} %pack.1), calls=%async_computation | async-start | bytes 2359296 | tf_op jit(solution)/shard_map/all_to_all | solution.py:249
  32.4 0.1 stack.25.place
  32.5 0.8 compact.1
  33.3 3.0 %collective-permute-start.3 = (bf16[32,1536]{1,0:T(8,128)(2,1)S(1)}, bf16[32,1536]{1,0:T(8,128)(2,1)S(1)}, u32[]{:S(2)}, u32[]{:S(2)}) collective-permute-start(bf16[32,1536]{1,0:T(8,128)(2,1)S(1)} %pad_maximum_fusion.1), channel_id=1, source_target_pairs={{0,128},{32,160},{64,192},{96,224},{128,0},{160,32},{192,64},{224,... | collective-permute-start | bytes 294920 | tf_op jit(solution)/shard_map/ppermute | solution.py:228
  36.3 0.1 collective-permute-start.4
  36.4 8.1 %collective-permute-done.3 = bf16[32,1536]{1,0:T(8,128)(2,1)S(1)} collective-permute-done((bf16[32,1536]{1,0:T(8,128)(2,1)S(1)}, bf16[32,1536]{1,0:T(8,128)(2,1)S(1)}, u32[]{:S(2)}, u32[]{:S(2)}) %collective-permute-start.3) | collective-permute-done | bytes 98336 | tf_op jit(solution)/shard_map/ppermute | solution.py:228
  44.5 1.7 %collective-permute-start.5 = (bf16[64,1536]{1,0:T(8,128)(2,1)S(1)}, bf16[64,1536]{1,0:T(8,128)(2,1)S(1)}, u32[]{:S(2)}, u32[]{:S(2)}) collective-permute-start(bf16[64,1536]{1,0:T(8,128)(2,1)S(1)} %pad_maximum_fusion.refs_0_), channel_id=1, source_target_pairs={{0,8},{8,0},{16,24},{24,16},{1,9},{9,1},{17,25},{25,17},{2,10},{10... | collective-permute-start | bytes 589832 | tf_op jit(solution)/shard_map/ppermute | solution.py:228
  46.2 2.9 %collective-permute-start.6 = (bf16[64,1536]{1,0:T(8,128)(2,1)S(1)}, bf16[64,1536]{1,0:T(8,128)(2,1)S(1)}, u32[]{:S(2)}, u32[]{:S(2)}) collective-permute-start(bf16[64,1536]{1,0:T(8,128)(2,1)S(1)} %pad_maximum_fusion.refs_0_), channel_id=1, source_target_pairs={{0,16},{8,24},{16,0},{24,8},{1,17},{9,25},{17,1},{25,9},{2,18},{10... | collective-permute-start | bytes 589832 | tf_op jit(solution)/shard_map/ppermute | solution.py:228
  49.1 0.2 collective-permute-start.7
  49.3 1.7 %collective-permute-start.8 = (bf16[128,1536]{1,0:T(8,128)(2,1)S(1)}, bf16[128,1536]{1,0:T(8,128)(2,1)S(1)}, u32[]{:S(2)}, u32[]{:S(2)}) collective-permute-start(bf16[128,1536]{1,0:T(8,128)(2,1)S(1)} %stack.26.u0), channel_id=1, source_target_pairs={{0,2},{2,0},{4,6},{6,4},{1,3},{3,1},{5,7},{7,5},{8,10},{10,8},{12,... | collective-permute-start | bytes 1179656 | tf_op jit(solution)/shard_map/ppermute | solution.py:228
  50.9 2.1 %collective-permute-start.9 = (bf16[128,1536]{1,0:T(8,128)(2,1)S(1)}, bf16[128,1536]{1,0:T(8,128)(2,1)S(1)}, u32[]{:S(2)}, u32[]{:S(2)}) collective-permute-start(bf16[128,1536]{1,0:T(8,128)(2,1)S(1)} %stack.26.u0), channel_id=1, source_target_pairs={{0,6},{2,4},{4,2},{6,0},{1,7},{3,5},{5,3},{7,1},{8,14},{10,12},{12... | collective-permute-start | bytes 1179656 | tf_op jit(solution)/shard_map/ppermute | solution.py:228
  53.0 0.0 collective-permute-done.5.refs_1_
  53.0 2.5 %collective-permute-start.10 = (bf16[128,1536]{1,0:T(8,128)(2,1)S(1)}, bf16[128,1536]{1,0:T(8,128)(2,1)S(1)}, u32[]{:S(2)}, u32[]{:S(2)}) collective-permute-start(bf16[128,1536]{1,0:T(8,128)(2,1)S(1)} %stack.26.u0), channel_id=1, source_target_pairs={{0,4},{2,6},{4,0},{6,2},{1,5},{3,7},{5,1},{7,3},{8,12},{10,14},{12... | collective-permute-start | bytes 1179656 | tf_op jit(solution)/shard_map/ppermute | solution.py:228
  55.5 0.7 copy-done.4
  56.2 5.0 %attn_fwd.1 = (f32[3,4,128,128]{3,2,1,0:T(8,128)S(1)}, bf16[512,384]{1,0:T(8,128)(2,1)S(1)}) custom-call(s32[5]{0:T(128)S(1)} %stack.25.place, f32[12,15]{1,0:T(8,128)S(1)} %copy-done.3, s32[8,384]{1,0:T(8,128)S(1)} %copy-done.4, bf16[8,3,64,384]{3,2,1,0:T(8,128)(2,1)S(1)} %all-to-all-done.qkv_ref.recv_ref), custom_call_target="tpu_custom_call" | custom-call | flops 20000000000 | bytes 2372324 | tf_op jit(solution)/shard_map/attn_fwd/pallas_call | solution.py:54
  61.3 0.0 collective-permute-done.6.refs_2_
  61.3 0.0 collective-permute-done.7.refs_3_
  61.3 0.0 collective-permute-done.8.u1
  61.3 9.2 %collective-permute-done.9.u3 = bf16[128,1536]{1,0:T(8,128)(2,1)S(1)} collective-permute-done((bf16[128,1536]{1,0:T(8,128)(2,1)S(1)}, bf16[128,1536]{1,0:T(8,128)(2,1)S(1)}, u32[]{:S(2)}, u32[]{:S(2)}) %collective-permute-start.9) | collective-permute-done | bytes 393248 | tf_op jit(solution)/shard_map/ppermute | solution.py:228
  70.6 0.1 stack.27.w0_ref
  70.6 0.1 collective-permute-start.12
  70.7 0.0 collective-permute-done.10.u2
  70.7 0.0 copy-start.1
  70.7 1.4 %grad_w.1 = (f32[192,1536]{1,0:T(8,128)S(1)}, bf16[192,1536]{1,0:T(8,128)(2,1)S(1)}, bf16[8,64,1536]{2,1,0:T(8,128)(2,1)S(1)}) custom-call(s32[5]{0:T(128)S(1)} %stack.25.place, bf16[512,384]{1,0:T(8,128)(2,1)S(1)} %get-tuple-element.59.mixed_ref, bf16[128,1536]{1,0:T(8,128)(2,1)S(1)} %stack.26.u0, bf16[128,1536]{1,0:T(8,128)(2,1)S(1)} %collective-permute-done.8.u1, ...), custom_call_target="tpu_custom_call" | custom-call | flops 20000000000 | bytes 5308436 | tf_op jit(solution)/shard_map/grad_w/pallas_call | solution.py:54
  72.2 0.6 collective-permute-start.11
  72.8 0.2 collective-permute-done.12.w1_ref
  73.0 2.3 %scores_bwd.1 = (bf16[8,64,384]{2,1,0:T(8,128)(2,1)S(1)}, bf16[3,4,128,128]{3,2,1,0:T(8,128)(2,1)S(1)}, f32[8,384]{1,0:T(8,128)S(1)}) custom-call(s32[5]{0:T(128)S(1)} %stack.25.place, s32[8,384]{1,0:T(8,128)S(1)} %copy-done.1, bf16[8,3,64,384]{3,2,1,0:T(8,128)(2,1)S(1)} %all-to-all-done.qkv_ref.recv_ref, ...), custom_call_target="tpu_custom_call" | custom-call | flops 900000000 | bytes 5922836 | tf_op jit(solution)/shard_map/scores_bwd/pallas_call | solution.py:54
  75.3 0.4 collective-permute-start.13
  75.7 1.2 grads.1
  76.9 0.0 collective-permute-done.13.s1
  76.9 1.5 %join.1 = bf16[32,8,1280]{2,1,0:T(8,128)(2,1)} custom-call(f32[192,1536]{1,0:T(8,128)S(1)} %get-tuple-element.69.mine_ref, bf16[192,1536]{1,0:T(8,128)(2,1)S(1)} %collective-permute-done.11.other_ref, f32[8,384]{1,0:T(8,128)S(1)} %get-tuple-element.77.s0, f32[8,384]{1,0:T(8,128)S(1)} %collective-permute-done.13.s1), custom_call_target="tpu_custom_call" | custom-call | bytes 2449408 | tf_op jit(solution)/shard_map/join/pallas_call | solution.py:54
  78.4 5.9 %all-to-all-start.2 = ((bf16[32,8,1280]{2,1,0:T(8,128)(2,1)}), bf16[32,8,1280]{2,1,0:T(8,128)(2,1)S(1)}, u32[]{:S(2)}, u32[]{:S(2)}) async-start(bf16[32,8,1280]{2,1,0:T(8,128)(2,1)} %join.1), calls=%async_computation.2 | async-start | bytes 1310720 | tf_op jit(solution)/shard_map/all_to_all | solution.py:327
  84.3 0.1 collective-permute-start.14
  84.4 0.1 collective-permute-start.15
  84.5 1.8 %collective-permute-start.16 = (bf16[3,64,384]{2,1,0:T(8,128)(2,1)S(1)}, bf16[3,64,384]{2,1,0:T(8,128)(2,1)S(1)}, u32[]{:S(2)}, u32[]{:S(2)}) collective-permute-start(bf16[3,64,384]{2,1,0:T(8,128)(2,1)S(1)} %get-tuple-element.91), channel_id=1, source_target_pairs={{0,3},{1,2},{2,1},{3,0},{4,7},{5,6},{6,5},{7,4},{8,11},{9,10},{10,... | collective-permute-start | bytes 442376 | tf_op jit(solution)/shard_map/ppermute | solution.py:228
  86.3 1.8 %collective-permute-start.17 = (bf16[3,64,384]{2,1,0:T(8,128)(2,1)S(1)}, bf16[3,64,384]{2,1,0:T(8,128)(2,1)S(1)}, u32[]{:S(2)}, u32[]{:S(2)}) collective-permute-start(bf16[3,64,384]{2,1,0:T(8,128)(2,1)S(1)} %get-tuple-element.92), channel_id=1, source_target_pairs={{0,4},{1,5},{2,6},{3,7},{4,0},{5,1},{6,2},{7,3},{8,12},{9,13},{10,... | collective-permute-start | bytes 442376 | tf_op jit(solution)/shard_map/ppermute | solution.py:228
  88.1 1.4 %collective-permute-start.18 = (bf16[3,64,384]{2,1,0:T(8,128)(2,1)S(1)}, bf16[3,64,384]{2,1,0:T(8,128)(2,1)S(1)}, u32[]{:S(2)}, u32[]{:S(2)}) collective-permute-start(bf16[3,64,384]{2,1,0:T(8,128)(2,1)S(1)} %get-tuple-element.93), channel_id=1, source_target_pairs={{0,5},{1,4},{2,7},{3,6},{4,1},{5,0},{6,3},{7,2},{8,13},{9,12},{10,... | collective-permute-start | bytes 442376 | tf_op jit(solution)/shard_map/ppermute | solution.py:228
  89.5 2.1 %collective-permute-start.20 = (bf16[3,64,384]{2,1,0:T(8,128)(2,1)S(1)}, bf16[3,64,384]{2,1,0:T(8,128)(2,1)S(1)}, u32[]{:S(2)}, u32[]{:S(2)}) collective-permute-start(bf16[3,64,384]{2,1,0:T(8,128)(2,1)S(1)} %get-tuple-element.102), channel_id=1, source_target_pairs={{0,6},{1,7},{2,4},{3,5},{4,2},{5,3},{6,0},{7,1},{8,14},{9,15},{10,... | collective-permute-start | bytes 442376 | tf_op jit(solution)/shard_map/ppermute | solution.py:228
  91.5 0.0 collective-permute-done.15.refs_2_
  91.6 0.9 collective-permute-start.21
  92.5 0.9 collective-permute-done.16.refs_3_
  93.3 5.7 %collective-permute-done.17.refs_4_ = bf16[3,64,384]{2,1,0:T(8,128)(2,1)S(1)} collective-permute-done((bf16[3,64,384]{2,1,0:T(8,128)(2,1)S(1)}, bf16[3,64,384]{2,1,0:T(8,128)(2,1)S(1)}, u32[]{:S(2)}, u32[]{:S(2)}) %collective-permute-start.17) | collective-permute-done | bytes 147488 | tf_op jit(solution)/shard_map/ppermute | solution.py:228
  99.1 2.2 %collective-permute-done.18.refs_5_ = bf16[3,64,384]{2,1,0:T(8,128)(2,1)S(1)} collective-permute-done((bf16[3,64,384]{2,1,0:T(8,128)(2,1)S(1)}, bf16[3,64,384]{2,1,0:T(8,128)(2,1)S(1)}, u32[]{:S(2)}, u32[]{:S(2)}) %collective-permute-start.18) | collective-permute-done | bytes 147488 | tf_op jit(solution)/shard_map/ppermute | solution.py:228
  101.3 3.0 %all-to-all-done.2.in_ref = bf16[32,8,1280]{2,1,0:T(8,128)(2,1)S(1)} async-done(((bf16[32,8,1280]{2,1,0:T(8,128)(2,1)}), bf16[32,8,1280]{2,1,0:T(8,128)(2,1)S(1)}, u32[]{:S(2)}, u32[]{:S(2)}) %all-to-all-start.2) | async-done | bytes 655392 | tf_op jit(solution)/shard_map/all_to_all | solution.py:327
  104.2 0.5 total.1
  104.7 1.9 %collective-permute-start.19 = (f32[8,1536]{1,0:T(8,128)S(1)}, f32[8,1536]{1,0:T(8,128)S(1)}, u32[]{:S(2)}, u32[]{:S(2)}) collective-permute-start(f32[8,1536]{1,0:T(8,128)S(1)} %get-tuple-element.95), channel_id=1, source_target_pairs={{0,0},{32,2},{64,4},{96,6},{128,32},{160,34},{192,36},{224,38},{2,... | collective-permute-start | bytes 147464 | tf_op jit(solution)/shard_map/ppermute | solution.py:331
  106.7 1.0 collective-permute-start.22
  107.6 3.4 %collective-permute-start.23 = (f32[16,128]{1,0:T(8,128)S(1)}, f32[16,128]{1,0:T(8,128)S(1)}, u32[]{:S(2)}, u32[]{:S(2)}) collective-permute-start(f32[16,128]{1,0:T(8,128)S(1)} %get-tuple-element.106.o0), channel_id=1, source_target_pairs={{0,4},{2,6},{4,0},{6,2},{1,5},{3,7},{5,1},{7,3},{8,12},{10,14},{12... | collective-permute-start | bytes 24584 | tf_op jit(solution)/shard_map/ppermute | solution.py:228
  111.0 0.0 collective-permute-done.20.refs_6_
  111.0 0.4 collective-permute-start.24
  111.5 1.8 %unpack.1 = bf16[3,128,1536]{2,1,0:T(8,128)(2,1)} custom-call(s32[5]{0:T(128)S(1)} %stack.25.place, bf16[3,64,384]{2,1,0:T(8,128)(2,1)S(1)} %get-tuple-element.96.refs_0_, bf16[3,64,384]{2,1,0:T(8,128)(2,1)S(1)} %collective-permute-done.14.refs_1_, bf16[3,64,384]{2,1,0:T(8,128)(2,1)S(1)} %collective-permute-done.15.refs_2_, ...), custom_call_target="tpu_custom_call" | custom-call | bytes 2359316 | tf_op jit(solution)/shard_map/unpack/pallas_call | solution.py:54
  113.2 0.9 collective-permute-done.19.home_ref
  114.1 1.8 %collective-permute-done.24.o3 = f32[16,128]{1,0:T(8,128)S(1)} collective-permute-done((f32[16,128]{1,0:T(8,128)S(1)}, f32[16,128]{1,0:T(8,128)S(1)}, u32[]{:S(2)}, u32[]{:S(2)}) %collective-permute-start.24) | collective-permute-done | bytes 8224 | tf_op jit(solution)/shard_map/ppermute | solution.py:228
  115.9 1.2 last.1
  (21 shorter events, 0.1 us)
Async XLA Ops:
  0.6 4.5 %copy-start = (bf16[3,1,1,128,1536]{4,3,2,1,0:T(8,128)(2,1)S(1)}, bf16[3,1,1,128,1536]{4,3,2,1,0:T(8,128)(2,1)}, u32[]{:S(2)}) copy-start(bf16[3,1,1,128,1536]{4,3,2,1,0:T(8,128)(2,1)} %param.7) | copy-start | bytes 3538948
  0.6 25.7 %all-to-all-start.1 = ((bf16[8,32,1536]{2,1,0:T(8,128)(2,1)}), bf16[8,32,1536]{2,1,0:T(8,128)(2,1)S(1)}, u32[]{:S(2)}, u32[]{:S(2)}) async-start(bf16[8,32,1536]{2,1,0:T(8,128)(2,1)} %bitcast.11), calls=%async_computation.1 | async-start | bytes 1572864 | tf_op jit(solution)/shard_map/all_to_all | solution.py:242
  5.1 1.1 copy-start.5
  6.2 10.0 %collective-permute-start.1 = (bf16[8,1536]{1,0:T(8,128)(2,1)S(1)}, bf16[8,1536]{1,0:T(8,128)(2,1)S(1)}, u32[]{:S(2)}, u32[]{:S(2)}) collective-permute-start(bf16[8,1536]{1,0:T(8,128)(2,1)S(1)} %pad.4), channel_id=1, source_target_pairs={{0,32},{2,0},{4,96},{6,64},{32,160},{34,128},{36,224},{38,192},{64... | collective-permute-start | bytes 73736 | tf_op jit(solution)/shard_map/ppermute | solution.py:245
  12.6 6.6 %collective-permute-start = (bf16[8,1536]{1,0:T(8,128)(2,1)S(1)}, bf16[8,1536]{1,0:T(8,128)(2,1)S(1)}, u32[]{:S(2)}, u32[]{:S(2)}) collective-permute-start(bf16[8,1536]{1,0:T(8,128)(2,1)S(1)} %pad.4), channel_id=1, source_target_pairs={{0,0},{2,32},{4,64},{6,96},{32,128},{34,160},{36,192},{38,224},{64... | collective-permute-start | bytes 73736 | tf_op jit(solution)/shard_map/ppermute | solution.py:245
  19.2 7.1 %collective-permute-start.2 = (bf16[16,1536]{1,0:T(8,128)(2,1)S(1)}, bf16[16,1536]{1,0:T(8,128)(2,1)S(1)}, u32[]{:S(2)}, u32[]{:S(2)}) collective-permute-start(bf16[16,1536]{1,0:T(8,128)(2,1)S(1)} %pad_maximum_fusion.2), channel_id=1, source_target_pairs={{0,64},{32,96},{64,0},{96,32},{128,192},{160,224},{192,128},{224,1... | collective-permute-start | bytes 147464 | tf_op jit(solution)/shard_map/ppermute | solution.py:228
  26.3 6.2 %copy-start.2 = (s32[1,8]{1,0:T(1,128)S(1)}, s32[1,8]{1,0:T(1,128)}, u32[]{:S(2)}) copy-start(s32[1,8]{1,0:T(1,128)} %sizes.1) | copy-start | bytes 100
  26.3 29.2 %all-to-all-start = ((bf16[8,3,64,384]{3,2,1,0:T(8,128)(2,1)}), bf16[8,3,64,384]{3,2,1,0:T(8,128)(2,1)S(1)}, u32[]{:S(2)}, u32[]{:S(2)}) async-start(bf16[8,3,64,384]{3,2,1,0:T(8,128)(2,1)} %pack.1), calls=%async_computation | async-start | bytes 2359296 | tf_op jit(solution)/shard_map/all_to_all | solution.py:249
  32.4 23.1 %copy-start.3 = (f32[12,15]{1,0:T(8,128)S(1)}, f32[12,15]{1,0:T(8,128)}, u32[]{:S(2)}) copy-start(f32[12,15]{1,0:T(8,128)} %bias.1) | copy-start | bytes 2164
  33.3 11.1 %collective-permute-start.3 = (bf16[32,1536]{1,0:T(8,128)(2,1)S(1)}, bf16[32,1536]{1,0:T(8,128)(2,1)S(1)}, u32[]{:S(2)}, u32[]{:S(2)}) collective-permute-start(bf16[32,1536]{1,0:T(8,128)(2,1)S(1)} %pad_maximum_fusion.1), channel_id=1, source_target_pairs={{0,128},{32,160},{64,192},{96,224},{128,0},{160,32},{192,64},{224,... | collective-permute-start | bytes 294920 | tf_op jit(solution)/shard_map/ppermute | solution.py:228
  36.3 8.2 %collective-permute-start.4 = (bf16[64,1536]{1,0:T(8,128)(2,1)S(1)}, bf16[64,1536]{1,0:T(8,128)(2,1)S(1)}, u32[]{:S(2)}, u32[]{:S(2)}) collective-permute-start(bf16[64,1536]{1,0:T(8,128)(2,1)S(1)} %get-tuple-element.64), channel_id=1, source_target_pairs={{0,1},{1,0},{2,3},{3,2},{4,5},{5,4},{6,7},{7,6},{8,9},{9,8},{10,11... | collective-permute-start | bytes 589832 | tf_op jit(solution)/shard_map/ppermute | solution.py:228
  44.5 8.5 %collective-permute-start.5 = (bf16[64,1536]{1,0:T(8,128)(2,1)S(1)}, bf16[64,1536]{1,0:T(8,128)(2,1)S(1)}, u32[]{:S(2)}, u32[]{:S(2)}) collective-permute-start(bf16[64,1536]{1,0:T(8,128)(2,1)S(1)} %pad_maximum_fusion.refs_0_), channel_id=1, source_target_pairs={{0,8},{8,0},{16,24},{24,16},{1,9},{9,1},{17,25},{25,17},{2,10},{10... | collective-permute-start | bytes 589832 | tf_op jit(solution)/shard_map/ppermute | solution.py:228
  46.2 15.1 %collective-permute-start.6 = (bf16[64,1536]{1,0:T(8,128)(2,1)S(1)}, bf16[64,1536]{1,0:T(8,128)(2,1)S(1)}, u32[]{:S(2)}, u32[]{:S(2)}) collective-permute-start(bf16[64,1536]{1,0:T(8,128)(2,1)S(1)} %pad_maximum_fusion.refs_0_), channel_id=1, source_target_pairs={{0,16},{8,24},{16,0},{24,8},{1,17},{9,25},{17,1},{25,9},{2,18},{10... | collective-permute-start | bytes 589832 | tf_op jit(solution)/shard_map/ppermute | solution.py:228
  49.1 12.2 %collective-permute-start.7 = (bf16[64,1536]{1,0:T(8,128)(2,1)S(1)}, bf16[64,1536]{1,0:T(8,128)(2,1)S(1)}, u32[]{:S(2)}, u32[]{:S(2)}) collective-permute-start(bf16[64,1536]{1,0:T(8,128)(2,1)S(1)} %pad_maximum_fusion.refs_0_), channel_id=1, source_target_pairs={{0,24},{8,16},{16,8},{24,0},{1,25},{9,17},{17,9},{25,1},{2,26},{10... | collective-permute-start | bytes 589832 | tf_op jit(solution)/shard_map/ppermute | solution.py:228
  49.3 12.1 %collective-permute-start.8 = (bf16[128,1536]{1,0:T(8,128)(2,1)S(1)}, bf16[128,1536]{1,0:T(8,128)(2,1)S(1)}, u32[]{:S(2)}, u32[]{:S(2)}) collective-permute-start(bf16[128,1536]{1,0:T(8,128)(2,1)S(1)} %stack.26.u0), channel_id=1, source_target_pairs={{0,2},{2,0},{4,6},{6,4},{1,3},{3,1},{5,7},{7,5},{8,10},{10,8},{12,... | collective-permute-start | bytes 1179656 | tf_op jit(solution)/shard_map/ppermute | solution.py:228
  50.9 19.6 %collective-permute-start.9 = (bf16[128,1536]{1,0:T(8,128)(2,1)S(1)}, bf16[128,1536]{1,0:T(8,128)(2,1)S(1)}, u32[]{:S(2)}, u32[]{:S(2)}) collective-permute-start(bf16[128,1536]{1,0:T(8,128)(2,1)S(1)} %stack.26.u0), channel_id=1, source_target_pairs={{0,6},{2,4},{4,2},{6,0},{1,7},{3,5},{5,3},{7,1},{8,14},{10,12},{12... | collective-permute-start | bytes 1179656 | tf_op jit(solution)/shard_map/ppermute | solution.py:228
  53.0 17.7 %collective-permute-start.10 = (bf16[128,1536]{1,0:T(8,128)(2,1)S(1)}, bf16[128,1536]{1,0:T(8,128)(2,1)S(1)}, u32[]{:S(2)}, u32[]{:S(2)}) collective-permute-start(bf16[128,1536]{1,0:T(8,128)(2,1)S(1)} %stack.26.u0), channel_id=1, source_target_pairs={{0,4},{2,6},{4,0},{6,2},{1,5},{3,7},{5,1},{7,3},{8,12},{10,14},{12... | collective-permute-start | bytes 1179656 | tf_op jit(solution)/shard_map/ppermute | solution.py:228
  55.5 0.7 copy-start.4
  70.6 2.4 %collective-permute-start.12 = (bf16[256,1536]{1,0:T(8,128)(2,1)S(1)}, bf16[256,1536]{1,0:T(8,128)(2,1)S(1)}, u32[]{:S(2)}, u32[]{:S(2)}) collective-permute-start(bf16[256,1536]{1,0:T(8,128)(2,1)S(1)} %stack.27.w0_ref), channel_id=1, source_target_pairs={{0,1},{1,0},{2,3},{3,2},{4,5},{5,4},{6,7},{7,6},{8,9},{9,8},{10,11... | collective-permute-start | bytes 2359304 | tf_op jit(solution)/shard_map/ppermute | solution.py:228
  70.7 2.3 %copy-start.1 = (s32[8,384]{1,0:T(8,128)S(1)}, s32[8,384]{1,0:T(8,128)}, u32[]{:S(2)}) copy-start(s32[8,384]{1,0:T(8,128)} %constant.26.clone.rows_ref) | copy-start | bytes 36868
  72.2 4.7 %collective-permute-start.11 = (bf16[192,1536]{1,0:T(8,128)(2,1)S(1)}, bf16[192,1536]{1,0:T(8,128)(2,1)S(1)}, u32[]{:S(2)}, u32[]{:S(2)}) collective-permute-start(bf16[192,1536]{1,0:T(8,128)(2,1)S(1)} %get-tuple-element.70), channel_id=1, source_target_pairs={{0,1},{1,0},{2,3},{3,2},{4,5},{5,4},{6,7},{7,6},{8,9},{9,8},{10,11... | collective-permute-start | bytes 1769480 | tf_op jit(solution)/shard_map/ppermute | solution.py:228
  75.3 1.6 %collective-permute-start.13 = (f32[8,384]{1,0:T(8,128)S(1)}, f32[8,384]{1,0:T(8,128)S(1)}, u32[]{:S(2)}, u32[]{:S(2)}) collective-permute-start(f32[8,384]{1,0:T(8,128)S(1)} %get-tuple-element.77.s0), channel_id=1, source_target_pairs={{0,1},{1,0},{2,3},{3,2},{4,5},{5,4},{6,7},{7,6},{8,9},{9,8},{10,11... | collective-permute-start | bytes 36872 | tf_op jit(solution)/shard_map/ppermute | solution.py:228
  78.4 25.8 %all-to-all-start.2 = ((bf16[32,8,1280]{2,1,0:T(8,128)(2,1)}), bf16[32,8,1280]{2,1,0:T(8,128)(2,1)S(1)}, u32[]{:S(2)}, u32[]{:S(2)}) async-start(bf16[32,8,1280]{2,1,0:T(8,128)(2,1)} %join.1), calls=%async_computation.2 | async-start | bytes 1310720 | tf_op jit(solution)/shard_map/all_to_all | solution.py:327
  84.3 5.2 %collective-permute-start.14 = (bf16[3,64,384]{2,1,0:T(8,128)(2,1)S(1)}, bf16[3,64,384]{2,1,0:T(8,128)(2,1)S(1)}, u32[]{:S(2)}, u32[]{:S(2)}) collective-permute-start(bf16[3,64,384]{2,1,0:T(8,128)(2,1)S(1)} %get-tuple-element.89), channel_id=1, source_target_pairs={{0,1},{1,0},{2,3},{3,2},{4,5},{5,4},{6,7},{7,6},{8,9},{9,8},{10,11... | collective-permute-start | bytes 442376 | tf_op jit(solution)/shard_map/ppermute | solution.py:228
  84.4 7.2 %collective-permute-start.15 = (bf16[3,64,384]{2,1,0:T(8,128)(2,1)S(1)}, bf16[3,64,384]{2,1,0:T(8,128)(2,1)S(1)}, u32[]{:S(2)}, u32[]{:S(2)}) collective-permute-start(bf16[3,64,384]{2,1,0:T(8,128)(2,1)S(1)} %get-tuple-element.90), channel_id=1, source_target_pairs={{0,2},{1,3},{2,0},{3,1},{4,6},{5,7},{6,4},{7,5},{8,10},{9,11},{10,... | collective-permute-start | bytes 442376 | tf_op jit(solution)/shard_map/ppermute | solution.py:228
  84.5 8.9 %collective-permute-start.16 = (bf16[3,64,384]{2,1,0:T(8,128)(2,1)S(1)}, bf16[3,64,384]{2,1,0:T(8,128)(2,1)S(1)}, u32[]{:S(2)}, u32[]{:S(2)}) collective-permute-start(bf16[3,64,384]{2,1,0:T(8,128)(2,1)S(1)} %get-tuple-element.91), channel_id=1, source_target_pairs={{0,3},{1,2},{2,1},{3,0},{4,7},{5,6},{6,5},{7,4},{8,11},{9,10},{10,... | collective-permute-start | bytes 442376 | tf_op jit(solution)/shard_map/ppermute | solution.py:228
  86.3 12.8 %collective-permute-start.17 = (bf16[3,64,384]{2,1,0:T(8,128)(2,1)S(1)}, bf16[3,64,384]{2,1,0:T(8,128)(2,1)S(1)}, u32[]{:S(2)}, u32[]{:S(2)}) collective-permute-start(bf16[3,64,384]{2,1,0:T(8,128)(2,1)S(1)} %get-tuple-element.92), channel_id=1, source_target_pairs={{0,4},{1,5},{2,6},{3,7},{4,0},{5,1},{6,2},{7,3},{8,12},{9,13},{10,... | collective-permute-start | bytes 442376 | tf_op jit(solution)/shard_map/ppermute | solution.py:228
  88.1 13.2 %collective-permute-start.18 = (bf16[3,64,384]{2,1,0:T(8,128)(2,1)S(1)}, bf16[3,64,384]{2,1,0:T(8,128)(2,1)S(1)}, u32[]{:S(2)}, u32[]{:S(2)}) collective-permute-start(bf16[3,64,384]{2,1,0:T(8,128)(2,1)S(1)} %get-tuple-element.93), channel_id=1, source_target_pairs={{0,5},{1,4},{2,7},{3,6},{4,1},{5,0},{6,3},{7,2},{8,13},{9,12},{10,... | collective-permute-start | bytes 442376 | tf_op jit(solution)/shard_map/ppermute | solution.py:228
  89.5 21.5 %collective-permute-start.20 = (bf16[3,64,384]{2,1,0:T(8,128)(2,1)S(1)}, bf16[3,64,384]{2,1,0:T(8,128)(2,1)S(1)}, u32[]{:S(2)}, u32[]{:S(2)}) collective-permute-start(bf16[3,64,384]{2,1,0:T(8,128)(2,1)S(1)} %get-tuple-element.102), channel_id=1, source_target_pairs={{0,6},{1,7},{2,4},{3,5},{4,2},{5,3},{6,0},{7,1},{8,14},{9,15},{10,... | collective-permute-start | bytes 442376 | tf_op jit(solution)/shard_map/ppermute | solution.py:228
  91.6 19.9 %collective-permute-start.21 = (bf16[3,64,384]{2,1,0:T(8,128)(2,1)S(1)}, bf16[3,64,384]{2,1,0:T(8,128)(2,1)S(1)}, u32[]{:S(2)}, u32[]{:S(2)}) collective-permute-start(bf16[3,64,384]{2,1,0:T(8,128)(2,1)S(1)} %get-tuple-element.103), channel_id=1, source_target_pairs={{0,7},{1,6},{2,5},{3,4},{4,3},{5,2},{6,1},{7,0},{8,15},{9,14},{10,... | collective-permute-start | bytes 442376 | tf_op jit(solution)/shard_map/ppermute | solution.py:228
  104.7 9.4 %collective-permute-start.19 = (f32[8,1536]{1,0:T(8,128)S(1)}, f32[8,1536]{1,0:T(8,128)S(1)}, u32[]{:S(2)}, u32[]{:S(2)}) collective-permute-start(f32[8,1536]{1,0:T(8,128)S(1)} %get-tuple-element.95), channel_id=1, source_target_pairs={{0,0},{32,2},{64,4},{96,6},{128,32},{160,34},{192,36},{224,38},{2,... | collective-permute-start | bytes 147464 | tf_op jit(solution)/shard_map/ppermute | solution.py:331
  106.7 7.4 %collective-permute-start.22 = (f32[16,128]{1,0:T(8,128)S(1)}, f32[16,128]{1,0:T(8,128)S(1)}, u32[]{:S(2)}, u32[]{:S(2)}) collective-permute-start(f32[16,128]{1,0:T(8,128)S(1)} %get-tuple-element.106.o0), channel_id=1, source_target_pairs={{0,2},{2,0},{4,6},{6,4},{1,3},{3,1},{5,7},{7,5},{8,10},{10,8},{12,... | collective-permute-start | bytes 24584 | tf_op jit(solution)/shard_map/ppermute | solution.py:228
  107.6 6.5 %collective-permute-start.23 = (f32[16,128]{1,0:T(8,128)S(1)}, f32[16,128]{1,0:T(8,128)S(1)}, u32[]{:S(2)}, u32[]{:S(2)}) collective-permute-start(f32[16,128]{1,0:T(8,128)S(1)} %get-tuple-element.106.o0), channel_id=1, source_target_pairs={{0,4},{2,6},{4,0},{6,2},{1,5},{3,7},{5,1},{7,3},{8,12},{10,14},{12... | collective-permute-start | bytes 24584 | tf_op jit(solution)/shard_map/ppermute | solution.py:228
  111.0 4.9 %collective-permute-start.24 = (f32[16,128]{1,0:T(8,128)S(1)}, f32[16,128]{1,0:T(8,128)S(1)}, u32[]{:S(2)}, u32[]{:S(2)}) collective-permute-start(f32[16,128]{1,0:T(8,128)S(1)} %get-tuple-element.106.o0), channel_id=1, source_target_pairs={{0,6},{2,4},{4,2},{6,0},{1,7},{3,5},{5,3},{7,1},{8,14},{10,12},{12... | collective-permute-start | bytes 24584 | tf_op jit(solution)/shard_map/ppermute | solution.py:228

commit v9 on v8

--- a/solution.py
+++ b/solution.py
@@ -66,12 +66,14 @@
 def stack_kernel(*refs):
     out_ref, row = refs[-1], 0
     for ref in refs[:-1]:
-        out_ref[row : row + HALF] = ref[...]
-        row += HALF
+        rows = ref.shape[0]
+        out_ref[row : row + rows] = ref[...]
+        row += rows
 
 
 def stack(parts):
-    return call(stack_kernel, "stack", [((len(parts) * HALF, DW), bf)], *parts)[0]
+    rows = sum(p.shape[0] for p in parts)
+    return call(stack_kernel, "stack", [((rows, DW), bf)], *parts)[0]
 
 
 def pack_kernel(qkv_ref, out_ref):
@@ -243,10 +245,10 @@
     (packed,) = call(pack_kernel, "pack", [((F, 3, HALF, COLS), bf)], qkv_time[:, 0, 0])
     rows8, packed = lax.optimization_barrier((jnp.pad(w_out, ((0, 2), (0, 0))), packed))
     held = [lax.ppermute(rows8, ("z", "x"), p) for p in (there, near)]
+    packed, held = lax.optimization_barrier((packed, held))
+    recv = lax.all_to_all(packed, SEQ, 0, 0, tiled=True)
     held = jnp.concatenate(held)
     held = jnp.concatenate([held, hop(held, "z", 2, Z)])
-    packed, held = lax.optimization_barrier((packed, held))
-    recv = lax.all_to_all(packed, SEQ, 0, 0, tiled=True)
 
     same, other = call(
         compact_kernel,
@@ -261,11 +263,11 @@
     held, same = lax.optimization_barrier((held, same))
     held = jnp.concatenate([held, hop(held, "z", 4, Z)])
     u0 = stack([same, hop(other, "core", 1, C)])
-    held, u0 = lax.optimization_barrier((held, u0))
+    held, _ = lax.optimization_barrier((held, u0))
     ups = [u0] + [hop(u0, "x", k, X) for k in range(1, X)]
-    held = [held] + [hop(held, "y", k, Y) for k in range(1, Y)]
-    held, ups[1], ups[3] = lax.optimization_barrier((held, ups[1], ups[3]))
-    held = stack(held)
+    held = stack([held, hop(held, "y", 1, Y)])
+    held, ups[1] = lax.optimization_barrier((held, ups[1]))
+    held = stack([held, hop(held, "y", 2, Y)])
     held2 = hop(held, "core", 1, C)
 
     probs, mixed = call(

time: 119 us -> 116 us (0.975)
  waiting for transfers between devices: 37.1 us -> 31 us
  starting transfers between devices: 61.3 us -> 65.5 us
    ppermute x22 -> x21, waiting for transfers between devices: 30.3 us -> 24.9 us  [hop(): return lax.ppermute(x, axis, [(i, i ^ k) for i in range(n)])]
    all_to_all x1, starting transfers between devices: 5.86 us -> 10.2 us  [per_device(): msgs = lax.all_to_all(msgs, ('z', 'y'), 0, 0, tiled=True)]
    ppermute x22 -> x21, starting transfers between devices: 33.1 us -> 29.1 us  [hop(): return lax.ppermute(x, axis, [(i, i ^ k) for i in range(n)])]
    ppermute x2, starting transfers between devices: 9.96 us -> 12.2 us  [per_device(): held = [lax.ppermute(rows8, ('z', 'x'), p) for p in (there, near)]]
    all_to_all x1, starting transfers between devices: 6.03 us -> 7.56 us  [per_device(): recv = lax.all_to_all(packed, SEQ, 0, 0, tiled=True)]
    ppermute x2, waiting for transfers between devices: 3 us -> 1.52 us  [per_device(): held = [lax.ppermute(rows8, ('z', 'x'), p) for p in (there, near)]]
    pallas_call x12 -> x13, Pallas kernels: 16.9 us -> 16.9 us  [call(): pl.pallas_call(body, out_shape=tuple((jax.ShapeDtypeStruct(s, d) for s, d...]
  transfers between devices with their start and end apart: 28 -> 27, of which waited for: 11 -> 14; matrix products, arithmetic and copies ran while one was open for 0% -> 0% of each run, Pallas kernels for 12% -> 12%
where the time goes in v9:
time: 116 us; the launch traced here: 115 us
  starting transfers between devices  65.5 us (56%)
  waiting for transfers between devices  31 us (27%)
  Pallas kernels  16.9 us (15%)
    ppermute x21, starting transfers between devices, hop(): return lax.ppermute(x, axis, [(i, i ^ k) for i in range(n)])  29.1 us
    ppermute x21, waiting for transfers between devices, hop(): return lax.ppermute(x, axis, [(i, i ^ k) for i in range(n)])  24.9 us
    pallas_call x13, Pallas kernels, call(): pl.pallas_call(body, out_shape=tuple((jax.ShapeDtypeStruct(s, d) for s, d...  16.9 us
    ppermute x2, starting transfers between devices, per_device(): held = [lax.ppermute(rows8, ('z', 'x'), p) for p in (there, near)]  12.2 us
    all_to_all x1, starting transfers between devices, per_device(): msgs = lax.all_to_all(msgs, ('z', 'y'), 0, 0, tiled=True)  10.2 us
    all_to_all x1, starting transfers between devices, per_device(): recv = lax.all_to_all(packed, SEQ, 0, 0, tiled=True)  7.56 us
    all_to_all x1, starting transfers between devices, per_device(): cot = lax.all_to_all(cot_out[0, 0], SEQ, 0, 0, tiled=True)  4.44 us
    all_to_all x1, waiting for transfers between devices, per_device(): msgs = lax.all_to_all(msgs, ('z', 'y'), 0, 0, tiled=True)  3.86 us
  transfers between devices with their start and end apart: 27, of which 14 were waited for; matrix products, arithmetic and copies ran while one was open for 0% of the time, Pallas kernels for 12%

profile of v9, /device:TPU:32, one launch (start us, length us, event | category | flops | bytes accessed | tf_op | source)
XLA Modules:
  0.0 115.1 jit_solution(12428960318675918308)
XLA Ops:
  0.6 4.4 %all-to-all-start.1 = ((bf16[8,32,1536]{2,1,0:T(8,128)(2,1)}), bf16[8,32,1536]{2,1,0:T(8,128)(2,1)S(1)}, u32[]{:S(2)}, u32[]{:S(2)}) async-start(bf16[8,32,1536]{2,1,0:T(8,128)(2,1)} %bitcast.11), calls=%async_computation.1 | async-start | bytes 1572864 | tf_op jit(solution)/shard_map/all_to_all | solution.py:244
  5.1 0.0 copy-start.5
  5.1 1.1 pack.1
  6.2 0.0 copy-start.2
  6.2 7.7 %collective-permute-start = (bf16[8,1536]{1,0:T(8,128)(2,1)S(1)}, bf16[8,1536]{1,0:T(8,128)(2,1)S(1)}, u32[]{:S(2)}, u32[]{:S(2)}) collective-permute-start(bf16[8,1536]{1,0:T(8,128)(2,1)S(1)} %pad.4), channel_id=1, source_target_pairs={{0,0},{2,32},{4,64},{6,96},{32,128},{34,160},{36,192},{38,224},{64... | collective-permute-start | bytes 73736 | tf_op jit(solution)/shard_map/ppermute | solution.py:247
  14.0 4.5 %collective-permute-start.1 = (bf16[8,1536]{1,0:T(8,128)(2,1)S(1)}, bf16[8,1536]{1,0:T(8,128)(2,1)S(1)}, u32[]{:S(2)}, u32[]{:S(2)}) collective-permute-start(bf16[8,1536]{1,0:T(8,128)(2,1)S(1)} %pad.4), channel_id=1, source_target_pairs={{0,32},{2,0},{4,96},{6,64},{32,160},{34,128},{36,224},{38,192},{64... | collective-permute-start | bytes 73736 | tf_op jit(solution)/shard_map/ppermute | solution.py:247
  18.5 1.5 %collective-permute-done.1 = bf16[8,1536]{1,0:T(8,128)(2,1)S(1)} collective-permute-done((bf16[8,1536]{1,0:T(8,128)(2,1)S(1)}, bf16[8,1536]{1,0:T(8,128)(2,1)S(1)}, u32[]{:S(2)}, u32[]{:S(2)}) %collective-permute-start.1) | collective-permute-done | bytes 24608 | tf_op jit(solution)/shard_map/ppermute | solution.py:247
  20.0 0.0 all-to-all-done.1.cot_ref
  20.0 7.6 %all-to-all-start = ((bf16[8,3,64,384]{3,2,1,0:T(8,128)(2,1)}), bf16[8,3,64,384]{3,2,1,0:T(8,128)(2,1)S(1)}, u32[]{:S(2)}, u32[]{:S(2)}) async-start(bf16[8,3,64,384]{3,2,1,0:T(8,128)(2,1)} %pack.1), calls=%async_computation | async-start | bytes 2359296 | tf_op jit(solution)/shard_map/all_to_all | solution.py:249
  27.6 1.7 %collective-permute-start.2 = (bf16[16,1536]{1,0:T(8,128)(2,1)S(1)}, bf16[16,1536]{1,0:T(8,128)(2,1)S(1)}, u32[]{:S(2)}, u32[]{:S(2)}) collective-permute-start(bf16[16,1536]{1,0:T(8,128)(2,1)S(1)} %pad_maximum_fusion.2), channel_id=1, source_target_pairs={{0,64},{32,96},{64,0},{96,32},{128,192},{160,224},{192,128},{224,1... | collective-permute-start | bytes 147464 | tf_op jit(solution)/shard_map/ppermute | solution.py:230
  29.2 0.1 stack.26.place
  29.3 0.8 compact.1
  30.1 0.0 copy-start.3
  30.1 0.3 collective-permute-start.3
  30.4 2.3 %collective-permute-done.2 = bf16[16,1536]{1,0:T(8,128)(2,1)S(1)} collective-permute-done((bf16[16,1536]{1,0:T(8,128)(2,1)S(1)}, bf16[16,1536]{1,0:T(8,128)(2,1)S(1)}, u32[]{:S(2)}, u32[]{:S(2)}) %collective-permute-start.2) | collective-permute-done | bytes 49184 | tf_op jit(solution)/shard_map/ppermute | solution.py:230
  32.7 2.3 %collective-permute-start.4 = (bf16[32,1536]{1,0:T(8,128)(2,1)S(1)}, bf16[32,1536]{1,0:T(8,128)(2,1)S(1)}, u32[]{:S(2)}, u32[]{:S(2)}) collective-permute-start(bf16[32,1536]{1,0:T(8,128)(2,1)S(1)} %pad_maximum_fusion.1), channel_id=1, source_target_pairs={{0,128},{32,160},{64,192},{96,224},{128,0},{160,32},{192,64},{224,... | collective-permute-start | bytes 294920 | tf_op jit(solution)/shard_map/ppermute | solution.py:230
  35.0 2.0 %collective-permute-start.6 = (bf16[128,1536]{1,0:T(8,128)(2,1)S(1)}, bf16[128,1536]{1,0:T(8,128)(2,1)S(1)}, u32[]{:S(2)}, u32[]{:S(2)}) collective-permute-start(bf16[128,1536]{1,0:T(8,128)(2,1)S(1)} %stack.27.u0), channel_id=1, source_target_pairs={{0,2},{2,0},{4,6},{6,4},{1,3},{3,1},{5,7},{7,5},{8,10},{10,8},{12,... | collective-permute-start | bytes 1179656 | tf_op jit(solution)/shard_map/ppermute | solution.py:230
  37.0 4.4 %collective-permute-done.4 = bf16[32,1536]{1,0:T(8,128)(2,1)S(1)} collective-permute-done((bf16[32,1536]{1,0:T(8,128)(2,1)S(1)}, bf16[32,1536]{1,0:T(8,128)(2,1)S(1)}, u32[]{:S(2)}, u32[]{:S(2)}) %collective-permute-start.4) | collective-permute-done | bytes 98336 | tf_op jit(solution)/shard_map/ppermute | solution.py:230
  41.4 1.7 %collective-permute-start.5 = (bf16[64,1536]{1,0:T(8,128)(2,1)S(1)}, bf16[64,1536]{1,0:T(8,128)(2,1)S(1)}, u32[]{:S(2)}, u32[]{:S(2)}) collective-permute-start(bf16[64,1536]{1,0:T(8,128)(2,1)S(1)} %pad_maximum_fusion.refs_0_), channel_id=1, source_target_pairs={{0,8},{8,0},{16,24},{24,16},{1,9},{9,1},{17,25},{25,17},{2,10},{10... | collective-permute-start | bytes 589832 | tf_op jit(solution)/shard_map/ppermute | solution.py:230
  43.1 3.6 %collective-permute-start.7 = (bf16[128,1536]{1,0:T(8,128)(2,1)S(1)}, bf16[128,1536]{1,0:T(8,128)(2,1)S(1)}, u32[]{:S(2)}, u32[]{:S(2)}) collective-permute-start(bf16[128,1536]{1,0:T(8,128)(2,1)S(1)} %stack.27.u0), channel_id=1, source_target_pairs={{0,4},{2,6},{4,0},{6,2},{1,5},{3,7},{5,1},{7,3},{8,12},{10,14},{12... | collective-permute-start | bytes 1179656 | tf_op jit(solution)/shard_map/ppermute | solution.py:230
  46.7 1.2 %collective-permute-start.8 = (bf16[128,1536]{1,0:T(8,128)(2,1)S(1)}, bf16[128,1536]{1,0:T(8,128)(2,1)S(1)}, u32[]{:S(2)}, u32[]{:S(2)}) collective-permute-start(bf16[128,1536]{1,0:T(8,128)(2,1)S(1)} %stack.27.u0), channel_id=1, source_target_pairs={{0,6},{2,4},{4,2},{6,0},{1,7},{3,5},{5,3},{7,1},{8,14},{10,12},{12... | collective-permute-start | bytes 1179656 | tf_op jit(solution)/shard_map/ppermute | solution.py:230
  47.8 0.0 collective-permute-done.5.refs_1_
  47.9 4.5 %collective-permute-done.6.u1 = bf16[128,1536]{1,0:T(8,128)(2,1)S(1)} collective-permute-done((bf16[128,1536]{1,0:T(8,128)(2,1)S(1)}, bf16[128,1536]{1,0:T(8,128)(2,1)S(1)}, u32[]{:S(2)}, u32[]{:S(2)}) %collective-permute-start.6) | collective-permute-done | bytes 393248 | tf_op jit(solution)/shard_map/ppermute | solution.py:230
  52.3 3.2 %collective-permute-start.10 = (bf16[128,1536]{1,0:T(8,128)(2,1)S(1)}, bf16[128,1536]{1,0:T(8,128)(2,1)S(1)}, u32[]{:S(2)}, u32[]{:S(2)}) collective-permute-start(bf16[128,1536]{1,0:T(8,128)(2,1)S(1)} %stack.28.refs_0_), channel_id=1, source_target_pairs={{0,16},{8,24},{16,0},{24,8},{1,17},{9,25},{17,1},{25,9},{2,18},{10... | collective-permute-start | bytes 1179656 | tf_op jit(solution)/shard_map/ppermute | solution.py:230
  55.5 0.0 all-to-all-done.qkv_ref.recv_ref
  55.5 0.7 copy-done.4
  56.2 5.0 %attn_fwd.1 = (f32[3,4,128,128]{3,2,1,0:T(8,128)S(1)}, bf16[512,384]{1,0:T(8,128)(2,1)S(1)}) custom-call(s32[5]{0:T(128)S(1)} %stack.26.place, f32[12,15]{1,0:T(8,128)S(1)} %copy-done.3, s32[8,384]{1,0:T(8,128)S(1)} %copy-done.4, bf16[8,3,64,384]{3,2,1,0:T(8,128)(2,1)S(1)} %all-to-all-done.qkv_ref.recv_ref), custom_call_target="tpu_custom_call" | custom-call | flops 20000000000 | bytes 2372324 | tf_op jit(solution)/shard_map/attn_fwd/pallas_call | solution.py:54
  61.3 2.7 %collective-permute-done.10.refs_1_ = bf16[128,1536]{1,0:T(8,128)(2,1)S(1)} collective-permute-done((bf16[128,1536]{1,0:T(8,128)(2,1)S(1)}, bf16[128,1536]{1,0:T(8,128)(2,1)S(1)}, u32[]{:S(2)}, u32[]{:S(2)}) %collective-permute-start.10) | collective-permute-done | bytes 393248 | tf_op jit(solution)/shard_map/ppermute | solution.py:230
  64.0 0.1 stack.29.w0_ref
  64.1 0.1 collective-permute-start.11
  64.2 0.0 collective-permute-done.7.u2
  64.2 0.6 collective-permute-done.8.u3
  64.8 1.4 %grad_w.1 = (f32[192,1536]{1,0:T(8,128)S(1)}, bf16[192,1536]{1,0:T(8,128)(2,1)S(1)}, bf16[8,64,1536]{2,1,0:T(8,128)(2,1)S(1)}) custom-call(s32[5]{0:T(128)S(1)} %stack.26.place, bf16[512,384]{1,0:T(8,128)(2,1)S(1)} %get-tuple-element.55.mixed_ref, bf16[128,1536]{1,0:T(8,128)(2,1)S(1)} %stack.27.u0, bf16[128,1536]{1,0:T(8,128)(2,1)S(1)} %collective-permute-done.6.u1, ...), custom_call_target="tpu_custom_call" | custom-call | flops 20000000000 | bytes 5308436 | tf_op jit(solution)/shard_map/grad_w/pallas_call | solution.py:54
  66.3 0.1 collective-permute-start.9
  66.4 0.1 collective-permute-done.11.w1_ref
  66.5 2.3 %scores_bwd.1 = (bf16[8,64,384]{2,1,0:T(8,128)(2,1)S(1)}, bf16[3,4,128,128]{3,2,1,0:T(8,128)(2,1)S(1)}, f32[8,384]{1,0:T(8,128)S(1)}) custom-call(s32[5]{0:T(128)S(1)} %stack.26.place, s32[8,384]{1,0:T(8,128)S(1)} %copy-done.1, bf16[8,3,64,384]{3,2,1,0:T(8,128)(2,1)S(1)} %all-to-all-done.qkv_ref.recv_ref, ...), custom_call_target="tpu_custom_call" | custom-call | flops 900000000 | bytes 5922836 | tf_op jit(solution)/shard_map/scores_bwd/pallas_call | solution.py:54
  68.7 0.7 collective-permute-start.12
  69.4 1.2 %grads.1 = (bf16[3,64,384]{2,1,0:T(8,128)(2,1)S(1)}, bf16[3,64,384]{2,1,0:T(8,128)(2,1)S(1)}, bf16[3,64,384]{2,1,0:T(8,128)(2,1)S(1)}, bf16[3,64,384]{2,1,0:T(8,...) custom-call(s32[5]{0:T(128)S(1)} %stack.26.place, ...), custom_call_target="tpu_custom_call" | custom-call | flops 150000000 | bytes 3932180 | tf_op jit(solution)/shard_map/grads/pallas_call | solution.py:54
  70.6 0.0 collective-permute-done.9.other_ref
  70.6 0.0 collective-permute-done.12.s1
  70.6 1.5 %join.1 = bf16[32,8,1280]{2,1,0:T(8,128)(2,1)} custom-call(f32[192,1536]{1,0:T(8,128)S(1)} %get-tuple-element.64.mine_ref, bf16[192,1536]{1,0:T(8,128)(2,1)S(1)} %collective-permute-done.9.other_ref, f32[8,384]{1,0:T(8,128)S(1)} %get-tuple-element.69.s0, f32[8,384]{1,0:T(8,128)S(1)} %collective-permute-done.12.s1), custom_call_target="tpu_custom_call" | custom-call | bytes 2449408 | tf_op jit(solution)/shard_map/join/pallas_call | solution.py:54
  72.1 10.2 %all-to-all-start.2 = ((bf16[32,8,1280]{2,1,0:T(8,128)(2,1)}), bf16[32,8,1280]{2,1,0:T(8,128)(2,1)S(1)}, u32[]{:S(2)}, u32[]{:S(2)}) async-start(bf16[32,8,1280]{2,1,0:T(8,128)(2,1)} %join.1), calls=%async_computation.2 | async-start | bytes 1310720 | tf_op jit(solution)/shard_map/all_to_all | solution.py:329
  82.4 0.1 collective-permute-start.13
  82.5 0.1 collective-permute-start.14
  82.6 1.8 %collective-permute-start.15 = (bf16[3,64,384]{2,1,0:T(8,128)(2,1)S(1)}, bf16[3,64,384]{2,1,0:T(8,128)(2,1)S(1)}, u32[]{:S(2)}, u32[]{:S(2)}) collective-permute-start(bf16[3,64,384]{2,1,0:T(8,128)(2,1)S(1)} %get-tuple-element.83), channel_id=1, source_target_pairs={{0,3},{1,2},{2,1},{3,0},{4,7},{5,6},{6,5},{7,4},{8,11},{9,10},{10,... | collective-permute-start | bytes 442376 | tf_op jit(solution)/shard_map/ppermute | solution.py:230
  84.3 0.9 collective-permute-start.16
  85.2 2.3 %collective-permute-start.17 = (bf16[3,64,384]{2,1,0:T(8,128)(2,1)S(1)}, bf16[3,64,384]{2,1,0:T(8,128)(2,1)S(1)}, u32[]{:S(2)}, u32[]{:S(2)}) collective-permute-start(bf16[3,64,384]{2,1,0:T(8,128)(2,1)S(1)} %get-tuple-element.85), channel_id=1, source_target_pairs={{0,5},{1,4},{2,7},{3,6},{4,1},{5,0},{6,3},{7,2},{8,13},{9,12},{10,... | collective-permute-start | bytes 442376 | tf_op jit(solution)/shard_map/ppermute | solution.py:230
  87.6 0.0 collective-permute-done.13.refs_1_
  87.6 1.2 %collective-permute-start.19 = (bf16[3,64,384]{2,1,0:T(8,128)(2,1)S(1)}, bf16[3,64,384]{2,1,0:T(8,128)(2,1)S(1)}, u32[]{:S(2)}, u32[]{:S(2)}) collective-permute-start(bf16[3,64,384]{2,1,0:T(8,128)(2,1)S(1)} %get-tuple-element.94), channel_id=1, source_target_pairs={{0,6},{1,7},{2,4},{3,5},{4,2},{5,3},{6,0},{7,1},{8,14},{9,15},{10,... | collective-permute-start | bytes 442376 | tf_op jit(solution)/shard_map/ppermute | solution.py:230
  88.7 0.5 collective-permute-done.14.refs_2_
  89.2 1.4 %collective-permute-start.20 = (bf16[3,64,384]{2,1,0:T(8,128)(2,1)S(1)}, bf16[3,64,384]{2,1,0:T(8,128)(2,1)S(1)}, u32[]{:S(2)}, u32[]{:S(2)}) collective-permute-start(bf16[3,64,384]{2,1,0:T(8,128)(2,1)S(1)} %get-tuple-element.95), channel_id=1, source_target_pairs={{0,7},{1,6},{2,5},{3,4},{4,3},{5,2},{6,1},{7,0},{8,15},{9,14},{10,... | collective-permute-start | bytes 442376 | tf_op jit(solution)/shard_map/ppermute | solution.py:230
  90.6 0.9 collective-permute-done.15.refs_3_
  91.4 4.8 %collective-permute-done.16.refs_4_ = bf16[3,64,384]{2,1,0:T(8,128)(2,1)S(1)} collective-permute-done((bf16[3,64,384]{2,1,0:T(8,128)(2,1)S(1)}, bf16[3,64,384]{2,1,0:T(8,128)(2,1)S(1)}, u32[]{:S(2)}, u32[]{:S(2)}) %collective-permute-start.16) | collective-permute-done | bytes 147488 | tf_op jit(solution)/shard_map/ppermute | solution.py:230
  96.2 2.2 %collective-permute-done.17.refs_5_ = bf16[3,64,384]{2,1,0:T(8,128)(2,1)S(1)} collective-permute-done((bf16[3,64,384]{2,1,0:T(8,128)(2,1)S(1)}, bf16[3,64,384]{2,1,0:T(8,128)(2,1)S(1)}, u32[]{:S(2)}, u32[]{:S(2)}) %collective-permute-start.17) | collective-permute-done | bytes 147488 | tf_op jit(solution)/shard_map/ppermute | solution.py:230
  98.4 3.9 %all-to-all-done.2.in_ref = bf16[32,8,1280]{2,1,0:T(8,128)(2,1)S(1)} async-done(((bf16[32,8,1280]{2,1,0:T(8,128)(2,1)}), bf16[32,8,1280]{2,1,0:T(8,128)(2,1)S(1)}, u32[]{:S(2)}, u32[]{:S(2)}) %all-to-all-start.2) | async-done | bytes 655392 | tf_op jit(solution)/shard_map/all_to_all | solution.py:329
  102.3 0.5 total.1
  102.8 1.9 %collective-permute-start.18 = (f32[8,1536]{1,0:T(8,128)S(1)}, f32[8,1536]{1,0:T(8,128)S(1)}, u32[]{:S(2)}, u32[]{:S(2)}) collective-permute-start(f32[8,1536]{1,0:T(8,128)S(1)} %get-tuple-element.87), channel_id=1, source_target_pairs={{0,0},{32,2},{64,4},{96,6},{128,32},{160,34},{192,36},{224,38},{2,... | collective-permute-start | bytes 147464 | tf_op jit(solution)/shard_map/ppermute | solution.py:333
  104.7 0.9 collective-permute-start.21
  105.7 3.4 %collective-permute-start.22 = (f32[16,128]{1,0:T(8,128)S(1)}, f32[16,128]{1,0:T(8,128)S(1)}, u32[]{:S(2)}, u32[]{:S(2)}) collective-permute-start(f32[16,128]{1,0:T(8,128)S(1)} %get-tuple-element.98.o0), channel_id=1, source_target_pairs={{0,4},{2,6},{4,0},{6,2},{1,5},{3,7},{5,1},{7,3},{8,12},{10,14},{12... | collective-permute-start | bytes 24584 | tf_op jit(solution)/shard_map/ppermute | solution.py:230
  109.1 0.4 collective-permute-start.23
  109.5 1.8 %unpack.1 = bf16[3,128,1536]{2,1,0:T(8,128)(2,1)} custom-call(s32[5]{0:T(128)S(1)} %stack.26.place, bf16[3,64,384]{2,1,0:T(8,128)(2,1)S(1)} %get-tuple-element.88.refs_0_, bf16[3,64,384]{2,1,0:T(8,128)(2,1)S(1)} %collective-permute-done.13.refs_1_, bf16[3,64,384]{2,1,0:T(8,128)(2,1)S(1)} %collective-permute-done.14.refs_2_, ...), custom_call_target="tpu_custom_call" | custom-call | bytes 2359316 | tf_op jit(solution)/shard_map/unpack/pallas_call | solution.py:54
  111.3 0.8 collective-permute-done.18.home_ref
  112.1 1.9 %collective-permute-done.23.o3 = f32[16,128]{1,0:T(8,128)S(1)} collective-permute-done((f32[16,128]{1,0:T(8,128)S(1)}, f32[16,128]{1,0:T(8,128)S(1)}, u32[]{:S(2)}, u32[]{:S(2)}) %collective-permute-start.23) | collective-permute-done | bytes 8224 | tf_op jit(solution)/shard_map/ppermute | solution.py:230
  114.0 1.2 %last.1 = (f32[6,1536]{1,0:T(8,128)}, f32[12,15]{1,0:T(8,128)}) custom-call(s32[5]{0:T(128)S(1)} %stack.26.place, f32[8,1536]{1,0:T(8,128)S(1)} %collective-permute-done.18.home_ref, f32[16,128]{1,0:T(8,128)S(1)} %get-tuple-element.98.o0, f32[16,128]{1,0:T(8,128)S(1)} %collective-permute-done.21.o1, f32[16,128]{1,0:T(8,128)S(1)} %collective-permute-done.22.o2, ...), custom_call_target="tpu_custom_call" | custom-call | bytes 119524 | tf_op jit(solution)/shard_map/last/pallas_call | solution.py:54
  (20 shorter events, 0.1 us)
Async XLA Ops:
  0.6 4.5 %copy-start = (bf16[3,1,1,128,1536]{4,3,2,1,0:T(8,128)(2,1)S(1)}, bf16[3,1,1,128,1536]{4,3,2,1,0:T(8,128)(2,1)}, u32[]{:S(2)}) copy-start(bf16[3,1,1,128,1536]{4,3,2,1,0:T(8,128)(2,1)} %param.7) | copy-start | bytes 3538948
  0.6 19.4 %all-to-all-start.1 = ((bf16[8,32,1536]{2,1,0:T(8,128)(2,1)}), bf16[8,32,1536]{2,1,0:T(8,128)(2,1)S(1)}, u32[]{:S(2)}, u32[]{:S(2)}) async-start(bf16[8,32,1536]{2,1,0:T(8,128)(2,1)} %bitcast.11), calls=%async_computation.1 | async-start | bytes 1572864 | tf_op jit(solution)/shard_map/all_to_all | solution.py:244
  5.1 1.1 copy-start.5
  6.2 23.1 %copy-start.2 = (s32[1,8]{1,0:T(1,128)S(1)}, s32[1,8]{1,0:T(1,128)}, u32[]{:S(2)}) copy-start(s32[1,8]{1,0:T(1,128)} %sizes.1) | copy-start | bytes 100
  6.2 12.2 %collective-permute-start = (bf16[8,1536]{1,0:T(8,128)(2,1)S(1)}, bf16[8,1536]{1,0:T(8,128)(2,1)S(1)}, u32[]{:S(2)}, u32[]{:S(2)}) collective-permute-start(bf16[8,1536]{1,0:T(8,128)(2,1)S(1)} %pad.4), channel_id=1, source_target_pairs={{0,0},{2,32},{4,64},{6,96},{32,128},{34,160},{36,192},{38,224},{64... | collective-permute-start | bytes 73736 | tf_op jit(solution)/shard_map/ppermute | solution.py:247
  14.0 6.0 %collective-permute-start.1 = (bf16[8,1536]{1,0:T(8,128)(2,1)S(1)}, bf16[8,1536]{1,0:T(8,128)(2,1)S(1)}, u32[]{:S(2)}, u32[]{:S(2)}) collective-permute-start(bf16[8,1536]{1,0:T(8,128)(2,1)S(1)} %pad.4), channel_id=1, source_target_pairs={{0,32},{2,0},{4,96},{6,64},{32,160},{34,128},{36,224},{38,192},{64... | collective-permute-start | bytes 73736 | tf_op jit(solution)/shard_map/ppermute | solution.py:247
  20.0 35.5 %all-to-all-start = ((bf16[8,3,64,384]{3,2,1,0:T(8,128)(2,1)}), bf16[8,3,64,384]{3,2,1,0:T(8,128)(2,1)S(1)}, u32[]{:S(2)}, u32[]{:S(2)}) async-start(bf16[8,3,64,384]{3,2,1,0:T(8,128)(2,1)} %pack.1), calls=%async_computation | async-start | bytes 2359296 | tf_op jit(solution)/shard_map/all_to_all | solution.py:249
  27.6 5.1 %collective-permute-start.2 = (bf16[16,1536]{1,0:T(8,128)(2,1)S(1)}, bf16[16,1536]{1,0:T(8,128)(2,1)S(1)}, u32[]{:S(2)}, u32[]{:S(2)}) collective-permute-start(bf16[16,1536]{1,0:T(8,128)(2,1)S(1)} %pad_maximum_fusion.2), channel_id=1, source_target_pairs={{0,64},{32,96},{64,0},{96,32},{128,192},{160,224},{192,128},{224,1... | collective-permute-start | bytes 147464 | tf_op jit(solution)/shard_map/ppermute | solution.py:230
  30.1 25.4 %copy-start.3 = (f32[12,15]{1,0:T(8,128)S(1)}, f32[12,15]{1,0:T(8,128)}, u32[]{:S(2)}) copy-start(f32[12,15]{1,0:T(8,128)} %bias.1) | copy-start | bytes 2164
  30.1 4.9 %collective-permute-start.3 = (bf16[64,1536]{1,0:T(8,128)(2,1)S(1)}, bf16[64,1536]{1,0:T(8,128)(2,1)S(1)}, u32[]{:S(2)}, u32[]{:S(2)}) collective-permute-start(bf16[64,1536]{1,0:T(8,128)(2,1)S(1)} %get-tuple-element.60), channel_id=1, source_target_pairs={{0,1},{1,0},{2,3},{3,2},{4,5},{5,4},{6,7},{7,6},{8,9},{9,8},{10,11... | collective-permute-start | bytes 589832 | tf_op jit(solution)/shard_map/ppermute | solution.py:230
  32.7 8.7 %collective-permute-start.4 = (bf16[32,1536]{1,0:T(8,128)(2,1)S(1)}, bf16[32,1536]{1,0:T(8,128)(2,1)S(1)}, u32[]{:S(2)}, u32[]{:S(2)}) collective-permute-start(bf16[32,1536]{1,0:T(8,128)(2,1)S(1)} %pad_maximum_fusion.1), channel_id=1, source_target_pairs={{0,128},{32,160},{64,192},{96,224},{128,0},{160,32},{192,64},{224,... | collective-permute-start | bytes 294920 | tf_op jit(solution)/shard_map/ppermute | solution.py:230
  35.0 17.3 %collective-permute-start.6 = (bf16[128,1536]{1,0:T(8,128)(2,1)S(1)}, bf16[128,1536]{1,0:T(8,128)(2,1)S(1)}, u32[]{:S(2)}, u32[]{:S(2)}) collective-permute-start(bf16[128,1536]{1,0:T(8,128)(2,1)S(1)} %stack.27.u0), channel_id=1, source_target_pairs={{0,2},{2,0},{4,6},{6,4},{1,3},{3,1},{5,7},{7,5},{8,10},{10,8},{12,... | collective-permute-start | bytes 1179656 | tf_op jit(solution)/shard_map/ppermute | solution.py:230
  41.4 6.4 %collective-permute-start.5 = (bf16[64,1536]{1,0:T(8,128)(2,1)S(1)}, bf16[64,1536]{1,0:T(8,128)(2,1)S(1)}, u32[]{:S(2)}, u32[]{:S(2)}) collective-permute-start(bf16[64,1536]{1,0:T(8,128)(2,1)S(1)} %pad_maximum_fusion.refs_0_), channel_id=1, source_target_pairs={{0,8},{8,0},{16,24},{24,16},{1,9},{9,1},{17,25},{25,17},{2,10},{10... | collective-permute-start | bytes 589832 | tf_op jit(solution)/shard_map/ppermute | solution.py:230
  43.1 21.1 %collective-permute-start.7 = (bf16[128,1536]{1,0:T(8,128)(2,1)S(1)}, bf16[128,1536]{1,0:T(8,128)(2,1)S(1)}, u32[]{:S(2)}, u32[]{:S(2)}) collective-permute-start(bf16[128,1536]{1,0:T(8,128)(2,1)S(1)} %stack.27.u0), channel_id=1, source_target_pairs={{0,4},{2,6},{4,0},{6,2},{1,5},{3,7},{5,1},{7,3},{8,12},{10,14},{12... | collective-permute-start | bytes 1179656 | tf_op jit(solution)/shard_map/ppermute | solution.py:230
  46.7 18.1 %collective-permute-start.8 = (bf16[128,1536]{1,0:T(8,128)(2,1)S(1)}, bf16[128,1536]{1,0:T(8,128)(2,1)S(1)}, u32[]{:S(2)}, u32[]{:S(2)}) collective-permute-start(bf16[128,1536]{1,0:T(8,128)(2,1)S(1)} %stack.27.u0), channel_id=1, source_target_pairs={{0,6},{2,4},{4,2},{6,0},{1,7},{3,5},{5,3},{7,1},{8,14},{10,12},{12... | collective-permute-start | bytes 1179656 | tf_op jit(solution)/shard_map/ppermute | solution.py:230
  52.3 11.7 %collective-permute-start.10 = (bf16[128,1536]{1,0:T(8,128)(2,1)S(1)}, bf16[128,1536]{1,0:T(8,128)(2,1)S(1)}, u32[]{:S(2)}, u32[]{:S(2)}) collective-permute-start(bf16[128,1536]{1,0:T(8,128)(2,1)S(1)} %stack.28.refs_0_), channel_id=1, source_target_pairs={{0,16},{8,24},{16,0},{24,8},{1,17},{9,25},{17,1},{25,9},{2,18},{10... | collective-permute-start | bytes 1179656 | tf_op jit(solution)/shard_map/ppermute | solution.py:230
  55.5 0.7 copy-start.4
  64.1 2.4 %collective-permute-start.11 = (bf16[256,1536]{1,0:T(8,128)(2,1)S(1)}, bf16[256,1536]{1,0:T(8,128)(2,1)S(1)}, u32[]{:S(2)}, u32[]{:S(2)}) collective-permute-start(bf16[256,1536]{1,0:T(8,128)(2,1)S(1)} %stack.29.w0_ref), channel_id=1, source_target_pairs={{0,1},{1,0},{2,3},{3,2},{4,5},{5,4},{6,7},{7,6},{8,9},{9,8},{10,11... | collective-permute-start | bytes 2359304 | tf_op jit(solution)/shard_map/ppermute | solution.py:230
  64.8 1.6 %copy-start.1 = (s32[8,384]{1,0:T(8,128)S(1)}, s32[8,384]{1,0:T(8,128)}, u32[]{:S(2)}) copy-start(s32[8,384]{1,0:T(8,128)} %constant.26.clone.rows_ref) | copy-start | bytes 36868
  66.3 4.3 %collective-permute-start.9 = (bf16[192,1536]{1,0:T(8,128)(2,1)S(1)}, bf16[192,1536]{1,0:T(8,128)(2,1)S(1)}, u32[]{:S(2)}, u32[]{:S(2)}) collective-permute-start(bf16[192,1536]{1,0:T(8,128)(2,1)S(1)} %get-tuple-element.65), channel_id=1, source_target_pairs={{0,1},{1,0},{2,3},{3,2},{4,5},{5,4},{6,7},{7,6},{8,9},{9,8},{10,11... | collective-permute-start | bytes 1769480 | tf_op jit(solution)/shard_map/ppermute | solution.py:230
  68.7 1.9 %collective-permute-start.12 = (f32[8,384]{1,0:T(8,128)S(1)}, f32[8,384]{1,0:T(8,128)S(1)}, u32[]{:S(2)}, u32[]{:S(2)}) collective-permute-start(f32[8,384]{1,0:T(8,128)S(1)} %get-tuple-element.69.s0), channel_id=1, source_target_pairs={{0,1},{1,0},{2,3},{3,2},{4,5},{5,4},{6,7},{7,6},{8,9},{9,8},{10,11... | collective-permute-start | bytes 36872 | tf_op jit(solution)/shard_map/ppermute | solution.py:230
  72.1 30.2 %all-to-all-start.2 = ((bf16[32,8,1280]{2,1,0:T(8,128)(2,1)}), bf16[32,8,1280]{2,1,0:T(8,128)(2,1)S(1)}, u32[]{:S(2)}, u32[]{:S(2)}) async-start(bf16[32,8,1280]{2,1,0:T(8,128)(2,1)} %join.1), calls=%async_computation.2 | async-start | bytes 1310720 | tf_op jit(solution)/shard_map/all_to_all | solution.py:329
  82.4 5.2 %collective-permute-start.13 = (bf16[3,64,384]{2,1,0:T(8,128)(2,1)S(1)}, bf16[3,64,384]{2,1,0:T(8,128)(2,1)S(1)}, u32[]{:S(2)}, u32[]{:S(2)}) collective-permute-start(bf16[3,64,384]{2,1,0:T(8,128)(2,1)S(1)} %get-tuple-element.81), channel_id=1, source_target_pairs={{0,1},{1,0},{2,3},{3,2},{4,5},{5,4},{6,7},{7,6},{8,9},{9,8},{10,11... | collective-permute-start | bytes 442376 | tf_op jit(solution)/shard_map/ppermute | solution.py:230
  82.5 6.7 %collective-permute-start.14 = (bf16[3,64,384]{2,1,0:T(8,128)(2,1)S(1)}, bf16[3,64,384]{2,1,0:T(8,128)(2,1)S(1)}, u32[]{:S(2)}, u32[]{:S(2)}) collective-permute-start(bf16[3,64,384]{2,1,0:T(8,128)(2,1)S(1)} %get-tuple-element.82), channel_id=1, source_target_pairs={{0,2},{1,3},{2,0},{3,1},{4,6},{5,7},{6,4},{7,5},{8,10},{9,11},{10,... | collective-permute-start | bytes 442376 | tf_op jit(solution)/shard_map/ppermute | solution.py:230
  82.6 8.9 %collective-permute-start.15 = (bf16[3,64,384]{2,1,0:T(8,128)(2,1)S(1)}, bf16[3,64,384]{2,1,0:T(8,128)(2,1)S(1)}, u32[]{:S(2)}, u32[]{:S(2)}) collective-permute-start(bf16[3,64,384]{2,1,0:T(8,128)(2,1)S(1)} %get-tuple-element.83), channel_id=1, source_target_pairs={{0,3},{1,2},{2,1},{3,0},{4,7},{5,6},{6,5},{7,4},{8,11},{9,10},{10,... | collective-permute-start | bytes 442376 | tf_op jit(solution)/shard_map/ppermute | solution.py:230
  84.3 11.9 %collective-permute-start.16 = (bf16[3,64,384]{2,1,0:T(8,128)(2,1)S(1)}, bf16[3,64,384]{2,1,0:T(8,128)(2,1)S(1)}, u32[]{:S(2)}, u32[]{:S(2)}) collective-permute-start(bf16[3,64,384]{2,1,0:T(8,128)(2,1)S(1)} %get-tuple-element.84), channel_id=1, source_target_pairs={{0,4},{1,5},{2,6},{3,7},{4,0},{5,1},{6,2},{7,3},{8,12},{9,13},{10,... | collective-permute-start | bytes 442376 | tf_op jit(solution)/shard_map/ppermute | solution.py:230
  85.2 13.2 %collective-permute-start.17 = (bf16[3,64,384]{2,1,0:T(8,128)(2,1)S(1)}, bf16[3,64,384]{2,1,0:T(8,128)(2,1)S(1)}, u32[]{:S(2)}, u32[]{:S(2)}) collective-permute-start(bf16[3,64,384]{2,1,0:T(8,128)(2,1)S(1)} %get-tuple-element.85), channel_id=1, source_target_pairs={{0,5},{1,4},{2,7},{3,6},{4,1},{5,0},{6,3},{7,2},{8,13},{9,12},{10,... | collective-permute-start | bytes 442376 | tf_op jit(solution)/shard_map/ppermute | solution.py:230
  87.6 21.5 %collective-permute-start.19 = (bf16[3,64,384]{2,1,0:T(8,128)(2,1)S(1)}, bf16[3,64,384]{2,1,0:T(8,128)(2,1)S(1)}, u32[]{:S(2)}, u32[]{:S(2)}) collective-permute-start(bf16[3,64,384]{2,1,0:T(8,128)(2,1)S(1)} %get-tuple-element.94), channel_id=1, source_target_pairs={{0,6},{1,7},{2,4},{3,5},{4,2},{5,3},{6,0},{7,1},{8,14},{9,15},{10,... | collective-permute-start | bytes 442376 | tf_op jit(solution)/shard_map/ppermute | solution.py:230
  89.2 20.3 %collective-permute-start.20 = (bf16[3,64,384]{2,1,0:T(8,128)(2,1)S(1)}, bf16[3,64,384]{2,1,0:T(8,128)(2,1)S(1)}, u32[]{:S(2)}, u32[]{:S(2)}) collective-permute-start(bf16[3,64,384]{2,1,0:T(8,128)(2,1)S(1)} %get-tuple-element.95), channel_id=1, source_target_pairs={{0,7},{1,6},{2,5},{3,4},{4,3},{5,2},{6,1},{7,0},{8,15},{9,14},{10,... | collective-permute-start | bytes 442376 | tf_op jit(solution)/shard_map/ppermute | solution.py:230
  102.8 9.2 %collective-permute-start.18 = (f32[8,1536]{1,0:T(8,128)S(1)}, f32[8,1536]{1,0:T(8,128)S(1)}, u32[]{:S(2)}, u32[]{:S(2)}) collective-permute-start(f32[8,1536]{1,0:T(8,128)S(1)} %get-tuple-element.87), channel_id=1, source_target_pairs={{0,0},{32,2},{64,4},{96,6},{128,32},{160,34},{192,36},{224,38},{2,... | collective-permute-start | bytes 147464 | tf_op jit(solution)/shard_map/ppermute | solution.py:333
  104.7 7.3 %collective-permute-start.21 = (f32[16,128]{1,0:T(8,128)S(1)}, f32[16,128]{1,0:T(8,128)S(1)}, u32[]{:S(2)}, u32[]{:S(2)}) collective-permute-start(f32[16,128]{1,0:T(8,128)S(1)} %get-tuple-element.98.o0), channel_id=1, source_target_pairs={{0,2},{2,0},{4,6},{6,4},{1,3},{3,1},{5,7},{7,5},{8,10},{10,8},{12,... | collective-permute-start | bytes 24584 | tf_op jit(solution)/shard_map/ppermute | solution.py:230
  105.7 6.4 %collective-permute-start.22 = (f32[16,128]{1,0:T(8,128)S(1)}, f32[16,128]{1,0:T(8,128)S(1)}, u32[]{:S(2)}, u32[]{:S(2)}) collective-permute-start(f32[16,128]{1,0:T(8,128)S(1)} %get-tuple-element.98.o0), channel_id=1, source_target_pairs={{0,4},{2,6},{4,0},{6,2},{1,5},{3,7},{5,1},{7,3},{8,12},{10,14},{12... | collective-permute-start | bytes 24584 | tf_op jit(solution)/shard_map/ppermute | solution.py:230
  109.1 4.9 %collective-permute-start.23 = (f32[16,128]{1,0:T(8,128)S(1)}, f32[16,128]{1,0:T(8,128)S(1)}, u32[]{:S(2)}, u32[]{:S(2)}) collective-permute-start(f32[16,128]{1,0:T(8,128)S(1)} %get-tuple-element.98.o0), channel_id=1, source_target_pairs={{0,6},{2,4},{4,2},{6,0},{1,7},{3,5},{5,3},{7,1},{8,14},{10,12},{12... | collective-permute-start | bytes 24584 | tf_op jit(solution)/shard_map/ppermute | solution.py:230

commit v10 on v9

--- a/solution.py
+++ b/solution.py
@@ -76,10 +76,21 @@
     return call(stack_kernel, "stack", [((rows, DW), bf)], *parts)[0]
 
 
-def pack_kernel(qkv_ref, out_ref):
-    for d in range(F):
-        r, c = d % C * HALF, d // C * COLS
-        out_ref[d] = qkv_ref[:, r : r + HALF, c : c + COLS]
+def pack_kernel(place, qkv_ref, *refs):
+    pieces, nat_ref = refs[:X], refs[X]
+    for c in range(X):
+        nat_ref[c] = qkv_ref[:, :, c * COLS : (c + 1) * COLS]
+    for k in range(X):
+        pieces[k][...] = nat_ref[place[XI] ^ k]
+
+
+def half(core):
+    return pl.ds(pl.multiple_of(core * HALF, HALF), HALF)
+
+
+def cross_kernel(place, *refs):
+    for k in range(X):
+        refs[X][k] = refs[k][:, half(1 - place[CORE]), :]
 
 
 def compact_kernel(place, sizes, cot_ref, same_ref, other_ref):
@@ -103,7 +114,11 @@
     return ref[:, i, b * 16 : (b + 1) * 16, h * HD : (h + 1) * HD].reshape(POS, HD)
 
 
-def fwd_kernel(place, bias, leave_ref, qkv_ref, probs_ref, mixed_ref, raw_ref):
+def fwd_kernel(place, bias, leave_ref, p0, p1, p2, p3, cross_ref, probs_ref, mixed_ref, qkv_ref, raw_ref):
+    for k, ref in enumerate((p0, p1, p2, p3)):
+        frame = (place[XI] ^ k) * C
+        qkv_ref[frame + place[CORE]] = ref[:, half(place[CORE]), :]
+        qkv_ref[frame + 1 - place[CORE]] = cross_ref[k]
     row, col = iota((POS, POS), 0), iota((POS, POS), 1)
     alike = (row & 15) == (col & 15)
     offset = (col >> 4) - (row >> 4) + 7
@@ -242,11 +257,20 @@
     ]
     near = [(a, b ^ X) for a, b in there]
     cot = lax.all_to_all(cot_out[0, 0], SEQ, 0, 0, tiled=True)
-    (packed,) = call(pack_kernel, "pack", [((F, 3, HALF, COLS), bf)], qkv_time[:, 0, 0])
-    rows8, packed = lax.optimization_barrier((jnp.pad(w_out, ((0, 2), (0, 0))), packed))
+    packed = call(
+        pack_kernel,
+        "pack",
+        [((3, POS, COLS), bf)] * X,
+        place,
+        qkv_time[:, 0, 0],
+        smem=1,
+        scratch=[pltpu.VMEM((X, 3, POS, COLS), bf)],
+    )
+    rows8 = jnp.pad(w_out, ((0, 2), (0, 0)))
+    rows8, packed = lax.optimization_barrier((rows8, packed))
     held = [lax.ppermute(rows8, ("z", "x"), p) for p in (there, near)]
     packed, held = lax.optimization_barrier((packed, held))
-    recv = lax.all_to_all(packed, SEQ, 0, 0, tiled=True)
+    packed = [packed[0]] + [hop(packed[k], "x", k, X) for k in range(1, X)]
     held = jnp.concatenate(held)
     held = jnp.concatenate([held, hop(held, "z", 2, Z)])
 
@@ -262,6 +286,7 @@
     )
     held, same = lax.optimization_barrier((held, same))
     held = jnp.concatenate([held, hop(held, "z", 4, Z)])
+    z4 = held
     u0 = stack([same, hop(other, "core", 1, C)])
     held, _ = lax.optimization_barrier((held, u0))
     ups = [u0] + [hop(u0, "x", k, X) for k in range(1, X)]
@@ -270,14 +295,18 @@
     held = stack([held, hop(held, "y", 2, Y)])
     held2 = hop(held, "core", 1, C)
 
-    probs, mixed = call(
+    packed, _, _ = lax.optimization_barrier((packed, u0, z4))
+    (cross,) = call(cross_kernel, "cross", [((X, 3, HALF, COLS), bf)], place, *packed, smem=1)
+    cross = hop(cross, "core", 1, C)
+    probs, mixed, recv = call(
         fwd_kernel,
         "attn_fwd",
-        [((HL, NB, POS, POS), f32), ((F * HALF, COLS), bf)],
+        [((HL, NB, POS, POS), f32), ((F * HALF, COLS), bf), ((F, 3, HALF, COLS), bf)],
         place,
         bias_time,
         LEAVE,
-        recv,
+        *packed,
+        cross,
         smem=2,
         scratch=[pltpu.VMEM((F, HALF, COLS), bf)],
         flops=20_000_000_000,

time: 116 us -> 117 us (level)
  waiting for transfers between devices: 31 us -> 34.3 us
  starting transfers between devices: 65.5 us -> 63.2 us
    ppermute x21 -> x25, starting transfers between devices: 29.1 us -> 36.7 us  [hop(): return lax.ppermute(x, axis, [(i, i ^ k) for i in range(n)])]
    all_to_all x1 -> x0, starting transfers between devices: 7.56 us -> none  [per_device(): recv = lax.all_to_all(packed, SEQ, 0, 0, tiled=True)]
    ppermute x21 -> x25, waiting for transfers between devices: 24.9 us -> 28.2 us  [hop(): return lax.ppermute(x, axis, [(i, i ^ k) for i in range(n)])]
    all_to_all x1, starting transfers between devices: 10.2 us -> 7.95 us  [per_device(): msgs = lax.all_to_all(msgs, ('z', 'y'), 0, 0, tiled=True)]
    pallas_call x13 -> x14, Pallas kernels: 16.9 us -> 17.3 us  [call(): pl.pallas_call(body, out_shape=tuple((jax.ShapeDtypeStruct(s, d) for s, d...]
  transfers between devices with their start and end apart: 27 -> 30, of which waited for: 14 -> 15; matrix products, arithmetic and copies ran while one was open for 0% -> 0% of each run, Pallas kernels for 12% -> 12%
where the time goes in v10:
time: 117 us; the launch traced here: 116 us
  starting transfers between devices  63.2 us (54%)
  waiting for transfers between devices  34.3 us (29%)
  Pallas kernels  17.3 us (15%)
    ppermute x25, starting transfers between devices, hop(): return lax.ppermute(x, axis, [(i, i ^ k) for i in range(n)])  36.7 us
    ppermute x25, waiting for transfers between devices, hop(): return lax.ppermute(x, axis, [(i, i ^ k) for i in range(n)])  28.2 us
    pallas_call x14, Pallas kernels, call(): pl.pallas_call(body, out_shape=tuple((jax.ShapeDtypeStruct(s, d) for s, d...  17.3 us
    ppermute x2, starting transfers between devices, per_device(): held = [lax.ppermute(rows8, ('z', 'x'), p) for p in (there, near)]  12.2 us
    all_to_all x1, starting transfers between devices, per_device(): msgs = lax.all_to_all(msgs, ('z', 'y'), 0, 0, tiled=True)  7.95 us
    all_to_all x1, starting transfers between devices, per_device(): cot = lax.all_to_all(cot_out[0, 0], SEQ, 0, 0, tiled=True)  4.44 us
    all_to_all x1, waiting for transfers between devices, per_device(): msgs = lax.all_to_all(msgs, ('z', 'y'), 0, 0, tiled=True)  4.05 us
  transfers between devices with their start and end apart: 30, of which 15 were waited for; matrix products, arithmetic and copies ran while one was open for 0% of the time, Pallas kernels for 12%

profile of v10, /device:TPU:32, one launch (start us, length us, event | category | flops | bytes accessed | tf_op | source)
XLA Modules:
  0.0 115.9 jit_solution(2601113913119743845)
XLA Ops:
  0.7 4.4 %all-to-all-start = ((bf16[8,32,1536]{2,1,0:T(8,128)(2,1)}), bf16[8,32,1536]{2,1,0:T(8,128)(2,1)S(1)}, u32[]{:S(2)}, u32[]{:S(2)}) async-start(bf16[8,32,1536]{2,1,0:T(8,128)(2,1)} %bitcast.11), calls=%async_computation | async-start | bytes 1572864 | tf_op jit(solution)/shard_map/all_to_all | solution.py:259
  5.1 0.1 stack.26.place
  5.2 0.7 pack.1
  6.0 7.7 %collective-permute-start = (bf16[8,1536]{1,0:T(8,128)(2,1)S(1)}, bf16[8,1536]{1,0:T(8,128)(2,1)S(1)}, u32[]{:S(2)}, u32[]{:S(2)}) collective-permute-start(bf16[8,1536]{1,0:T(8,128)(2,1)S(1)} %pad.4), channel_id=1, source_target_pairs={{0,0},{2,32},{4,64},{6,96},{32,128},{34,160},{36,192},{38,224},{64... | collective-permute-start | bytes 73736 | tf_op jit(solution)/shard_map/ppermute | solution.py:271
  13.7 4.5 %collective-permute-start.1 = (bf16[8,1536]{1,0:T(8,128)(2,1)S(1)}, bf16[8,1536]{1,0:T(8,128)(2,1)S(1)}, u32[]{:S(2)}, u32[]{:S(2)}) collective-permute-start(bf16[8,1536]{1,0:T(8,128)(2,1)S(1)} %pad.4), channel_id=1, source_target_pairs={{0,32},{2,0},{4,96},{6,64},{32,160},{34,128},{36,224},{38,192},{64... | collective-permute-start | bytes 73736 | tf_op jit(solution)/shard_map/ppermute | solution.py:271
  18.2 0.0 collective-permute-done
  18.2 1.5 %collective-permute-done.1 = bf16[8,1536]{1,0:T(8,128)(2,1)S(1)} collective-permute-done((bf16[8,1536]{1,0:T(8,128)(2,1)S(1)}, bf16[8,1536]{1,0:T(8,128)(2,1)S(1)}, u32[]{:S(2)}, u32[]{:S(2)}) %collective-permute-start.1) | collective-permute-done | bytes 24608 | tf_op jit(solution)/shard_map/ppermute | solution.py:271
  19.8 4.1 %collective-permute-start.5 = (bf16[16,1536]{1,0:T(8,128)(2,1)S(1)}, bf16[16,1536]{1,0:T(8,128)(2,1)S(1)}, u32[]{:S(2)}, u32[]{:S(2)}) collective-permute-start(bf16[16,1536]{1,0:T(8,128)(2,1)S(1)} %pad_maximum_fusion.1), channel_id=1, source_target_pairs={{0,64},{32,96},{64,0},{96,32},{128,192},{160,224},{192,128},{224,1... | collective-permute-start | bytes 147464 | tf_op jit(solution)/shard_map/ppermute | solution.py:245
  23.8 5.5 %collective-permute-start.3 = (bf16[3,128,384]{2,1,0:T(8,128)(2,1)S(1)}, bf16[3,128,384]{2,1,0:T(8,128)(2,1)S(1)}, u32[]{:S(2)}, u32[]{:S(2)}) collective-permute-start(bf16[3,128,384]{2,1,0:T(8,128)(2,1)S(1)} %get-tuple-element.78), channel_id=1, source_target_pairs={{0,4},{2,6},{4,0},{6,2},{1,5},{3,7},{5,1},{7,3},{8,12},{10,14},{12... | collective-permute-start | bytes 884744 | tf_op jit(solution)/shard_map/ppermute | solution.py:245
  29.3 0.0 collective-permute-start.4
  29.3 0.0 collective-permute-done.5
  29.3 0.0 all-to-all-done.cot_ref
  29.3 0.8 compact.1
  30.2 4.1 %collective-permute-start.7 = (bf16[32,1536]{1,0:T(8,128)(2,1)S(1)}, bf16[32,1536]{1,0:T(8,128)(2,1)S(1)}, u32[]{:S(2)}, u32[]{:S(2)}) collective-permute-start(bf16[32,1536]{1,0:T(8,128)(2,1)S(1)} %pad_maximum_fusion), channel_id=1, source_target_pairs={{0,128},{32,160},{64,192},{96,224},{128,0},{160,32},{192,64},{224,... | collective-permute-start | bytes 294920 | tf_op jit(solution)/shard_map/ppermute | solution.py:245
  34.3 0.1 collective-permute-start.6
  34.4 5.1 %collective-permute-done.7 = bf16[32,1536]{1,0:T(8,128)(2,1)S(1)} collective-permute-done((bf16[32,1536]{1,0:T(8,128)(2,1)S(1)}, bf16[32,1536]{1,0:T(8,128)(2,1)S(1)}, u32[]{:S(2)}, u32[]{:S(2)}) %collective-permute-start.7) | collective-permute-done | bytes 98336 | tf_op jit(solution)/shard_map/ppermute | solution.py:245
  39.5 0.0 copy-start.3
  39.5 0.0 copy-start.4
  39.6 0.0 collective-permute-done.2.refs_1_.p1
  39.6 1.2 %collective-permute-done.3.refs_2_.p2 = bf16[3,128,384]{2,1,0:T(8,128)(2,1)S(1)} collective-permute-done((bf16[3,128,384]{2,1,0:T(8,128)(2,1)S(1)}, bf16[3,128,384]{2,1,0:T(8,128)(2,1)S(1)}, u32[]{:S(2)}, u32[]{:S(2)}) %collective-permute-start.3) | collective-permute-done | bytes 294944 | tf_op jit(solution)/shard_map/ppermute | solution.py:245
  40.8 2.6 %collective-permute-done.4.refs_3_.p3 = bf16[3,128,384]{2,1,0:T(8,128)(2,1)S(1)} collective-permute-done((bf16[3,128,384]{2,1,0:T(8,128)(2,1)S(1)}, bf16[3,128,384]{2,1,0:T(8,128)(2,1)S(1)}, u32[]{:S(2)}, u32[]{:S(2)}) %collective-permute-start.4) | collective-permute-done | bytes 294944 | tf_op jit(solution)/shard_map/ppermute | solution.py:245
  43.4 0.6 cross.1
  44.0 0.1 collective-permute-start.8
  44.1 0.1 collective-permute-start.10
  44.2 1.7 %collective-permute-start.9 = (bf16[64,1536]{1,0:T(8,128)(2,1)S(1)}, bf16[64,1536]{1,0:T(8,128)(2,1)S(1)}, u32[]{:S(2)}, u32[]{:S(2)}) collective-permute-start(bf16[64,1536]{1,0:T(8,128)(2,1)S(1)} %constant_dynamic-update-slice_fusion.refs_0_), channel_id=1, source_target_pairs={{0,8},{8,0},{16,24},{24,16},{1,9},{9,1},{17,25},{25,17},{2,10},{10... | collective-permute-start | bytes 589832 | tf_op jit(solution)/shard_map/ppermute | solution.py:245
  45.8 1.6 %collective-permute-start.11 = (bf16[128,1536]{1,0:T(8,128)(2,1)S(1)}, bf16[128,1536]{1,0:T(8,128)(2,1)S(1)}, u32[]{:S(2)}, u32[]{:S(2)}) collective-permute-start(bf16[128,1536]{1,0:T(8,128)(2,1)S(1)} %stack.27.u0), channel_id=1, source_target_pairs={{0,4},{2,6},{4,0},{6,2},{1,5},{3,7},{5,1},{7,3},{8,12},{10,14},{12... | collective-permute-start | bytes 1179656 | tf_op jit(solution)/shard_map/ppermute | solution.py:245
  47.5 3.0 %collective-permute-start.12 = (bf16[128,1536]{1,0:T(8,128)(2,1)S(1)}, bf16[128,1536]{1,0:T(8,128)(2,1)S(1)}, u32[]{:S(2)}, u32[]{:S(2)}) collective-permute-start(bf16[128,1536]{1,0:T(8,128)(2,1)S(1)} %stack.27.u0), channel_id=1, source_target_pairs={{0,6},{2,4},{4,2},{6,0},{1,7},{3,5},{5,3},{7,1},{8,14},{10,12},{12... | collective-permute-start | bytes 1179656 | tf_op jit(solution)/shard_map/ppermute | solution.py:245
  50.4 0.9 collective-permute-done.9.refs_1_
  51.4 4.7 %collective-permute-done.10.u1 = bf16[128,1536]{1,0:T(8,128)(2,1)S(1)} collective-permute-done((bf16[128,1536]{1,0:T(8,128)(2,1)S(1)}, bf16[128,1536]{1,0:T(8,128)(2,1)S(1)}, u32[]{:S(2)}, u32[]{:S(2)}) %collective-permute-start.10) | collective-permute-done | bytes 393248 | tf_op jit(solution)/shard_map/ppermute | solution.py:245
  56.1 3.2 %collective-permute-start.14 = (bf16[128,1536]{1,0:T(8,128)(2,1)S(1)}, bf16[128,1536]{1,0:T(8,128)(2,1)S(1)}, u32[]{:S(2)}, u32[]{:S(2)}) collective-permute-start(bf16[128,1536]{1,0:T(8,128)(2,1)S(1)} %stack.28.refs_0_), channel_id=1, source_target_pairs={{0,16},{8,24},{16,0},{24,8},{1,17},{9,25},{17,1},{25,9},{2,18},{10... | collective-permute-start | bytes 1179656 | tf_op jit(solution)/shard_map/ppermute | solution.py:245
  59.3 5.2 %attn_fwd.1 = (f32[3,4,128,128]{3,2,1,0:T(8,128)S(1)}, bf16[512,384]{1,0:T(8,128)(2,1)S(1)}, bf16[8,3,64,384]{3,2,1,0:T(8,128)(2,1)S(1)}) custom-call(s32[5]{0:T(128)S(1)} %stack.26.place, f32[12,15]{1,0:T(8,128)S(1)} %copy-done.3, s32[8,384]{1,0:T(8,128)S(1)} %copy-done.4, bf16[3,128,384]{2,1,0:T(8,128)(2,1)S(1)} %get-tuple-element.86.refs_0_.p0, ...), custom_call_target="tpu_custom_call" | custom-call | flops 20000000000 | bytes 4141796 | tf_op jit(solution)/shard_map/attn_fwd/pallas_call | solution.py:54
  64.5 3.3 %collective-permute-done.14.refs_1_ = bf16[128,1536]{1,0:T(8,128)(2,1)S(1)} collective-permute-done((bf16[128,1536]{1,0:T(8,128)(2,1)S(1)}, bf16[128,1536]{1,0:T(8,128)(2,1)S(1)}, u32[]{:S(2)}, u32[]{:S(2)}) %collective-permute-start.14) | collective-permute-done | bytes 393248 | tf_op jit(solution)/shard_map/ppermute | solution.py:245
  67.8 0.1 stack.29.w0_ref
  67.8 0.1 collective-permute-start.15
  68.0 0.0 copy-start.1
  68.0 1.4 %grad_w.1 = (f32[192,1536]{1,0:T(8,128)S(1)}, bf16[192,1536]{1,0:T(8,128)(2,1)S(1)}, bf16[8,64,1536]{2,1,0:T(8,128)(2,1)S(1)}) custom-call(s32[5]{0:T(128)S(1)} %stack.26.place, bf16[512,384]{1,0:T(8,128)(2,1)S(1)} %get-tuple-element.90.mixed_ref, bf16[128,1536]{1,0:T(8,128)(2,1)S(1)} %stack.27.u0, bf16[128,1536]{1,0:T(8,128)(2,1)S(1)} %collective-permute-done.10.u1, ...), custom_call_target="tpu_custom_call" | custom-call | flops 20000000000 | bytes 5308436 | tf_op jit(solution)/shard_map/grad_w/pallas_call | solution.py:54
  69.4 0.7 collective-permute-start.13
  70.1 0.1 collective-permute-done.15.w1_ref
  70.2 2.3 %scores_bwd.1 = (bf16[8,64,384]{2,1,0:T(8,128)(2,1)S(1)}, bf16[3,4,128,128]{3,2,1,0:T(8,128)(2,1)S(1)}, f32[8,384]{1,0:T(8,128)S(1)}) custom-call(s32[5]{0:T(128)S(1)} %stack.26.place, s32[8,384]{1,0:T(8,128)S(1)} %copy-done.1, bf16[8,3,64,384]{3,2,1,0:T(8,128)(2,1)S(1)} %get-tuple-element.95.recv_ref.qkv_ref, ...), custom_call_target="tpu_custom_call" | custom-call | flops 900000000 | bytes 5922836 | tf_op jit(solution)/shard_map/scores_bwd/pallas_call | solution.py:54
  72.5 0.2 collective-permute-start.16
  72.7 1.2 %grads.1 = (bf16[3,64,384]{2,1,0:T(8,128)(2,1)S(1)}, bf16[3,64,384]{2,1,0:T(8,128)(2,1)S(1)}, bf16[3,64,384]{2,1,0:T(8,128)(2,1)S(1)}, bf16[3,64,384]{2,1,0:T(8,...) custom-call(s32[5]{0:T(128)S(1)} %stack.26.place, ...), custom_call_target="tpu_custom_call" | custom-call | flops 150000000 | bytes 3932180 | tf_op jit(solution)/shard_map/grads/pallas_call | solution.py:54
  73.9 1.6 %join.1 = bf16[32,8,1280]{2,1,0:T(8,128)(2,1)} custom-call(f32[192,1536]{1,0:T(8,128)S(1)} %get-tuple-element.93.mine_ref, bf16[192,1536]{1,0:T(8,128)(2,1)S(1)} %collective-permute-done.13.other_ref, f32[8,384]{1,0:T(8,128)S(1)} %get-tuple-element.99.s0, f32[8,384]{1,0:T(8,128)S(1)} %collective-permute-done.16.s1), custom_call_target="tpu_custom_call" | custom-call | bytes 2449408 | tf_op jit(solution)/shard_map/join/pallas_call | solution.py:54
  75.4 8.0 %all-to-all-start.1 = ((bf16[32,8,1280]{2,1,0:T(8,128)(2,1)}), bf16[32,8,1280]{2,1,0:T(8,128)(2,1)S(1)}, u32[]{:S(2)}, u32[]{:S(2)}) async-start(bf16[32,8,1280]{2,1,0:T(8,128)(2,1)} %join.1), calls=%async_computation.1 | async-start | bytes 1310720 | tf_op jit(solution)/shard_map/all_to_all | solution.py:358
  83.4 0.1 collective-permute-start.17
  83.5 0.1 collective-permute-start.18
  83.6 1.8 %collective-permute-start.19 = (bf16[3,64,384]{2,1,0:T(8,128)(2,1)S(1)}, bf16[3,64,384]{2,1,0:T(8,128)(2,1)S(1)}, u32[]{:S(2)}, u32[]{:S(2)}) collective-permute-start(bf16[3,64,384]{2,1,0:T(8,128)(2,1)S(1)} %get-tuple-element.113), channel_id=1, source_target_pairs={{0,3},{1,2},{2,1},{3,0},{4,7},{5,6},{6,5},{7,4},{8,11},{9,10},{10,... | collective-permute-start | bytes 442376 | tf_op jit(solution)/shard_map/ppermute | solution.py:245
  85.4 0.9 collective-permute-start.20
  86.2 2.3 %collective-permute-start.21 = (bf16[3,64,384]{2,1,0:T(8,128)(2,1)S(1)}, bf16[3,64,384]{2,1,0:T(8,128)(2,1)S(1)}, u32[]{:S(2)}, u32[]{:S(2)}) collective-permute-start(bf16[3,64,384]{2,1,0:T(8,128)(2,1)S(1)} %get-tuple-element.115), channel_id=1, source_target_pairs={{0,5},{1,4},{2,7},{3,6},{4,1},{5,0},{6,3},{7,2},{8,13},{9,12},{10,... | collective-permute-start | bytes 442376 | tf_op jit(solution)/shard_map/ppermute | solution.py:245
  88.6 1.0 collective-permute-start.23
  89.6 0.7 collective-permute-done.18.refs_2_
  90.2 1.4 %collective-permute-start.24 = (bf16[3,64,384]{2,1,0:T(8,128)(2,1)S(1)}, bf16[3,64,384]{2,1,0:T(8,128)(2,1)S(1)}, u32[]{:S(2)}, u32[]{:S(2)}) collective-permute-start(bf16[3,64,384]{2,1,0:T(8,128)(2,1)S(1)} %get-tuple-element.125), channel_id=1, source_target_pairs={{0,7},{1,6},{2,5},{3,4},{4,3},{5,2},{6,1},{7,0},{8,15},{9,14},{10,... | collective-permute-start | bytes 442376 | tf_op jit(solution)/shard_map/ppermute | solution.py:245
  91.6 0.9 collective-permute-done.19.refs_3_
  92.5 4.6 %collective-permute-done.20.refs_4_ = bf16[3,64,384]{2,1,0:T(8,128)(2,1)S(1)} collective-permute-done((bf16[3,64,384]{2,1,0:T(8,128)(2,1)S(1)}, bf16[3,64,384]{2,1,0:T(8,128)(2,1)S(1)}, u32[]{:S(2)}, u32[]{:S(2)}) %collective-permute-start.20) | collective-permute-done | bytes 147488 | tf_op jit(solution)/shard_map/ppermute | solution.py:245
  97.1 2.2 %collective-permute-done.21.refs_5_ = bf16[3,64,384]{2,1,0:T(8,128)(2,1)S(1)} collective-permute-done((bf16[3,64,384]{2,1,0:T(8,128)(2,1)S(1)}, bf16[3,64,384]{2,1,0:T(8,128)(2,1)S(1)}, u32[]{:S(2)}, u32[]{:S(2)}) %collective-permute-start.21) | collective-permute-done | bytes 147488 | tf_op jit(solution)/shard_map/ppermute | solution.py:245
  99.3 4.0 %all-to-all-done.1.in_ref = bf16[32,8,1280]{2,1,0:T(8,128)(2,1)S(1)} async-done(((bf16[32,8,1280]{2,1,0:T(8,128)(2,1)}), bf16[32,8,1280]{2,1,0:T(8,128)(2,1)S(1)}, u32[]{:S(2)}, u32[]{:S(2)}) %all-to-all-start.1) | async-done | bytes 655392 | tf_op jit(solution)/shard_map/all_to_all | solution.py:358
  103.3 0.5 total.1
  103.8 1.9 %collective-permute-start.22 = (f32[8,1536]{1,0:T(8,128)S(1)}, f32[8,1536]{1,0:T(8,128)S(1)}, u32[]{:S(2)}, u32[]{:S(2)}) collective-permute-start(f32[8,1536]{1,0:T(8,128)S(1)} %get-tuple-element.117), channel_id=1, source_target_pairs={{0,0},{32,2},{64,4},{96,6},{128,32},{160,34},{192,36},{224,38},{2,... | collective-permute-start | bytes 147464 | tf_op jit(solution)/shard_map/ppermute | solution.py:362
  105.8 0.6 collective-permute-start.25
  106.4 3.5 %collective-permute-start.26 = (f32[16,128]{1,0:T(8,128)S(1)}, f32[16,128]{1,0:T(8,128)S(1)}, u32[]{:S(2)}, u32[]{:S(2)}) collective-permute-start(f32[16,128]{1,0:T(8,128)S(1)} %get-tuple-element.128.o0), channel_id=1, source_target_pairs={{0,4},{2,6},{4,0},{6,2},{1,5},{3,7},{5,1},{7,3},{8,12},{10,14},{12... | collective-permute-start | bytes 24584 | tf_op jit(solution)/shard_map/ppermute | solution.py:245
  109.9 0.7 collective-permute-start.27
  110.6 1.8 %unpack.1 = bf16[3,128,1536]{2,1,0:T(8,128)(2,1)} custom-call(s32[5]{0:T(128)S(1)} %stack.26.place, bf16[3,64,384]{2,1,0:T(8,128)(2,1)S(1)} %get-tuple-element.118.refs_0_, bf16[3,64,384]{2,1,0:T(8,128)(2,1)S(1)} %collective-permute-done.17.refs_1_, bf16[3,64,384]{2,1,0:T(8,128)(2,1)S(1)} %collective-permute-done.18.refs_2_, ...), custom_call_target="tpu_custom_call" | custom-call | bytes 2359316 | tf_op jit(solution)/shard_map/unpack/pallas_call | solution.py:54
  112.3 0.5 collective-permute-done.22.home_ref
  112.8 1.9 %collective-permute-done.27.o3 = f32[16,128]{1,0:T(8,128)S(1)} collective-permute-done((f32[16,128]{1,0:T(8,128)S(1)}, f32[16,128]{1,0:T(8,128)S(1)}, u32[]{:S(2)}, u32[]{:S(2)}) %collective-permute-start.27) | collective-permute-done | bytes 8224 | tf_op jit(solution)/shard_map/ppermute | solution.py:245
  114.7 1.2 %last.1 = (f32[6,1536]{1,0:T(8,128)}, f32[12,15]{1,0:T(8,128)}) custom-call(s32[5]{0:T(128)S(1)} %stack.26.place, f32[8,1536]{1,0:T(8,128)S(1)} %collective-permute-done.22.home_ref, f32[16,128]{1,0:T(8,128)S(1)} %get-tuple-element.128.o0, f32[16,128]{1,0:T(8,128)S(1)} %collective-permute-done.25.o1, f32[16,128]{1,0:T(8,128)S(1)} %collective-permute-done.26.o2, ...), custom_call_target="tpu_custom_call" | custom-call | bytes 119524 | tf_op jit(solution)/shard_map/last/pallas_call | solution.py:54
  (28 shorter events, 0.1 us)
Async XLA Ops:
  0.6 4.5 %copy-start.5 = (bf16[6,1536]{1,0:T(8,128)(2,1)S(1)}, bf16[6,1536]{1,0:T(8,128)(2,1)}, u32[]{:S(2)}) copy-start(bf16[6,1536]{1,0:T(8,128)(2,1)} %param.10) | copy-start | bytes 55300
  0.6 4.6 %copy-start = (bf16[3,1,1,128,1536]{4,3,2,1,0:T(8,128)(2,1)S(1)}, bf16[3,1,1,128,1536]{4,3,2,1,0:T(8,128)(2,1)}, u32[]{:S(2)}) copy-start(bf16[3,1,1,128,1536]{4,3,2,1,0:T(8,128)(2,1)} %param.7) | copy-start | bytes 3538948
  0.7 28.7 %all-to-all-start = ((bf16[8,32,1536]{2,1,0:T(8,128)(2,1)}), bf16[8,32,1536]{2,1,0:T(8,128)(2,1)S(1)}, u32[]{:S(2)}, u32[]{:S(2)}) async-start(bf16[8,32,1536]{2,1,0:T(8,128)(2,1)} %bitcast.11), calls=%async_computation | async-start | bytes 1572864 | tf_op jit(solution)/shard_map/all_to_all | solution.py:259
  5.1 24.2 %copy-start.2 = (s32[1,8]{1,0:T(1,128)S(1)}, s32[1,8]{1,0:T(1,128)}, u32[]{:S(2)}) copy-start(s32[1,8]{1,0:T(1,128)} %sizes.1) | copy-start | bytes 100
  6.0 12.2 %collective-permute-start = (bf16[8,1536]{1,0:T(8,128)(2,1)S(1)}, bf16[8,1536]{1,0:T(8,128)(2,1)S(1)}, u32[]{:S(2)}, u32[]{:S(2)}) collective-permute-start(bf16[8,1536]{1,0:T(8,128)(2,1)S(1)} %pad.4), channel_id=1, source_target_pairs={{0,0},{2,32},{4,64},{6,96},{32,128},{34,160},{36,192},{38,224},{64... | collective-permute-start | bytes 73736 | tf_op jit(solution)/shard_map/ppermute | solution.py:271
  13.7 6.0 %collective-permute-start.1 = (bf16[8,1536]{1,0:T(8,128)(2,1)S(1)}, bf16[8,1536]{1,0:T(8,128)(2,1)S(1)}, u32[]{:S(2)}, u32[]{:S(2)}) collective-permute-start(bf16[8,1536]{1,0:T(8,128)(2,1)S(1)} %pad.4), channel_id=1, source_target_pairs={{0,32},{2,0},{4,96},{6,64},{32,160},{34,128},{36,224},{38,192},{64... | collective-permute-start | bytes 73736 | tf_op jit(solution)/shard_map/ppermute | solution.py:271
  19.8 9.6 %collective-permute-start.5 = (bf16[16,1536]{1,0:T(8,128)(2,1)S(1)}, bf16[16,1536]{1,0:T(8,128)(2,1)S(1)}, u32[]{:S(2)}, u32[]{:S(2)}) collective-permute-start(bf16[16,1536]{1,0:T(8,128)(2,1)S(1)} %pad_maximum_fusion.1), channel_id=1, source_target_pairs={{0,64},{32,96},{64,0},{96,32},{128,192},{160,224},{192,128},{224,1... | collective-permute-start | bytes 147464 | tf_op jit(solution)/shard_map/ppermute | solution.py:245
  23.8 15.7 %collective-permute-start.2 = (bf16[3,128,384]{2,1,0:T(8,128)(2,1)S(1)}, bf16[3,128,384]{2,1,0:T(8,128)(2,1)S(1)}, u32[]{:S(2)}, u32[]{:S(2)}) collective-permute-start(bf16[3,128,384]{2,1,0:T(8,128)(2,1)S(1)} %get-tuple-element.77), channel_id=1, source_target_pairs={{0,2},{2,0},{4,6},{6,4},{1,3},{3,1},{5,7},{7,5},{8,10},{10,8},{12,... | collective-permute-start | bytes 884744 | tf_op jit(solution)/shard_map/ppermute | solution.py:245
  23.8 17.0 %collective-permute-start.3 = (bf16[3,128,384]{2,1,0:T(8,128)(2,1)S(1)}, bf16[3,128,384]{2,1,0:T(8,128)(2,1)S(1)}, u32[]{:S(2)}, u32[]{:S(2)}) collective-permute-start(bf16[3,128,384]{2,1,0:T(8,128)(2,1)S(1)} %get-tuple-element.78), channel_id=1, source_target_pairs={{0,4},{2,6},{4,0},{6,2},{1,5},{3,7},{5,1},{7,3},{8,12},{10,14},{12... | collective-permute-start | bytes 884744 | tf_op jit(solution)/shard_map/ppermute | solution.py:245
  29.3 14.1 %collective-permute-start.4 = (bf16[3,128,384]{2,1,0:T(8,128)(2,1)S(1)}, bf16[3,128,384]{2,1,0:T(8,128)(2,1)S(1)}, u32[]{:S(2)}, u32[]{:S(2)}) collective-permute-start(bf16[3,128,384]{2,1,0:T(8,128)(2,1)S(1)} %get-tuple-element.79), channel_id=1, source_target_pairs={{0,6},{2,4},{4,2},{6,0},{1,7},{3,5},{5,3},{7,1},{8,14},{10,12},{12... | collective-permute-start | bytes 884744 | tf_op jit(solution)/shard_map/ppermute | solution.py:245
  30.2 9.3 %collective-permute-start.7 = (bf16[32,1536]{1,0:T(8,128)(2,1)S(1)}, bf16[32,1536]{1,0:T(8,128)(2,1)S(1)}, u32[]{:S(2)}, u32[]{:S(2)}) collective-permute-start(bf16[32,1536]{1,0:T(8,128)(2,1)S(1)} %pad_maximum_fusion), channel_id=1, source_target_pairs={{0,128},{32,160},{64,192},{96,224},{128,0},{160,32},{192,64},{224,... | collective-permute-start | bytes 294920 | tf_op jit(solution)/shard_map/ppermute | solution.py:245
  34.3 5.2 %collective-permute-start.6 = (bf16[64,1536]{1,0:T(8,128)(2,1)S(1)}, bf16[64,1536]{1,0:T(8,128)(2,1)S(1)}, u32[]{:S(2)}, u32[]{:S(2)}) collective-permute-start(bf16[64,1536]{1,0:T(8,128)(2,1)S(1)} %get-tuple-element.84), channel_id=1, source_target_pairs={{0,1},{1,0},{2,3},{3,2},{4,5},{5,4},{6,7},{7,6},{8,9},{9,8},{10,11... | collective-permute-start | bytes 589832 | tf_op jit(solution)/shard_map/ppermute | solution.py:245
  39.5 19.8 %copy-start.3 = (f32[12,15]{1,0:T(8,128)S(1)}, f32[12,15]{1,0:T(8,128)}, u32[]{:S(2)}) copy-start(f32[12,15]{1,0:T(8,128)} %bias.1) | copy-start | bytes 2164
  39.5 19.7 %copy-start.4 = (s32[8,384]{1,0:T(8,128)S(1)}, s32[8,384]{1,0:T(8,128)}, u32[]{:S(2)}) copy-start(s32[8,384]{1,0:T(8,128)} %constant.25.clone.leave_ref) | copy-start | bytes 36868
  44.0 15.3 %collective-permute-start.8 = (bf16[4,3,64,384]{3,2,1,0:T(8,128)(2,1)S(1)}, bf16[4,3,64,384]{3,2,1,0:T(8,128)(2,1)S(1)}, u32[]{:S(2)}, u32[]{:S(2)}) collective-permute-start(bf16[4,3,64,384]{3,2,1,0:T(8,128)(2,1)S(1)} %cross.1), channel_id=1, source_target_pairs={{0,1},{1,0},{2,3},{3,2},{4,5},{5,4},{6,7},{7,6},{8,9},{9,8},{10,11... | collective-permute-start | bytes 1769480 | tf_op jit(solution)/shard_map/ppermute | solution.py:245
  44.1 12.0 %collective-permute-start.10 = (bf16[128,1536]{1,0:T(8,128)(2,1)S(1)}, bf16[128,1536]{1,0:T(8,128)(2,1)S(1)}, u32[]{:S(2)}, u32[]{:S(2)}) collective-permute-start(bf16[128,1536]{1,0:T(8,128)(2,1)S(1)} %stack.27.u0), channel_id=1, source_target_pairs={{0,2},{2,0},{4,6},{6,4},{1,3},{3,1},{5,7},{7,5},{8,10},{10,8},{12,... | collective-permute-start | bytes 1179656 | tf_op jit(solution)/shard_map/ppermute | solution.py:245
  44.2 7.2 %collective-permute-start.9 = (bf16[64,1536]{1,0:T(8,128)(2,1)S(1)}, bf16[64,1536]{1,0:T(8,128)(2,1)S(1)}, u32[]{:S(2)}, u32[]{:S(2)}) collective-permute-start(bf16[64,1536]{1,0:T(8,128)(2,1)S(1)} %constant_dynamic-update-slice_fusion.refs_0_), channel_id=1, source_target_pairs={{0,8},{8,0},{16,24},{24,16},{1,9},{9,1},{17,25},{25,17},{2,10},{10... | collective-permute-start | bytes 589832 | tf_op jit(solution)/shard_map/ppermute | solution.py:245
  45.8 22.1 %collective-permute-start.11 = (bf16[128,1536]{1,0:T(8,128)(2,1)S(1)}, bf16[128,1536]{1,0:T(8,128)(2,1)S(1)}, u32[]{:S(2)}, u32[]{:S(2)}) collective-permute-start(bf16[128,1536]{1,0:T(8,128)(2,1)S(1)} %stack.27.u0), channel_id=1, source_target_pairs={{0,4},{2,6},{4,0},{6,2},{1,5},{3,7},{5,1},{7,3},{8,12},{10,14},{12... | collective-permute-start | bytes 1179656 | tf_op jit(solution)/shard_map/ppermute | solution.py:245
  47.5 20.5 %collective-permute-start.12 = (bf16[128,1536]{1,0:T(8,128)(2,1)S(1)}, bf16[128,1536]{1,0:T(8,128)(2,1)S(1)}, u32[]{:S(2)}, u32[]{:S(2)}) collective-permute-start(bf16[128,1536]{1,0:T(8,128)(2,1)S(1)} %stack.27.u0), channel_id=1, source_target_pairs={{0,6},{2,4},{4,2},{6,0},{1,7},{3,5},{5,3},{7,1},{8,14},{10,12},{12... | collective-permute-start | bytes 1179656 | tf_op jit(solution)/shard_map/ppermute | solution.py:245
  56.1 11.7 %collective-permute-start.14 = (bf16[128,1536]{1,0:T(8,128)(2,1)S(1)}, bf16[128,1536]{1,0:T(8,128)(2,1)S(1)}, u32[]{:S(2)}, u32[]{:S(2)}) collective-permute-start(bf16[128,1536]{1,0:T(8,128)(2,1)S(1)} %stack.28.refs_0_), channel_id=1, source_target_pairs={{0,16},{8,24},{16,0},{24,8},{1,17},{9,25},{17,1},{25,9},{2,18},{10... | collective-permute-start | bytes 1179656 | tf_op jit(solution)/shard_map/ppermute | solution.py:245
  67.8 2.4 %collective-permute-start.15 = (bf16[256,1536]{1,0:T(8,128)(2,1)S(1)}, bf16[256,1536]{1,0:T(8,128)(2,1)S(1)}, u32[]{:S(2)}, u32[]{:S(2)}) collective-permute-start(bf16[256,1536]{1,0:T(8,128)(2,1)S(1)} %stack.29.w0_ref), channel_id=1, source_target_pairs={{0,1},{1,0},{2,3},{3,2},{4,5},{5,4},{6,7},{7,6},{8,9},{9,8},{10,11... | collective-permute-start | bytes 2359304 | tf_op jit(solution)/shard_map/ppermute | solution.py:245
  68.0 2.3 %copy-start.1 = (s32[8,384]{1,0:T(8,128)S(1)}, s32[8,384]{1,0:T(8,128)}, u32[]{:S(2)}) copy-start(s32[8,384]{1,0:T(8,128)} %constant.26.clone.rows_ref) | copy-start | bytes 36868
  69.4 4.5 %collective-permute-start.13 = (bf16[192,1536]{1,0:T(8,128)(2,1)S(1)}, bf16[192,1536]{1,0:T(8,128)(2,1)S(1)}, u32[]{:S(2)}, u32[]{:S(2)}) collective-permute-start(bf16[192,1536]{1,0:T(8,128)(2,1)S(1)} %get-tuple-element.94), channel_id=1, source_target_pairs={{0,1},{1,0},{2,3},{3,2},{4,5},{5,4},{6,7},{7,6},{8,9},{9,8},{10,11... | collective-permute-start | bytes 1769480 | tf_op jit(solution)/shard_map/ppermute | solution.py:245
  72.5 1.4 %collective-permute-start.16 = (f32[8,384]{1,0:T(8,128)S(1)}, f32[8,384]{1,0:T(8,128)S(1)}, u32[]{:S(2)}, u32[]{:S(2)}) collective-permute-start(f32[8,384]{1,0:T(8,128)S(1)} %get-tuple-element.99.s0), channel_id=1, source_target_pairs={{0,1},{1,0},{2,3},{3,2},{4,5},{5,4},{6,7},{7,6},{8,9},{9,8},{10,11... | collective-permute-start | bytes 36872 | tf_op jit(solution)/shard_map/ppermute | solution.py:245
  75.4 27.9 %all-to-all-start.1 = ((bf16[32,8,1280]{2,1,0:T(8,128)(2,1)}), bf16[32,8,1280]{2,1,0:T(8,128)(2,1)S(1)}, u32[]{:S(2)}, u32[]{:S(2)}) async-start(bf16[32,8,1280]{2,1,0:T(8,128)(2,1)} %join.1), calls=%async_computation.1 | async-start | bytes 1310720 | tf_op jit(solution)/shard_map/all_to_all | solution.py:358
  83.4 5.2 %collective-permute-start.17 = (bf16[3,64,384]{2,1,0:T(8,128)(2,1)S(1)}, bf16[3,64,384]{2,1,0:T(8,128)(2,1)S(1)}, u32[]{:S(2)}, u32[]{:S(2)}) collective-permute-start(bf16[3,64,384]{2,1,0:T(8,128)(2,1)S(1)} %get-tuple-element.111), channel_id=1, source_target_pairs={{0,1},{1,0},{2,3},{3,2},{4,5},{5,4},{6,7},{7,6},{8,9},{9,8},{10,11... | collective-permute-start | bytes 442376 | tf_op jit(solution)/shard_map/ppermute | solution.py:245
  83.5 6.7 %collective-permute-start.18 = (bf16[3,64,384]{2,1,0:T(8,128)(2,1)S(1)}, bf16[3,64,384]{2,1,0:T(8,128)(2,1)S(1)}, u32[]{:S(2)}, u32[]{:S(2)}) collective-permute-start(bf16[3,64,384]{2,1,0:T(8,128)(2,1)S(1)} %get-tuple-element.112), channel_id=1, source_target_pairs={{0,2},{1,3},{2,0},{3,1},{4,6},{5,7},{6,4},{7,5},{8,10},{9,11},{10,... | collective-permute-start | bytes 442376 | tf_op jit(solution)/shard_map/ppermute | solution.py:245
  83.6 8.9 %collective-permute-start.19 = (bf16[3,64,384]{2,1,0:T(8,128)(2,1)S(1)}, bf16[3,64,384]{2,1,0:T(8,128)(2,1)S(1)}, u32[]{:S(2)}, u32[]{:S(2)}) collective-permute-start(bf16[3,64,384]{2,1,0:T(8,128)(2,1)S(1)} %get-tuple-element.113), channel_id=1, source_target_pairs={{0,3},{1,2},{2,1},{3,0},{4,7},{5,6},{6,5},{7,4},{8,11},{9,10},{10,... | collective-permute-start | bytes 442376 | tf_op jit(solution)/shard_map/ppermute | solution.py:245
  85.4 11.7 %collective-permute-start.20 = (bf16[3,64,384]{2,1,0:T(8,128)(2,1)S(1)}, bf16[3,64,384]{2,1,0:T(8,128)(2,1)S(1)}, u32[]{:S(2)}, u32[]{:S(2)}) collective-permute-start(bf16[3,64,384]{2,1,0:T(8,128)(2,1)S(1)} %get-tuple-element.114), channel_id=1, source_target_pairs={{0,4},{1,5},{2,6},{3,7},{4,0},{5,1},{6,2},{7,3},{8,12},{9,13},{10,... | collective-permute-start | bytes 442376 | tf_op jit(solution)/shard_map/ppermute | solution.py:245
  86.2 13.0 %collective-permute-start.21 = (bf16[3,64,384]{2,1,0:T(8,128)(2,1)S(1)}, bf16[3,64,384]{2,1,0:T(8,128)(2,1)S(1)}, u32[]{:S(2)}, u32[]{:S(2)}) collective-permute-start(bf16[3,64,384]{2,1,0:T(8,128)(2,1)S(1)} %get-tuple-element.115), channel_id=1, source_target_pairs={{0,5},{1,4},{2,7},{3,6},{4,1},{5,0},{6,3},{7,2},{8,13},{9,12},{10,... | collective-permute-start | bytes 442376 | tf_op jit(solution)/shard_map/ppermute | solution.py:245
  88.6 21.3 %collective-permute-start.23 = (bf16[3,64,384]{2,1,0:T(8,128)(2,1)S(1)}, bf16[3,64,384]{2,1,0:T(8,128)(2,1)S(1)}, u32[]{:S(2)}, u32[]{:S(2)}) collective-permute-start(bf16[3,64,384]{2,1,0:T(8,128)(2,1)S(1)} %get-tuple-element.124), channel_id=1, source_target_pairs={{0,6},{1,7},{2,4},{3,5},{4,2},{5,3},{6,0},{7,1},{8,14},{9,15},{10,... | collective-permute-start | bytes 442376 | tf_op jit(solution)/shard_map/ppermute | solution.py:245
  90.2 20.3 %collective-permute-start.24 = (bf16[3,64,384]{2,1,0:T(8,128)(2,1)S(1)}, bf16[3,64,384]{2,1,0:T(8,128)(2,1)S(1)}, u32[]{:S(2)}, u32[]{:S(2)}) collective-permute-start(bf16[3,64,384]{2,1,0:T(8,128)(2,1)S(1)} %get-tuple-element.125), channel_id=1, source_target_pairs={{0,7},{1,6},{2,5},{3,4},{4,3},{5,2},{6,1},{7,0},{8,15},{9,14},{10,... | collective-permute-start | bytes 442376 | tf_op jit(solution)/shard_map/ppermute | solution.py:245
  103.8 9.0 %collective-permute-start.22 = (f32[8,1536]{1,0:T(8,128)S(1)}, f32[8,1536]{1,0:T(8,128)S(1)}, u32[]{:S(2)}, u32[]{:S(2)}) collective-permute-start(f32[8,1536]{1,0:T(8,128)S(1)} %get-tuple-element.117), channel_id=1, source_target_pairs={{0,0},{32,2},{64,4},{96,6},{128,32},{160,34},{192,36},{224,38},{2,... | collective-permute-start | bytes 147464 | tf_op jit(solution)/shard_map/ppermute | solution.py:362
  105.8 7.1 %collective-permute-start.25 = (f32[16,128]{1,0:T(8,128)S(1)}, f32[16,128]{1,0:T(8,128)S(1)}, u32[]{:S(2)}, u32[]{:S(2)}) collective-permute-start(f32[16,128]{1,0:T(8,128)S(1)} %get-tuple-element.128.o0), channel_id=1, source_target_pairs={{0,2},{2,0},{4,6},{6,4},{1,3},{3,1},{5,7},{7,5},{8,10},{10,8},{12,... | collective-permute-start | bytes 24584 | tf_op jit(solution)/shard_map/ppermute | solution.py:245
  106.4 6.5 %collective-permute-start.26 = (f32[16,128]{1,0:T(8,128)S(1)}, f32[16,128]{1,0:T(8,128)S(1)}, u32[]{:S(2)}, u32[]{:S(2)}) collective-permute-start(f32[16,128]{1,0:T(8,128)S(1)} %get-tuple-element.128.o0), channel_id=1, source_target_pairs={{0,4},{2,6},{4,0},{6,2},{1,5},{3,7},{5,1},{7,3},{8,12},{10,14},{12... | collective-permute-start | bytes 24584 | tf_op jit(solution)/shard_map/ppermute | solution.py:245
  109.9 4.9 %collective-permute-start.27 = (f32[16,128]{1,0:T(8,128)S(1)}, f32[16,128]{1,0:T(8,128)S(1)}, u32[]{:S(2)}, u32[]{:S(2)}) collective-permute-start(f32[16,128]{1,0:T(8,128)S(1)} %get-tuple-element.128.o0), channel_id=1, source_target_pairs={{0,6},{2,4},{4,2},{6,0},{1,7},{3,5},{5,3},{7,1},{8,14},{10,12},{12... | collective-permute-start | bytes 24584 | tf_op jit(solution)/shard_map/ppermute | solution.py:245

commit v11 on v10

--- a/solution.py
+++ b/solution.py
@@ -286,16 +286,14 @@
     )
     held, same = lax.optimization_barrier((held, same))
     held = jnp.concatenate([held, hop(held, "z", 4, Z)])
-    z4 = held
     u0 = stack([same, hop(other, "core", 1, C)])
-    held, _ = lax.optimization_barrier((held, u0))
     ups = [u0] + [hop(u0, "x", k, X) for k in range(1, X)]
     held = stack([held, hop(held, "y", 1, Y)])
-    held, ups[1] = lax.optimization_barrier((held, ups[1]))
+    y1 = held
     held = stack([held, hop(held, "y", 2, Y)])
     held2 = hop(held, "core", 1, C)
 
-    packed, _, _ = lax.optimization_barrier((packed, u0, z4))
+    packed, _, _ = lax.optimization_barrier((packed, u0, y1))
     (cross,) = call(cross_kernel, "cross", [((X, 3, HALF, COLS), bf)], place, *packed, smem=1)
     cross = hop(cross, "core", 1, C)
     probs, mixed, recv = call(

time: 117 us -> 121 us (1.034)
  waiting for transfers between devices: 34.3 us -> 40.2 us
  starting transfers between devices: 63.2 us -> 60.4 us
    ppermute x25, waiting for transfers between devices: 28.2 us -> 36 us  [hop(): return lax.ppermute(x, axis, [(i, i ^ k) for i in range(n)])]
    all_to_all x1, starting transfers between devices: 7.95 us -> 3.94 us  [per_device(): msgs = lax.all_to_all(msgs, ('z', 'y'), 0, 0, tiled=True)]
    all_to_all x1, waiting for transfers between devices: 4.05 us -> 2.18 us  [per_device(): msgs = lax.all_to_all(msgs, ('z', 'y'), 0, 0, tiled=True)]
  transfers between devices with their start and end apart: 30 -> 30, of which waited for: 15 -> 12; matrix products, arithmetic and copies ran while one was open for 0% -> 0% of each run, Pallas kernels for 12% -> 12%
where the time goes in v11:
time: 121 us; the launch traced here: 119 us
  starting transfers between devices  60.4 us (50%)
  waiting for transfers between devices  40.2 us (33%)
  Pallas kernels  17.3 us (14%)
    ppermute x25, starting transfers between devices, hop(): return lax.ppermute(x, axis, [(i, i ^ k) for i in range(n)])  37.9 us
    ppermute x25, waiting for transfers between devices, hop(): return lax.ppermute(x, axis, [(i, i ^ k) for i in range(n)])  36 us
    pallas_call x14, Pallas kernels, call(): pl.pallas_call(body, out_shape=tuple((jax.ShapeDtypeStruct(s, d) for s, d...  17.3 us
    ppermute x2, starting transfers between devices, per_device(): held = [lax.ppermute(rows8, ('z', 'x'), p) for p in (there, near)]  12.2 us
    all_to_all x1, starting transfers between devices, per_device(): cot = lax.all_to_all(cot_out[0, 0], SEQ, 0, 0, tiled=True)  4.44 us
    all_to_all x1, starting transfers between devices, per_device(): msgs = lax.all_to_all(msgs, ('z', 'y'), 0, 0, tiled=True)  3.94 us
  transfers between devices with their start and end apart: 30, of which 12 were waited for; matrix products, arithmetic and copies ran while one was open for 0% of the time, Pallas kernels for 12%

profile of v11, /device:TPU:32, one launch (start us, length us, event | category | flops | bytes accessed | tf_op | source)
XLA Modules:
  0.0 118.9 jit_solution(3431261087160418423)
XLA Ops:
  0.7 4.4 %all-to-all-start = ((bf16[8,32,1536]{2,1,0:T(8,128)(2,1)}), bf16[8,32,1536]{2,1,0:T(8,128)(2,1)S(1)}, u32[]{:S(2)}, u32[]{:S(2)}) async-start(bf16[8,32,1536]{2,1,0:T(8,128)(2,1)} %bitcast.11), calls=%async_computation | async-start | bytes 1572864 | tf_op jit(solution)/shard_map/all_to_all | solution.py:259
  5.1 0.1 stack.26.place
  5.2 0.7 pack.1
  6.0 7.7 %collective-permute-start = (bf16[8,1536]{1,0:T(8,128)(2,1)S(1)}, bf16[8,1536]{1,0:T(8,128)(2,1)S(1)}, u32[]{:S(2)}, u32[]{:S(2)}) collective-permute-start(bf16[8,1536]{1,0:T(8,128)(2,1)S(1)} %pad.4), channel_id=1, source_target_pairs={{0,0},{2,32},{4,64},{6,96},{32,128},{34,160},{36,192},{38,224},{64... | collective-permute-start | bytes 73736 | tf_op jit(solution)/shard_map/ppermute | solution.py:271
  13.7 4.5 %collective-permute-start.1 = (bf16[8,1536]{1,0:T(8,128)(2,1)S(1)}, bf16[8,1536]{1,0:T(8,128)(2,1)S(1)}, u32[]{:S(2)}, u32[]{:S(2)}) collective-permute-start(bf16[8,1536]{1,0:T(8,128)(2,1)S(1)} %pad.4), channel_id=1, source_target_pairs={{0,32},{2,0},{4,96},{6,64},{32,160},{34,128},{36,224},{38,192},{64... | collective-permute-start | bytes 73736 | tf_op jit(solution)/shard_map/ppermute | solution.py:271
  18.2 1.5 %collective-permute-done.1 = bf16[8,1536]{1,0:T(8,128)(2,1)S(1)} collective-permute-done((bf16[8,1536]{1,0:T(8,128)(2,1)S(1)}, bf16[8,1536]{1,0:T(8,128)(2,1)S(1)}, u32[]{:S(2)}, u32[]{:S(2)}) %collective-permute-start.1) | collective-permute-done | bytes 24608 | tf_op jit(solution)/shard_map/ppermute | solution.py:271
  19.8 4.1 %collective-permute-start.5 = (bf16[16,1536]{1,0:T(8,128)(2,1)S(1)}, bf16[16,1536]{1,0:T(8,128)(2,1)S(1)}, u32[]{:S(2)}, u32[]{:S(2)}) collective-permute-start(bf16[16,1536]{1,0:T(8,128)(2,1)S(1)} %pad_maximum_fusion.1), channel_id=1, source_target_pairs={{0,64},{32,96},{64,0},{96,32},{128,192},{160,224},{192,128},{224,1... | collective-permute-start | bytes 147464 | tf_op jit(solution)/shard_map/ppermute | solution.py:245
  23.8 0.0 collective-permute-start.2
  23.8 5.5 %collective-permute-start.3 = (bf16[3,128,384]{2,1,0:T(8,128)(2,1)S(1)}, bf16[3,128,384]{2,1,0:T(8,128)(2,1)S(1)}, u32[]{:S(2)}, u32[]{:S(2)}) collective-permute-start(bf16[3,128,384]{2,1,0:T(8,128)(2,1)S(1)} %get-tuple-element.75), channel_id=1, source_target_pairs={{0,4},{2,6},{4,0},{6,2},{1,5},{3,7},{5,1},{7,3},{8,12},{10,14},{12... | collective-permute-start | bytes 884744 | tf_op jit(solution)/shard_map/ppermute | solution.py:245
  29.3 0.0 collective-permute-start.4
  29.3 0.0 collective-permute-done.5
  29.3 0.0 all-to-all-done.cot_ref
  29.3 0.8 compact.1
  30.2 4.1 %collective-permute-start.7 = (bf16[32,1536]{1,0:T(8,128)(2,1)S(1)}, bf16[32,1536]{1,0:T(8,128)(2,1)S(1)}, u32[]{:S(2)}, u32[]{:S(2)}) collective-permute-start(bf16[32,1536]{1,0:T(8,128)(2,1)S(1)} %pad_maximum_fusion), channel_id=1, source_target_pairs={{0,128},{32,160},{64,192},{96,224},{128,0},{160,32},{192,64},{224,... | collective-permute-start | bytes 294920 | tf_op jit(solution)/shard_map/ppermute | solution.py:245
  34.3 0.1 collective-permute-start.6
  34.4 5.1 %collective-permute-done.7 = bf16[32,1536]{1,0:T(8,128)(2,1)S(1)} collective-permute-done((bf16[32,1536]{1,0:T(8,128)(2,1)S(1)}, bf16[32,1536]{1,0:T(8,128)(2,1)S(1)}, u32[]{:S(2)}, u32[]{:S(2)}) %collective-permute-start.7) | collective-permute-done | bytes 98336 | tf_op jit(solution)/shard_map/ppermute | solution.py:245
  39.5 1.7 %collective-permute-start.8 = (bf16[64,1536]{1,0:T(8,128)(2,1)S(1)}, bf16[64,1536]{1,0:T(8,128)(2,1)S(1)}, u32[]{:S(2)}, u32[]{:S(2)}) collective-permute-start(bf16[64,1536]{1,0:T(8,128)(2,1)S(1)} %constant_dynamic-update-slice_fusion.refs_0_), channel_id=1, source_target_pairs={{0,8},{8,0},{16,24},{24,16},{1,9},{9,1},{17,25},{25,17},{2,10},{10... | collective-permute-start | bytes 589832 | tf_op jit(solution)/shard_map/ppermute | solution.py:245
  41.2 0.0 collective-permute-done.6.refs_1_
  41.2 4.1 %collective-permute-done.8.refs_1_ = bf16[64,1536]{1,0:T(8,128)(2,1)S(1)} collective-permute-done((bf16[64,1536]{1,0:T(8,128)(2,1)S(1)}, bf16[64,1536]{1,0:T(8,128)(2,1)S(1)}, u32[]{:S(2)}, u32[]{:S(2)}) %collective-permute-start.8) | collective-permute-done | bytes 196640 | tf_op jit(solution)/shard_map/ppermute | solution.py:245
  45.3 0.0 collective-permute-done.2.refs_1_.p1
  45.3 0.6 cross.1
  45.9 0.0 copy-start.3
  45.9 0.0 copy-start.4
  45.9 0.1 collective-permute-start.9
  46.0 3.3 %collective-permute-start.14 = (bf16[128,1536]{1,0:T(8,128)(2,1)S(1)}, bf16[128,1536]{1,0:T(8,128)(2,1)S(1)}, u32[]{:S(2)}, u32[]{:S(2)}) collective-permute-start(bf16[128,1536]{1,0:T(8,128)(2,1)S(1)} %stack.28.refs_0_), channel_id=1, source_target_pairs={{0,16},{8,24},{16,0},{24,8},{1,17},{9,25},{17,1},{25,9},{2,18},{10... | collective-permute-start | bytes 1179656 | tf_op jit(solution)/shard_map/ppermute | solution.py:245
  49.3 0.3 collective-permute-start.10
  49.6 4.5 %collective-permute-start.11 = (bf16[128,1536]{1,0:T(8,128)(2,1)S(1)}, bf16[128,1536]{1,0:T(8,128)(2,1)S(1)}, u32[]{:S(2)}, u32[]{:S(2)}) collective-permute-start(bf16[128,1536]{1,0:T(8,128)(2,1)S(1)} %stack.27.u0), channel_id=1, source_target_pairs={{0,4},{2,6},{4,0},{6,2},{1,5},{3,7},{5,1},{7,3},{8,12},{10,14},{12... | collective-permute-start | bytes 1179656 | tf_op jit(solution)/shard_map/ppermute | solution.py:245
  54.1 0.0 collective-permute-start.12
  54.1 5.0 %collective-permute-done.14.refs_1_ = bf16[128,1536]{1,0:T(8,128)(2,1)S(1)} collective-permute-done((bf16[128,1536]{1,0:T(8,128)(2,1)S(1)}, bf16[128,1536]{1,0:T(8,128)(2,1)S(1)}, u32[]{:S(2)}, u32[]{:S(2)}) %collective-permute-start.14) | collective-permute-done | bytes 393248 | tf_op jit(solution)/shard_map/ppermute | solution.py:245
  59.1 0.1 stack.29.w0_ref
  59.1 0.1 collective-permute-start.15
  59.3 5.2 %attn_fwd.1 = (f32[3,4,128,128]{3,2,1,0:T(8,128)S(1)}, bf16[512,384]{1,0:T(8,128)(2,1)S(1)}, bf16[8,3,64,384]{3,2,1,0:T(8,128)(2,1)S(1)}) custom-call(s32[5]{0:T(128)S(1)} %stack.26.place, f32[12,15]{1,0:T(8,128)S(1)} %copy-done.3, s32[8,384]{1,0:T(8,128)S(1)} %copy-done.4, bf16[3,128,384]{2,1,0:T(8,128)(2,1)S(1)} %get-tuple-element.83.refs_0_.p0, ...), custom_call_target="tpu_custom_call" | custom-call | flops 20000000000 | bytes 4141796 | tf_op jit(solution)/shard_map/attn_fwd/pallas_call | solution.py:54
  64.5 7.3 %collective-permute-done.11.u2 = bf16[128,1536]{1,0:T(8,128)(2,1)S(1)} collective-permute-done((bf16[128,1536]{1,0:T(8,128)(2,1)S(1)}, bf16[128,1536]{1,0:T(8,128)(2,1)S(1)}, u32[]{:S(2)}, u32[]{:S(2)}) %collective-permute-start.11) | collective-permute-done | bytes 393248 | tf_op jit(solution)/shard_map/ppermute | solution.py:245
  71.8 2.6 %collective-permute-done.12.u3 = bf16[128,1536]{1,0:T(8,128)(2,1)S(1)} collective-permute-done((bf16[128,1536]{1,0:T(8,128)(2,1)S(1)}, bf16[128,1536]{1,0:T(8,128)(2,1)S(1)}, u32[]{:S(2)}, u32[]{:S(2)}) %collective-permute-start.12) | collective-permute-done | bytes 393248 | tf_op jit(solution)/shard_map/ppermute | solution.py:245
  74.3 1.4 %grad_w.1 = (f32[192,1536]{1,0:T(8,128)S(1)}, bf16[192,1536]{1,0:T(8,128)(2,1)S(1)}, bf16[8,64,1536]{2,1,0:T(8,128)(2,1)S(1)}) custom-call(s32[5]{0:T(128)S(1)} %stack.26.place, bf16[512,384]{1,0:T(8,128)(2,1)S(1)} %get-tuple-element.87.mixed_ref, bf16[128,1536]{1,0:T(8,128)(2,1)S(1)} %stack.27.u0, bf16[128,1536]{1,0:T(8,128)(2,1)S(1)} %collective-permute-done.10.u1, ...), custom_call_target="tpu_custom_call" | custom-call | flops 20000000000 | bytes 5308436 | tf_op jit(solution)/shard_map/grad_w/pallas_call | solution.py:54
  75.8 0.3 collective-permute-start.13
  76.1 2.3 %scores_bwd.1 = (bf16[8,64,384]{2,1,0:T(8,128)(2,1)S(1)}, bf16[3,4,128,128]{3,2,1,0:T(8,128)(2,1)S(1)}, f32[8,384]{1,0:T(8,128)S(1)}) custom-call(s32[5]{0:T(128)S(1)} %stack.26.place, s32[8,384]{1,0:T(8,128)S(1)} %copy-done.1, bf16[8,3,64,384]{3,2,1,0:T(8,128)(2,1)S(1)} %get-tuple-element.90.recv_ref.qkv_ref, ...), custom_call_target="tpu_custom_call" | custom-call | flops 900000000 | bytes 5922836 | tf_op jit(solution)/shard_map/scores_bwd/pallas_call | solution.py:54
  78.4 0.6 collective-permute-start.16
  78.9 1.2 grads.1
  80.1 0.0 collective-permute-done.13.other_ref
  80.1 1.6 %join.1 = bf16[32,8,1280]{2,1,0:T(8,128)(2,1)} custom-call(f32[192,1536]{1,0:T(8,128)S(1)} %get-tuple-element.88.mine_ref, bf16[192,1536]{1,0:T(8,128)(2,1)S(1)} %collective-permute-done.13.other_ref, f32[8,384]{1,0:T(8,128)S(1)} %get-tuple-element.93.s0, f32[8,384]{1,0:T(8,128)S(1)} %collective-permute-done.16.s1), custom_call_target="tpu_custom_call" | custom-call | bytes 2449408 | tf_op jit(solution)/shard_map/join/pallas_call | solution.py:54
  81.7 3.9 %all-to-all-start.1 = ((bf16[32,8,1280]{2,1,0:T(8,128)(2,1)}), bf16[32,8,1280]{2,1,0:T(8,128)(2,1)S(1)}, u32[]{:S(2)}, u32[]{:S(2)}) async-start(bf16[32,8,1280]{2,1,0:T(8,128)(2,1)} %join.1), calls=%async_computation.1 | async-start | bytes 1310720 | tf_op jit(solution)/shard_map/all_to_all | solution.py:356
  85.6 0.1 collective-permute-start.17
  85.7 0.1 collective-permute-start.18
  85.8 1.8 %collective-permute-start.19 = (bf16[3,64,384]{2,1,0:T(8,128)(2,1)S(1)}, bf16[3,64,384]{2,1,0:T(8,128)(2,1)S(1)}, u32[]{:S(2)}, u32[]{:S(2)}) collective-permute-start(bf16[3,64,384]{2,1,0:T(8,128)(2,1)S(1)} %get-tuple-element.107), channel_id=1, source_target_pairs={{0,3},{1,2},{2,1},{3,0},{4,7},{5,6},{6,5},{7,4},{8,11},{9,10},{10,... | collective-permute-start | bytes 442376 | tf_op jit(solution)/shard_map/ppermute | solution.py:245
  87.6 2.6 %collective-permute-start.20 = (bf16[3,64,384]{2,1,0:T(8,128)(2,1)S(1)}, bf16[3,64,384]{2,1,0:T(8,128)(2,1)S(1)}, u32[]{:S(2)}, u32[]{:S(2)}) collective-permute-start(bf16[3,64,384]{2,1,0:T(8,128)(2,1)S(1)} %get-tuple-element.108), channel_id=1, source_target_pairs={{0,4},{1,5},{2,6},{3,7},{4,0},{5,1},{6,2},{7,3},{8,12},{9,13},{10,... | collective-permute-start | bytes 442376 | tf_op jit(solution)/shard_map/ppermute | solution.py:245
  90.2 0.6 collective-permute-start.21
  90.8 0.0 collective-permute-done.17.refs_1_
  90.8 2.8 %collective-permute-start.23 = (bf16[3,64,384]{2,1,0:T(8,128)(2,1)S(1)}, bf16[3,64,384]{2,1,0:T(8,128)(2,1)S(1)}, u32[]{:S(2)}, u32[]{:S(2)}) collective-permute-start(bf16[3,64,384]{2,1,0:T(8,128)(2,1)S(1)} %get-tuple-element.118), channel_id=1, source_target_pairs={{0,6},{1,7},{2,4},{3,5},{4,2},{5,3},{6,0},{7,1},{8,14},{9,15},{10,... | collective-permute-start | bytes 442376 | tf_op jit(solution)/shard_map/ppermute | solution.py:245
  93.7 0.4 collective-permute-start.24
  94.1 0.6 collective-permute-done.19.refs_3_
  94.7 6.5 %collective-permute-done.20.refs_4_ = bf16[3,64,384]{2,1,0:T(8,128)(2,1)S(1)} collective-permute-done((bf16[3,64,384]{2,1,0:T(8,128)(2,1)S(1)}, bf16[3,64,384]{2,1,0:T(8,128)(2,1)S(1)}, u32[]{:S(2)}, u32[]{:S(2)}) %collective-permute-start.20) | collective-permute-done | bytes 147488 | tf_op jit(solution)/shard_map/ppermute | solution.py:245
  101.2 2.2 %collective-permute-done.21.refs_5_ = bf16[3,64,384]{2,1,0:T(8,128)(2,1)S(1)} collective-permute-done((bf16[3,64,384]{2,1,0:T(8,128)(2,1)S(1)}, bf16[3,64,384]{2,1,0:T(8,128)(2,1)S(1)}, u32[]{:S(2)}, u32[]{:S(2)}) %collective-permute-start.21) | collective-permute-done | bytes 147488 | tf_op jit(solution)/shard_map/ppermute | solution.py:245
  103.4 2.2 %all-to-all-done.1.in_ref = bf16[32,8,1280]{2,1,0:T(8,128)(2,1)S(1)} async-done(((bf16[32,8,1280]{2,1,0:T(8,128)(2,1)}), bf16[32,8,1280]{2,1,0:T(8,128)(2,1)S(1)}, u32[]{:S(2)}, u32[]{:S(2)}) %all-to-all-start.1) | async-done | bytes 655392 | tf_op jit(solution)/shard_map/all_to_all | solution.py:356
  105.6 0.5 total.1
  106.1 1.9 %collective-permute-start.22 = (f32[8,1536]{1,0:T(8,128)S(1)}, f32[8,1536]{1,0:T(8,128)S(1)}, u32[]{:S(2)}, u32[]{:S(2)}) collective-permute-start(f32[8,1536]{1,0:T(8,128)S(1)} %get-tuple-element.111), channel_id=1, source_target_pairs={{0,0},{32,2},{64,4},{96,6},{128,32},{160,34},{192,36},{224,38},{2,... | collective-permute-start | bytes 147464 | tf_op jit(solution)/shard_map/ppermute | solution.py:360
  108.0 0.8 collective-permute-start.25
  108.8 4.2 %collective-permute-start.26 = (f32[16,128]{1,0:T(8,128)S(1)}, f32[16,128]{1,0:T(8,128)S(1)}, u32[]{:S(2)}, u32[]{:S(2)}) collective-permute-start(f32[16,128]{1,0:T(8,128)S(1)} %get-tuple-element.122.o0), channel_id=1, source_target_pairs={{0,4},{2,6},{4,0},{6,2},{1,5},{3,7},{5,1},{7,3},{8,12},{10,14},{12... | collective-permute-start | bytes 24584 | tf_op jit(solution)/shard_map/ppermute | solution.py:245
  112.9 0.0 collective-permute-start.27
  112.9 0.0 collective-permute-done.24.refs_7_
  112.9 1.8 %unpack.1 = bf16[3,128,1536]{2,1,0:T(8,128)(2,1)} custom-call(s32[5]{0:T(128)S(1)} %stack.26.place, bf16[3,64,384]{2,1,0:T(8,128)(2,1)S(1)} %get-tuple-element.112.refs_0_, bf16[3,64,384]{2,1,0:T(8,128)(2,1)S(1)} %collective-permute-done.17.refs_1_, bf16[3,64,384]{2,1,0:T(8,128)(2,1)S(1)} %collective-permute-done.18.refs_2_, ...), custom_call_target="tpu_custom_call" | custom-call | bytes 2359316 | tf_op jit(solution)/shard_map/unpack/pallas_call | solution.py:54
  114.7 0.5 collective-permute-done.22.home_ref
  115.2 2.6 %collective-permute-done.27.o3 = f32[16,128]{1,0:T(8,128)S(1)} collective-permute-done((f32[16,128]{1,0:T(8,128)S(1)}, f32[16,128]{1,0:T(8,128)S(1)}, u32[]{:S(2)}, u32[]{:S(2)}) %collective-permute-start.27) | collective-permute-done | bytes 8224 | tf_op jit(solution)/shard_map/ppermute | solution.py:245
  117.8 1.2 last.1
  (28 shorter events, 0.1 us)
Async XLA Ops:
  0.6 4.5 %copy-start.5 = (bf16[6,1536]{1,0:T(8,128)(2,1)S(1)}, bf16[6,1536]{1,0:T(8,128)(2,1)}, u32[]{:S(2)}) copy-start(bf16[6,1536]{1,0:T(8,128)(2,1)} %param.10) | copy-start | bytes 55300
  0.6 4.6 %copy-start = (bf16[3,1,1,128,1536]{4,3,2,1,0:T(8,128)(2,1)S(1)}, bf16[3,1,1,128,1536]{4,3,2,1,0:T(8,128)(2,1)}, u32[]{:S(2)}) copy-start(bf16[3,1,1,128,1536]{4,3,2,1,0:T(8,128)(2,1)} %param.7) | copy-start | bytes 3538948
  0.7 28.7 %all-to-all-start = ((bf16[8,32,1536]{2,1,0:T(8,128)(2,1)}), bf16[8,32,1536]{2,1,0:T(8,128)(2,1)S(1)}, u32[]{:S(2)}, u32[]{:S(2)}) async-start(bf16[8,32,1536]{2,1,0:T(8,128)(2,1)} %bitcast.11), calls=%async_computation | async-start | bytes 1572864 | tf_op jit(solution)/shard_map/all_to_all | solution.py:259
  5.1 24.2 %copy-start.2 = (s32[1,8]{1,0:T(1,128)S(1)}, s32[1,8]{1,0:T(1,128)}, u32[]{:S(2)}) copy-start(s32[1,8]{1,0:T(1,128)} %sizes.1) | copy-start | bytes 100
  6.0 12.2 %collective-permute-start = (bf16[8,1536]{1,0:T(8,128)(2,1)S(1)}, bf16[8,1536]{1,0:T(8,128)(2,1)S(1)}, u32[]{:S(2)}, u32[]{:S(2)}) collective-permute-start(bf16[8,1536]{1,0:T(8,128)(2,1)S(1)} %pad.4), channel_id=1, source_target_pairs={{0,0},{2,32},{4,64},{6,96},{32,128},{34,160},{36,192},{38,224},{64... | collective-permute-start | bytes 73736 | tf_op jit(solution)/shard_map/ppermute | solution.py:271
  13.7 6.0 %collective-permute-start.1 = (bf16[8,1536]{1,0:T(8,128)(2,1)S(1)}, bf16[8,1536]{1,0:T(8,128)(2,1)S(1)}, u32[]{:S(2)}, u32[]{:S(2)}) collective-permute-start(bf16[8,1536]{1,0:T(8,128)(2,1)S(1)} %pad.4), channel_id=1, source_target_pairs={{0,32},{2,0},{4,96},{6,64},{32,160},{34,128},{36,224},{38,192},{64... | collective-permute-start | bytes 73736 | tf_op jit(solution)/shard_map/ppermute | solution.py:271
  19.8 9.6 %collective-permute-start.5 = (bf16[16,1536]{1,0:T(8,128)(2,1)S(1)}, bf16[16,1536]{1,0:T(8,128)(2,1)S(1)}, u32[]{:S(2)}, u32[]{:S(2)}) collective-permute-start(bf16[16,1536]{1,0:T(8,128)(2,1)S(1)} %pad_maximum_fusion.1), channel_id=1, source_target_pairs={{0,64},{32,96},{64,0},{96,32},{128,192},{160,224},{192,128},{224,1... | collective-permute-start | bytes 147464 | tf_op jit(solution)/shard_map/ppermute | solution.py:245
  23.8 21.4 %collective-permute-start.2 = (bf16[3,128,384]{2,1,0:T(8,128)(2,1)S(1)}, bf16[3,128,384]{2,1,0:T(8,128)(2,1)S(1)}, u32[]{:S(2)}, u32[]{:S(2)}) collective-permute-start(bf16[3,128,384]{2,1,0:T(8,128)(2,1)S(1)} %get-tuple-element.74), channel_id=1, source_target_pairs={{0,2},{2,0},{4,6},{6,4},{1,3},{3,1},{5,7},{7,5},{8,10},{10,8},{12,... | collective-permute-start | bytes 884744 | tf_op jit(solution)/shard_map/ppermute | solution.py:245
  23.8 21.4 %collective-permute-start.3 = (bf16[3,128,384]{2,1,0:T(8,128)(2,1)S(1)}, bf16[3,128,384]{2,1,0:T(8,128)(2,1)S(1)}, u32[]{:S(2)}, u32[]{:S(2)}) collective-permute-start(bf16[3,128,384]{2,1,0:T(8,128)(2,1)S(1)} %get-tuple-element.75), channel_id=1, source_target_pairs={{0,4},{2,6},{4,0},{6,2},{1,5},{3,7},{5,1},{7,3},{8,12},{10,14},{12... | collective-permute-start | bytes 884744 | tf_op jit(solution)/shard_map/ppermute | solution.py:245
  29.3 16.0 %collective-permute-start.4 = (bf16[3,128,384]{2,1,0:T(8,128)(2,1)S(1)}, bf16[3,128,384]{2,1,0:T(8,128)(2,1)S(1)}, u32[]{:S(2)}, u32[]{:S(2)}) collective-permute-start(bf16[3,128,384]{2,1,0:T(8,128)(2,1)S(1)} %get-tuple-element.76), channel_id=1, source_target_pairs={{0,6},{2,4},{4,2},{6,0},{1,7},{3,5},{5,3},{7,1},{8,14},{10,12},{12... | collective-permute-start | bytes 884744 | tf_op jit(solution)/shard_map/ppermute | solution.py:245
  30.2 9.3 %collective-permute-start.7 = (bf16[32,1536]{1,0:T(8,128)(2,1)S(1)}, bf16[32,1536]{1,0:T(8,128)(2,1)S(1)}, u32[]{:S(2)}, u32[]{:S(2)}) collective-permute-start(bf16[32,1536]{1,0:T(8,128)(2,1)S(1)} %pad_maximum_fusion), channel_id=1, source_target_pairs={{0,128},{32,160},{64,192},{96,224},{128,0},{160,32},{192,64},{224,... | collective-permute-start | bytes 294920 | tf_op jit(solution)/shard_map/ppermute | solution.py:245
  34.3 6.9 %collective-permute-start.6 = (bf16[64,1536]{1,0:T(8,128)(2,1)S(1)}, bf16[64,1536]{1,0:T(8,128)(2,1)S(1)}, u32[]{:S(2)}, u32[]{:S(2)}) collective-permute-start(bf16[64,1536]{1,0:T(8,128)(2,1)S(1)} %get-tuple-element.81), channel_id=1, source_target_pairs={{0,1},{1,0},{2,3},{3,2},{4,5},{5,4},{6,7},{7,6},{8,9},{9,8},{10,11... | collective-permute-start | bytes 589832 | tf_op jit(solution)/shard_map/ppermute | solution.py:245
  39.5 5.8 %collective-permute-start.8 = (bf16[64,1536]{1,0:T(8,128)(2,1)S(1)}, bf16[64,1536]{1,0:T(8,128)(2,1)S(1)}, u32[]{:S(2)}, u32[]{:S(2)}) collective-permute-start(bf16[64,1536]{1,0:T(8,128)(2,1)S(1)} %constant_dynamic-update-slice_fusion.refs_0_), channel_id=1, source_target_pairs={{0,8},{8,0},{16,24},{24,16},{1,9},{9,1},{17,25},{25,17},{2,10},{10... | collective-permute-start | bytes 589832 | tf_op jit(solution)/shard_map/ppermute | solution.py:245
  45.9 13.3 %copy-start.3 = (f32[12,15]{1,0:T(8,128)S(1)}, f32[12,15]{1,0:T(8,128)}, u32[]{:S(2)}) copy-start(f32[12,15]{1,0:T(8,128)} %bias.1) | copy-start | bytes 2164
  45.9 13.3 %copy-start.4 = (s32[8,384]{1,0:T(8,128)S(1)}, s32[8,384]{1,0:T(8,128)}, u32[]{:S(2)}) copy-start(s32[8,384]{1,0:T(8,128)} %constant.25.clone.leave_ref) | copy-start | bytes 36868
  45.9 13.3 %collective-permute-start.9 = (bf16[4,3,64,384]{3,2,1,0:T(8,128)(2,1)S(1)}, bf16[4,3,64,384]{3,2,1,0:T(8,128)(2,1)S(1)}, u32[]{:S(2)}, u32[]{:S(2)}) collective-permute-start(bf16[4,3,64,384]{3,2,1,0:T(8,128)(2,1)S(1)} %cross.1), channel_id=1, source_target_pairs={{0,1},{1,0},{2,3},{3,2},{4,5},{5,4},{6,7},{7,6},{8,9},{9,8},{10,11... | collective-permute-start | bytes 1769480 | tf_op jit(solution)/shard_map/ppermute | solution.py:245
  46.0 13.0 %collective-permute-start.14 = (bf16[128,1536]{1,0:T(8,128)(2,1)S(1)}, bf16[128,1536]{1,0:T(8,128)(2,1)S(1)}, u32[]{:S(2)}, u32[]{:S(2)}) collective-permute-start(bf16[128,1536]{1,0:T(8,128)(2,1)S(1)} %stack.28.refs_0_), channel_id=1, source_target_pairs={{0,16},{8,24},{16,0},{24,8},{1,17},{9,25},{17,1},{25,9},{2,18},{10... | collective-permute-start | bytes 1179656 | tf_op jit(solution)/shard_map/ppermute | solution.py:245
  49.3 15.1 %collective-permute-start.10 = (bf16[128,1536]{1,0:T(8,128)(2,1)S(1)}, bf16[128,1536]{1,0:T(8,128)(2,1)S(1)}, u32[]{:S(2)}, u32[]{:S(2)}) collective-permute-start(bf16[128,1536]{1,0:T(8,128)(2,1)S(1)} %stack.27.u0), channel_id=1, source_target_pairs={{0,2},{2,0},{4,6},{6,4},{1,3},{3,1},{5,7},{7,5},{8,10},{10,8},{12,... | collective-permute-start | bytes 1179656 | tf_op jit(solution)/shard_map/ppermute | solution.py:245
  49.6 22.1 %collective-permute-start.11 = (bf16[128,1536]{1,0:T(8,128)(2,1)S(1)}, bf16[128,1536]{1,0:T(8,128)(2,1)S(1)}, u32[]{:S(2)}, u32[]{:S(2)}) collective-permute-start(bf16[128,1536]{1,0:T(8,128)(2,1)S(1)} %stack.27.u0), channel_id=1, source_target_pairs={{0,4},{2,6},{4,0},{6,2},{1,5},{3,7},{5,1},{7,3},{8,12},{10,14},{12... | collective-permute-start | bytes 1179656 | tf_op jit(solution)/shard_map/ppermute | solution.py:245
  54.1 20.2 %collective-permute-start.12 = (bf16[128,1536]{1,0:T(8,128)(2,1)S(1)}, bf16[128,1536]{1,0:T(8,128)(2,1)S(1)}, u32[]{:S(2)}, u32[]{:S(2)}) collective-permute-start(bf16[128,1536]{1,0:T(8,128)(2,1)S(1)} %stack.27.u0), channel_id=1, source_target_pairs={{0,6},{2,4},{4,2},{6,0},{1,7},{3,5},{5,3},{7,1},{8,14},{10,12},{12... | collective-permute-start | bytes 1179656 | tf_op jit(solution)/shard_map/ppermute | solution.py:245
  59.1 16.9 %collective-permute-start.15 = (bf16[256,1536]{1,0:T(8,128)(2,1)S(1)}, bf16[256,1536]{1,0:T(8,128)(2,1)S(1)}, u32[]{:S(2)}, u32[]{:S(2)}) collective-permute-start(bf16[256,1536]{1,0:T(8,128)(2,1)S(1)} %stack.29.w0_ref), channel_id=1, source_target_pairs={{0,1},{1,0},{2,3},{3,2},{4,5},{5,4},{6,7},{7,6},{8,9},{9,8},{10,11... | collective-permute-start | bytes 2359304 | tf_op jit(solution)/shard_map/ppermute | solution.py:245
  74.3 1.7 %copy-start.1 = (s32[8,384]{1,0:T(8,128)S(1)}, s32[8,384]{1,0:T(8,128)}, u32[]{:S(2)}) copy-start(s32[8,384]{1,0:T(8,128)} %constant.26.clone.rows_ref) | copy-start | bytes 36868
  75.8 4.3 %collective-permute-start.13 = (bf16[192,1536]{1,0:T(8,128)(2,1)S(1)}, bf16[192,1536]{1,0:T(8,128)(2,1)S(1)}, u32[]{:S(2)}, u32[]{:S(2)}) collective-permute-start(bf16[192,1536]{1,0:T(8,128)(2,1)S(1)} %get-tuple-element.89), channel_id=1, source_target_pairs={{0,1},{1,0},{2,3},{3,2},{4,5},{5,4},{6,7},{7,6},{8,9},{9,8},{10,11... | collective-permute-start | bytes 1769480 | tf_op jit(solution)/shard_map/ppermute | solution.py:245
  78.4 1.8 %collective-permute-start.16 = (f32[8,384]{1,0:T(8,128)S(1)}, f32[8,384]{1,0:T(8,128)S(1)}, u32[]{:S(2)}, u32[]{:S(2)}) collective-permute-start(f32[8,384]{1,0:T(8,128)S(1)} %get-tuple-element.93.s0), channel_id=1, source_target_pairs={{0,1},{1,0},{2,3},{3,2},{4,5},{5,4},{6,7},{7,6},{8,9},{9,8},{10,11... | collective-permute-start | bytes 36872 | tf_op jit(solution)/shard_map/ppermute | solution.py:245
  81.7 23.9 %all-to-all-start.1 = ((bf16[32,8,1280]{2,1,0:T(8,128)(2,1)}), bf16[32,8,1280]{2,1,0:T(8,128)(2,1)S(1)}, u32[]{:S(2)}, u32[]{:S(2)}) async-start(bf16[32,8,1280]{2,1,0:T(8,128)(2,1)} %join.1), calls=%async_computation.1 | async-start | bytes 1310720 | tf_op jit(solution)/shard_map/all_to_all | solution.py:356
  85.6 5.2 %collective-permute-start.17 = (bf16[3,64,384]{2,1,0:T(8,128)(2,1)S(1)}, bf16[3,64,384]{2,1,0:T(8,128)(2,1)S(1)}, u32[]{:S(2)}, u32[]{:S(2)}) collective-permute-start(bf16[3,64,384]{2,1,0:T(8,128)(2,1)S(1)} %get-tuple-element.105), channel_id=1, source_target_pairs={{0,1},{1,0},{2,3},{3,2},{4,5},{5,4},{6,7},{7,6},{8,9},{9,8},{10,11... | collective-permute-start | bytes 442376 | tf_op jit(solution)/shard_map/ppermute | solution.py:245
  85.7 7.9 %collective-permute-start.18 = (bf16[3,64,384]{2,1,0:T(8,128)(2,1)S(1)}, bf16[3,64,384]{2,1,0:T(8,128)(2,1)S(1)}, u32[]{:S(2)}, u32[]{:S(2)}) collective-permute-start(bf16[3,64,384]{2,1,0:T(8,128)(2,1)S(1)} %get-tuple-element.106), channel_id=1, source_target_pairs={{0,2},{1,3},{2,0},{3,1},{4,6},{5,7},{6,4},{7,5},{8,10},{9,11},{10,... | collective-permute-start | bytes 442376 | tf_op jit(solution)/shard_map/ppermute | solution.py:245
  85.8 8.9 %collective-permute-start.19 = (bf16[3,64,384]{2,1,0:T(8,128)(2,1)S(1)}, bf16[3,64,384]{2,1,0:T(8,128)(2,1)S(1)}, u32[]{:S(2)}, u32[]{:S(2)}) collective-permute-start(bf16[3,64,384]{2,1,0:T(8,128)(2,1)S(1)} %get-tuple-element.107), channel_id=1, source_target_pairs={{0,3},{1,2},{2,1},{3,0},{4,7},{5,6},{6,5},{7,4},{8,11},{9,10},{10,... | collective-permute-start | bytes 442376 | tf_op jit(solution)/shard_map/ppermute | solution.py:245
  87.6 13.6 %collective-permute-start.20 = (bf16[3,64,384]{2,1,0:T(8,128)(2,1)S(1)}, bf16[3,64,384]{2,1,0:T(8,128)(2,1)S(1)}, u32[]{:S(2)}, u32[]{:S(2)}) collective-permute-start(bf16[3,64,384]{2,1,0:T(8,128)(2,1)S(1)} %get-tuple-element.108), channel_id=1, source_target_pairs={{0,4},{1,5},{2,6},{3,7},{4,0},{5,1},{6,2},{7,3},{8,12},{9,13},{10,... | collective-permute-start | bytes 442376 | tf_op jit(solution)/shard_map/ppermute | solution.py:245
  90.2 13.2 %collective-permute-start.21 = (bf16[3,64,384]{2,1,0:T(8,128)(2,1)S(1)}, bf16[3,64,384]{2,1,0:T(8,128)(2,1)S(1)}, u32[]{:S(2)}, u32[]{:S(2)}) collective-permute-start(bf16[3,64,384]{2,1,0:T(8,128)(2,1)S(1)} %get-tuple-element.109), channel_id=1, source_target_pairs={{0,5},{1,4},{2,7},{3,6},{4,1},{5,0},{6,3},{7,2},{8,13},{9,12},{10,... | collective-permute-start | bytes 442376 | tf_op jit(solution)/shard_map/ppermute | solution.py:245
  90.8 22.1 %collective-permute-start.23 = (bf16[3,64,384]{2,1,0:T(8,128)(2,1)S(1)}, bf16[3,64,384]{2,1,0:T(8,128)(2,1)S(1)}, u32[]{:S(2)}, u32[]{:S(2)}) collective-permute-start(bf16[3,64,384]{2,1,0:T(8,128)(2,1)S(1)} %get-tuple-element.118), channel_id=1, source_target_pairs={{0,6},{1,7},{2,4},{3,5},{4,2},{5,3},{6,0},{7,1},{8,14},{9,15},{10,... | collective-permute-start | bytes 442376 | tf_op jit(solution)/shard_map/ppermute | solution.py:245
  93.7 19.3 %collective-permute-start.24 = (bf16[3,64,384]{2,1,0:T(8,128)(2,1)S(1)}, bf16[3,64,384]{2,1,0:T(8,128)(2,1)S(1)}, u32[]{:S(2)}, u32[]{:S(2)}) collective-permute-start(bf16[3,64,384]{2,1,0:T(8,128)(2,1)S(1)} %get-tuple-element.119), channel_id=1, source_target_pairs={{0,7},{1,6},{2,5},{3,4},{4,3},{5,2},{6,1},{7,0},{8,15},{9,14},{10,... | collective-permute-start | bytes 442376 | tf_op jit(solution)/shard_map/ppermute | solution.py:245
  106.1 9.1 %collective-permute-start.22 = (f32[8,1536]{1,0:T(8,128)S(1)}, f32[8,1536]{1,0:T(8,128)S(1)}, u32[]{:S(2)}, u32[]{:S(2)}) collective-permute-start(f32[8,1536]{1,0:T(8,128)S(1)} %get-tuple-element.111), channel_id=1, source_target_pairs={{0,0},{32,2},{64,4},{96,6},{128,32},{160,34},{192,36},{224,38},{2,... | collective-permute-start | bytes 147464 | tf_op jit(solution)/shard_map/ppermute | solution.py:360
  108.0 7.2 %collective-permute-start.25 = (f32[16,128]{1,0:T(8,128)S(1)}, f32[16,128]{1,0:T(8,128)S(1)}, u32[]{:S(2)}, u32[]{:S(2)}) collective-permute-start(f32[16,128]{1,0:T(8,128)S(1)} %get-tuple-element.122.o0), channel_id=1, source_target_pairs={{0,2},{2,0},{4,6},{6,4},{1,3},{3,1},{5,7},{7,5},{8,10},{10,8},{12,... | collective-permute-start | bytes 24584 | tf_op jit(solution)/shard_map/ppermute | solution.py:245
  108.8 6.4 %collective-permute-start.26 = (f32[16,128]{1,0:T(8,128)S(1)}, f32[16,128]{1,0:T(8,128)S(1)}, u32[]{:S(2)}, u32[]{:S(2)}) collective-permute-start(f32[16,128]{1,0:T(8,128)S(1)} %get-tuple-element.122.o0), channel_id=1, source_target_pairs={{0,4},{2,6},{4,0},{6,2},{1,5},{3,7},{5,1},{7,3},{8,12},{10,14},{12... | collective-permute-start | bytes 24584 | tf_op jit(solution)/shard_map/ppermute | solution.py:245
  112.9 4.9 %collective-permute-start.27 = (f32[16,128]{1,0:T(8,128)S(1)}, f32[16,128]{1,0:T(8,128)S(1)}, u32[]{:S(2)}, u32[]{:S(2)}) collective-permute-start(f32[16,128]{1,0:T(8,128)S(1)} %get-tuple-element.122.o0), channel_id=1, source_target_pairs={{0,6},{2,4},{4,2},{6,0},{1,7},{3,5},{5,3},{7,1},{8,14},{10,12},{12... | collective-permute-start | bytes 24584 | tf_op jit(solution)/shard_map/ppermute | solution.py:245

commit v12 on v9

--- a/solution.py
+++ b/solution.py
@@ -265,9 +265,9 @@
     u0 = stack([same, hop(other, "core", 1, C)])
     held, _ = lax.optimization_barrier((held, u0))
     ups = [u0] + [hop(u0, "x", k, X) for k in range(1, X)]
-    held = stack([held, hop(held, "y", 1, Y)])
-    held, ups[1] = lax.optimization_barrier((held, ups[1]))
-    held = stack([held, hop(held, "y", 2, Y)])
+    w1, w2 = hop(held, "y", 1, Y), hop(held, "y", 2, Y)
+    far, ups[1] = lax.optimization_barrier((w1, ups[1]))
+    held = stack([held, w1, w2, hop(far, "y", 2, Y)])
     held2 = hop(held, "core", 1, C)
 
     probs, mixed = call(

time: 116 us -> 116 us (level)
  starting transfers between devices: 65.5 us -> 68.5 us
  waiting for transfers between devices: 31 us -> 28 us
    ppermute x21 -> x22, waiting for transfers between devices: 24.9 us -> 21.9 us  [hop(): return lax.ppermute(x, axis, [(i, i ^ k) for i in range(n)])]
    ppermute x21 -> x22, starting transfers between devices: 29.1 us -> 32.1 us  [hop(): return lax.ppermute(x, axis, [(i, i ^ k) for i in range(n)])]
    pallas_call x13 -> x12, Pallas kernels: 16.9 us -> 16.9 us  [call(): pl.pallas_call(body, out_shape=tuple((jax.ShapeDtypeStruct(s, d) for s, d...]
  transfers between devices with their start and end apart: 27 -> 28, of which waited for: 14 -> 13; matrix products, arithmetic and copies ran while one was open for 0% -> 0% of each run, Pallas kernels for 12% -> 12%
where the time goes in v12:
time: 116 us; the launch traced here: 115 us
  starting transfers between devices  68.5 us (59%)
  waiting for transfers between devices  28 us (24%)
  Pallas kernels  16.9 us (15%)
    ppermute x22, starting transfers between devices, hop(): return lax.ppermute(x, axis, [(i, i ^ k) for i in range(n)])  32.1 us
    ppermute x22, waiting for transfers between devices, hop(): return lax.ppermute(x, axis, [(i, i ^ k) for i in range(n)])  21.9 us
    pallas_call x12, Pallas kernels, call(): pl.pallas_call(body, out_shape=tuple((jax.ShapeDtypeStruct(s, d) for s, d...  16.9 us
    ppermute x2, starting transfers between devices, per_device(): held = [lax.ppermute(rows8, ('z', 'x'), p) for p in (there, near)]  12.2 us
    all_to_all x1, starting transfers between devices, per_device(): msgs = lax.all_to_all(msgs, ('z', 'y'), 0, 0, tiled=True)  10.2 us
    all_to_all x1, starting transfers between devices, per_device(): recv = lax.all_to_all(packed, SEQ, 0, 0, tiled=True)  7.56 us
    all_to_all x1, starting transfers between devices, per_device(): cot = lax.all_to_all(cot_out[0, 0], SEQ, 0, 0, tiled=True)  4.44 us
    all_to_all x1, waiting for transfers between devices, per_device(): msgs = lax.all_to_all(msgs, ('z', 'y'), 0, 0, tiled=True)  3.88 us
  transfers between devices with their start and end apart: 28, of which 13 were waited for; matrix products, arithmetic and copies ran while one was open for 0% of the time, Pallas kernels for 12%

profile of v12, /device:TPU:32, one launch (start us, length us, event | category | flops | bytes accessed | tf_op | source)
XLA Modules:
  0.0 115.1 jit_solution(1481572397398936226)
XLA Ops:
  0.6 4.4 %all-to-all-start.1 = ((bf16[8,32,1536]{2,1,0:T(8,128)(2,1)}), bf16[8,32,1536]{2,1,0:T(8,128)(2,1)S(1)}, u32[]{:S(2)}, u32[]{:S(2)}) async-start(bf16[8,32,1536]{2,1,0:T(8,128)(2,1)} %bitcast.11), calls=%async_computation.1 | async-start | bytes 1572864 | tf_op jit(solution)/shard_map/all_to_all | solution.py:244
  5.1 0.0 copy-start.5
  5.1 1.1 pack.1
  6.2 0.0 copy-start.2
  6.2 7.7 %collective-permute-start = (bf16[8,1536]{1,0:T(8,128)(2,1)S(1)}, bf16[8,1536]{1,0:T(8,128)(2,1)S(1)}, u32[]{:S(2)}, u32[]{:S(2)}) collective-permute-start(bf16[8,1536]{1,0:T(8,128)(2,1)S(1)} %pad.4), channel_id=1, source_target_pairs={{0,0},{2,32},{4,64},{6,96},{32,128},{34,160},{36,192},{38,224},{64... | collective-permute-start | bytes 73736 | tf_op jit(solution)/shard_map/ppermute | solution.py:247
  14.0 4.5 %collective-permute-start.1 = (bf16[8,1536]{1,0:T(8,128)(2,1)S(1)}, bf16[8,1536]{1,0:T(8,128)(2,1)S(1)}, u32[]{:S(2)}, u32[]{:S(2)}) collective-permute-start(bf16[8,1536]{1,0:T(8,128)(2,1)S(1)} %pad.4), channel_id=1, source_target_pairs={{0,32},{2,0},{4,96},{6,64},{32,160},{34,128},{36,224},{38,192},{64... | collective-permute-start | bytes 73736 | tf_op jit(solution)/shard_map/ppermute | solution.py:247
  18.5 0.0 collective-permute-done
  18.5 1.5 %collective-permute-done.1 = bf16[8,1536]{1,0:T(8,128)(2,1)S(1)} collective-permute-done((bf16[8,1536]{1,0:T(8,128)(2,1)S(1)}, bf16[8,1536]{1,0:T(8,128)(2,1)S(1)}, u32[]{:S(2)}, u32[]{:S(2)}) %collective-permute-start.1) | collective-permute-done | bytes 24608 | tf_op jit(solution)/shard_map/ppermute | solution.py:247
  20.0 7.6 %all-to-all-start = ((bf16[8,3,64,384]{3,2,1,0:T(8,128)(2,1)}), bf16[8,3,64,384]{3,2,1,0:T(8,128)(2,1)S(1)}, u32[]{:S(2)}, u32[]{:S(2)}) async-start(bf16[8,3,64,384]{3,2,1,0:T(8,128)(2,1)} %pack.1), calls=%async_computation | async-start | bytes 2359296 | tf_op jit(solution)/shard_map/all_to_all | solution.py:249
  27.6 1.7 %collective-permute-start.2 = (bf16[16,1536]{1,0:T(8,128)(2,1)S(1)}, bf16[16,1536]{1,0:T(8,128)(2,1)S(1)}, u32[]{:S(2)}, u32[]{:S(2)}) collective-permute-start(bf16[16,1536]{1,0:T(8,128)(2,1)S(1)} %pad_maximum_fusion.2), channel_id=1, source_target_pairs={{0,64},{32,96},{64,0},{96,32},{128,192},{160,224},{192,128},{224,1... | collective-permute-start | bytes 147464 | tf_op jit(solution)/shard_map/ppermute | solution.py:230
  29.2 0.1 stack.25.place
  29.3 0.8 compact.1
  30.1 0.3 collective-permute-start.3
  30.4 2.3 %collective-permute-done.2 = bf16[16,1536]{1,0:T(8,128)(2,1)S(1)} collective-permute-done((bf16[16,1536]{1,0:T(8,128)(2,1)S(1)}, bf16[16,1536]{1,0:T(8,128)(2,1)S(1)}, u32[]{:S(2)}, u32[]{:S(2)}) %collective-permute-start.2) | collective-permute-done | bytes 49184 | tf_op jit(solution)/shard_map/ppermute | solution.py:230
  32.7 2.3 %collective-permute-start.4 = (bf16[32,1536]{1,0:T(8,128)(2,1)S(1)}, bf16[32,1536]{1,0:T(8,128)(2,1)S(1)}, u32[]{:S(2)}, u32[]{:S(2)}) collective-permute-start(bf16[32,1536]{1,0:T(8,128)(2,1)S(1)} %pad_maximum_fusion.1), channel_id=1, source_target_pairs={{0,128},{32,160},{64,192},{96,224},{128,0},{160,32},{192,64},{224,... | collective-permute-start | bytes 294920 | tf_op jit(solution)/shard_map/ppermute | solution.py:230
  35.0 0.0 collective-permute-done.3.refs_1_
  35.1 2.0 %collective-permute-start.6 = (bf16[128,1536]{1,0:T(8,128)(2,1)S(1)}, bf16[128,1536]{1,0:T(8,128)(2,1)S(1)}, u32[]{:S(2)}, u32[]{:S(2)}) collective-permute-start(bf16[128,1536]{1,0:T(8,128)(2,1)S(1)} %stack.26.u0), channel_id=1, source_target_pairs={{0,2},{2,0},{4,6},{6,4},{1,3},{3,1},{5,7},{7,5},{8,10},{10,8},{12,... | collective-permute-start | bytes 1179656 | tf_op jit(solution)/shard_map/ppermute | solution.py:230
  37.0 4.4 %collective-permute-done.4 = bf16[32,1536]{1,0:T(8,128)(2,1)S(1)} collective-permute-done((bf16[32,1536]{1,0:T(8,128)(2,1)S(1)}, bf16[32,1536]{1,0:T(8,128)(2,1)S(1)}, u32[]{:S(2)}, u32[]{:S(2)}) %collective-permute-start.4) | collective-permute-done | bytes 98336 | tf_op jit(solution)/shard_map/ppermute | solution.py:230
  41.4 1.7 %collective-permute-start.5 = (bf16[64,1536]{1,0:T(8,128)(2,1)S(1)}, bf16[64,1536]{1,0:T(8,128)(2,1)S(1)}, u32[]{:S(2)}, u32[]{:S(2)}) collective-permute-start(bf16[64,1536]{1,0:T(8,128)(2,1)S(1)} %pad_maximum_fusion.refs_0_), channel_id=1, source_target_pairs={{0,8},{8,0},{16,24},{24,16},{1,9},{9,1},{17,25},{25,17},{2,10},{10... | collective-permute-start | bytes 589832 | tf_op jit(solution)/shard_map/ppermute | solution.py:230
  43.1 3.6 %collective-permute-start.7 = (bf16[128,1536]{1,0:T(8,128)(2,1)S(1)}, bf16[128,1536]{1,0:T(8,128)(2,1)S(1)}, u32[]{:S(2)}, u32[]{:S(2)}) collective-permute-start(bf16[128,1536]{1,0:T(8,128)(2,1)S(1)} %stack.26.u0), channel_id=1, source_target_pairs={{0,4},{2,6},{4,0},{6,2},{1,5},{3,7},{5,1},{7,3},{8,12},{10,14},{12... | collective-permute-start | bytes 1179656 | tf_op jit(solution)/shard_map/ppermute | solution.py:230
  46.7 1.2 %collective-permute-start.8 = (bf16[128,1536]{1,0:T(8,128)(2,1)S(1)}, bf16[128,1536]{1,0:T(8,128)(2,1)S(1)}, u32[]{:S(2)}, u32[]{:S(2)}) collective-permute-start(bf16[128,1536]{1,0:T(8,128)(2,1)S(1)} %stack.26.u0), channel_id=1, source_target_pairs={{0,6},{2,4},{4,2},{6,0},{1,7},{3,5},{5,3},{7,1},{8,14},{10,12},{12... | collective-permute-start | bytes 1179656 | tf_op jit(solution)/shard_map/ppermute | solution.py:230
  47.8 2.9 %collective-permute-start.10 = (bf16[64,1536]{1,0:T(8,128)(2,1)S(1)}, bf16[64,1536]{1,0:T(8,128)(2,1)S(1)}, u32[]{:S(2)}, u32[]{:S(2)}) collective-permute-start(bf16[64,1536]{1,0:T(8,128)(2,1)S(1)} %pad_maximum_fusion.refs_0_), channel_id=1, source_target_pairs={{0,16},{8,24},{16,0},{24,8},{1,17},{9,25},{17,1},{25,9},{2,18},{10... | collective-permute-start | bytes 589832 | tf_op jit(solution)/shard_map/ppermute | solution.py:230
  50.7 1.6 %collective-permute-done.6.u1 = bf16[128,1536]{1,0:T(8,128)(2,1)S(1)} collective-permute-done((bf16[128,1536]{1,0:T(8,128)(2,1)S(1)}, bf16[128,1536]{1,0:T(8,128)(2,1)S(1)}, u32[]{:S(2)}, u32[]{:S(2)}) %collective-permute-start.6) | collective-permute-done | bytes 393248 | tf_op jit(solution)/shard_map/ppermute | solution.py:230
  52.3 3.2 %collective-permute-start.11 = (bf16[64,1536]{1,0:T(8,128)(2,1)S(1)}, bf16[64,1536]{1,0:T(8,128)(2,1)S(1)}, u32[]{:S(2)}, u32[]{:S(2)}) collective-permute-start(bf16[64,1536]{1,0:T(8,128)(2,1)S(1)} %collective-permute-done.5.refs_1_), channel_id=1, source_target_pairs={{0,16},{8,24},{16,0},{24,8},{1,17},{9,25},{17,1},{25,9},{2,18},{10... | collective-permute-start | bytes 589832 | tf_op jit(solution)/shard_map/ppermute | solution.py:230
  55.5 0.0 all-to-all-done.qkv_ref.recv_ref
  55.5 0.7 copy-done.4
  56.2 5.0 %attn_fwd.1 = (f32[3,4,128,128]{3,2,1,0:T(8,128)S(1)}, bf16[512,384]{1,0:T(8,128)(2,1)S(1)}) custom-call(s32[5]{0:T(128)S(1)} %stack.25.place, f32[12,15]{1,0:T(8,128)S(1)} %copy-done.3, s32[8,384]{1,0:T(8,128)S(1)} %copy-done.4, bf16[8,3,64,384]{3,2,1,0:T(8,128)(2,1)S(1)} %all-to-all-done.qkv_ref.recv_ref), custom_call_target="tpu_custom_call" | custom-call | flops 20000000000 | bytes 2372324 | tf_op jit(solution)/shard_map/attn_fwd/pallas_call | solution.py:54
  61.3 0.1 stack.27.w0_ref
  61.4 0.1 collective-permute-start.12
  61.5 0.4 collective-permute-done.7.u2
  61.9 2.9 %collective-permute-done.8.u3 = bf16[128,1536]{1,0:T(8,128)(2,1)S(1)} collective-permute-done((bf16[128,1536]{1,0:T(8,128)(2,1)S(1)}, bf16[128,1536]{1,0:T(8,128)(2,1)S(1)}, u32[]{:S(2)}, u32[]{:S(2)}) %collective-permute-start.8) | collective-permute-done | bytes 393248 | tf_op jit(solution)/shard_map/ppermute | solution.py:230
  64.8 1.4 %grad_w.1 = (f32[192,1536]{1,0:T(8,128)S(1)}, bf16[192,1536]{1,0:T(8,128)(2,1)S(1)}, bf16[8,64,1536]{2,1,0:T(8,128)(2,1)S(1)}) custom-call(s32[5]{0:T(128)S(1)} %stack.25.place, bf16[512,384]{1,0:T(8,128)(2,1)S(1)} %get-tuple-element.55.mixed_ref, bf16[128,1536]{1,0:T(8,128)(2,1)S(1)} %stack.26.u0, bf16[128,1536]{1,0:T(8,128)(2,1)S(1)} %collective-permute-done.6.u1, ...), custom_call_target="tpu_custom_call" | custom-call | flops 20000000000 | bytes 5308436 | tf_op jit(solution)/shard_map/grad_w/pallas_call | solution.py:54
  66.3 0.1 collective-permute-start.9
  66.4 2.3 %scores_bwd.1 = (bf16[8,64,384]{2,1,0:T(8,128)(2,1)S(1)}, bf16[3,4,128,128]{3,2,1,0:T(8,128)(2,1)S(1)}, f32[8,384]{1,0:T(8,128)S(1)}) custom-call(s32[5]{0:T(128)S(1)} %stack.25.place, s32[8,384]{1,0:T(8,128)S(1)} %copy-done.1, bf16[8,3,64,384]{3,2,1,0:T(8,128)(2,1)S(1)} %all-to-all-done.qkv_ref.recv_ref, ...), custom_call_target="tpu_custom_call" | custom-call | flops 900000000 | bytes 5922836 | tf_op jit(solution)/shard_map/scores_bwd/pallas_call | solution.py:54
  68.7 0.7 collective-permute-start.13
  69.4 1.2 %grads.1 = (bf16[3,64,384]{2,1,0:T(8,128)(2,1)S(1)}, bf16[3,64,384]{2,1,0:T(8,128)(2,1)S(1)}, bf16[3,64,384]{2,1,0:T(8,128)(2,1)S(1)}, bf16[3,64,384]{2,1,0:T(8,...) custom-call(s32[5]{0:T(128)S(1)} %stack.25.place, ...), custom_call_target="tpu_custom_call" | custom-call | flops 150000000 | bytes 3932180 | tf_op jit(solution)/shard_map/grads/pallas_call | solution.py:54
  70.6 0.0 collective-permute-done.9.other_ref
  70.6 0.0 collective-permute-done.13.s1
  70.6 1.5 %join.1 = bf16[32,8,1280]{2,1,0:T(8,128)(2,1)} custom-call(f32[192,1536]{1,0:T(8,128)S(1)} %get-tuple-element.64.mine_ref, bf16[192,1536]{1,0:T(8,128)(2,1)S(1)} %collective-permute-done.9.other_ref, f32[8,384]{1,0:T(8,128)S(1)} %get-tuple-element.69.s0, f32[8,384]{1,0:T(8,128)S(1)} %collective-permute-done.13.s1), custom_call_target="tpu_custom_call" | custom-call | bytes 2449408 | tf_op jit(solution)/shard_map/join/pallas_call | solution.py:54
  72.2 10.2 %all-to-all-start.2 = ((bf16[32,8,1280]{2,1,0:T(8,128)(2,1)}), bf16[32,8,1280]{2,1,0:T(8,128)(2,1)S(1)}, u32[]{:S(2)}, u32[]{:S(2)}) async-start(bf16[32,8,1280]{2,1,0:T(8,128)(2,1)} %join.1), calls=%async_computation.2 | async-start | bytes 1310720 | tf_op jit(solution)/shard_map/all_to_all | solution.py:329
  82.4 0.1 collective-permute-start.14
  82.5 0.1 collective-permute-start.15
  82.6 1.8 %collective-permute-start.16 = (bf16[3,64,384]{2,1,0:T(8,128)(2,1)S(1)}, bf16[3,64,384]{2,1,0:T(8,128)(2,1)S(1)}, u32[]{:S(2)}, u32[]{:S(2)}) collective-permute-start(bf16[3,64,384]{2,1,0:T(8,128)(2,1)S(1)} %get-tuple-element.83), channel_id=1, source_target_pairs={{0,3},{1,2},{2,1},{3,0},{4,7},{5,6},{6,5},{7,4},{8,11},{9,10},{10,... | collective-permute-start | bytes 442376 | tf_op jit(solution)/shard_map/ppermute | solution.py:230
  84.4 0.9 collective-permute-start.17
  85.2 2.3 %collective-permute-start.18 = (bf16[3,64,384]{2,1,0:T(8,128)(2,1)S(1)}, bf16[3,64,384]{2,1,0:T(8,128)(2,1)S(1)}, u32[]{:S(2)}, u32[]{:S(2)}) collective-permute-start(bf16[3,64,384]{2,1,0:T(8,128)(2,1)S(1)} %get-tuple-element.85), channel_id=1, source_target_pairs={{0,5},{1,4},{2,7},{3,6},{4,1},{5,0},{6,3},{7,2},{8,13},{9,12},{10,... | collective-permute-start | bytes 442376 | tf_op jit(solution)/shard_map/ppermute | solution.py:230
  87.6 0.0 collective-permute-done.14.refs_1_
  87.6 1.1 collective-permute-start.20
  88.7 0.5 collective-permute-done.15.refs_2_
  89.2 1.4 %collective-permute-start.21 = (bf16[3,64,384]{2,1,0:T(8,128)(2,1)S(1)}, bf16[3,64,384]{2,1,0:T(8,128)(2,1)S(1)}, u32[]{:S(2)}, u32[]{:S(2)}) collective-permute-start(bf16[3,64,384]{2,1,0:T(8,128)(2,1)S(1)} %get-tuple-element.95), channel_id=1, source_target_pairs={{0,7},{1,6},{2,5},{3,4},{4,3},{5,2},{6,1},{7,0},{8,15},{9,14},{10,... | collective-permute-start | bytes 442376 | tf_op jit(solution)/shard_map/ppermute | solution.py:230
  90.6 0.9 collective-permute-done.16.refs_3_
  91.4 4.8 %collective-permute-done.17.refs_4_ = bf16[3,64,384]{2,1,0:T(8,128)(2,1)S(1)} collective-permute-done((bf16[3,64,384]{2,1,0:T(8,128)(2,1)S(1)}, bf16[3,64,384]{2,1,0:T(8,128)(2,1)S(1)}, u32[]{:S(2)}, u32[]{:S(2)}) %collective-permute-start.17) | collective-permute-done | bytes 147488 | tf_op jit(solution)/shard_map/ppermute | solution.py:230
  96.2 2.2 %collective-permute-done.18.refs_5_ = bf16[3,64,384]{2,1,0:T(8,128)(2,1)S(1)} collective-permute-done((bf16[3,64,384]{2,1,0:T(8,128)(2,1)S(1)}, bf16[3,64,384]{2,1,0:T(8,128)(2,1)S(1)}, u32[]{:S(2)}, u32[]{:S(2)}) %collective-permute-start.18) | collective-permute-done | bytes 147488 | tf_op jit(solution)/shard_map/ppermute | solution.py:230
  98.5 3.9 %all-to-all-done.2.in_ref = bf16[32,8,1280]{2,1,0:T(8,128)(2,1)S(1)} async-done(((bf16[32,8,1280]{2,1,0:T(8,128)(2,1)}), bf16[32,8,1280]{2,1,0:T(8,128)(2,1)S(1)}, u32[]{:S(2)}, u32[]{:S(2)}) %all-to-all-start.2) | async-done | bytes 655392 | tf_op jit(solution)/shard_map/all_to_all | solution.py:329
  102.3 0.5 total.1
  102.8 1.9 %collective-permute-start.19 = (f32[8,1536]{1,0:T(8,128)S(1)}, f32[8,1536]{1,0:T(8,128)S(1)}, u32[]{:S(2)}, u32[]{:S(2)}) collective-permute-start(f32[8,1536]{1,0:T(8,128)S(1)} %get-tuple-element.87), channel_id=1, source_target_pairs={{0,0},{32,2},{64,4},{96,6},{128,32},{160,34},{192,36},{224,38},{2,... | collective-permute-start | bytes 147464 | tf_op jit(solution)/shard_map/ppermute | solution.py:333
  104.8 0.9 collective-permute-start.22
  105.7 3.4 %collective-permute-start.23 = (f32[16,128]{1,0:T(8,128)S(1)}, f32[16,128]{1,0:T(8,128)S(1)}, u32[]{:S(2)}, u32[]{:S(2)}) collective-permute-start(f32[16,128]{1,0:T(8,128)S(1)} %get-tuple-element.98.o0), channel_id=1, source_target_pairs={{0,4},{2,6},{4,0},{6,2},{1,5},{3,7},{5,1},{7,3},{8,12},{10,14},{12... | collective-permute-start | bytes 24584 | tf_op jit(solution)/shard_map/ppermute | solution.py:230
  109.1 0.0 collective-permute-done.20.refs_6_
  109.1 0.5 collective-permute-start.24
  109.6 0.0 collective-permute-done.21.refs_7_
  109.6 1.8 %unpack.1 = bf16[3,128,1536]{2,1,0:T(8,128)(2,1)} custom-call(s32[5]{0:T(128)S(1)} %stack.25.place, bf16[3,64,384]{2,1,0:T(8,128)(2,1)S(1)} %get-tuple-element.88.refs_0_, bf16[3,64,384]{2,1,0:T(8,128)(2,1)S(1)} %collective-permute-done.14.refs_1_, bf16[3,64,384]{2,1,0:T(8,128)(2,1)S(1)} %collective-permute-done.15.refs_2_, ...), custom_call_target="tpu_custom_call" | custom-call | bytes 2359316 | tf_op jit(solution)/shard_map/unpack/pallas_call | solution.py:54
  111.3 0.7 collective-permute-done.19.home_ref
  112.1 1.9 %collective-permute-done.24.o3 = f32[16,128]{1,0:T(8,128)S(1)} collective-permute-done((f32[16,128]{1,0:T(8,128)S(1)}, f32[16,128]{1,0:T(8,128)S(1)}, u32[]{:S(2)}, u32[]{:S(2)}) %collective-permute-start.24) | collective-permute-done | bytes 8224 | tf_op jit(solution)/shard_map/ppermute | solution.py:230
  113.9 1.2 %last.1 = (f32[6,1536]{1,0:T(8,128)}, f32[12,15]{1,0:T(8,128)}) custom-call(s32[5]{0:T(128)S(1)} %stack.25.place, f32[8,1536]{1,0:T(8,128)S(1)} %collective-permute-done.19.home_ref, f32[16,128]{1,0:T(8,128)S(1)} %get-tuple-element.98.o0, f32[16,128]{1,0:T(8,128)S(1)} %collective-permute-done.22.o1, f32[16,128]{1,0:T(8,128)S(1)} %collective-permute-done.23.o2, ...), custom_call_target="tpu_custom_call" | custom-call | bytes 119524 | tf_op jit(solution)/shard_map/last/pallas_call | solution.py:54
  (21 shorter events, 0.1 us)
Async XLA Ops:
  0.6 4.5 %copy-start = (bf16[3,1,1,128,1536]{4,3,2,1,0:T(8,128)(2,1)S(1)}, bf16[3,1,1,128,1536]{4,3,2,1,0:T(8,128)(2,1)}, u32[]{:S(2)}) copy-start(bf16[3,1,1,128,1536]{4,3,2,1,0:T(8,128)(2,1)} %param.7) | copy-start | bytes 3538948
  0.6 19.4 %all-to-all-start.1 = ((bf16[8,32,1536]{2,1,0:T(8,128)(2,1)}), bf16[8,32,1536]{2,1,0:T(8,128)(2,1)S(1)}, u32[]{:S(2)}, u32[]{:S(2)}) async-start(bf16[8,32,1536]{2,1,0:T(8,128)(2,1)} %bitcast.11), calls=%async_computation.1 | async-start | bytes 1572864 | tf_op jit(solution)/shard_map/all_to_all | solution.py:244
  5.1 1.1 copy-start.5
  6.2 23.1 %copy-start.2 = (s32[1,8]{1,0:T(1,128)S(1)}, s32[1,8]{1,0:T(1,128)}, u32[]{:S(2)}) copy-start(s32[1,8]{1,0:T(1,128)} %sizes.1) | copy-start | bytes 100
  6.2 12.2 %collective-permute-start = (bf16[8,1536]{1,0:T(8,128)(2,1)S(1)}, bf16[8,1536]{1,0:T(8,128)(2,1)S(1)}, u32[]{:S(2)}, u32[]{:S(2)}) collective-permute-start(bf16[8,1536]{1,0:T(8,128)(2,1)S(1)} %pad.4), channel_id=1, source_target_pairs={{0,0},{2,32},{4,64},{6,96},{32,128},{34,160},{36,192},{38,224},{64... | collective-permute-start | bytes 73736 | tf_op jit(solution)/shard_map/ppermute | solution.py:247
  14.0 6.0 %collective-permute-start.1 = (bf16[8,1536]{1,0:T(8,128)(2,1)S(1)}, bf16[8,1536]{1,0:T(8,128)(2,1)S(1)}, u32[]{:S(2)}, u32[]{:S(2)}) collective-permute-start(bf16[8,1536]{1,0:T(8,128)(2,1)S(1)} %pad.4), channel_id=1, source_target_pairs={{0,32},{2,0},{4,96},{6,64},{32,160},{34,128},{36,224},{38,192},{64... | collective-permute-start | bytes 73736 | tf_op jit(solution)/shard_map/ppermute | solution.py:247
  20.0 35.5 %all-to-all-start = ((bf16[8,3,64,384]{3,2,1,0:T(8,128)(2,1)}), bf16[8,3,64,384]{3,2,1,0:T(8,128)(2,1)S(1)}, u32[]{:S(2)}, u32[]{:S(2)}) async-start(bf16[8,3,64,384]{3,2,1,0:T(8,128)(2,1)} %pack.1), calls=%async_computation | async-start | bytes 2359296 | tf_op jit(solution)/shard_map/all_to_all | solution.py:249
  27.6 28.0 %copy-start.3 = (f32[12,15]{1,0:T(8,128)S(1)}, f32[12,15]{1,0:T(8,128)}, u32[]{:S(2)}) copy-start(f32[12,15]{1,0:T(8,128)} %bias.1) | copy-start | bytes 2164
  27.6 5.1 %collective-permute-start.2 = (bf16[16,1536]{1,0:T(8,128)(2,1)S(1)}, bf16[16,1536]{1,0:T(8,128)(2,1)S(1)}, u32[]{:S(2)}, u32[]{:S(2)}) collective-permute-start(bf16[16,1536]{1,0:T(8,128)(2,1)S(1)} %pad_maximum_fusion.2), channel_id=1, source_target_pairs={{0,64},{32,96},{64,0},{96,32},{128,192},{160,224},{192,128},{224,1... | collective-permute-start | bytes 147464 | tf_op jit(solution)/shard_map/ppermute | solution.py:230
  30.1 4.9 %collective-permute-start.3 = (bf16[64,1536]{1,0:T(8,128)(2,1)S(1)}, bf16[64,1536]{1,0:T(8,128)(2,1)S(1)}, u32[]{:S(2)}, u32[]{:S(2)}) collective-permute-start(bf16[64,1536]{1,0:T(8,128)(2,1)S(1)} %get-tuple-element.60), channel_id=1, source_target_pairs={{0,1},{1,0},{2,3},{3,2},{4,5},{5,4},{6,7},{7,6},{8,9},{9,8},{10,11... | collective-permute-start | bytes 589832 | tf_op jit(solution)/shard_map/ppermute | solution.py:230
  32.7 8.7 %collective-permute-start.4 = (bf16[32,1536]{1,0:T(8,128)(2,1)S(1)}, bf16[32,1536]{1,0:T(8,128)(2,1)S(1)}, u32[]{:S(2)}, u32[]{:S(2)}) collective-permute-start(bf16[32,1536]{1,0:T(8,128)(2,1)S(1)} %pad_maximum_fusion.1), channel_id=1, source_target_pairs={{0,128},{32,160},{64,192},{96,224},{128,0},{160,32},{192,64},{224,... | collective-permute-start | bytes 294920 | tf_op jit(solution)/shard_map/ppermute | solution.py:230
  35.1 17.3 %collective-permute-start.6 = (bf16[128,1536]{1,0:T(8,128)(2,1)S(1)}, bf16[128,1536]{1,0:T(8,128)(2,1)S(1)}, u32[]{:S(2)}, u32[]{:S(2)}) collective-permute-start(bf16[128,1536]{1,0:T(8,128)(2,1)S(1)} %stack.26.u0), channel_id=1, source_target_pairs={{0,2},{2,0},{4,6},{6,4},{1,3},{3,1},{5,7},{7,5},{8,10},{10,8},{12,... | collective-permute-start | bytes 1179656 | tf_op jit(solution)/shard_map/ppermute | solution.py:230
  41.4 9.3 %collective-permute-start.5 = (bf16[64,1536]{1,0:T(8,128)(2,1)S(1)}, bf16[64,1536]{1,0:T(8,128)(2,1)S(1)}, u32[]{:S(2)}, u32[]{:S(2)}) collective-permute-start(bf16[64,1536]{1,0:T(8,128)(2,1)S(1)} %pad_maximum_fusion.refs_0_), channel_id=1, source_target_pairs={{0,8},{8,0},{16,24},{24,16},{1,9},{9,1},{17,25},{25,17},{2,10},{10... | collective-permute-start | bytes 589832 | tf_op jit(solution)/shard_map/ppermute | solution.py:230
  43.1 18.8 %collective-permute-start.7 = (bf16[128,1536]{1,0:T(8,128)(2,1)S(1)}, bf16[128,1536]{1,0:T(8,128)(2,1)S(1)}, u32[]{:S(2)}, u32[]{:S(2)}) collective-permute-start(bf16[128,1536]{1,0:T(8,128)(2,1)S(1)} %stack.26.u0), channel_id=1, source_target_pairs={{0,4},{2,6},{4,0},{6,2},{1,5},{3,7},{5,1},{7,3},{8,12},{10,14},{12... | collective-permute-start | bytes 1179656 | tf_op jit(solution)/shard_map/ppermute | solution.py:230
  46.7 18.1 %collective-permute-start.8 = (bf16[128,1536]{1,0:T(8,128)(2,1)S(1)}, bf16[128,1536]{1,0:T(8,128)(2,1)S(1)}, u32[]{:S(2)}, u32[]{:S(2)}) collective-permute-start(bf16[128,1536]{1,0:T(8,128)(2,1)S(1)} %stack.26.u0), channel_id=1, source_target_pairs={{0,6},{2,4},{4,2},{6,0},{1,7},{3,5},{5,3},{7,1},{8,14},{10,12},{12... | collective-permute-start | bytes 1179656 | tf_op jit(solution)/shard_map/ppermute | solution.py:230
  47.8 13.5 %collective-permute-start.10 = (bf16[64,1536]{1,0:T(8,128)(2,1)S(1)}, bf16[64,1536]{1,0:T(8,128)(2,1)S(1)}, u32[]{:S(2)}, u32[]{:S(2)}) collective-permute-start(bf16[64,1536]{1,0:T(8,128)(2,1)S(1)} %pad_maximum_fusion.refs_0_), channel_id=1, source_target_pairs={{0,16},{8,24},{16,0},{24,8},{1,17},{9,25},{17,1},{25,9},{2,18},{10... | collective-permute-start | bytes 589832 | tf_op jit(solution)/shard_map/ppermute | solution.py:230
  52.3 9.0 %collective-permute-start.11 = (bf16[64,1536]{1,0:T(8,128)(2,1)S(1)}, bf16[64,1536]{1,0:T(8,128)(2,1)S(1)}, u32[]{:S(2)}, u32[]{:S(2)}) collective-permute-start(bf16[64,1536]{1,0:T(8,128)(2,1)S(1)} %collective-permute-done.5.refs_1_), channel_id=1, source_target_pairs={{0,16},{8,24},{16,0},{24,8},{1,17},{9,25},{17,1},{25,9},{2,18},{10... | collective-permute-start | bytes 589832 | tf_op jit(solution)/shard_map/ppermute | solution.py:230
  55.5 0.7 copy-start.4
  61.4 5.0 %collective-permute-start.12 = (bf16[256,1536]{1,0:T(8,128)(2,1)S(1)}, bf16[256,1536]{1,0:T(8,128)(2,1)S(1)}, u32[]{:S(2)}, u32[]{:S(2)}) collective-permute-start(bf16[256,1536]{1,0:T(8,128)(2,1)S(1)} %stack.27.w0_ref), channel_id=1, source_target_pairs={{0,1},{1,0},{2,3},{3,2},{4,5},{5,4},{6,7},{7,6},{8,9},{9,8},{10,11... | collective-permute-start | bytes 2359304 | tf_op jit(solution)/shard_map/ppermute | solution.py:230
  64.8 1.6 %copy-start.1 = (s32[8,384]{1,0:T(8,128)S(1)}, s32[8,384]{1,0:T(8,128)}, u32[]{:S(2)}) copy-start(s32[8,384]{1,0:T(8,128)} %constant.26.clone.rows_ref) | copy-start | bytes 36868
  66.3 4.3 %collective-permute-start.9 = (bf16[192,1536]{1,0:T(8,128)(2,1)S(1)}, bf16[192,1536]{1,0:T(8,128)(2,1)S(1)}, u32[]{:S(2)}, u32[]{:S(2)}) collective-permute-start(bf16[192,1536]{1,0:T(8,128)(2,1)S(1)} %get-tuple-element.65), channel_id=1, source_target_pairs={{0,1},{1,0},{2,3},{3,2},{4,5},{5,4},{6,7},{7,6},{8,9},{9,8},{10,11... | collective-permute-start | bytes 1769480 | tf_op jit(solution)/shard_map/ppermute | solution.py:230
  68.7 1.9 %collective-permute-start.13 = (f32[8,384]{1,0:T(8,128)S(1)}, f32[8,384]{1,0:T(8,128)S(1)}, u32[]{:S(2)}, u32[]{:S(2)}) collective-permute-start(f32[8,384]{1,0:T(8,128)S(1)} %get-tuple-element.69.s0), channel_id=1, source_target_pairs={{0,1},{1,0},{2,3},{3,2},{4,5},{5,4},{6,7},{7,6},{8,9},{9,8},{10,11... | collective-permute-start | bytes 36872 | tf_op jit(solution)/shard_map/ppermute | solution.py:230
  72.2 30.2 %all-to-all-start.2 = ((bf16[32,8,1280]{2,1,0:T(8,128)(2,1)}), bf16[32,8,1280]{2,1,0:T(8,128)(2,1)S(1)}, u32[]{:S(2)}, u32[]{:S(2)}) async-start(bf16[32,8,1280]{2,1,0:T(8,128)(2,1)} %join.1), calls=%async_computation.2 | async-start | bytes 1310720 | tf_op jit(solution)/shard_map/all_to_all | solution.py:329
  82.4 5.2 %collective-permute-start.14 = (bf16[3,64,384]{2,1,0:T(8,128)(2,1)S(1)}, bf16[3,64,384]{2,1,0:T(8,128)(2,1)S(1)}, u32[]{:S(2)}, u32[]{:S(2)}) collective-permute-start(bf16[3,64,384]{2,1,0:T(8,128)(2,1)S(1)} %get-tuple-element.81), channel_id=1, source_target_pairs={{0,1},{1,0},{2,3},{3,2},{4,5},{5,4},{6,7},{7,6},{8,9},{9,8},{10,11... | collective-permute-start | bytes 442376 | tf_op jit(solution)/shard_map/ppermute | solution.py:230
  82.5 6.7 %collective-permute-start.15 = (bf16[3,64,384]{2,1,0:T(8,128)(2,1)S(1)}, bf16[3,64,384]{2,1,0:T(8,128)(2,1)S(1)}, u32[]{:S(2)}, u32[]{:S(2)}) collective-permute-start(bf16[3,64,384]{2,1,0:T(8,128)(2,1)S(1)} %get-tuple-element.82), channel_id=1, source_target_pairs={{0,2},{1,3},{2,0},{3,1},{4,6},{5,7},{6,4},{7,5},{8,10},{9,11},{10,... | collective-permute-start | bytes 442376 | tf_op jit(solution)/shard_map/ppermute | solution.py:230
  82.6 8.9 %collective-permute-start.16 = (bf16[3,64,384]{2,1,0:T(8,128)(2,1)S(1)}, bf16[3,64,384]{2,1,0:T(8,128)(2,1)S(1)}, u32[]{:S(2)}, u32[]{:S(2)}) collective-permute-start(bf16[3,64,384]{2,1,0:T(8,128)(2,1)S(1)} %get-tuple-element.83), channel_id=1, source_target_pairs={{0,3},{1,2},{2,1},{3,0},{4,7},{5,6},{6,5},{7,4},{8,11},{9,10},{10,... | collective-permute-start | bytes 442376 | tf_op jit(solution)/shard_map/ppermute | solution.py:230
  84.4 11.9 %collective-permute-start.17 = (bf16[3,64,384]{2,1,0:T(8,128)(2,1)S(1)}, bf16[3,64,384]{2,1,0:T(8,128)(2,1)S(1)}, u32[]{:S(2)}, u32[]{:S(2)}) collective-permute-start(bf16[3,64,384]{2,1,0:T(8,128)(2,1)S(1)} %get-tuple-element.84), channel_id=1, source_target_pairs={{0,4},{1,5},{2,6},{3,7},{4,0},{5,1},{6,2},{7,3},{8,12},{9,13},{10,... | collective-permute-start | bytes 442376 | tf_op jit(solution)/shard_map/ppermute | solution.py:230
  85.2 13.2 %collective-permute-start.18 = (bf16[3,64,384]{2,1,0:T(8,128)(2,1)S(1)}, bf16[3,64,384]{2,1,0:T(8,128)(2,1)S(1)}, u32[]{:S(2)}, u32[]{:S(2)}) collective-permute-start(bf16[3,64,384]{2,1,0:T(8,128)(2,1)S(1)} %get-tuple-element.85), channel_id=1, source_target_pairs={{0,5},{1,4},{2,7},{3,6},{4,1},{5,0},{6,3},{7,2},{8,13},{9,12},{10,... | collective-permute-start | bytes 442376 | tf_op jit(solution)/shard_map/ppermute | solution.py:230
  87.6 21.5 %collective-permute-start.20 = (bf16[3,64,384]{2,1,0:T(8,128)(2,1)S(1)}, bf16[3,64,384]{2,1,0:T(8,128)(2,1)S(1)}, u32[]{:S(2)}, u32[]{:S(2)}) collective-permute-start(bf16[3,64,384]{2,1,0:T(8,128)(2,1)S(1)} %get-tuple-element.94), channel_id=1, source_target_pairs={{0,6},{1,7},{2,4},{3,5},{4,2},{5,3},{6,0},{7,1},{8,14},{9,15},{10,... | collective-permute-start | bytes 442376 | tf_op jit(solution)/shard_map/ppermute | solution.py:230
  89.2 20.3 %collective-permute-start.21 = (bf16[3,64,384]{2,1,0:T(8,128)(2,1)S(1)}, bf16[3,64,384]{2,1,0:T(8,128)(2,1)S(1)}, u32[]{:S(2)}, u32[]{:S(2)}) collective-permute-start(bf16[3,64,384]{2,1,0:T(8,128)(2,1)S(1)} %get-tuple-element.95), channel_id=1, source_target_pairs={{0,7},{1,6},{2,5},{3,4},{4,3},{5,2},{6,1},{7,0},{8,15},{9,14},{10,... | collective-permute-start | bytes 442376 | tf_op jit(solution)/shard_map/ppermute | solution.py:230
  102.8 9.2 %collective-permute-start.19 = (f32[8,1536]{1,0:T(8,128)S(1)}, f32[8,1536]{1,0:T(8,128)S(1)}, u32[]{:S(2)}, u32[]{:S(2)}) collective-permute-start(f32[8,1536]{1,0:T(8,128)S(1)} %get-tuple-element.87), channel_id=1, source_target_pairs={{0,0},{32,2},{64,4},{96,6},{128,32},{160,34},{192,36},{224,38},{2,... | collective-permute-start | bytes 147464 | tf_op jit(solution)/shard_map/ppermute | solution.py:333
  104.8 7.3 %collective-permute-start.22 = (f32[16,128]{1,0:T(8,128)S(1)}, f32[16,128]{1,0:T(8,128)S(1)}, u32[]{:S(2)}, u32[]{:S(2)}) collective-permute-start(f32[16,128]{1,0:T(8,128)S(1)} %get-tuple-element.98.o0), channel_id=1, source_target_pairs={{0,2},{2,0},{4,6},{6,4},{1,3},{3,1},{5,7},{7,5},{8,10},{10,8},{12,... | collective-permute-start | bytes 24584 | tf_op jit(solution)/shard_map/ppermute | solution.py:230
  105.7 6.4 %collective-permute-start.23 = (f32[16,128]{1,0:T(8,128)S(1)}, f32[16,128]{1,0:T(8,128)S(1)}, u32[]{:S(2)}, u32[]{:S(2)}) collective-permute-start(f32[16,128]{1,0:T(8,128)S(1)} %get-tuple-element.98.o0), channel_id=1, source_target_pairs={{0,4},{2,6},{4,0},{6,2},{1,5},{3,7},{5,1},{7,3},{8,12},{10,14},{12... | collective-permute-start | bytes 24584 | tf_op jit(solution)/shard_map/ppermute | solution.py:230
  109.1 4.9 %collective-permute-start.24 = (f32[16,128]{1,0:T(8,128)S(1)}, f32[16,128]{1,0:T(8,128)S(1)}, u32[]{:S(2)}, u32[]{:S(2)}) collective-permute-start(f32[16,128]{1,0:T(8,128)S(1)} %get-tuple-element.98.o0), channel_id=1, source_target_pairs={{0,6},{2,4},{4,2},{6,0},{1,7},{3,5},{5,3},{7,1},{8,14},{10,12},{12... | collective-permute-start | bytes 24584 | tf_op jit(solution)/shard_map/ppermute | solution.py:230

commit v13 on v12

--- a/solution.py
+++ b/solution.py
@@ -245,7 +245,6 @@
     (packed,) = call(pack_kernel, "pack", [((F, 3, HALF, COLS), bf)], qkv_time[:, 0, 0])
     rows8, packed = lax.optimization_barrier((jnp.pad(w_out, ((0, 2), (0, 0))), packed))
     held = [lax.ppermute(rows8, ("z", "x"), p) for p in (there, near)]
-    packed, held = lax.optimization_barrier((packed, held))
     recv = lax.all_to_all(packed, SEQ, 0, 0, tiled=True)
     held = jnp.concatenate(held)
     held = jnp.concatenate([held, hop(held, "z", 2, Z)])

time: 116 us -> 113 us (0.974)
  waiting for transfers between devices: 28 us -> 25 us
    ppermute x22, starting transfers between devices: 32.1 us -> 36.9 us  [hop(): return lax.ppermute(x, axis, [(i, i ^ k) for i in range(n)])]
    all_to_all x1, starting transfers between devices: 7.56 us -> 3.57 us  [per_device(): recv = lax.all_to_all(packed, SEQ, 0, 0, tiled=True)]
    ppermute x22, waiting for transfers between devices: 21.9 us -> 18.4 us  [hop(): return lax.ppermute(x, axis, [(i, i ^ k) for i in range(n)])]
    ppermute x2, starting transfers between devices: 12.2 us -> 9.96 us  [per_device(): held = [lax.ppermute(rows8, ('z', 'x'), p) for p in (there, near)]]
    all_to_all x1, waiting for transfers between devices: 0.01 us -> 2.03 us  [per_device(): cot = lax.all_to_all(cot_out[0, 0], SEQ, 0, 0, tiled=True)]
    ppermute x2, waiting for transfers between devices: 1.52 us -> 0.01 us  [per_device(): held = [lax.ppermute(rows8, ('z', 'x'), p) for p in (there, near)]]
  transfers between devices with their start and end apart: 28 -> 28, of which waited for: 13 -> 13; matrix products, arithmetic and copies ran while one was open for 0% -> 0% of each run, Pallas kernels for 12% -> 13%
where the time goes in v13:
time: 113 us; the launch traced here: 112 us
  starting transfers between devices  68.2 us (60%)
  waiting for transfers between devices  25 us (22%)
  Pallas kernels  16.9 us (15%)
    ppermute x22, starting transfers between devices, hop(): return lax.ppermute(x, axis, [(i, i ^ k) for i in range(n)])  36.9 us
    ppermute x22, waiting for transfers between devices, hop(): return lax.ppermute(x, axis, [(i, i ^ k) for i in range(n)])  18.4 us
    pallas_call x12, Pallas kernels, call(): pl.pallas_call(body, out_shape=tuple((jax.ShapeDtypeStruct(s, d) for s, d...  16.9 us
    all_to_all x1, starting transfers between devices, per_device(): msgs = lax.all_to_all(msgs, ('z', 'y'), 0, 0, tiled=True)  11.4 us
    ppermute x2, starting transfers between devices, per_device(): held = [lax.ppermute(rows8, ('z', 'x'), p) for p in (there, near)]  9.96 us
    all_to_all x1, starting transfers between devices, per_device(): cot = lax.all_to_all(cot_out[0, 0], SEQ, 0, 0, tiled=True)  4.44 us
    all_to_all x1, waiting for transfers between devices, per_device(): msgs = lax.all_to_all(msgs, ('z', 'y'), 0, 0, tiled=True)  3.86 us
    all_to_all x1, starting transfers between devices, per_device(): recv = lax.all_to_all(packed, SEQ, 0, 0, tiled=True)  3.57 us
  transfers between devices with their start and end apart: 28, of which 13 were waited for; matrix products, arithmetic and copies ran while one was open for 0% of the time, Pallas kernels for 13%

profile of v13, /device:TPU:32, one launch (start us, length us, event | category | flops | bytes accessed | tf_op | source)
XLA Modules:
  0.0 111.9 jit_solution(3188125539322596366)
XLA Ops:
  0.6 4.4 %all-to-all-start.1 = ((bf16[8,32,1536]{2,1,0:T(8,128)(2,1)}), bf16[8,32,1536]{2,1,0:T(8,128)(2,1)S(1)}, u32[]{:S(2)}, u32[]{:S(2)}) async-start(bf16[8,32,1536]{2,1,0:T(8,128)(2,1)} %bitcast.11), calls=%async_computation.1 | async-start | bytes 1572864 | tf_op jit(solution)/shard_map/all_to_all | solution.py:244
  5.1 0.0 copy-start.5
  5.1 1.1 pack.1
  6.2 0.0 copy-start.2
  6.2 6.4 %collective-permute-start.1 = (bf16[8,1536]{1,0:T(8,128)(2,1)S(1)}, bf16[8,1536]{1,0:T(8,128)(2,1)S(1)}, u32[]{:S(2)}, u32[]{:S(2)}) collective-permute-start(bf16[8,1536]{1,0:T(8,128)(2,1)S(1)} %pad.4), channel_id=1, source_target_pairs={{0,32},{2,0},{4,96},{6,64},{32,160},{34,128},{36,224},{38,192},{64... | collective-permute-start | bytes 73736 | tf_op jit(solution)/shard_map/ppermute | solution.py:247
  12.6 3.6 %collective-permute-start = (bf16[8,1536]{1,0:T(8,128)(2,1)S(1)}, bf16[8,1536]{1,0:T(8,128)(2,1)S(1)}, u32[]{:S(2)}, u32[]{:S(2)}) collective-permute-start(bf16[8,1536]{1,0:T(8,128)(2,1)S(1)} %pad.4), channel_id=1, source_target_pairs={{0,0},{2,32},{4,64},{6,96},{32,128},{34,160},{36,192},{38,224},{64... | collective-permute-start | bytes 73736 | tf_op jit(solution)/shard_map/ppermute | solution.py:247
  16.2 2.0 %all-to-all-done.1.cot_ref = bf16[8,32,1536]{2,1,0:T(8,128)(2,1)S(1)} async-done(((bf16[8,32,1536]{2,1,0:T(8,128)(2,1)}), bf16[8,32,1536]{2,1,0:T(8,128)(2,1)S(1)}, u32[]{:S(2)}, u32[]{:S(2)}) %all-to-all-start.1) | async-done | bytes 786464 | tf_op jit(solution)/shard_map/all_to_all | solution.py:244
  18.2 3.6 %all-to-all-start = ((bf16[8,3,64,384]{3,2,1,0:T(8,128)(2,1)}), bf16[8,3,64,384]{3,2,1,0:T(8,128)(2,1)S(1)}, u32[]{:S(2)}, u32[]{:S(2)}) async-start(bf16[8,3,64,384]{3,2,1,0:T(8,128)(2,1)} %pack.1), calls=%async_computation | async-start | bytes 2359296 | tf_op jit(solution)/shard_map/all_to_all | solution.py:248
  21.8 0.0 copy-start.3
  21.8 0.0 collective-permute-done.1
  21.8 0.0 collective-permute-done
  21.9 4.4 %collective-permute-start.2 = (bf16[16,1536]{1,0:T(8,128)(2,1)S(1)}, bf16[16,1536]{1,0:T(8,128)(2,1)S(1)}, u32[]{:S(2)}, u32[]{:S(2)}) collective-permute-start(bf16[16,1536]{1,0:T(8,128)(2,1)S(1)} %pad_maximum_fusion.2), channel_id=1, source_target_pairs={{0,64},{32,96},{64,0},{96,32},{128,192},{160,224},{192,128},{224,1... | collective-permute-start | bytes 147464 | tf_op jit(solution)/shard_map/ppermute | solution.py:230
  26.3 0.1 stack.25.place
  26.4 0.8 compact.1
  27.2 0.2 collective-permute-start.3
  27.4 1.2 %collective-permute-done.2 = bf16[16,1536]{1,0:T(8,128)(2,1)S(1)} collective-permute-done((bf16[16,1536]{1,0:T(8,128)(2,1)S(1)}, bf16[16,1536]{1,0:T(8,128)(2,1)S(1)}, u32[]{:S(2)}, u32[]{:S(2)}) %collective-permute-start.2) | collective-permute-done | bytes 49184 | tf_op jit(solution)/shard_map/ppermute | solution.py:230
  28.6 4.8 %collective-permute-start.4 = (bf16[32,1536]{1,0:T(8,128)(2,1)S(1)}, bf16[32,1536]{1,0:T(8,128)(2,1)S(1)}, u32[]{:S(2)}, u32[]{:S(2)}) collective-permute-start(bf16[32,1536]{1,0:T(8,128)(2,1)S(1)} %pad_maximum_fusion.1), channel_id=1, source_target_pairs={{0,128},{32,160},{64,192},{96,224},{128,0},{160,32},{192,64},{224,... | collective-permute-start | bytes 294920 | tf_op jit(solution)/shard_map/ppermute | solution.py:230
  33.4 0.0 collective-permute-done.3.refs_1_
  33.4 2.0 %collective-permute-start.6 = (bf16[128,1536]{1,0:T(8,128)(2,1)S(1)}, bf16[128,1536]{1,0:T(8,128)(2,1)S(1)}, u32[]{:S(2)}, u32[]{:S(2)}) collective-permute-start(bf16[128,1536]{1,0:T(8,128)(2,1)S(1)} %stack.26.u0), channel_id=1, source_target_pairs={{0,2},{2,0},{4,6},{6,4},{1,3},{3,1},{5,7},{7,5},{8,10},{10,8},{12,... | collective-permute-start | bytes 1179656 | tf_op jit(solution)/shard_map/ppermute | solution.py:230
  35.4 1.9 %collective-permute-done.4 = bf16[32,1536]{1,0:T(8,128)(2,1)S(1)} collective-permute-done((bf16[32,1536]{1,0:T(8,128)(2,1)S(1)}, bf16[32,1536]{1,0:T(8,128)(2,1)S(1)}, u32[]{:S(2)}, u32[]{:S(2)}) %collective-permute-start.4) | collective-permute-done | bytes 98336 | tf_op jit(solution)/shard_map/ppermute | solution.py:230
  37.2 1.7 %collective-permute-start.5 = (bf16[64,1536]{1,0:T(8,128)(2,1)S(1)}, bf16[64,1536]{1,0:T(8,128)(2,1)S(1)}, u32[]{:S(2)}, u32[]{:S(2)}) collective-permute-start(bf16[64,1536]{1,0:T(8,128)(2,1)S(1)} %pad_maximum_fusion.refs_0_), channel_id=1, source_target_pairs={{0,8},{8,0},{16,24},{24,16},{1,9},{9,1},{17,25},{25,17},{2,10},{10... | collective-permute-start | bytes 589832 | tf_op jit(solution)/shard_map/ppermute | solution.py:230
  38.9 3.3 %collective-permute-start.7 = (bf16[128,1536]{1,0:T(8,128)(2,1)S(1)}, bf16[128,1536]{1,0:T(8,128)(2,1)S(1)}, u32[]{:S(2)}, u32[]{:S(2)}) collective-permute-start(bf16[128,1536]{1,0:T(8,128)(2,1)S(1)} %stack.26.u0), channel_id=1, source_target_pairs={{0,4},{2,6},{4,0},{6,2},{1,5},{3,7},{5,1},{7,3},{8,12},{10,14},{12... | collective-permute-start | bytes 1179656 | tf_op jit(solution)/shard_map/ppermute | solution.py:230
  42.2 1.2 %collective-permute-start.8 = (bf16[128,1536]{1,0:T(8,128)(2,1)S(1)}, bf16[128,1536]{1,0:T(8,128)(2,1)S(1)}, u32[]{:S(2)}, u32[]{:S(2)}) collective-permute-start(bf16[128,1536]{1,0:T(8,128)(2,1)S(1)} %stack.26.u0), channel_id=1, source_target_pairs={{0,6},{2,4},{4,2},{6,0},{1,7},{3,5},{5,3},{7,1},{8,14},{10,12},{12... | collective-permute-start | bytes 1179656 | tf_op jit(solution)/shard_map/ppermute | solution.py:230
  43.3 2.9 %collective-permute-start.10 = (bf16[64,1536]{1,0:T(8,128)(2,1)S(1)}, bf16[64,1536]{1,0:T(8,128)(2,1)S(1)}, u32[]{:S(2)}, u32[]{:S(2)}) collective-permute-start(bf16[64,1536]{1,0:T(8,128)(2,1)S(1)} %pad_maximum_fusion.refs_0_), channel_id=1, source_target_pairs={{0,16},{8,24},{16,0},{24,8},{1,17},{9,25},{17,1},{25,9},{2,18},{10... | collective-permute-start | bytes 589832 | tf_op jit(solution)/shard_map/ppermute | solution.py:230
  46.2 0.0 collective-permute-done.5.refs_1_
  46.2 0.2 collective-permute-done.6.u1
  46.5 3.2 %collective-permute-start.11 = (bf16[64,1536]{1,0:T(8,128)(2,1)S(1)}, bf16[64,1536]{1,0:T(8,128)(2,1)S(1)}, u32[]{:S(2)}, u32[]{:S(2)}) collective-permute-start(bf16[64,1536]{1,0:T(8,128)(2,1)S(1)} %collective-permute-done.5.refs_1_), channel_id=1, source_target_pairs={{0,16},{8,24},{16,0},{24,8},{1,17},{9,25},{17,1},{25,9},{2,18},{10... | collective-permute-start | bytes 589832 | tf_op jit(solution)/shard_map/ppermute | solution.py:230
  49.7 0.7 copy-done.4
  50.4 5.0 %attn_fwd.1 = (f32[3,4,128,128]{3,2,1,0:T(8,128)S(1)}, bf16[512,384]{1,0:T(8,128)(2,1)S(1)}) custom-call(s32[5]{0:T(128)S(1)} %stack.25.place, f32[12,15]{1,0:T(8,128)S(1)} %copy-done.3, s32[8,384]{1,0:T(8,128)S(1)} %copy-done.4, bf16[8,3,64,384]{3,2,1,0:T(8,128)(2,1)S(1)} %all-to-all-done.qkv_ref.recv_ref), custom_call_target="tpu_custom_call" | custom-call | flops 20000000000 | bytes 2372324 | tf_op jit(solution)/shard_map/attn_fwd/pallas_call | solution.py:54
  55.5 0.0 collective-permute-done.11.refs_3_
  55.5 0.1 stack.27.w0_ref
  55.5 0.1 collective-permute-start.12
  55.6 0.4 collective-permute-done.7.u2
  56.1 4.4 %collective-permute-done.8.u3 = bf16[128,1536]{1,0:T(8,128)(2,1)S(1)} collective-permute-done((bf16[128,1536]{1,0:T(8,128)(2,1)S(1)}, bf16[128,1536]{1,0:T(8,128)(2,1)S(1)}, u32[]{:S(2)}, u32[]{:S(2)}) %collective-permute-start.8) | collective-permute-done | bytes 393248 | tf_op jit(solution)/shard_map/ppermute | solution.py:230
  60.5 1.4 %grad_w.1 = (f32[192,1536]{1,0:T(8,128)S(1)}, bf16[192,1536]{1,0:T(8,128)(2,1)S(1)}, bf16[8,64,1536]{2,1,0:T(8,128)(2,1)S(1)}) custom-call(s32[5]{0:T(128)S(1)} %stack.25.place, bf16[512,384]{1,0:T(8,128)(2,1)S(1)} %get-tuple-element.50.mixed_ref, bf16[128,1536]{1,0:T(8,128)(2,1)S(1)} %stack.26.u0, bf16[128,1536]{1,0:T(8,128)(2,1)S(1)} %collective-permute-done.6.u1, ...), custom_call_target="tpu_custom_call" | custom-call | flops 20000000000 | bytes 5308436 | tf_op jit(solution)/shard_map/grad_w/pallas_call | solution.py:54
  61.9 0.1 collective-permute-start.9
  62.0 2.3 %scores_bwd.1 = (bf16[8,64,384]{2,1,0:T(8,128)(2,1)S(1)}, bf16[3,4,128,128]{3,2,1,0:T(8,128)(2,1)S(1)}, f32[8,384]{1,0:T(8,128)S(1)}) custom-call(s32[5]{0:T(128)S(1)} %stack.25.place, s32[8,384]{1,0:T(8,128)S(1)} %copy-done.1, bf16[8,3,64,384]{3,2,1,0:T(8,128)(2,1)S(1)} %all-to-all-done.qkv_ref.recv_ref, ...), custom_call_target="tpu_custom_call" | custom-call | flops 900000000 | bytes 5922836 | tf_op jit(solution)/shard_map/scores_bwd/pallas_call | solution.py:54
  64.3 0.8 collective-permute-start.13
  65.1 1.2 %grads.1 = (bf16[3,64,384]{2,1,0:T(8,128)(2,1)S(1)}, bf16[3,64,384]{2,1,0:T(8,128)(2,1)S(1)}, bf16[3,64,384]{2,1,0:T(8,128)(2,1)S(1)}, bf16[3,64,384]{2,1,0:T(8,...) custom-call(s32[5]{0:T(128)S(1)} %stack.25.place, ...), custom_call_target="tpu_custom_call" | custom-call | flops 150000000 | bytes 3932180 | tf_op jit(solution)/shard_map/grads/pallas_call | solution.py:54
  66.2 0.0 collective-permute-done.9.other_ref
  66.2 1.5 %join.1 = bf16[32,8,1280]{2,1,0:T(8,128)(2,1)} custom-call(f32[192,1536]{1,0:T(8,128)S(1)} %get-tuple-element.58.mine_ref, bf16[192,1536]{1,0:T(8,128)(2,1)S(1)} %collective-permute-done.9.other_ref, f32[8,384]{1,0:T(8,128)S(1)} %get-tuple-element.63.s0, f32[8,384]{1,0:T(8,128)S(1)} %collective-permute-done.13.s1), custom_call_target="tpu_custom_call" | custom-call | bytes 2449408 | tf_op jit(solution)/shard_map/join/pallas_call | solution.py:54
  67.8 11.4 %all-to-all-start.2 = ((bf16[32,8,1280]{2,1,0:T(8,128)(2,1)}), bf16[32,8,1280]{2,1,0:T(8,128)(2,1)S(1)}, u32[]{:S(2)}, u32[]{:S(2)}) async-start(bf16[32,8,1280]{2,1,0:T(8,128)(2,1)} %join.1), calls=%async_computation.2 | async-start | bytes 1310720 | tf_op jit(solution)/shard_map/all_to_all | solution.py:328
  79.2 0.1 collective-permute-start.14
  79.3 0.1 collective-permute-start.15
  79.4 1.8 %collective-permute-start.16 = (bf16[3,64,384]{2,1,0:T(8,128)(2,1)S(1)}, bf16[3,64,384]{2,1,0:T(8,128)(2,1)S(1)}, u32[]{:S(2)}, u32[]{:S(2)}) collective-permute-start(bf16[3,64,384]{2,1,0:T(8,128)(2,1)S(1)} %get-tuple-element.77), channel_id=1, source_target_pairs={{0,3},{1,2},{2,1},{3,0},{4,7},{5,6},{6,5},{7,4},{8,11},{9,10},{10,... | collective-permute-start | bytes 442376 | tf_op jit(solution)/shard_map/ppermute | solution.py:230
  81.1 0.9 collective-permute-start.17
  82.0 2.3 %collective-permute-start.18 = (bf16[3,64,384]{2,1,0:T(8,128)(2,1)S(1)}, bf16[3,64,384]{2,1,0:T(8,128)(2,1)S(1)}, u32[]{:S(2)}, u32[]{:S(2)}) collective-permute-start(bf16[3,64,384]{2,1,0:T(8,128)(2,1)S(1)} %get-tuple-element.79), channel_id=1, source_target_pairs={{0,5},{1,4},{2,7},{3,6},{4,1},{5,0},{6,3},{7,2},{8,13},{9,12},{10,... | collective-permute-start | bytes 442376 | tf_op jit(solution)/shard_map/ppermute | solution.py:230
  84.4 1.2 %collective-permute-start.20 = (bf16[3,64,384]{2,1,0:T(8,128)(2,1)S(1)}, bf16[3,64,384]{2,1,0:T(8,128)(2,1)S(1)}, u32[]{:S(2)}, u32[]{:S(2)}) collective-permute-start(bf16[3,64,384]{2,1,0:T(8,128)(2,1)S(1)} %get-tuple-element.88), channel_id=1, source_target_pairs={{0,6},{1,7},{2,4},{3,5},{4,2},{5,3},{6,0},{7,1},{8,14},{9,15},{10,... | collective-permute-start | bytes 442376 | tf_op jit(solution)/shard_map/ppermute | solution.py:230
  85.5 0.5 collective-permute-done.15.refs_2_
  86.0 1.4 %collective-permute-start.21 = (bf16[3,64,384]{2,1,0:T(8,128)(2,1)S(1)}, bf16[3,64,384]{2,1,0:T(8,128)(2,1)S(1)}, u32[]{:S(2)}, u32[]{:S(2)}) collective-permute-start(bf16[3,64,384]{2,1,0:T(8,128)(2,1)S(1)} %get-tuple-element.89), channel_id=1, source_target_pairs={{0,7},{1,6},{2,5},{3,4},{4,3},{5,2},{6,1},{7,0},{8,15},{9,14},{10,... | collective-permute-start | bytes 442376 | tf_op jit(solution)/shard_map/ppermute | solution.py:230
  87.4 0.9 collective-permute-done.16.refs_3_
  88.2 4.8 %collective-permute-done.17.refs_4_ = bf16[3,64,384]{2,1,0:T(8,128)(2,1)S(1)} collective-permute-done((bf16[3,64,384]{2,1,0:T(8,128)(2,1)S(1)}, bf16[3,64,384]{2,1,0:T(8,128)(2,1)S(1)}, u32[]{:S(2)}, u32[]{:S(2)}) %collective-permute-start.17) | collective-permute-done | bytes 147488 | tf_op jit(solution)/shard_map/ppermute | solution.py:230
  93.0 2.2 %collective-permute-done.18.refs_5_ = bf16[3,64,384]{2,1,0:T(8,128)(2,1)S(1)} collective-permute-done((bf16[3,64,384]{2,1,0:T(8,128)(2,1)S(1)}, bf16[3,64,384]{2,1,0:T(8,128)(2,1)S(1)}, u32[]{:S(2)}, u32[]{:S(2)}) %collective-permute-start.18) | collective-permute-done | bytes 147488 | tf_op jit(solution)/shard_map/ppermute | solution.py:230
  95.2 3.9 %all-to-all-done.2.in_ref = bf16[32,8,1280]{2,1,0:T(8,128)(2,1)S(1)} async-done(((bf16[32,8,1280]{2,1,0:T(8,128)(2,1)}), bf16[32,8,1280]{2,1,0:T(8,128)(2,1)S(1)}, u32[]{:S(2)}, u32[]{:S(2)}) %all-to-all-start.2) | async-done | bytes 655392 | tf_op jit(solution)/shard_map/all_to_all | solution.py:328
  99.1 0.5 total.1
  99.6 1.9 %collective-permute-start.19 = (f32[8,1536]{1,0:T(8,128)S(1)}, f32[8,1536]{1,0:T(8,128)S(1)}, u32[]{:S(2)}, u32[]{:S(2)}) collective-permute-start(f32[8,1536]{1,0:T(8,128)S(1)} %get-tuple-element.81), channel_id=1, source_target_pairs={{0,0},{32,2},{64,4},{96,6},{128,32},{160,34},{192,36},{224,38},{2,... | collective-permute-start | bytes 147464 | tf_op jit(solution)/shard_map/ppermute | solution.py:332
  101.5 0.9 collective-permute-start.22
  102.4 3.4 %collective-permute-start.23 = (f32[16,128]{1,0:T(8,128)S(1)}, f32[16,128]{1,0:T(8,128)S(1)}, u32[]{:S(2)}, u32[]{:S(2)}) collective-permute-start(f32[16,128]{1,0:T(8,128)S(1)} %get-tuple-element.92.o0), channel_id=1, source_target_pairs={{0,4},{2,6},{4,0},{6,2},{1,5},{3,7},{5,1},{7,3},{8,12},{10,14},{12... | collective-permute-start | bytes 24584 | tf_op jit(solution)/shard_map/ppermute | solution.py:230
  105.8 0.5 collective-permute-start.24
  106.3 0.0 collective-permute-done.21.refs_7_
  106.3 1.8 %unpack.1 = bf16[3,128,1536]{2,1,0:T(8,128)(2,1)} custom-call(s32[5]{0:T(128)S(1)} %stack.25.place, bf16[3,64,384]{2,1,0:T(8,128)(2,1)S(1)} %get-tuple-element.82.refs_0_, bf16[3,64,384]{2,1,0:T(8,128)(2,1)S(1)} %collective-permute-done.14.refs_1_, bf16[3,64,384]{2,1,0:T(8,128)(2,1)S(1)} %collective-permute-done.15.refs_2_, ...), custom_call_target="tpu_custom_call" | custom-call | bytes 2359316 | tf_op jit(solution)/shard_map/unpack/pallas_call | solution.py:54
  108.1 0.7 collective-permute-done.19.home_ref
  108.8 1.9 %collective-permute-done.24.o3 = f32[16,128]{1,0:T(8,128)S(1)} collective-permute-done((f32[16,128]{1,0:T(8,128)S(1)}, f32[16,128]{1,0:T(8,128)S(1)}, u32[]{:S(2)}, u32[]{:S(2)}) %collective-permute-start.24) | collective-permute-done | bytes 8224 | tf_op jit(solution)/shard_map/ppermute | solution.py:230
  110.7 1.2 %last.1 = (f32[6,1536]{1,0:T(8,128)}, f32[12,15]{1,0:T(8,128)}) custom-call(s32[5]{0:T(128)S(1)} %stack.25.place, f32[8,1536]{1,0:T(8,128)S(1)} %collective-permute-done.19.home_ref, f32[16,128]{1,0:T(8,128)S(1)} %get-tuple-element.92.o0, f32[16,128]{1,0:T(8,128)S(1)} %collective-permute-done.22.o1, f32[16,128]{1,0:T(8,128)S(1)} %collective-permute-done.23.o2, ...), custom_call_target="tpu_custom_call" | custom-call | bytes 119524 | tf_op jit(solution)/shard_map/last/pallas_call | solution.py:54
  (21 shorter events, 0.1 us)
Async XLA Ops:
  0.6 4.5 %copy-start = (bf16[3,1,1,128,1536]{4,3,2,1,0:T(8,128)(2,1)S(1)}, bf16[3,1,1,128,1536]{4,3,2,1,0:T(8,128)(2,1)}, u32[]{:S(2)}) copy-start(bf16[3,1,1,128,1536]{4,3,2,1,0:T(8,128)(2,1)} %param.7) | copy-start | bytes 3538948
  0.6 17.6 %all-to-all-start.1 = ((bf16[8,32,1536]{2,1,0:T(8,128)(2,1)}), bf16[8,32,1536]{2,1,0:T(8,128)(2,1)S(1)}, u32[]{:S(2)}, u32[]{:S(2)}) async-start(bf16[8,32,1536]{2,1,0:T(8,128)(2,1)} %bitcast.11), calls=%async_computation.1 | async-start | bytes 1572864 | tf_op jit(solution)/shard_map/all_to_all | solution.py:244
  5.1 1.1 %copy-start.5 = (bf16[6,1536]{1,0:T(8,128)(2,1)S(1)}, bf16[6,1536]{1,0:T(8,128)(2,1)}, u32[]{:S(2)}) copy-start(bf16[6,1536]{1,0:T(8,128)(2,1)} %param.10) | copy-start | bytes 55300
  6.2 20.2 %copy-start.2 = (s32[1,8]{1,0:T(1,128)S(1)}, s32[1,8]{1,0:T(1,128)}, u32[]{:S(2)}) copy-start(s32[1,8]{1,0:T(1,128)} %sizes.1) | copy-start | bytes 100
  6.2 15.6 %collective-permute-start.1 = (bf16[8,1536]{1,0:T(8,128)(2,1)S(1)}, bf16[8,1536]{1,0:T(8,128)(2,1)S(1)}, u32[]{:S(2)}, u32[]{:S(2)}) collective-permute-start(bf16[8,1536]{1,0:T(8,128)(2,1)S(1)} %pad.4), channel_id=1, source_target_pairs={{0,32},{2,0},{4,96},{6,64},{32,160},{34,128},{36,224},{38,192},{64... | collective-permute-start | bytes 73736 | tf_op jit(solution)/shard_map/ppermute | solution.py:247
  12.6 9.2 %collective-permute-start = (bf16[8,1536]{1,0:T(8,128)(2,1)S(1)}, bf16[8,1536]{1,0:T(8,128)(2,1)S(1)}, u32[]{:S(2)}, u32[]{:S(2)}) collective-permute-start(bf16[8,1536]{1,0:T(8,128)(2,1)S(1)} %pad.4), channel_id=1, source_target_pairs={{0,0},{2,32},{4,64},{6,96},{32,128},{34,160},{36,192},{38,224},{64... | collective-permute-start | bytes 73736 | tf_op jit(solution)/shard_map/ppermute | solution.py:247
  18.2 31.4 %all-to-all-start = ((bf16[8,3,64,384]{3,2,1,0:T(8,128)(2,1)}), bf16[8,3,64,384]{3,2,1,0:T(8,128)(2,1)S(1)}, u32[]{:S(2)}, u32[]{:S(2)}) async-start(bf16[8,3,64,384]{3,2,1,0:T(8,128)(2,1)} %pack.1), calls=%async_computation | async-start | bytes 2359296 | tf_op jit(solution)/shard_map/all_to_all | solution.py:248
  21.8 27.9 %copy-start.3 = (f32[12,15]{1,0:T(8,128)S(1)}, f32[12,15]{1,0:T(8,128)}, u32[]{:S(2)}) copy-start(f32[12,15]{1,0:T(8,128)} %bias.1) | copy-start | bytes 2164
  21.9 6.7 %collective-permute-start.2 = (bf16[16,1536]{1,0:T(8,128)(2,1)S(1)}, bf16[16,1536]{1,0:T(8,128)(2,1)S(1)}, u32[]{:S(2)}, u32[]{:S(2)}) collective-permute-start(bf16[16,1536]{1,0:T(8,128)(2,1)S(1)} %pad_maximum_fusion.2), channel_id=1, source_target_pairs={{0,64},{32,96},{64,0},{96,32},{128,192},{160,224},{192,128},{224,1... | collective-permute-start | bytes 147464 | tf_op jit(solution)/shard_map/ppermute | solution.py:230
  27.2 6.2 %collective-permute-start.3 = (bf16[64,1536]{1,0:T(8,128)(2,1)S(1)}, bf16[64,1536]{1,0:T(8,128)(2,1)S(1)}, u32[]{:S(2)}, u32[]{:S(2)}) collective-permute-start(bf16[64,1536]{1,0:T(8,128)(2,1)S(1)} %get-tuple-element.54), channel_id=1, source_target_pairs={{0,1},{1,0},{2,3},{3,2},{4,5},{5,4},{6,7},{7,6},{8,9},{9,8},{10,11... | collective-permute-start | bytes 589832 | tf_op jit(solution)/shard_map/ppermute | solution.py:230
  28.6 8.6 %collective-permute-start.4 = (bf16[32,1536]{1,0:T(8,128)(2,1)S(1)}, bf16[32,1536]{1,0:T(8,128)(2,1)S(1)}, u32[]{:S(2)}, u32[]{:S(2)}) collective-permute-start(bf16[32,1536]{1,0:T(8,128)(2,1)S(1)} %pad_maximum_fusion.1), channel_id=1, source_target_pairs={{0,128},{32,160},{64,192},{96,224},{128,0},{160,32},{192,64},{224,... | collective-permute-start | bytes 294920 | tf_op jit(solution)/shard_map/ppermute | solution.py:230
  33.4 13.1 %collective-permute-start.6 = (bf16[128,1536]{1,0:T(8,128)(2,1)S(1)}, bf16[128,1536]{1,0:T(8,128)(2,1)S(1)}, u32[]{:S(2)}, u32[]{:S(2)}) collective-permute-start(bf16[128,1536]{1,0:T(8,128)(2,1)S(1)} %stack.26.u0), channel_id=1, source_target_pairs={{0,2},{2,0},{4,6},{6,4},{1,3},{3,1},{5,7},{7,5},{8,10},{10,8},{12,... | collective-permute-start | bytes 1179656 | tf_op jit(solution)/shard_map/ppermute | solution.py:230
  37.2 9.0 %collective-permute-start.5 = (bf16[64,1536]{1,0:T(8,128)(2,1)S(1)}, bf16[64,1536]{1,0:T(8,128)(2,1)S(1)}, u32[]{:S(2)}, u32[]{:S(2)}) collective-permute-start(bf16[64,1536]{1,0:T(8,128)(2,1)S(1)} %pad_maximum_fusion.refs_0_), channel_id=1, source_target_pairs={{0,8},{8,0},{16,24},{24,16},{1,9},{9,1},{17,25},{25,17},{2,10},{10... | collective-permute-start | bytes 589832 | tf_op jit(solution)/shard_map/ppermute | solution.py:230
  38.9 17.2 %collective-permute-start.7 = (bf16[128,1536]{1,0:T(8,128)(2,1)S(1)}, bf16[128,1536]{1,0:T(8,128)(2,1)S(1)}, u32[]{:S(2)}, u32[]{:S(2)}) collective-permute-start(bf16[128,1536]{1,0:T(8,128)(2,1)S(1)} %stack.26.u0), channel_id=1, source_target_pairs={{0,4},{2,6},{4,0},{6,2},{1,5},{3,7},{5,1},{7,3},{8,12},{10,14},{12... | collective-permute-start | bytes 1179656 | tf_op jit(solution)/shard_map/ppermute | solution.py:230
  42.2 18.3 %collective-permute-start.8 = (bf16[128,1536]{1,0:T(8,128)(2,1)S(1)}, bf16[128,1536]{1,0:T(8,128)(2,1)S(1)}, u32[]{:S(2)}, u32[]{:S(2)}) collective-permute-start(bf16[128,1536]{1,0:T(8,128)(2,1)S(1)} %stack.26.u0), channel_id=1, source_target_pairs={{0,6},{2,4},{4,2},{6,0},{1,7},{3,5},{5,3},{7,1},{8,14},{10,12},{12... | collective-permute-start | bytes 1179656 | tf_op jit(solution)/shard_map/ppermute | solution.py:230
  43.3 12.1 %collective-permute-start.10 = (bf16[64,1536]{1,0:T(8,128)(2,1)S(1)}, bf16[64,1536]{1,0:T(8,128)(2,1)S(1)}, u32[]{:S(2)}, u32[]{:S(2)}) collective-permute-start(bf16[64,1536]{1,0:T(8,128)(2,1)S(1)} %pad_maximum_fusion.refs_0_), channel_id=1, source_target_pairs={{0,16},{8,24},{16,0},{24,8},{1,17},{9,25},{17,1},{25,9},{2,18},{10... | collective-permute-start | bytes 589832 | tf_op jit(solution)/shard_map/ppermute | solution.py:230
  46.5 9.0 %collective-permute-start.11 = (bf16[64,1536]{1,0:T(8,128)(2,1)S(1)}, bf16[64,1536]{1,0:T(8,128)(2,1)S(1)}, u32[]{:S(2)}, u32[]{:S(2)}) collective-permute-start(bf16[64,1536]{1,0:T(8,128)(2,1)S(1)} %collective-permute-done.5.refs_1_), channel_id=1, source_target_pairs={{0,16},{8,24},{16,0},{24,8},{1,17},{9,25},{17,1},{25,9},{2,18},{10... | collective-permute-start | bytes 589832 | tf_op jit(solution)/shard_map/ppermute | solution.py:230
  49.7 0.7 copy-start.4
  55.5 6.5 %collective-permute-start.12 = (bf16[256,1536]{1,0:T(8,128)(2,1)S(1)}, bf16[256,1536]{1,0:T(8,128)(2,1)S(1)}, u32[]{:S(2)}, u32[]{:S(2)}) collective-permute-start(bf16[256,1536]{1,0:T(8,128)(2,1)S(1)} %stack.27.w0_ref), channel_id=1, source_target_pairs={{0,1},{1,0},{2,3},{3,2},{4,5},{5,4},{6,7},{7,6},{8,9},{9,8},{10,11... | collective-permute-start | bytes 2359304 | tf_op jit(solution)/shard_map/ppermute | solution.py:230
  60.5 1.6 %copy-start.1 = (s32[8,384]{1,0:T(8,128)S(1)}, s32[8,384]{1,0:T(8,128)}, u32[]{:S(2)}) copy-start(s32[8,384]{1,0:T(8,128)} %constant.26.clone.rows_ref) | copy-start | bytes 36868
  61.9 4.3 %collective-permute-start.9 = (bf16[192,1536]{1,0:T(8,128)(2,1)S(1)}, bf16[192,1536]{1,0:T(8,128)(2,1)S(1)}, u32[]{:S(2)}, u32[]{:S(2)}) collective-permute-start(bf16[192,1536]{1,0:T(8,128)(2,1)S(1)} %get-tuple-element.59), channel_id=1, source_target_pairs={{0,1},{1,0},{2,3},{3,2},{4,5},{5,4},{6,7},{7,6},{8,9},{9,8},{10,11... | collective-permute-start | bytes 1769480 | tf_op jit(solution)/shard_map/ppermute | solution.py:230
  64.3 1.9 %collective-permute-start.13 = (f32[8,384]{1,0:T(8,128)S(1)}, f32[8,384]{1,0:T(8,128)S(1)}, u32[]{:S(2)}, u32[]{:S(2)}) collective-permute-start(f32[8,384]{1,0:T(8,128)S(1)} %get-tuple-element.63.s0), channel_id=1, source_target_pairs={{0,1},{1,0},{2,3},{3,2},{4,5},{5,4},{6,7},{7,6},{8,9},{9,8},{10,11... | collective-permute-start | bytes 36872 | tf_op jit(solution)/shard_map/ppermute | solution.py:230
  67.8 31.3 %all-to-all-start.2 = ((bf16[32,8,1280]{2,1,0:T(8,128)(2,1)}), bf16[32,8,1280]{2,1,0:T(8,128)(2,1)S(1)}, u32[]{:S(2)}, u32[]{:S(2)}) async-start(bf16[32,8,1280]{2,1,0:T(8,128)(2,1)} %join.1), calls=%async_computation.2 | async-start | bytes 1310720 | tf_op jit(solution)/shard_map/all_to_all | solution.py:328
  79.2 5.2 %collective-permute-start.14 = (bf16[3,64,384]{2,1,0:T(8,128)(2,1)S(1)}, bf16[3,64,384]{2,1,0:T(8,128)(2,1)S(1)}, u32[]{:S(2)}, u32[]{:S(2)}) collective-permute-start(bf16[3,64,384]{2,1,0:T(8,128)(2,1)S(1)} %get-tuple-element.75), channel_id=1, source_target_pairs={{0,1},{1,0},{2,3},{3,2},{4,5},{5,4},{6,7},{7,6},{8,9},{9,8},{10,11... | collective-permute-start | bytes 442376 | tf_op jit(solution)/shard_map/ppermute | solution.py:230
  79.3 6.7 %collective-permute-start.15 = (bf16[3,64,384]{2,1,0:T(8,128)(2,1)S(1)}, bf16[3,64,384]{2,1,0:T(8,128)(2,1)S(1)}, u32[]{:S(2)}, u32[]{:S(2)}) collective-permute-start(bf16[3,64,384]{2,1,0:T(8,128)(2,1)S(1)} %get-tuple-element.76), channel_id=1, source_target_pairs={{0,2},{1,3},{2,0},{3,1},{4,6},{5,7},{6,4},{7,5},{8,10},{9,11},{10,... | collective-permute-start | bytes 442376 | tf_op jit(solution)/shard_map/ppermute | solution.py:230
  79.4 8.9 %collective-permute-start.16 = (bf16[3,64,384]{2,1,0:T(8,128)(2,1)S(1)}, bf16[3,64,384]{2,1,0:T(8,128)(2,1)S(1)}, u32[]{:S(2)}, u32[]{:S(2)}) collective-permute-start(bf16[3,64,384]{2,1,0:T(8,128)(2,1)S(1)} %get-tuple-element.77), channel_id=1, source_target_pairs={{0,3},{1,2},{2,1},{3,0},{4,7},{5,6},{6,5},{7,4},{8,11},{9,10},{10,... | collective-permute-start | bytes 442376 | tf_op jit(solution)/shard_map/ppermute | solution.py:230
  81.1 11.9 %collective-permute-start.17 = (bf16[3,64,384]{2,1,0:T(8,128)(2,1)S(1)}, bf16[3,64,384]{2,1,0:T(8,128)(2,1)S(1)}, u32[]{:S(2)}, u32[]{:S(2)}) collective-permute-start(bf16[3,64,384]{2,1,0:T(8,128)(2,1)S(1)} %get-tuple-element.78), channel_id=1, source_target_pairs={{0,4},{1,5},{2,6},{3,7},{4,0},{5,1},{6,2},{7,3},{8,12},{9,13},{10,... | collective-permute-start | bytes 442376 | tf_op jit(solution)/shard_map/ppermute | solution.py:230
  82.0 13.2 %collective-permute-start.18 = (bf16[3,64,384]{2,1,0:T(8,128)(2,1)S(1)}, bf16[3,64,384]{2,1,0:T(8,128)(2,1)S(1)}, u32[]{:S(2)}, u32[]{:S(2)}) collective-permute-start(bf16[3,64,384]{2,1,0:T(8,128)(2,1)S(1)} %get-tuple-element.79), channel_id=1, source_target_pairs={{0,5},{1,4},{2,7},{3,6},{4,1},{5,0},{6,3},{7,2},{8,13},{9,12},{10,... | collective-permute-start | bytes 442376 | tf_op jit(solution)/shard_map/ppermute | solution.py:230
  84.4 21.5 %collective-permute-start.20 = (bf16[3,64,384]{2,1,0:T(8,128)(2,1)S(1)}, bf16[3,64,384]{2,1,0:T(8,128)(2,1)S(1)}, u32[]{:S(2)}, u32[]{:S(2)}) collective-permute-start(bf16[3,64,384]{2,1,0:T(8,128)(2,1)S(1)} %get-tuple-element.88), channel_id=1, source_target_pairs={{0,6},{1,7},{2,4},{3,5},{4,2},{5,3},{6,0},{7,1},{8,14},{9,15},{10,... | collective-permute-start | bytes 442376 | tf_op jit(solution)/shard_map/ppermute | solution.py:230
  86.0 20.3 %collective-permute-start.21 = (bf16[3,64,384]{2,1,0:T(8,128)(2,1)S(1)}, bf16[3,64,384]{2,1,0:T(8,128)(2,1)S(1)}, u32[]{:S(2)}, u32[]{:S(2)}) collective-permute-start(bf16[3,64,384]{2,1,0:T(8,128)(2,1)S(1)} %get-tuple-element.89), channel_id=1, source_target_pairs={{0,7},{1,6},{2,5},{3,4},{4,3},{5,2},{6,1},{7,0},{8,15},{9,14},{10,... | collective-permute-start | bytes 442376 | tf_op jit(solution)/shard_map/ppermute | solution.py:230
  99.6 9.2 %collective-permute-start.19 = (f32[8,1536]{1,0:T(8,128)S(1)}, f32[8,1536]{1,0:T(8,128)S(1)}, u32[]{:S(2)}, u32[]{:S(2)}) collective-permute-start(f32[8,1536]{1,0:T(8,128)S(1)} %get-tuple-element.81), channel_id=1, source_target_pairs={{0,0},{32,2},{64,4},{96,6},{128,32},{160,34},{192,36},{224,38},{2,... | collective-permute-start | bytes 147464 | tf_op jit(solution)/shard_map/ppermute | solution.py:332
  101.5 7.3 %collective-permute-start.22 = (f32[16,128]{1,0:T(8,128)S(1)}, f32[16,128]{1,0:T(8,128)S(1)}, u32[]{:S(2)}, u32[]{:S(2)}) collective-permute-start(f32[16,128]{1,0:T(8,128)S(1)} %get-tuple-element.92.o0), channel_id=1, source_target_pairs={{0,2},{2,0},{4,6},{6,4},{1,3},{3,1},{5,7},{7,5},{8,10},{10,8},{12,... | collective-permute-start | bytes 24584 | tf_op jit(solution)/shard_map/ppermute | solution.py:230
  102.4 6.4 %collective-permute-start.23 = (f32[16,128]{1,0:T(8,128)S(1)}, f32[16,128]{1,0:T(8,128)S(1)}, u32[]{:S(2)}, u32[]{:S(2)}) collective-permute-start(f32[16,128]{1,0:T(8,128)S(1)} %get-tuple-element.92.o0), channel_id=1, source_target_pairs={{0,4},{2,6},{4,0},{6,2},{1,5},{3,7},{5,1},{7,3},{8,12},{10,14},{12... | collective-permute-start | bytes 24584 | tf_op jit(solution)/shard_map/ppermute | solution.py:230
  105.8 4.9 %collective-permute-start.24 = (f32[16,128]{1,0:T(8,128)S(1)}, f32[16,128]{1,0:T(8,128)S(1)}, u32[]{:S(2)}, u32[]{:S(2)}) collective-permute-start(f32[16,128]{1,0:T(8,128)S(1)} %get-tuple-element.92.o0), channel_id=1, source_target_pairs={{0,6},{2,4},{4,2},{6,0},{1,7},{3,5},{5,3},{7,1},{8,14},{10,12},{12... | collective-permute-start | bytes 24584 | tf_op jit(solution)/shard_map/ppermute | solution.py:230

commit v14 on v13

--- a/solution.py
+++ b/solution.py
@@ -243,7 +243,7 @@
     near = [(a, b ^ X) for a, b in there]
     cot = lax.all_to_all(cot_out[0, 0], SEQ, 0, 0, tiled=True)
     (packed,) = call(pack_kernel, "pack", [((F, 3, HALF, COLS), bf)], qkv_time[:, 0, 0])
-    rows8, packed = lax.optimization_barrier((jnp.pad(w_out, ((0, 2), (0, 0))), packed))
+    rows8 = jnp.pad(w_out, ((0, 2), (0, 0)))
     held = [lax.ppermute(rows8, ("z", "x"), p) for p in (there, near)]
     recv = lax.all_to_all(packed, SEQ, 0, 0, tiled=True)
     held = jnp.concatenate(held)

time: 113 us -> 113 us (level)
  no operation moved by 1% of the time
where the time goes in v14:
time: 113 us; the launch traced here: 112 us
  starting transfers between devices  67.7 us (60%)
  waiting for transfers between devices  25.3 us (22%)
  Pallas kernels  16.9 us (15%)
    ppermute x22, starting transfers between devices, hop(): return lax.ppermute(x, axis, [(i, i ^ k) for i in range(n)])  37 us
    ppermute x22, waiting for transfers between devices, hop(): return lax.ppermute(x, axis, [(i, i ^ k) for i in range(n)])  18.7 us
    pallas_call x12, Pallas kernels, call(): pl.pallas_call(body, out_shape=tuple((jax.ShapeDtypeStruct(s, d) for s, d...  16.9 us
    all_to_all x1, starting transfers between devices, per_device(): msgs = lax.all_to_all(msgs, ('z', 'y'), 0, 0, tiled=True)  10.8 us
    ppermute x2, starting transfers between devices, per_device(): held = [lax.ppermute(rows8, ('z', 'x'), p) for p in (there, near)]  9.96 us
    all_to_all x1, starting transfers between devices, per_device(): cot = lax.all_to_all(cot_out[0, 0], SEQ, 0, 0, tiled=True)  4.44 us
    all_to_all x1, waiting for transfers between devices, per_device(): msgs = lax.all_to_all(msgs, ('z', 'y'), 0, 0, tiled=True)  3.83 us
    all_to_all x1, starting transfers between devices, per_device(): recv = lax.all_to_all(packed, SEQ, 0, 0, tiled=True)  3.57 us
  transfers between devices with their start and end apart: 28, of which 13 were waited for; matrix products, arithmetic and copies ran while one was open for 0% of the time, Pallas kernels for 13%

profile of v14, /device:TPU:32, one launch (start us, length us, event | category | flops | bytes accessed | tf_op | source)
XLA Modules:
  0.0 111.6 jit_solution(1910828351458426143)
XLA Ops:
  0.7 4.4 %all-to-all-start.1 = ((bf16[8,32,1536]{2,1,0:T(8,128)(2,1)}), bf16[8,32,1536]{2,1,0:T(8,128)(2,1)S(1)}, u32[]{:S(2)}, u32[]{:S(2)}) async-start(bf16[8,32,1536]{2,1,0:T(8,128)(2,1)} %bitcast.11), calls=%async_computation.1 | async-start | bytes 1572864 | tf_op jit(solution)/shard_map/all_to_all | solution.py:244
  5.1 6.4 %collective-permute-start.1 = (bf16[8,1536]{1,0:T(8,128)(2,1)S(1)}, bf16[8,1536]{1,0:T(8,128)(2,1)S(1)}, u32[]{:S(2)}, u32[]{:S(2)}) collective-permute-start(bf16[8,1536]{1,0:T(8,128)(2,1)S(1)} %pad.4), channel_id=1, source_target_pairs={{0,32},{2,0},{4,96},{6,64},{32,160},{34,128},{36,224},{38,192},{64... | collective-permute-start | bytes 73736 | tf_op jit(solution)/shard_map/ppermute | solution.py:247
  11.5 3.6 %collective-permute-start = (bf16[8,1536]{1,0:T(8,128)(2,1)S(1)}, bf16[8,1536]{1,0:T(8,128)(2,1)S(1)}, u32[]{:S(2)}, u32[]{:S(2)}) collective-permute-start(bf16[8,1536]{1,0:T(8,128)(2,1)S(1)} %pad.4), channel_id=1, source_target_pairs={{0,0},{2,32},{4,64},{6,96},{32,128},{34,160},{36,192},{38,224},{64... | collective-permute-start | bytes 73736 | tf_op jit(solution)/shard_map/ppermute | solution.py:247
  15.1 1.1 pack.1
  16.2 2.0 %all-to-all-done.1.cot_ref = bf16[8,32,1536]{2,1,0:T(8,128)(2,1)S(1)} async-done(((bf16[8,32,1536]{2,1,0:T(8,128)(2,1)}), bf16[8,32,1536]{2,1,0:T(8,128)(2,1)S(1)}, u32[]{:S(2)}, u32[]{:S(2)}) %all-to-all-start.1) | async-done | bytes 786464 | tf_op jit(solution)/shard_map/all_to_all | solution.py:244
  18.3 3.6 %all-to-all-start = ((bf16[8,3,64,384]{3,2,1,0:T(8,128)(2,1)}), bf16[8,3,64,384]{3,2,1,0:T(8,128)(2,1)S(1)}, u32[]{:S(2)}, u32[]{:S(2)}) async-start(bf16[8,3,64,384]{3,2,1,0:T(8,128)(2,1)} %pack.1), calls=%async_computation | async-start | bytes 2359296 | tf_op jit(solution)/shard_map/all_to_all | solution.py:248
  21.8 0.0 collective-permute-done.1
  21.8 0.0 collective-permute-done
  21.9 4.7 %collective-permute-start.2 = (bf16[16,1536]{1,0:T(8,128)(2,1)S(1)}, bf16[16,1536]{1,0:T(8,128)(2,1)S(1)}, u32[]{:S(2)}, u32[]{:S(2)}) collective-permute-start(bf16[16,1536]{1,0:T(8,128)(2,1)S(1)} %pad_maximum_fusion.2), channel_id=1, source_target_pairs={{0,64},{32,96},{64,0},{96,32},{128,192},{160,224},{192,128},{224,1... | collective-permute-start | bytes 147464 | tf_op jit(solution)/shard_map/ppermute | solution.py:230
  26.6 0.1 stack.25.place
  26.7 0.8 compact.1
  27.5 0.2 collective-permute-start.3
  27.6 1.2 %collective-permute-done.2 = bf16[16,1536]{1,0:T(8,128)(2,1)S(1)} collective-permute-done((bf16[16,1536]{1,0:T(8,128)(2,1)S(1)}, bf16[16,1536]{1,0:T(8,128)(2,1)S(1)}, u32[]{:S(2)}, u32[]{:S(2)}) %collective-permute-start.2) | collective-permute-done | bytes 49184 | tf_op jit(solution)/shard_map/ppermute | solution.py:230
  28.9 4.5 %collective-permute-start.4 = (bf16[32,1536]{1,0:T(8,128)(2,1)S(1)}, bf16[32,1536]{1,0:T(8,128)(2,1)S(1)}, u32[]{:S(2)}, u32[]{:S(2)}) collective-permute-start(bf16[32,1536]{1,0:T(8,128)(2,1)S(1)} %pad_maximum_fusion.1), channel_id=1, source_target_pairs={{0,128},{32,160},{64,192},{96,224},{128,0},{160,32},{192,64},{224,... | collective-permute-start | bytes 294920 | tf_op jit(solution)/shard_map/ppermute | solution.py:230
  33.4 0.0 collective-permute-done.3.refs_1_
  33.4 2.0 %collective-permute-start.6 = (bf16[128,1536]{1,0:T(8,128)(2,1)S(1)}, bf16[128,1536]{1,0:T(8,128)(2,1)S(1)}, u32[]{:S(2)}, u32[]{:S(2)}) collective-permute-start(bf16[128,1536]{1,0:T(8,128)(2,1)S(1)} %stack.26.u0), channel_id=1, source_target_pairs={{0,2},{2,0},{4,6},{6,4},{1,3},{3,1},{5,7},{7,5},{8,10},{10,8},{12,... | collective-permute-start | bytes 1179656 | tf_op jit(solution)/shard_map/ppermute | solution.py:230
  35.4 2.1 %collective-permute-done.4 = bf16[32,1536]{1,0:T(8,128)(2,1)S(1)} collective-permute-done((bf16[32,1536]{1,0:T(8,128)(2,1)S(1)}, bf16[32,1536]{1,0:T(8,128)(2,1)S(1)}, u32[]{:S(2)}, u32[]{:S(2)}) %collective-permute-start.4) | collective-permute-done | bytes 98336 | tf_op jit(solution)/shard_map/ppermute | solution.py:230
  37.5 1.7 %collective-permute-start.5 = (bf16[64,1536]{1,0:T(8,128)(2,1)S(1)}, bf16[64,1536]{1,0:T(8,128)(2,1)S(1)}, u32[]{:S(2)}, u32[]{:S(2)}) collective-permute-start(bf16[64,1536]{1,0:T(8,128)(2,1)S(1)} %pad_maximum_fusion.refs_0_), channel_id=1, source_target_pairs={{0,8},{8,0},{16,24},{24,16},{1,9},{9,1},{17,25},{25,17},{2,10},{10... | collective-permute-start | bytes 589832 | tf_op jit(solution)/shard_map/ppermute | solution.py:230
  39.2 3.3 %collective-permute-start.7 = (bf16[128,1536]{1,0:T(8,128)(2,1)S(1)}, bf16[128,1536]{1,0:T(8,128)(2,1)S(1)}, u32[]{:S(2)}, u32[]{:S(2)}) collective-permute-start(bf16[128,1536]{1,0:T(8,128)(2,1)S(1)} %stack.26.u0), channel_id=1, source_target_pairs={{0,4},{2,6},{4,0},{6,2},{1,5},{3,7},{5,1},{7,3},{8,12},{10,14},{12... | collective-permute-start | bytes 1179656 | tf_op jit(solution)/shard_map/ppermute | solution.py:230
  42.5 1.2 %collective-permute-start.8 = (bf16[128,1536]{1,0:T(8,128)(2,1)S(1)}, bf16[128,1536]{1,0:T(8,128)(2,1)S(1)}, u32[]{:S(2)}, u32[]{:S(2)}) collective-permute-start(bf16[128,1536]{1,0:T(8,128)(2,1)S(1)} %stack.26.u0), channel_id=1, source_target_pairs={{0,6},{2,4},{4,2},{6,0},{1,7},{3,5},{5,3},{7,1},{8,14},{10,12},{12... | collective-permute-start | bytes 1179656 | tf_op jit(solution)/shard_map/ppermute | solution.py:230
  43.6 2.9 %collective-permute-start.10 = (bf16[64,1536]{1,0:T(8,128)(2,1)S(1)}, bf16[64,1536]{1,0:T(8,128)(2,1)S(1)}, u32[]{:S(2)}, u32[]{:S(2)}) collective-permute-start(bf16[64,1536]{1,0:T(8,128)(2,1)S(1)} %pad_maximum_fusion.refs_0_), channel_id=1, source_target_pairs={{0,16},{8,24},{16,0},{24,8},{1,17},{9,25},{17,1},{25,9},{2,18},{10... | collective-permute-start | bytes 589832 | tf_op jit(solution)/shard_map/ppermute | solution.py:230
  46.5 0.0 collective-permute-done.5.refs_1_
  46.5 0.1 collective-permute-done.6.u1
  46.6 3.2 %collective-permute-start.11 = (bf16[64,1536]{1,0:T(8,128)(2,1)S(1)}, bf16[64,1536]{1,0:T(8,128)(2,1)S(1)}, u32[]{:S(2)}, u32[]{:S(2)}) collective-permute-start(bf16[64,1536]{1,0:T(8,128)(2,1)S(1)} %collective-permute-done.5.refs_1_), channel_id=1, source_target_pairs={{0,16},{8,24},{16,0},{24,8},{1,17},{9,25},{17,1},{25,9},{2,18},{10... | collective-permute-start | bytes 589832 | tf_op jit(solution)/shard_map/ppermute | solution.py:230
  49.8 0.0 all-to-all-done.qkv_ref.recv_ref
  49.8 0.7 copy-done.4
  50.5 5.0 %attn_fwd.1 = (f32[3,4,128,128]{3,2,1,0:T(8,128)S(1)}, bf16[512,384]{1,0:T(8,128)(2,1)S(1)}) custom-call(s32[5]{0:T(128)S(1)} %stack.25.place, f32[12,15]{1,0:T(8,128)S(1)} %copy-done.3, s32[8,384]{1,0:T(8,128)S(1)} %copy-done.4, bf16[8,3,64,384]{3,2,1,0:T(8,128)(2,1)S(1)} %all-to-all-done.qkv_ref.recv_ref), custom_call_target="tpu_custom_call" | custom-call | flops 20000000000 | bytes 2372324 | tf_op jit(solution)/shard_map/attn_fwd/pallas_call | solution.py:54
  55.6 0.0 collective-permute-done.10.refs_2_
  55.6 0.1 stack.27.w0_ref
  55.6 0.1 collective-permute-start.12
  55.7 0.4 collective-permute-done.7.u2
  56.2 4.6 %collective-permute-done.8.u3 = bf16[128,1536]{1,0:T(8,128)(2,1)S(1)} collective-permute-done((bf16[128,1536]{1,0:T(8,128)(2,1)S(1)}, bf16[128,1536]{1,0:T(8,128)(2,1)S(1)}, u32[]{:S(2)}, u32[]{:S(2)}) %collective-permute-start.8) | collective-permute-done | bytes 393248 | tf_op jit(solution)/shard_map/ppermute | solution.py:230
  60.8 1.4 %grad_w.1 = (f32[192,1536]{1,0:T(8,128)S(1)}, bf16[192,1536]{1,0:T(8,128)(2,1)S(1)}, bf16[8,64,1536]{2,1,0:T(8,128)(2,1)S(1)}) custom-call(s32[5]{0:T(128)S(1)} %stack.25.place, bf16[512,384]{1,0:T(8,128)(2,1)S(1)} %get-tuple-element.47.mixed_ref, bf16[128,1536]{1,0:T(8,128)(2,1)S(1)} %stack.26.u0, bf16[128,1536]{1,0:T(8,128)(2,1)S(1)} %collective-permute-done.6.u1, ...), custom_call_target="tpu_custom_call" | custom-call | flops 20000000000 | bytes 5308436 | tf_op jit(solution)/shard_map/grad_w/pallas_call | solution.py:54
  62.2 0.1 collective-permute-start.9
  62.3 2.3 %scores_bwd.1 = (bf16[8,64,384]{2,1,0:T(8,128)(2,1)S(1)}, bf16[3,4,128,128]{3,2,1,0:T(8,128)(2,1)S(1)}, f32[8,384]{1,0:T(8,128)S(1)}) custom-call(s32[5]{0:T(128)S(1)} %stack.25.place, s32[8,384]{1,0:T(8,128)S(1)} %copy-done.1, bf16[8,3,64,384]{3,2,1,0:T(8,128)(2,1)S(1)} %all-to-all-done.qkv_ref.recv_ref, ...), custom_call_target="tpu_custom_call" | custom-call | flops 900000000 | bytes 5922836 | tf_op jit(solution)/shard_map/scores_bwd/pallas_call | solution.py:54
  64.6 0.7 collective-permute-start.13
  65.3 1.2 %grads.1 = (bf16[3,64,384]{2,1,0:T(8,128)(2,1)S(1)}, bf16[3,64,384]{2,1,0:T(8,128)(2,1)S(1)}, bf16[3,64,384]{2,1,0:T(8,128)(2,1)S(1)}, bf16[3,64,384]{2,1,0:T(8,...) custom-call(s32[5]{0:T(128)S(1)} %stack.25.place, ...), custom_call_target="tpu_custom_call" | custom-call | flops 150000000 | bytes 3932180 | tf_op jit(solution)/shard_map/grads/pallas_call | solution.py:54
  66.5 0.0 collective-permute-done.9.other_ref
  66.5 1.5 %join.1 = bf16[32,8,1280]{2,1,0:T(8,128)(2,1)} custom-call(f32[192,1536]{1,0:T(8,128)S(1)} %get-tuple-element.54.mine_ref, bf16[192,1536]{1,0:T(8,128)(2,1)S(1)} %collective-permute-done.9.other_ref, f32[8,384]{1,0:T(8,128)S(1)} %get-tuple-element.59.s0, f32[8,384]{1,0:T(8,128)S(1)} %collective-permute-done.13.s1), custom_call_target="tpu_custom_call" | custom-call | bytes 2449408 | tf_op jit(solution)/shard_map/join/pallas_call | solution.py:54
  68.1 10.8 %all-to-all-start.2 = ((bf16[32,8,1280]{2,1,0:T(8,128)(2,1)}), bf16[32,8,1280]{2,1,0:T(8,128)(2,1)S(1)}, u32[]{:S(2)}, u32[]{:S(2)}) async-start(bf16[32,8,1280]{2,1,0:T(8,128)(2,1)} %join.1), calls=%async_computation.2 | async-start | bytes 1310720 | tf_op jit(solution)/shard_map/all_to_all | solution.py:328
  78.9 0.1 collective-permute-start.14
  79.0 0.1 collective-permute-start.15
  79.1 1.8 %collective-permute-start.16 = (bf16[3,64,384]{2,1,0:T(8,128)(2,1)S(1)}, bf16[3,64,384]{2,1,0:T(8,128)(2,1)S(1)}, u32[]{:S(2)}, u32[]{:S(2)}) collective-permute-start(bf16[3,64,384]{2,1,0:T(8,128)(2,1)S(1)} %get-tuple-element.73), channel_id=1, source_target_pairs={{0,3},{1,2},{2,1},{3,0},{4,7},{5,6},{6,5},{7,4},{8,11},{9,10},{10,... | collective-permute-start | bytes 442376 | tf_op jit(solution)/shard_map/ppermute | solution.py:230
  80.9 0.9 collective-permute-start.17
  81.8 2.3 %collective-permute-start.18 = (bf16[3,64,384]{2,1,0:T(8,128)(2,1)S(1)}, bf16[3,64,384]{2,1,0:T(8,128)(2,1)S(1)}, u32[]{:S(2)}, u32[]{:S(2)}) collective-permute-start(bf16[3,64,384]{2,1,0:T(8,128)(2,1)S(1)} %get-tuple-element.75), channel_id=1, source_target_pairs={{0,5},{1,4},{2,7},{3,6},{4,1},{5,0},{6,3},{7,2},{8,13},{9,12},{10,... | collective-permute-start | bytes 442376 | tf_op jit(solution)/shard_map/ppermute | solution.py:230
  84.1 1.2 %collective-permute-start.20 = (bf16[3,64,384]{2,1,0:T(8,128)(2,1)S(1)}, bf16[3,64,384]{2,1,0:T(8,128)(2,1)S(1)}, u32[]{:S(2)}, u32[]{:S(2)}) collective-permute-start(bf16[3,64,384]{2,1,0:T(8,128)(2,1)S(1)} %get-tuple-element.84), channel_id=1, source_target_pairs={{0,6},{1,7},{2,4},{3,5},{4,2},{5,3},{6,0},{7,1},{8,14},{9,15},{10,... | collective-permute-start | bytes 442376 | tf_op jit(solution)/shard_map/ppermute | solution.py:230
  85.3 0.5 collective-permute-done.15.refs_2_
  85.7 1.4 %collective-permute-start.21 = (bf16[3,64,384]{2,1,0:T(8,128)(2,1)S(1)}, bf16[3,64,384]{2,1,0:T(8,128)(2,1)S(1)}, u32[]{:S(2)}, u32[]{:S(2)}) collective-permute-start(bf16[3,64,384]{2,1,0:T(8,128)(2,1)S(1)} %get-tuple-element.85), channel_id=1, source_target_pairs={{0,7},{1,6},{2,5},{3,4},{4,3},{5,2},{6,1},{7,0},{8,15},{9,14},{10,... | collective-permute-start | bytes 442376 | tf_op jit(solution)/shard_map/ppermute | solution.py:230
  87.1 0.9 collective-permute-done.16.refs_3_
  87.9 4.8 %collective-permute-done.17.refs_4_ = bf16[3,64,384]{2,1,0:T(8,128)(2,1)S(1)} collective-permute-done((bf16[3,64,384]{2,1,0:T(8,128)(2,1)S(1)}, bf16[3,64,384]{2,1,0:T(8,128)(2,1)S(1)}, u32[]{:S(2)}, u32[]{:S(2)}) %collective-permute-start.17) | collective-permute-done | bytes 147488 | tf_op jit(solution)/shard_map/ppermute | solution.py:230
  92.8 2.2 %collective-permute-done.18.refs_5_ = bf16[3,64,384]{2,1,0:T(8,128)(2,1)S(1)} collective-permute-done((bf16[3,64,384]{2,1,0:T(8,128)(2,1)S(1)}, bf16[3,64,384]{2,1,0:T(8,128)(2,1)S(1)}, u32[]{:S(2)}, u32[]{:S(2)}) %collective-permute-start.18) | collective-permute-done | bytes 147488 | tf_op jit(solution)/shard_map/ppermute | solution.py:230
  95.0 3.8 %all-to-all-done.2.in_ref = bf16[32,8,1280]{2,1,0:T(8,128)(2,1)S(1)} async-done(((bf16[32,8,1280]{2,1,0:T(8,128)(2,1)}), bf16[32,8,1280]{2,1,0:T(8,128)(2,1)S(1)}, u32[]{:S(2)}, u32[]{:S(2)}) %all-to-all-start.2) | async-done | bytes 655392 | tf_op jit(solution)/shard_map/all_to_all | solution.py:328
  98.8 0.5 total.1
  99.3 1.9 %collective-permute-start.19 = (f32[8,1536]{1,0:T(8,128)S(1)}, f32[8,1536]{1,0:T(8,128)S(1)}, u32[]{:S(2)}, u32[]{:S(2)}) collective-permute-start(f32[8,1536]{1,0:T(8,128)S(1)} %get-tuple-element.77), channel_id=1, source_target_pairs={{0,0},{32,2},{64,4},{96,6},{128,32},{160,34},{192,36},{224,38},{2,... | collective-permute-start | bytes 147464 | tf_op jit(solution)/shard_map/ppermute | solution.py:332
  101.3 0.9 collective-permute-start.22
  102.1 3.4 %collective-permute-start.23 = (f32[16,128]{1,0:T(8,128)S(1)}, f32[16,128]{1,0:T(8,128)S(1)}, u32[]{:S(2)}, u32[]{:S(2)}) collective-permute-start(f32[16,128]{1,0:T(8,128)S(1)} %get-tuple-element.88.o0), channel_id=1, source_target_pairs={{0,4},{2,6},{4,0},{6,2},{1,5},{3,7},{5,1},{7,3},{8,12},{10,14},{12... | collective-permute-start | bytes 24584 | tf_op jit(solution)/shard_map/ppermute | solution.py:230
  105.6 0.0 collective-permute-done.20.refs_6_
  105.6 0.5 collective-permute-start.24
  106.1 0.0 collective-permute-done.21.refs_7_
  106.1 1.8 %unpack.1 = bf16[3,128,1536]{2,1,0:T(8,128)(2,1)} custom-call(s32[5]{0:T(128)S(1)} %stack.25.place, bf16[3,64,384]{2,1,0:T(8,128)(2,1)S(1)} %get-tuple-element.78.refs_0_, bf16[3,64,384]{2,1,0:T(8,128)(2,1)S(1)} %collective-permute-done.14.refs_1_, bf16[3,64,384]{2,1,0:T(8,128)(2,1)S(1)} %collective-permute-done.15.refs_2_, ...), custom_call_target="tpu_custom_call" | custom-call | bytes 2359316 | tf_op jit(solution)/shard_map/unpack/pallas_call | solution.py:54
  107.8 0.7 collective-permute-done.19.home_ref
  108.5 0.0 collective-permute-done.22.o1
  108.5 1.9 %collective-permute-done.24.o3 = f32[16,128]{1,0:T(8,128)S(1)} collective-permute-done((f32[16,128]{1,0:T(8,128)S(1)}, f32[16,128]{1,0:T(8,128)S(1)}, u32[]{:S(2)}, u32[]{:S(2)}) %collective-permute-start.24) | collective-permute-done | bytes 8224 | tf_op jit(solution)/shard_map/ppermute | solution.py:230
  110.4 1.2 %last.1 = (f32[6,1536]{1,0:T(8,128)}, f32[12,15]{1,0:T(8,128)}) custom-call(s32[5]{0:T(128)S(1)} %stack.25.place, f32[8,1536]{1,0:T(8,128)S(1)} %collective-permute-done.19.home_ref, f32[16,128]{1,0:T(8,128)S(1)} %get-tuple-element.88.o0, f32[16,128]{1,0:T(8,128)S(1)} %collective-permute-done.22.o1, f32[16,128]{1,0:T(8,128)S(1)} %collective-permute-done.23.o2, ...), custom_call_target="tpu_custom_call" | custom-call | bytes 119524 | tf_op jit(solution)/shard_map/last/pallas_call | solution.py:54
  (21 shorter events, 0.1 us)
Async XLA Ops:
  0.6 4.5 %copy-start.5 = (bf16[6,1536]{1,0:T(8,128)(2,1)S(1)}, bf16[6,1536]{1,0:T(8,128)(2,1)}, u32[]{:S(2)}) copy-start(bf16[6,1536]{1,0:T(8,128)(2,1)} %param.10) | copy-start | bytes 55300
  0.6 14.4 %copy-start = (bf16[3,1,1,128,1536]{4,3,2,1,0:T(8,128)(2,1)S(1)}, bf16[3,1,1,128,1536]{4,3,2,1,0:T(8,128)(2,1)}, u32[]{:S(2)}) copy-start(bf16[3,1,1,128,1536]{4,3,2,1,0:T(8,128)(2,1)} %param.7) | copy-start | bytes 3538948
  0.7 17.6 %all-to-all-start.1 = ((bf16[8,32,1536]{2,1,0:T(8,128)(2,1)}), bf16[8,32,1536]{2,1,0:T(8,128)(2,1)S(1)}, u32[]{:S(2)}, u32[]{:S(2)}) async-start(bf16[8,32,1536]{2,1,0:T(8,128)(2,1)} %bitcast.11), calls=%async_computation.1 | async-start | bytes 1572864 | tf_op jit(solution)/shard_map/all_to_all | solution.py:244
  5.1 16.7 %collective-permute-start.1 = (bf16[8,1536]{1,0:T(8,128)(2,1)S(1)}, bf16[8,1536]{1,0:T(8,128)(2,1)S(1)}, u32[]{:S(2)}, u32[]{:S(2)}) collective-permute-start(bf16[8,1536]{1,0:T(8,128)(2,1)S(1)} %pad.4), channel_id=1, source_target_pairs={{0,32},{2,0},{4,96},{6,64},{32,160},{34,128},{36,224},{38,192},{64... | collective-permute-start | bytes 73736 | tf_op jit(solution)/shard_map/ppermute | solution.py:247
  11.5 10.4 %collective-permute-start = (bf16[8,1536]{1,0:T(8,128)(2,1)S(1)}, bf16[8,1536]{1,0:T(8,128)(2,1)S(1)}, u32[]{:S(2)}, u32[]{:S(2)}) collective-permute-start(bf16[8,1536]{1,0:T(8,128)(2,1)S(1)} %pad.4), channel_id=1, source_target_pairs={{0,0},{2,32},{4,64},{6,96},{32,128},{34,160},{36,192},{38,224},{64... | collective-permute-start | bytes 73736 | tf_op jit(solution)/shard_map/ppermute | solution.py:247
  16.2 10.4 %copy-start.2 = (s32[1,8]{1,0:T(1,128)S(1)}, s32[1,8]{1,0:T(1,128)}, u32[]{:S(2)}) copy-start(s32[1,8]{1,0:T(1,128)} %sizes.1) | copy-start | bytes 100
  18.3 31.5 %all-to-all-start = ((bf16[8,3,64,384]{3,2,1,0:T(8,128)(2,1)}), bf16[8,3,64,384]{3,2,1,0:T(8,128)(2,1)S(1)}, u32[]{:S(2)}, u32[]{:S(2)}) async-start(bf16[8,3,64,384]{3,2,1,0:T(8,128)(2,1)} %pack.1), calls=%async_computation | async-start | bytes 2359296 | tf_op jit(solution)/shard_map/all_to_all | solution.py:248
  21.8 28.0 %copy-start.3 = (f32[12,15]{1,0:T(8,128)S(1)}, f32[12,15]{1,0:T(8,128)}, u32[]{:S(2)}) copy-start(f32[12,15]{1,0:T(8,128)} %bias.1) | copy-start | bytes 2164
  21.9 7.0 %collective-permute-start.2 = (bf16[16,1536]{1,0:T(8,128)(2,1)S(1)}, bf16[16,1536]{1,0:T(8,128)(2,1)S(1)}, u32[]{:S(2)}, u32[]{:S(2)}) collective-permute-start(bf16[16,1536]{1,0:T(8,128)(2,1)S(1)} %pad_maximum_fusion.2), channel_id=1, source_target_pairs={{0,64},{32,96},{64,0},{96,32},{128,192},{160,224},{192,128},{224,1... | collective-permute-start | bytes 147464 | tf_op jit(solution)/shard_map/ppermute | solution.py:230
  27.5 5.9 %collective-permute-start.3 = (bf16[64,1536]{1,0:T(8,128)(2,1)S(1)}, bf16[64,1536]{1,0:T(8,128)(2,1)S(1)}, u32[]{:S(2)}, u32[]{:S(2)}) collective-permute-start(bf16[64,1536]{1,0:T(8,128)(2,1)S(1)} %get-tuple-element.50), channel_id=1, source_target_pairs={{0,1},{1,0},{2,3},{3,2},{4,5},{5,4},{6,7},{7,6},{8,9},{9,8},{10,11... | collective-permute-start | bytes 589832 | tf_op jit(solution)/shard_map/ppermute | solution.py:230
  28.9 8.6 %collective-permute-start.4 = (bf16[32,1536]{1,0:T(8,128)(2,1)S(1)}, bf16[32,1536]{1,0:T(8,128)(2,1)S(1)}, u32[]{:S(2)}, u32[]{:S(2)}) collective-permute-start(bf16[32,1536]{1,0:T(8,128)(2,1)S(1)} %pad_maximum_fusion.1), channel_id=1, source_target_pairs={{0,128},{32,160},{64,192},{96,224},{128,0},{160,32},{192,64},{224,... | collective-permute-start | bytes 294920 | tf_op jit(solution)/shard_map/ppermute | solution.py:230
  33.4 13.2 %collective-permute-start.6 = (bf16[128,1536]{1,0:T(8,128)(2,1)S(1)}, bf16[128,1536]{1,0:T(8,128)(2,1)S(1)}, u32[]{:S(2)}, u32[]{:S(2)}) collective-permute-start(bf16[128,1536]{1,0:T(8,128)(2,1)S(1)} %stack.26.u0), channel_id=1, source_target_pairs={{0,2},{2,0},{4,6},{6,4},{1,3},{3,1},{5,7},{7,5},{8,10},{10,8},{12,... | collective-permute-start | bytes 1179656 | tf_op jit(solution)/shard_map/ppermute | solution.py:230
  37.5 9.0 %collective-permute-start.5 = (bf16[64,1536]{1,0:T(8,128)(2,1)S(1)}, bf16[64,1536]{1,0:T(8,128)(2,1)S(1)}, u32[]{:S(2)}, u32[]{:S(2)}) collective-permute-start(bf16[64,1536]{1,0:T(8,128)(2,1)S(1)} %pad_maximum_fusion.refs_0_), channel_id=1, source_target_pairs={{0,8},{8,0},{16,24},{24,16},{1,9},{9,1},{17,25},{25,17},{2,10},{10... | collective-permute-start | bytes 589832 | tf_op jit(solution)/shard_map/ppermute | solution.py:230
  39.2 17.0 %collective-permute-start.7 = (bf16[128,1536]{1,0:T(8,128)(2,1)S(1)}, bf16[128,1536]{1,0:T(8,128)(2,1)S(1)}, u32[]{:S(2)}, u32[]{:S(2)}) collective-permute-start(bf16[128,1536]{1,0:T(8,128)(2,1)S(1)} %stack.26.u0), channel_id=1, source_target_pairs={{0,4},{2,6},{4,0},{6,2},{1,5},{3,7},{5,1},{7,3},{8,12},{10,14},{12... | collective-permute-start | bytes 1179656 | tf_op jit(solution)/shard_map/ppermute | solution.py:230
  42.5 18.3 %collective-permute-start.8 = (bf16[128,1536]{1,0:T(8,128)(2,1)S(1)}, bf16[128,1536]{1,0:T(8,128)(2,1)S(1)}, u32[]{:S(2)}, u32[]{:S(2)}) collective-permute-start(bf16[128,1536]{1,0:T(8,128)(2,1)S(1)} %stack.26.u0), channel_id=1, source_target_pairs={{0,6},{2,4},{4,2},{6,0},{1,7},{3,5},{5,3},{7,1},{8,14},{10,12},{12... | collective-permute-start | bytes 1179656 | tf_op jit(solution)/shard_map/ppermute | solution.py:230
  43.6 12.0 %collective-permute-start.10 = (bf16[64,1536]{1,0:T(8,128)(2,1)S(1)}, bf16[64,1536]{1,0:T(8,128)(2,1)S(1)}, u32[]{:S(2)}, u32[]{:S(2)}) collective-permute-start(bf16[64,1536]{1,0:T(8,128)(2,1)S(1)} %pad_maximum_fusion.refs_0_), channel_id=1, source_target_pairs={{0,16},{8,24},{16,0},{24,8},{1,17},{9,25},{17,1},{25,9},{2,18},{10... | collective-permute-start | bytes 589832 | tf_op jit(solution)/shard_map/ppermute | solution.py:230
  46.6 9.0 %collective-permute-start.11 = (bf16[64,1536]{1,0:T(8,128)(2,1)S(1)}, bf16[64,1536]{1,0:T(8,128)(2,1)S(1)}, u32[]{:S(2)}, u32[]{:S(2)}) collective-permute-start(bf16[64,1536]{1,0:T(8,128)(2,1)S(1)} %collective-permute-done.5.refs_1_), channel_id=1, source_target_pairs={{0,16},{8,24},{16,0},{24,8},{1,17},{9,25},{17,1},{25,9},{2,18},{10... | collective-permute-start | bytes 589832 | tf_op jit(solution)/shard_map/ppermute | solution.py:230
  49.8 0.7 copy-start.4
  55.6 6.7 %collective-permute-start.12 = (bf16[256,1536]{1,0:T(8,128)(2,1)S(1)}, bf16[256,1536]{1,0:T(8,128)(2,1)S(1)}, u32[]{:S(2)}, u32[]{:S(2)}) collective-permute-start(bf16[256,1536]{1,0:T(8,128)(2,1)S(1)} %stack.27.w0_ref), channel_id=1, source_target_pairs={{0,1},{1,0},{2,3},{3,2},{4,5},{5,4},{6,7},{7,6},{8,9},{9,8},{10,11... | collective-permute-start | bytes 2359304 | tf_op jit(solution)/shard_map/ppermute | solution.py:230
  60.8 1.6 %copy-start.1 = (s32[8,384]{1,0:T(8,128)S(1)}, s32[8,384]{1,0:T(8,128)}, u32[]{:S(2)}) copy-start(s32[8,384]{1,0:T(8,128)} %constant.26.clone.rows_ref) | copy-start | bytes 36868
  62.2 4.3 %collective-permute-start.9 = (bf16[192,1536]{1,0:T(8,128)(2,1)S(1)}, bf16[192,1536]{1,0:T(8,128)(2,1)S(1)}, u32[]{:S(2)}, u32[]{:S(2)}) collective-permute-start(bf16[192,1536]{1,0:T(8,128)(2,1)S(1)} %get-tuple-element.55), channel_id=1, source_target_pairs={{0,1},{1,0},{2,3},{3,2},{4,5},{5,4},{6,7},{7,6},{8,9},{9,8},{10,11... | collective-permute-start | bytes 1769480 | tf_op jit(solution)/shard_map/ppermute | solution.py:230
  64.6 1.9 %collective-permute-start.13 = (f32[8,384]{1,0:T(8,128)S(1)}, f32[8,384]{1,0:T(8,128)S(1)}, u32[]{:S(2)}, u32[]{:S(2)}) collective-permute-start(f32[8,384]{1,0:T(8,128)S(1)} %get-tuple-element.59.s0), channel_id=1, source_target_pairs={{0,1},{1,0},{2,3},{3,2},{4,5},{5,4},{6,7},{7,6},{8,9},{9,8},{10,11... | collective-permute-start | bytes 36872 | tf_op jit(solution)/shard_map/ppermute | solution.py:230
  68.1 30.7 %all-to-all-start.2 = ((bf16[32,8,1280]{2,1,0:T(8,128)(2,1)}), bf16[32,8,1280]{2,1,0:T(8,128)(2,1)S(1)}, u32[]{:S(2)}, u32[]{:S(2)}) async-start(bf16[32,8,1280]{2,1,0:T(8,128)(2,1)} %join.1), calls=%async_computation.2 | async-start | bytes 1310720 | tf_op jit(solution)/shard_map/all_to_all | solution.py:328
  78.9 5.2 %collective-permute-start.14 = (bf16[3,64,384]{2,1,0:T(8,128)(2,1)S(1)}, bf16[3,64,384]{2,1,0:T(8,128)(2,1)S(1)}, u32[]{:S(2)}, u32[]{:S(2)}) collective-permute-start(bf16[3,64,384]{2,1,0:T(8,128)(2,1)S(1)} %get-tuple-element.71), channel_id=1, source_target_pairs={{0,1},{1,0},{2,3},{3,2},{4,5},{5,4},{6,7},{7,6},{8,9},{9,8},{10,11... | collective-permute-start | bytes 442376 | tf_op jit(solution)/shard_map/ppermute | solution.py:230
  79.0 6.7 %collective-permute-start.15 = (bf16[3,64,384]{2,1,0:T(8,128)(2,1)S(1)}, bf16[3,64,384]{2,1,0:T(8,128)(2,1)S(1)}, u32[]{:S(2)}, u32[]{:S(2)}) collective-permute-start(bf16[3,64,384]{2,1,0:T(8,128)(2,1)S(1)} %get-tuple-element.72), channel_id=1, source_target_pairs={{0,2},{1,3},{2,0},{3,1},{4,6},{5,7},{6,4},{7,5},{8,10},{9,11},{10,... | collective-permute-start | bytes 442376 | tf_op jit(solution)/shard_map/ppermute | solution.py:230
  79.1 8.9 %collective-permute-start.16 = (bf16[3,64,384]{2,1,0:T(8,128)(2,1)S(1)}, bf16[3,64,384]{2,1,0:T(8,128)(2,1)S(1)}, u32[]{:S(2)}, u32[]{:S(2)}) collective-permute-start(bf16[3,64,384]{2,1,0:T(8,128)(2,1)S(1)} %get-tuple-element.73), channel_id=1, source_target_pairs={{0,3},{1,2},{2,1},{3,0},{4,7},{5,6},{6,5},{7,4},{8,11},{9,10},{10,... | collective-permute-start | bytes 442376 | tf_op jit(solution)/shard_map/ppermute | solution.py:230
  80.9 11.9 %collective-permute-start.17 = (bf16[3,64,384]{2,1,0:T(8,128)(2,1)S(1)}, bf16[3,64,384]{2,1,0:T(8,128)(2,1)S(1)}, u32[]{:S(2)}, u32[]{:S(2)}) collective-permute-start(bf16[3,64,384]{2,1,0:T(8,128)(2,1)S(1)} %get-tuple-element.74), channel_id=1, source_target_pairs={{0,4},{1,5},{2,6},{3,7},{4,0},{5,1},{6,2},{7,3},{8,12},{9,13},{10,... | collective-permute-start | bytes 442376 | tf_op jit(solution)/shard_map/ppermute | solution.py:230
  81.8 13.2 %collective-permute-start.18 = (bf16[3,64,384]{2,1,0:T(8,128)(2,1)S(1)}, bf16[3,64,384]{2,1,0:T(8,128)(2,1)S(1)}, u32[]{:S(2)}, u32[]{:S(2)}) collective-permute-start(bf16[3,64,384]{2,1,0:T(8,128)(2,1)S(1)} %get-tuple-element.75), channel_id=1, source_target_pairs={{0,5},{1,4},{2,7},{3,6},{4,1},{5,0},{6,3},{7,2},{8,13},{9,12},{10,... | collective-permute-start | bytes 442376 | tf_op jit(solution)/shard_map/ppermute | solution.py:230
  84.1 21.5 %collective-permute-start.20 = (bf16[3,64,384]{2,1,0:T(8,128)(2,1)S(1)}, bf16[3,64,384]{2,1,0:T(8,128)(2,1)S(1)}, u32[]{:S(2)}, u32[]{:S(2)}) collective-permute-start(bf16[3,64,384]{2,1,0:T(8,128)(2,1)S(1)} %get-tuple-element.84), channel_id=1, source_target_pairs={{0,6},{1,7},{2,4},{3,5},{4,2},{5,3},{6,0},{7,1},{8,14},{9,15},{10,... | collective-permute-start | bytes 442376 | tf_op jit(solution)/shard_map/ppermute | solution.py:230
  85.7 20.3 %collective-permute-start.21 = (bf16[3,64,384]{2,1,0:T(8,128)(2,1)S(1)}, bf16[3,64,384]{2,1,0:T(8,128)(2,1)S(1)}, u32[]{:S(2)}, u32[]{:S(2)}) collective-permute-start(bf16[3,64,384]{2,1,0:T(8,128)(2,1)S(1)} %get-tuple-element.85), channel_id=1, source_target_pairs={{0,7},{1,6},{2,5},{3,4},{4,3},{5,2},{6,1},{7,0},{8,15},{9,14},{10,... | collective-permute-start | bytes 442376 | tf_op jit(solution)/shard_map/ppermute | solution.py:230
  99.3 9.2 %collective-permute-start.19 = (f32[8,1536]{1,0:T(8,128)S(1)}, f32[8,1536]{1,0:T(8,128)S(1)}, u32[]{:S(2)}, u32[]{:S(2)}) collective-permute-start(f32[8,1536]{1,0:T(8,128)S(1)} %get-tuple-element.77), channel_id=1, source_target_pairs={{0,0},{32,2},{64,4},{96,6},{128,32},{160,34},{192,36},{224,38},{2,... | collective-permute-start | bytes 147464 | tf_op jit(solution)/shard_map/ppermute | solution.py:332
  101.3 7.3 %collective-permute-start.22 = (f32[16,128]{1,0:T(8,128)S(1)}, f32[16,128]{1,0:T(8,128)S(1)}, u32[]{:S(2)}, u32[]{:S(2)}) collective-permute-start(f32[16,128]{1,0:T(8,128)S(1)} %get-tuple-element.88.o0), channel_id=1, source_target_pairs={{0,2},{2,0},{4,6},{6,4},{1,3},{3,1},{5,7},{7,5},{8,10},{10,8},{12,... | collective-permute-start | bytes 24584 | tf_op jit(solution)/shard_map/ppermute | solution.py:230
  102.1 6.4 %collective-permute-start.23 = (f32[16,128]{1,0:T(8,128)S(1)}, f32[16,128]{1,0:T(8,128)S(1)}, u32[]{:S(2)}, u32[]{:S(2)}) collective-permute-start(f32[16,128]{1,0:T(8,128)S(1)} %get-tuple-element.88.o0), channel_id=1, source_target_pairs={{0,4},{2,6},{4,0},{6,2},{1,5},{3,7},{5,1},{7,3},{8,12},{10,14},{12... | collective-permute-start | bytes 24584 | tf_op jit(solution)/shard_map/ppermute | solution.py:230
  105.6 4.9 %collective-permute-start.24 = (f32[16,128]{1,0:T(8,128)S(1)}, f32[16,128]{1,0:T(8,128)S(1)}, u32[]{:S(2)}, u32[]{:S(2)}) collective-permute-start(f32[16,128]{1,0:T(8,128)S(1)} %get-tuple-element.88.o0), channel_id=1, source_target_pairs={{0,6},{2,4},{4,2},{6,0},{1,7},{3,5},{5,3},{7,1},{8,14},{10,12},{12... | collective-permute-start | bytes 24584 | tf_op jit(solution)/shard_map/ppermute | solution.py:230

commit v15 on v14

--- a/solution.py
+++ b/solution.py
@@ -327,7 +327,7 @@
     msgs, *pieces = lax.optimization_barrier((msgs, *pieces))
     msgs = lax.all_to_all(msgs, ("z", "y"), 0, 0, tiled=True)
     pieces = pieces[:1] + [hop(p, SEQ, k, F) for k, p in enumerate(pieces[1:], 1)]
-    msgs, *pieces[1:6] = lax.optimization_barrier((msgs, *pieces[1:6]))
+    msgs, *pieces[1:5] = lax.optimization_barrier((msgs, *pieces[1:5]))
     total, off = call(total_kernel, "total", [((8, DW), f32), ((16, 128), f32)], msgs)
     home = lax.ppermute(total, ("z", "x"), [(b, a) for a, b in there])
     offs = [off] + [hop(off, "x", k, X) for k in range(1, X)]

time: 113 us -> 113 us (level)
    all_to_all x1, waiting for transfers between devices: 3.83 us -> 6.04 us  [per_device(): msgs = lax.all_to_all(msgs, ('z', 'y'), 0, 0, tiled=True)]
    ppermute x22, waiting for transfers between devices: 18.7 us -> 16.5 us  [hop(): return lax.ppermute(x, axis, [(i, i ^ k) for i in range(n)])]
  transfers between devices with their start and end apart: 28 -> 28, of which waited for: 13 -> 12; matrix products, arithmetic and copies ran while one was open for 0% -> 0% of each run, Pallas kernels for 13% -> 13%
where the time goes in v15:
time: 113 us; the launch traced here: 112 us
  starting transfers between devices  67.7 us (60%)
  waiting for transfers between devices  25.3 us (22%)
  Pallas kernels  16.9 us (15%)
    ppermute x22, starting transfers between devices, hop(): return lax.ppermute(x, axis, [(i, i ^ k) for i in range(n)])  37 us
    pallas_call x12, Pallas kernels, call(): pl.pallas_call(body, out_shape=tuple((jax.ShapeDtypeStruct(s, d) for s, d...  16.9 us
    ppermute x22, waiting for transfers between devices, hop(): return lax.ppermute(x, axis, [(i, i ^ k) for i in range(n)])  16.5 us
    all_to_all x1, starting transfers between devices, per_device(): msgs = lax.all_to_all(msgs, ('z', 'y'), 0, 0, tiled=True)  10.8 us
    ppermute x2, starting transfers between devices, per_device(): held = [lax.ppermute(rows8, ('z', 'x'), p) for p in (there, near)]  9.96 us
    all_to_all x1, waiting for transfers between devices, per_device(): msgs = lax.all_to_all(msgs, ('z', 'y'), 0, 0, tiled=True)  6.04 us
    all_to_all x1, starting transfers between devices, per_device(): cot = lax.all_to_all(cot_out[0, 0], SEQ, 0, 0, tiled=True)  4.44 us
    all_to_all x1, starting transfers between devices, per_device(): recv = lax.all_to_all(packed, SEQ, 0, 0, tiled=True)  3.57 us
  transfers between devices with their start and end apart: 28, of which 12 were waited for; matrix products, arithmetic and copies ran while one was open for 0% of the time, Pallas kernels for 13%

profile of v15, /device:TPU:32, one launch (start us, length us, event | category | flops | bytes accessed | tf_op | source)
XLA Modules:
  0.0 111.6 jit_solution(15353705491232635711)
XLA Ops:
  0.7 4.4 %all-to-all-start.1 = ((bf16[8,32,1536]{2,1,0:T(8,128)(2,1)}), bf16[8,32,1536]{2,1,0:T(8,128)(2,1)S(1)}, u32[]{:S(2)}, u32[]{:S(2)}) async-start(bf16[8,32,1536]{2,1,0:T(8,128)(2,1)} %bitcast.11), calls=%async_computation.1 | async-start | bytes 1572864 | tf_op jit(solution)/shard_map/all_to_all | solution.py:244
  5.1 6.4 %collective-permute-start.1 = (bf16[8,1536]{1,0:T(8,128)(2,1)S(1)}, bf16[8,1536]{1,0:T(8,128)(2,1)S(1)}, u32[]{:S(2)}, u32[]{:S(2)}) collective-permute-start(bf16[8,1536]{1,0:T(8,128)(2,1)S(1)} %pad.4), channel_id=1, source_target_pairs={{0,32},{2,0},{4,96},{6,64},{32,160},{34,128},{36,224},{38,192},{64... | collective-permute-start | bytes 73736 | tf_op jit(solution)/shard_map/ppermute | solution.py:247
  11.5 3.6 %collective-permute-start = (bf16[8,1536]{1,0:T(8,128)(2,1)S(1)}, bf16[8,1536]{1,0:T(8,128)(2,1)S(1)}, u32[]{:S(2)}, u32[]{:S(2)}) collective-permute-start(bf16[8,1536]{1,0:T(8,128)(2,1)S(1)} %pad.4), channel_id=1, source_target_pairs={{0,0},{2,32},{4,64},{6,96},{32,128},{34,160},{36,192},{38,224},{64... | collective-permute-start | bytes 73736 | tf_op jit(solution)/shard_map/ppermute | solution.py:247
  15.1 1.1 pack.1
  16.2 2.0 %all-to-all-done.1.cot_ref = bf16[8,32,1536]{2,1,0:T(8,128)(2,1)S(1)} async-done(((bf16[8,32,1536]{2,1,0:T(8,128)(2,1)}), bf16[8,32,1536]{2,1,0:T(8,128)(2,1)S(1)}, u32[]{:S(2)}, u32[]{:S(2)}) %all-to-all-start.1) | async-done | bytes 786464 | tf_op jit(solution)/shard_map/all_to_all | solution.py:244
  18.3 3.6 %all-to-all-start = ((bf16[8,3,64,384]{3,2,1,0:T(8,128)(2,1)}), bf16[8,3,64,384]{3,2,1,0:T(8,128)(2,1)S(1)}, u32[]{:S(2)}, u32[]{:S(2)}) async-start(bf16[8,3,64,384]{3,2,1,0:T(8,128)(2,1)} %pack.1), calls=%async_computation | async-start | bytes 2359296 | tf_op jit(solution)/shard_map/all_to_all | solution.py:248
  21.8 0.0 collective-permute-done.1
  21.8 0.0 collective-permute-done
  21.9 4.7 %collective-permute-start.2 = (bf16[16,1536]{1,0:T(8,128)(2,1)S(1)}, bf16[16,1536]{1,0:T(8,128)(2,1)S(1)}, u32[]{:S(2)}, u32[]{:S(2)}) collective-permute-start(bf16[16,1536]{1,0:T(8,128)(2,1)S(1)} %pad_maximum_fusion.2), channel_id=1, source_target_pairs={{0,64},{32,96},{64,0},{96,32},{128,192},{160,224},{192,128},{224,1... | collective-permute-start | bytes 147464 | tf_op jit(solution)/shard_map/ppermute | solution.py:230
  26.6 0.1 stack.25.place
  26.7 0.8 compact.1
  27.5 0.2 collective-permute-start.3
  27.6 1.2 %collective-permute-done.2 = bf16[16,1536]{1,0:T(8,128)(2,1)S(1)} collective-permute-done((bf16[16,1536]{1,0:T(8,128)(2,1)S(1)}, bf16[16,1536]{1,0:T(8,128)(2,1)S(1)}, u32[]{:S(2)}, u32[]{:S(2)}) %collective-permute-start.2) | collective-permute-done | bytes 49184 | tf_op jit(solution)/shard_map/ppermute | solution.py:230
  28.9 4.5 %collective-permute-start.4 = (bf16[32,1536]{1,0:T(8,128)(2,1)S(1)}, bf16[32,1536]{1,0:T(8,128)(2,1)S(1)}, u32[]{:S(2)}, u32[]{:S(2)}) collective-permute-start(bf16[32,1536]{1,0:T(8,128)(2,1)S(1)} %pad_maximum_fusion.1), channel_id=1, source_target_pairs={{0,128},{32,160},{64,192},{96,224},{128,0},{160,32},{192,64},{224,... | collective-permute-start | bytes 294920 | tf_op jit(solution)/shard_map/ppermute | solution.py:230
  33.4 0.0 collective-permute-done.3.refs_1_
  33.4 2.0 %collective-permute-start.6 = (bf16[128,1536]{1,0:T(8,128)(2,1)S(1)}, bf16[128,1536]{1,0:T(8,128)(2,1)S(1)}, u32[]{:S(2)}, u32[]{:S(2)}) collective-permute-start(bf16[128,1536]{1,0:T(8,128)(2,1)S(1)} %stack.26.u0), channel_id=1, source_target_pairs={{0,2},{2,0},{4,6},{6,4},{1,3},{3,1},{5,7},{7,5},{8,10},{10,8},{12,... | collective-permute-start | bytes 1179656 | tf_op jit(solution)/shard_map/ppermute | solution.py:230
  35.4 2.1 %collective-permute-done.4 = bf16[32,1536]{1,0:T(8,128)(2,1)S(1)} collective-permute-done((bf16[32,1536]{1,0:T(8,128)(2,1)S(1)}, bf16[32,1536]{1,0:T(8,128)(2,1)S(1)}, u32[]{:S(2)}, u32[]{:S(2)}) %collective-permute-start.4) | collective-permute-done | bytes 98336 | tf_op jit(solution)/shard_map/ppermute | solution.py:230
  37.5 1.7 %collective-permute-start.5 = (bf16[64,1536]{1,0:T(8,128)(2,1)S(1)}, bf16[64,1536]{1,0:T(8,128)(2,1)S(1)}, u32[]{:S(2)}, u32[]{:S(2)}) collective-permute-start(bf16[64,1536]{1,0:T(8,128)(2,1)S(1)} %pad_maximum_fusion.refs_0_), channel_id=1, source_target_pairs={{0,8},{8,0},{16,24},{24,16},{1,9},{9,1},{17,25},{25,17},{2,10},{10... | collective-permute-start | bytes 589832 | tf_op jit(solution)/shard_map/ppermute | solution.py:230
  39.2 3.3 %collective-permute-start.7 = (bf16[128,1536]{1,0:T(8,128)(2,1)S(1)}, bf16[128,1536]{1,0:T(8,128)(2,1)S(1)}, u32[]{:S(2)}, u32[]{:S(2)}) collective-permute-start(bf16[128,1536]{1,0:T(8,128)(2,1)S(1)} %stack.26.u0), channel_id=1, source_target_pairs={{0,4},{2,6},{4,0},{6,2},{1,5},{3,7},{5,1},{7,3},{8,12},{10,14},{12... | collective-permute-start | bytes 1179656 | tf_op jit(solution)/shard_map/ppermute | solution.py:230
  42.5 1.2 %collective-permute-start.8 = (bf16[128,1536]{1,0:T(8,128)(2,1)S(1)}, bf16[128,1536]{1,0:T(8,128)(2,1)S(1)}, u32[]{:S(2)}, u32[]{:S(2)}) collective-permute-start(bf16[128,1536]{1,0:T(8,128)(2,1)S(1)} %stack.26.u0), channel_id=1, source_target_pairs={{0,6},{2,4},{4,2},{6,0},{1,7},{3,5},{5,3},{7,1},{8,14},{10,12},{12... | collective-permute-start | bytes 1179656 | tf_op jit(solution)/shard_map/ppermute | solution.py:230
  43.6 2.9 %collective-permute-start.10 = (bf16[64,1536]{1,0:T(8,128)(2,1)S(1)}, bf16[64,1536]{1,0:T(8,128)(2,1)S(1)}, u32[]{:S(2)}, u32[]{:S(2)}) collective-permute-start(bf16[64,1536]{1,0:T(8,128)(2,1)S(1)} %pad_maximum_fusion.refs_0_), channel_id=1, source_target_pairs={{0,16},{8,24},{16,0},{24,8},{1,17},{9,25},{17,1},{25,9},{2,18},{10... | collective-permute-start | bytes 589832 | tf_op jit(solution)/shard_map/ppermute | solution.py:230
  46.5 0.0 collective-permute-done.5.refs_1_
  46.5 0.1 collective-permute-done.6.u1
  46.6 3.2 %collective-permute-start.11 = (bf16[64,1536]{1,0:T(8,128)(2,1)S(1)}, bf16[64,1536]{1,0:T(8,128)(2,1)S(1)}, u32[]{:S(2)}, u32[]{:S(2)}) collective-permute-start(bf16[64,1536]{1,0:T(8,128)(2,1)S(1)} %collective-permute-done.5.refs_1_), channel_id=1, source_target_pairs={{0,16},{8,24},{16,0},{24,8},{1,17},{9,25},{17,1},{25,9},{2,18},{10... | collective-permute-start | bytes 589832 | tf_op jit(solution)/shard_map/ppermute | solution.py:230
  49.8 0.0 all-to-all-done.qkv_ref.recv_ref
  49.8 0.7 copy-done.4
  50.5 5.0 %attn_fwd.1 = (f32[3,4,128,128]{3,2,1,0:T(8,128)S(1)}, bf16[512,384]{1,0:T(8,128)(2,1)S(1)}) custom-call(s32[5]{0:T(128)S(1)} %stack.25.place, f32[12,15]{1,0:T(8,128)S(1)} %copy-done.3, s32[8,384]{1,0:T(8,128)S(1)} %copy-done.4, bf16[8,3,64,384]{3,2,1,0:T(8,128)(2,1)S(1)} %all-to-all-done.qkv_ref.recv_ref), custom_call_target="tpu_custom_call" | custom-call | flops 20000000000 | bytes 2372324 | tf_op jit(solution)/shard_map/attn_fwd/pallas_call | solution.py:54
  55.6 0.0 collective-permute-done.10.refs_2_
  55.6 0.0 collective-permute-done.11.refs_3_
  55.6 0.1 stack.27.w0_ref
  55.6 0.1 collective-permute-start.12
  55.7 0.4 collective-permute-done.7.u2
  56.2 4.6 %collective-permute-done.8.u3 = bf16[128,1536]{1,0:T(8,128)(2,1)S(1)} collective-permute-done((bf16[128,1536]{1,0:T(8,128)(2,1)S(1)}, bf16[128,1536]{1,0:T(8,128)(2,1)S(1)}, u32[]{:S(2)}, u32[]{:S(2)}) %collective-permute-start.8) | collective-permute-done | bytes 393248 | tf_op jit(solution)/shard_map/ppermute | solution.py:230
  60.8 1.4 %grad_w.1 = (f32[192,1536]{1,0:T(8,128)S(1)}, bf16[192,1536]{1,0:T(8,128)(2,1)S(1)}, bf16[8,64,1536]{2,1,0:T(8,128)(2,1)S(1)}) custom-call(s32[5]{0:T(128)S(1)} %stack.25.place, bf16[512,384]{1,0:T(8,128)(2,1)S(1)} %get-tuple-element.46.mixed_ref, bf16[128,1536]{1,0:T(8,128)(2,1)S(1)} %stack.26.u0, bf16[128,1536]{1,0:T(8,128)(2,1)S(1)} %collective-permute-done.6.u1, ...), custom_call_target="tpu_custom_call" | custom-call | flops 20000000000 | bytes 5308436 | tf_op jit(solution)/shard_map/grad_w/pallas_call | solution.py:54
  62.2 0.1 collective-permute-start.9
  62.3 2.3 %scores_bwd.1 = (bf16[8,64,384]{2,1,0:T(8,128)(2,1)S(1)}, bf16[3,4,128,128]{3,2,1,0:T(8,128)(2,1)S(1)}, f32[8,384]{1,0:T(8,128)S(1)}) custom-call(s32[5]{0:T(128)S(1)} %stack.25.place, s32[8,384]{1,0:T(8,128)S(1)} %copy-done.1, bf16[8,3,64,384]{3,2,1,0:T(8,128)(2,1)S(1)} %all-to-all-done.qkv_ref.recv_ref, ...), custom_call_target="tpu_custom_call" | custom-call | flops 900000000 | bytes 5922836 | tf_op jit(solution)/shard_map/scores_bwd/pallas_call | solution.py:54
  64.6 0.7 collective-permute-start.13
  65.3 1.2 %grads.1 = (bf16[3,64,384]{2,1,0:T(8,128)(2,1)S(1)}, bf16[3,64,384]{2,1,0:T(8,128)(2,1)S(1)}, bf16[3,64,384]{2,1,0:T(8,128)(2,1)S(1)}, bf16[3,64,384]{2,1,0:T(8,...) custom-call(s32[5]{0:T(128)S(1)} %stack.25.place, ...), custom_call_target="tpu_custom_call" | custom-call | flops 150000000 | bytes 3932180 | tf_op jit(solution)/shard_map/grads/pallas_call | solution.py:54
  66.5 0.0 collective-permute-done.9.other_ref
  66.5 1.5 %join.1 = bf16[32,8,1280]{2,1,0:T(8,128)(2,1)} custom-call(f32[192,1536]{1,0:T(8,128)S(1)} %get-tuple-element.53.mine_ref, bf16[192,1536]{1,0:T(8,128)(2,1)S(1)} %collective-permute-done.9.other_ref, f32[8,384]{1,0:T(8,128)S(1)} %get-tuple-element.58.s0, f32[8,384]{1,0:T(8,128)S(1)} %collective-permute-done.13.s1), custom_call_target="tpu_custom_call" | custom-call | bytes 2449408 | tf_op jit(solution)/shard_map/join/pallas_call | solution.py:54
  68.1 10.8 %all-to-all-start.2 = ((bf16[32,8,1280]{2,1,0:T(8,128)(2,1)}), bf16[32,8,1280]{2,1,0:T(8,128)(2,1)S(1)}, u32[]{:S(2)}, u32[]{:S(2)}) async-start(bf16[32,8,1280]{2,1,0:T(8,128)(2,1)} %join.1), calls=%async_computation.2 | async-start | bytes 1310720 | tf_op jit(solution)/shard_map/all_to_all | solution.py:328
  78.9 0.1 collective-permute-start.14
  79.0 0.1 collective-permute-start.15
  79.1 1.8 %collective-permute-start.16 = (bf16[3,64,384]{2,1,0:T(8,128)(2,1)S(1)}, bf16[3,64,384]{2,1,0:T(8,128)(2,1)S(1)}, u32[]{:S(2)}, u32[]{:S(2)}) collective-permute-start(bf16[3,64,384]{2,1,0:T(8,128)(2,1)S(1)} %get-tuple-element.72), channel_id=1, source_target_pairs={{0,3},{1,2},{2,1},{3,0},{4,7},{5,6},{6,5},{7,4},{8,11},{9,10},{10,... | collective-permute-start | bytes 442376 | tf_op jit(solution)/shard_map/ppermute | solution.py:230
  80.9 0.9 collective-permute-start.17
  81.8 2.3 %collective-permute-start.19 = (bf16[3,64,384]{2,1,0:T(8,128)(2,1)S(1)}, bf16[3,64,384]{2,1,0:T(8,128)(2,1)S(1)}, u32[]{:S(2)}, u32[]{:S(2)}) collective-permute-start(bf16[3,64,384]{2,1,0:T(8,128)(2,1)S(1)} %get-tuple-element.81), channel_id=1, source_target_pairs={{0,5},{1,4},{2,7},{3,6},{4,1},{5,0},{6,3},{7,2},{8,13},{9,12},{10,... | collective-permute-start | bytes 442376 | tf_op jit(solution)/shard_map/ppermute | solution.py:230
  84.1 1.2 %collective-permute-start.20 = (bf16[3,64,384]{2,1,0:T(8,128)(2,1)S(1)}, bf16[3,64,384]{2,1,0:T(8,128)(2,1)S(1)}, u32[]{:S(2)}, u32[]{:S(2)}) collective-permute-start(bf16[3,64,384]{2,1,0:T(8,128)(2,1)S(1)} %get-tuple-element.82), channel_id=1, source_target_pairs={{0,6},{1,7},{2,4},{3,5},{4,2},{5,3},{6,0},{7,1},{8,14},{9,15},{10,... | collective-permute-start | bytes 442376 | tf_op jit(solution)/shard_map/ppermute | solution.py:230
  85.3 0.5 collective-permute-done.15.refs_2_
  85.7 1.4 %collective-permute-start.21 = (bf16[3,64,384]{2,1,0:T(8,128)(2,1)S(1)}, bf16[3,64,384]{2,1,0:T(8,128)(2,1)S(1)}, u32[]{:S(2)}, u32[]{:S(2)}) collective-permute-start(bf16[3,64,384]{2,1,0:T(8,128)(2,1)S(1)} %get-tuple-element.83), channel_id=1, source_target_pairs={{0,7},{1,6},{2,5},{3,4},{4,3},{5,2},{6,1},{7,0},{8,15},{9,14},{10,... | collective-permute-start | bytes 442376 | tf_op jit(solution)/shard_map/ppermute | solution.py:230
  87.1 0.9 collective-permute-done.16.refs_3_
  87.9 4.8 %collective-permute-done.17.refs_4_ = bf16[3,64,384]{2,1,0:T(8,128)(2,1)S(1)} collective-permute-done((bf16[3,64,384]{2,1,0:T(8,128)(2,1)S(1)}, bf16[3,64,384]{2,1,0:T(8,128)(2,1)S(1)}, u32[]{:S(2)}, u32[]{:S(2)}) %collective-permute-start.17) | collective-permute-done | bytes 147488 | tf_op jit(solution)/shard_map/ppermute | solution.py:230
  92.8 6.0 %all-to-all-done.2.in_ref = bf16[32,8,1280]{2,1,0:T(8,128)(2,1)S(1)} async-done(((bf16[32,8,1280]{2,1,0:T(8,128)(2,1)}), bf16[32,8,1280]{2,1,0:T(8,128)(2,1)S(1)}, u32[]{:S(2)}, u32[]{:S(2)}) %all-to-all-start.2) | async-done | bytes 655392 | tf_op jit(solution)/shard_map/all_to_all | solution.py:328
  98.8 0.5 total.1
  99.3 1.9 %collective-permute-start.18 = (f32[8,1536]{1,0:T(8,128)S(1)}, f32[8,1536]{1,0:T(8,128)S(1)}, u32[]{:S(2)}, u32[]{:S(2)}) collective-permute-start(f32[8,1536]{1,0:T(8,128)S(1)} %get-tuple-element.75), channel_id=1, source_target_pairs={{0,0},{32,2},{64,4},{96,6},{128,32},{160,34},{192,36},{224,38},{2,... | collective-permute-start | bytes 147464 | tf_op jit(solution)/shard_map/ppermute | solution.py:332
  101.3 0.9 collective-permute-start.22
  102.2 3.4 %collective-permute-start.23 = (f32[16,128]{1,0:T(8,128)S(1)}, f32[16,128]{1,0:T(8,128)S(1)}, u32[]{:S(2)}, u32[]{:S(2)}) collective-permute-start(f32[16,128]{1,0:T(8,128)S(1)} %get-tuple-element.86.o0), channel_id=1, source_target_pairs={{0,4},{2,6},{4,0},{6,2},{1,5},{3,7},{5,1},{7,3},{8,12},{10,14},{12... | collective-permute-start | bytes 24584 | tf_op jit(solution)/shard_map/ppermute | solution.py:230
  105.6 0.5 collective-permute-start.24
  106.1 0.0 collective-permute-done.21.refs_7_
  106.1 1.8 %unpack.1 = bf16[3,128,1536]{2,1,0:T(8,128)(2,1)} custom-call(s32[5]{0:T(128)S(1)} %stack.25.place, bf16[3,64,384]{2,1,0:T(8,128)(2,1)S(1)} %get-tuple-element.76.refs_0_, bf16[3,64,384]{2,1,0:T(8,128)(2,1)S(1)} %collective-permute-done.14.refs_1_, bf16[3,64,384]{2,1,0:T(8,128)(2,1)S(1)} %collective-permute-done.15.refs_2_, ...), custom_call_target="tpu_custom_call" | custom-call | bytes 2359316 | tf_op jit(solution)/shard_map/unpack/pallas_call | solution.py:54
  107.8 0.7 collective-permute-done.18.home_ref
  108.5 0.0 collective-permute-done.22.o1
  108.5 0.0 collective-permute-done.23.o2
  108.5 1.9 %collective-permute-done.24.o3 = f32[16,128]{1,0:T(8,128)S(1)} collective-permute-done((f32[16,128]{1,0:T(8,128)S(1)}, f32[16,128]{1,0:T(8,128)S(1)}, u32[]{:S(2)}, u32[]{:S(2)}) %collective-permute-start.24) | collective-permute-done | bytes 8224 | tf_op jit(solution)/shard_map/ppermute | solution.py:230
  110.4 1.2 %last.1 = (f32[6,1536]{1,0:T(8,128)}, f32[12,15]{1,0:T(8,128)}) custom-call(s32[5]{0:T(128)S(1)} %stack.25.place, f32[8,1536]{1,0:T(8,128)S(1)} %collective-permute-done.18.home_ref, f32[16,128]{1,0:T(8,128)S(1)} %get-tuple-element.86.o0, f32[16,128]{1,0:T(8,128)S(1)} %collective-permute-done.22.o1, f32[16,128]{1,0:T(8,128)S(1)} %collective-permute-done.23.o2, ...), custom_call_target="tpu_custom_call" | custom-call | bytes 119524 | tf_op jit(solution)/shard_map/last/pallas_call | solution.py:54
  (21 shorter events, 0.1 us)
Async XLA Ops:
  0.6 4.5 %copy-start.5 = (bf16[6,1536]{1,0:T(8,128)(2,1)S(1)}, bf16[6,1536]{1,0:T(8,128)(2,1)}, u32[]{:S(2)}) copy-start(bf16[6,1536]{1,0:T(8,128)(2,1)} %param.10) | copy-start | bytes 55300
  0.6 14.4 %copy-start = (bf16[3,1,1,128,1536]{4,3,2,1,0:T(8,128)(2,1)S(1)}, bf16[3,1,1,128,1536]{4,3,2,1,0:T(8,128)(2,1)}, u32[]{:S(2)}) copy-start(bf16[3,1,1,128,1536]{4,3,2,1,0:T(8,128)(2,1)} %param.7) | copy-start | bytes 3538948
  0.7 17.6 %all-to-all-start.1 = ((bf16[8,32,1536]{2,1,0:T(8,128)(2,1)}), bf16[8,32,1536]{2,1,0:T(8,128)(2,1)S(1)}, u32[]{:S(2)}, u32[]{:S(2)}) async-start(bf16[8,32,1536]{2,1,0:T(8,128)(2,1)} %bitcast.11), calls=%async_computation.1 | async-start | bytes 1572864 | tf_op jit(solution)/shard_map/all_to_all | solution.py:244
  5.1 16.7 %collective-permute-start.1 = (bf16[8,1536]{1,0:T(8,128)(2,1)S(1)}, bf16[8,1536]{1,0:T(8,128)(2,1)S(1)}, u32[]{:S(2)}, u32[]{:S(2)}) collective-permute-start(bf16[8,1536]{1,0:T(8,128)(2,1)S(1)} %pad.4), channel_id=1, source_target_pairs={{0,32},{2,0},{4,96},{6,64},{32,160},{34,128},{36,224},{38,192},{64... | collective-permute-start | bytes 73736 | tf_op jit(solution)/shard_map/ppermute | solution.py:247
  11.5 10.4 %collective-permute-start = (bf16[8,1536]{1,0:T(8,128)(2,1)S(1)}, bf16[8,1536]{1,0:T(8,128)(2,1)S(1)}, u32[]{:S(2)}, u32[]{:S(2)}) collective-permute-start(bf16[8,1536]{1,0:T(8,128)(2,1)S(1)} %pad.4), channel_id=1, source_target_pairs={{0,0},{2,32},{4,64},{6,96},{32,128},{34,160},{36,192},{38,224},{64... | collective-permute-start | bytes 73736 | tf_op jit(solution)/shard_map/ppermute | solution.py:247
  16.2 10.4 %copy-start.2 = (s32[1,8]{1,0:T(1,128)S(1)}, s32[1,8]{1,0:T(1,128)}, u32[]{:S(2)}) copy-start(s32[1,8]{1,0:T(1,128)} %sizes.1) | copy-start | bytes 100
  18.3 31.5 %all-to-all-start = ((bf16[8,3,64,384]{3,2,1,0:T(8,128)(2,1)}), bf16[8,3,64,384]{3,2,1,0:T(8,128)(2,1)S(1)}, u32[]{:S(2)}, u32[]{:S(2)}) async-start(bf16[8,3,64,384]{3,2,1,0:T(8,128)(2,1)} %pack.1), calls=%async_computation | async-start | bytes 2359296 | tf_op jit(solution)/shard_map/all_to_all | solution.py:248
  21.8 28.0 %copy-start.3 = (f32[12,15]{1,0:T(8,128)S(1)}, f32[12,15]{1,0:T(8,128)}, u32[]{:S(2)}) copy-start(f32[12,15]{1,0:T(8,128)} %bias.1) | copy-start | bytes 2164
  21.9 7.0 %collective-permute-start.2 = (bf16[16,1536]{1,0:T(8,128)(2,1)S(1)}, bf16[16,1536]{1,0:T(8,128)(2,1)S(1)}, u32[]{:S(2)}, u32[]{:S(2)}) collective-permute-start(bf16[16,1536]{1,0:T(8,128)(2,1)S(1)} %pad_maximum_fusion.2), channel_id=1, source_target_pairs={{0,64},{32,96},{64,0},{96,32},{128,192},{160,224},{192,128},{224,1... | collective-permute-start | bytes 147464 | tf_op jit(solution)/shard_map/ppermute | solution.py:230
  27.5 5.9 %collective-permute-start.3 = (bf16[64,1536]{1,0:T(8,128)(2,1)S(1)}, bf16[64,1536]{1,0:T(8,128)(2,1)S(1)}, u32[]{:S(2)}, u32[]{:S(2)}) collective-permute-start(bf16[64,1536]{1,0:T(8,128)(2,1)S(1)} %get-tuple-element.49), channel_id=1, source_target_pairs={{0,1},{1,0},{2,3},{3,2},{4,5},{5,4},{6,7},{7,6},{8,9},{9,8},{10,11... | collective-permute-start | bytes 589832 | tf_op jit(solution)/shard_map/ppermute | solution.py:230
  28.9 8.6 %collective-permute-start.4 = (bf16[32,1536]{1,0:T(8,128)(2,1)S(1)}, bf16[32,1536]{1,0:T(8,128)(2,1)S(1)}, u32[]{:S(2)}, u32[]{:S(2)}) collective-permute-start(bf16[32,1536]{1,0:T(8,128)(2,1)S(1)} %pad_maximum_fusion.1), channel_id=1, source_target_pairs={{0,128},{32,160},{64,192},{96,224},{128,0},{160,32},{192,64},{224,... | collective-permute-start | bytes 294920 | tf_op jit(solution)/shard_map/ppermute | solution.py:230
  33.4 13.2 %collective-permute-start.6 = (bf16[128,1536]{1,0:T(8,128)(2,1)S(1)}, bf16[128,1536]{1,0:T(8,128)(2,1)S(1)}, u32[]{:S(2)}, u32[]{:S(2)}) collective-permute-start(bf16[128,1536]{1,0:T(8,128)(2,1)S(1)} %stack.26.u0), channel_id=1, source_target_pairs={{0,2},{2,0},{4,6},{6,4},{1,3},{3,1},{5,7},{7,5},{8,10},{10,8},{12,... | collective-permute-start | bytes 1179656 | tf_op jit(solution)/shard_map/ppermute | solution.py:230
  37.5 9.0 %collective-permute-start.5 = (bf16[64,1536]{1,0:T(8,128)(2,1)S(1)}, bf16[64,1536]{1,0:T(8,128)(2,1)S(1)}, u32[]{:S(2)}, u32[]{:S(2)}) collective-permute-start(bf16[64,1536]{1,0:T(8,128)(2,1)S(1)} %pad_maximum_fusion.refs_0_), channel_id=1, source_target_pairs={{0,8},{8,0},{16,24},{24,16},{1,9},{9,1},{17,25},{25,17},{2,10},{10... | collective-permute-start | bytes 589832 | tf_op jit(solution)/shard_map/ppermute | solution.py:230
  39.2 17.0 %collective-permute-start.7 = (bf16[128,1536]{1,0:T(8,128)(2,1)S(1)}, bf16[128,1536]{1,0:T(8,128)(2,1)S(1)}, u32[]{:S(2)}, u32[]{:S(2)}) collective-permute-start(bf16[128,1536]{1,0:T(8,128)(2,1)S(1)} %stack.26.u0), channel_id=1, source_target_pairs={{0,4},{2,6},{4,0},{6,2},{1,5},{3,7},{5,1},{7,3},{8,12},{10,14},{12... | collective-permute-start | bytes 1179656 | tf_op jit(solution)/shard_map/ppermute | solution.py:230
  42.5 18.3 %collective-permute-start.8 = (bf16[128,1536]{1,0:T(8,128)(2,1)S(1)}, bf16[128,1536]{1,0:T(8,128)(2,1)S(1)}, u32[]{:S(2)}, u32[]{:S(2)}) collective-permute-start(bf16[128,1536]{1,0:T(8,128)(2,1)S(1)} %stack.26.u0), channel_id=1, source_target_pairs={{0,6},{2,4},{4,2},{6,0},{1,7},{3,5},{5,3},{7,1},{8,14},{10,12},{12... | collective-permute-start | bytes 1179656 | tf_op jit(solution)/shard_map/ppermute | solution.py:230
  43.6 12.0 %collective-permute-start.10 = (bf16[64,1536]{1,0:T(8,128)(2,1)S(1)}, bf16[64,1536]{1,0:T(8,128)(2,1)S(1)}, u32[]{:S(2)}, u32[]{:S(2)}) collective-permute-start(bf16[64,1536]{1,0:T(8,128)(2,1)S(1)} %pad_maximum_fusion.refs_0_), channel_id=1, source_target_pairs={{0,16},{8,24},{16,0},{24,8},{1,17},{9,25},{17,1},{25,9},{2,18},{10... | collective-permute-start | bytes 589832 | tf_op jit(solution)/shard_map/ppermute | solution.py:230
  46.6 9.0 %collective-permute-start.11 = (bf16[64,1536]{1,0:T(8,128)(2,1)S(1)}, bf16[64,1536]{1,0:T(8,128)(2,1)S(1)}, u32[]{:S(2)}, u32[]{:S(2)}) collective-permute-start(bf16[64,1536]{1,0:T(8,128)(2,1)S(1)} %collective-permute-done.5.refs_1_), channel_id=1, source_target_pairs={{0,16},{8,24},{16,0},{24,8},{1,17},{9,25},{17,1},{25,9},{2,18},{10... | collective-permute-start | bytes 589832 | tf_op jit(solution)/shard_map/ppermute | solution.py:230
  49.8 0.7 copy-start.4
  55.6 6.7 %collective-permute-start.12 = (bf16[256,1536]{1,0:T(8,128)(2,1)S(1)}, bf16[256,1536]{1,0:T(8,128)(2,1)S(1)}, u32[]{:S(2)}, u32[]{:S(2)}) collective-permute-start(bf16[256,1536]{1,0:T(8,128)(2,1)S(1)} %stack.27.w0_ref), channel_id=1, source_target_pairs={{0,1},{1,0},{2,3},{3,2},{4,5},{5,4},{6,7},{7,6},{8,9},{9,8},{10,11... | collective-permute-start | bytes 2359304 | tf_op jit(solution)/shard_map/ppermute | solution.py:230
  60.8 1.6 %copy-start.1 = (s32[8,384]{1,0:T(8,128)S(1)}, s32[8,384]{1,0:T(8,128)}, u32[]{:S(2)}) copy-start(s32[8,384]{1,0:T(8,128)} %constant.26.clone.rows_ref) | copy-start | bytes 36868
  62.2 4.3 %collective-permute-start.9 = (bf16[192,1536]{1,0:T(8,128)(2,1)S(1)}, bf16[192,1536]{1,0:T(8,128)(2,1)S(1)}, u32[]{:S(2)}, u32[]{:S(2)}) collective-permute-start(bf16[192,1536]{1,0:T(8,128)(2,1)S(1)} %get-tuple-element.54), channel_id=1, source_target_pairs={{0,1},{1,0},{2,3},{3,2},{4,5},{5,4},{6,7},{7,6},{8,9},{9,8},{10,11... | collective-permute-start | bytes 1769480 | tf_op jit(solution)/shard_map/ppermute | solution.py:230
  64.6 1.9 %collective-permute-start.13 = (f32[8,384]{1,0:T(8,128)S(1)}, f32[8,384]{1,0:T(8,128)S(1)}, u32[]{:S(2)}, u32[]{:S(2)}) collective-permute-start(f32[8,384]{1,0:T(8,128)S(1)} %get-tuple-element.58.s0), channel_id=1, source_target_pairs={{0,1},{1,0},{2,3},{3,2},{4,5},{5,4},{6,7},{7,6},{8,9},{9,8},{10,11... | collective-permute-start | bytes 36872 | tf_op jit(solution)/shard_map/ppermute | solution.py:230
  68.1 30.7 %all-to-all-start.2 = ((bf16[32,8,1280]{2,1,0:T(8,128)(2,1)}), bf16[32,8,1280]{2,1,0:T(8,128)(2,1)S(1)}, u32[]{:S(2)}, u32[]{:S(2)}) async-start(bf16[32,8,1280]{2,1,0:T(8,128)(2,1)} %join.1), calls=%async_computation.2 | async-start | bytes 1310720 | tf_op jit(solution)/shard_map/all_to_all | solution.py:328
  78.9 5.2 %collective-permute-start.14 = (bf16[3,64,384]{2,1,0:T(8,128)(2,1)S(1)}, bf16[3,64,384]{2,1,0:T(8,128)(2,1)S(1)}, u32[]{:S(2)}, u32[]{:S(2)}) collective-permute-start(bf16[3,64,384]{2,1,0:T(8,128)(2,1)S(1)} %get-tuple-element.70), channel_id=1, source_target_pairs={{0,1},{1,0},{2,3},{3,2},{4,5},{5,4},{6,7},{7,6},{8,9},{9,8},{10,11... | collective-permute-start | bytes 442376 | tf_op jit(solution)/shard_map/ppermute | solution.py:230
  79.0 6.7 %collective-permute-start.15 = (bf16[3,64,384]{2,1,0:T(8,128)(2,1)S(1)}, bf16[3,64,384]{2,1,0:T(8,128)(2,1)S(1)}, u32[]{:S(2)}, u32[]{:S(2)}) collective-permute-start(bf16[3,64,384]{2,1,0:T(8,128)(2,1)S(1)} %get-tuple-element.71), channel_id=1, source_target_pairs={{0,2},{1,3},{2,0},{3,1},{4,6},{5,7},{6,4},{7,5},{8,10},{9,11},{10,... | collective-permute-start | bytes 442376 | tf_op jit(solution)/shard_map/ppermute | solution.py:230
  79.1 8.9 %collective-permute-start.16 = (bf16[3,64,384]{2,1,0:T(8,128)(2,1)S(1)}, bf16[3,64,384]{2,1,0:T(8,128)(2,1)S(1)}, u32[]{:S(2)}, u32[]{:S(2)}) collective-permute-start(bf16[3,64,384]{2,1,0:T(8,128)(2,1)S(1)} %get-tuple-element.72), channel_id=1, source_target_pairs={{0,3},{1,2},{2,1},{3,0},{4,7},{5,6},{6,5},{7,4},{8,11},{9,10},{10,... | collective-permute-start | bytes 442376 | tf_op jit(solution)/shard_map/ppermute | solution.py:230
  80.9 11.9 %collective-permute-start.17 = (bf16[3,64,384]{2,1,0:T(8,128)(2,1)S(1)}, bf16[3,64,384]{2,1,0:T(8,128)(2,1)S(1)}, u32[]{:S(2)}, u32[]{:S(2)}) collective-permute-start(bf16[3,64,384]{2,1,0:T(8,128)(2,1)S(1)} %get-tuple-element.73), channel_id=1, source_target_pairs={{0,4},{1,5},{2,6},{3,7},{4,0},{5,1},{6,2},{7,3},{8,12},{9,13},{10,... | collective-permute-start | bytes 442376 | tf_op jit(solution)/shard_map/ppermute | solution.py:230
  81.8 20.4 %collective-permute-start.19 = (bf16[3,64,384]{2,1,0:T(8,128)(2,1)S(1)}, bf16[3,64,384]{2,1,0:T(8,128)(2,1)S(1)}, u32[]{:S(2)}, u32[]{:S(2)}) collective-permute-start(bf16[3,64,384]{2,1,0:T(8,128)(2,1)S(1)} %get-tuple-element.81), channel_id=1, source_target_pairs={{0,5},{1,4},{2,7},{3,6},{4,1},{5,0},{6,3},{7,2},{8,13},{9,12},{10,... | collective-permute-start | bytes 442376 | tf_op jit(solution)/shard_map/ppermute | solution.py:230
  84.1 21.5 %collective-permute-start.20 = (bf16[3,64,384]{2,1,0:T(8,128)(2,1)S(1)}, bf16[3,64,384]{2,1,0:T(8,128)(2,1)S(1)}, u32[]{:S(2)}, u32[]{:S(2)}) collective-permute-start(bf16[3,64,384]{2,1,0:T(8,128)(2,1)S(1)} %get-tuple-element.82), channel_id=1, source_target_pairs={{0,6},{1,7},{2,4},{3,5},{4,2},{5,3},{6,0},{7,1},{8,14},{9,15},{10,... | collective-permute-start | bytes 442376 | tf_op jit(solution)/shard_map/ppermute | solution.py:230
  85.7 20.3 %collective-permute-start.21 = (bf16[3,64,384]{2,1,0:T(8,128)(2,1)S(1)}, bf16[3,64,384]{2,1,0:T(8,128)(2,1)S(1)}, u32[]{:S(2)}, u32[]{:S(2)}) collective-permute-start(bf16[3,64,384]{2,1,0:T(8,128)(2,1)S(1)} %get-tuple-element.83), channel_id=1, source_target_pairs={{0,7},{1,6},{2,5},{3,4},{4,3},{5,2},{6,1},{7,0},{8,15},{9,14},{10,... | collective-permute-start | bytes 442376 | tf_op jit(solution)/shard_map/ppermute | solution.py:230
  99.3 9.2 %collective-permute-start.18 = (f32[8,1536]{1,0:T(8,128)S(1)}, f32[8,1536]{1,0:T(8,128)S(1)}, u32[]{:S(2)}, u32[]{:S(2)}) collective-permute-start(f32[8,1536]{1,0:T(8,128)S(1)} %get-tuple-element.75), channel_id=1, source_target_pairs={{0,0},{32,2},{64,4},{96,6},{128,32},{160,34},{192,36},{224,38},{2,... | collective-permute-start | bytes 147464 | tf_op jit(solution)/shard_map/ppermute | solution.py:332
  101.3 7.3 %collective-permute-start.22 = (f32[16,128]{1,0:T(8,128)S(1)}, f32[16,128]{1,0:T(8,128)S(1)}, u32[]{:S(2)}, u32[]{:S(2)}) collective-permute-start(f32[16,128]{1,0:T(8,128)S(1)} %get-tuple-element.86.o0), channel_id=1, source_target_pairs={{0,2},{2,0},{4,6},{6,4},{1,3},{3,1},{5,7},{7,5},{8,10},{10,8},{12,... | collective-permute-start | bytes 24584 | tf_op jit(solution)/shard_map/ppermute | solution.py:230
  102.2 6.4 %collective-permute-start.23 = (f32[16,128]{1,0:T(8,128)S(1)}, f32[16,128]{1,0:T(8,128)S(1)}, u32[]{:S(2)}, u32[]{:S(2)}) collective-permute-start(f32[16,128]{1,0:T(8,128)S(1)} %get-tuple-element.86.o0), channel_id=1, source_target_pairs={{0,4},{2,6},{4,0},{6,2},{1,5},{3,7},{5,1},{7,3},{8,12},{10,14},{12... | collective-permute-start | bytes 24584 | tf_op jit(solution)/shard_map/ppermute | solution.py:230
  105.6 4.9 %collective-permute-start.24 = (f32[16,128]{1,0:T(8,128)S(1)}, f32[16,128]{1,0:T(8,128)S(1)}, u32[]{:S(2)}, u32[]{:S(2)}) collective-permute-start(f32[16,128]{1,0:T(8,128)S(1)} %get-tuple-element.86.o0), channel_id=1, source_target_pairs={{0,6},{2,4},{4,2},{6,0},{1,7},{3,5},{5,3},{7,1},{8,14},{10,12},{12... | collective-permute-start | bytes 24584 | tf_op jit(solution)/shard_map/ppermute | solution.py:230
